TPU v7x, 32 devices: a whole 2x2x4 slice. The times are simulated.
32 devices in a mesh: sweep: 4 (over x, core), cross: 8 (over z, y).
Axes of the slice: x: 2, y: 2, z: 4, core: 2. Of those that a mesh axis runs over, the one named last changes fastest.
Arguments:
- right_sides: bfloat16 [16, 64, 32, 135], P('sweep', 'cross'), may hold values from -0.099609375 to 0.099609375
- initial: bfloat16 [16, 64, 32, 135], P('sweep', 'cross'), may hold values from -0.099609375 to 0.099609375
- inverse_blocks: bfloat16 [16, 64, 135, 135], P('sweep', 'cross'), may hold values from -0.5 to 0.5
- couplings: bfloat16 [16, 64, 6, 45, 135], P('sweep', 'cross'), may hold values from -0.875 to 0.875
- neighbours: int32 [64, 4], P('cross'), may hold values from 0 to 63, as said below
Outputs:
- result: bfloat16 [16, 64, 32, 135], P('sweep', 'cross')
Inputs may be any that keep to these rules, and one draw needn't show every extreme that they name: `neighbours`: columns are numbered device by device along cross, 8 to a device. For a column with local index l on cross device k: face b- names column l of device k - 1 and face b+ column l of device k + 1 (cyclically); face c- names a column of device k - 1 or k, face c+ one of device k or k + 1.
All inputs are finite; a program needn't handle non-finite values.
Results may differ from a plain program's by a relative error of at most 0.029.
Values may be sent and summed in bfloat16 or wider, within the bound.
No kernel may reach another device: no remote copies, remote signals or barrier semaphores. Data moves between devices by JAX's collectives and lax.ppermute only.
A program may use at most 64 MiB of HBM per device.

v0:
```python
import jax
import jax.numpy as jnp
from jax import lax
from jax.sharding import PartitionSpec as P


def from_behind(shard, axis, by):
    peers = lax.axis_size(axis)
    return lax.ppermute(shard, axis, [(i, (i + by) % peers) for i in range(peers)])


def passed_along(block, axis, distance):
    devices = range(lax.axis_size(axis))
    route = [(i - distance, i) for i in devices if i - distance in devices]
    return lax.ppermute(block, axis, route)


def selector(axis_place, which):
    slot = jnp.arange(45, dtype=jnp.int32)
    variable = slot // 9
    first = slot // 3 % 3
    second = slot % 3
    if axis_place == 0:
        target = variable * 27 + which * 9 + first * 3 + second
    elif axis_place == 1:
        target = variable * 27 + first * 9 + which * 3 + second
    else:
        target = variable * 27 + first * 9 + second * 3 + which
    unknown = jnp.arange(135, dtype=jnp.int32)[:, None]
    return (unknown == target[None, :]).astype(jnp.bfloat16)


def face_trace(field, axis_place, which):
    return jnp.dot(field, selector(axis_place, which), preferred_element_type=jnp.float32).astype(
        jnp.bfloat16
    )


def pair_trace(field, which):
    table = jnp.concatenate([selector(1, which), selector(2, which)], 1)
    return jnp.dot(field, table, preferred_element_type=jnp.float32).astype(jnp.bfloat16)


def apply_faces(coupling, traces):
    return jnp.einsum("pcrt,pcti->pcri", traces, coupling, preferred_element_type=jnp.float32)


def cross_terms(field, couplings, neighbours):
    width = field.shape[1]
    place = lax.axis_index("cross")
    all_columns = width * lax.axis_size("cross")
    lower_which = (neighbours - (place - 1) * width) % all_columns
    total = jnp.zeros(field.shape, jnp.float32)
    toward_upper = pair_trace(field, 2)
    toward_lower = pair_trace(field, 0)
    from_lower = from_behind(toward_upper, "cross", 1)
    from_upper = from_behind(toward_lower, "cross", -1)
    upper_which = (neighbours - place * width) % all_columns
    pools = (
        (jnp.concatenate([from_lower[..., :45], toward_upper[..., :45]], 1), lower_which[:, 0]),
        (jnp.concatenate([toward_lower[..., :45], from_upper[..., :45]], 1), upper_which[:, 1]),
        (jnp.concatenate([from_lower[..., 45:], toward_upper[..., 45:]], 1), lower_which[:, 2]),
        (jnp.concatenate([toward_lower[..., 45:], from_upper[..., 45:]], 1), upper_which[:, 3]),
    )
    for face in range(4):
        gathered = jnp.take(pools[face][0], pools[face][1], axis=1)
        total = total + apply_faces(couplings[:, :, 2 + face], gathered)
    return total


def plane_chain(base, inverse, coupling, incoming, outgoing_face, backwards):
    count = base.shape[0]
    order = list(range(count))
    if backwards:
        order = order[::-1]
    solved_planes = {}
    trace_in = incoming
    for plane in order:
        term = jnp.einsum(
            "crt,cti->cri", trace_in, coupling[plane], preferred_element_type=jnp.float32
        )
        residue = (base[plane] - term).astype(jnp.bfloat16)
        solved = jnp.einsum(
            "crj,cij->cri", residue, inverse[plane], preferred_element_type=jnp.float32
        ).astype(jnp.bfloat16)
        solved_planes[plane] = solved
        trace_in = face_trace(solved, 0, outgoing_face)
    return (jnp.stack([solved_planes[plane] for plane in range(count)]), trace_in)


def chain_sections(base, inverse, coupling, outgoing_face, backwards, sender):
    sections = lax.axis_size("sweep")
    incoming = jnp.zeros((base.shape[1], base.shape[2], 45), jnp.bfloat16)
    solved = None
    for section in range(sections):
        solved, leaving = plane_chain(base, inverse, coupling, incoming, outgoing_face, backwards)
        if section + 1 < sections:
            incoming = sender(leaving)
    return (solved, incoming)


def run_chain(base, inverse, coupling, outgoing_face, backwards, direction):

    def sender(outgoing):
        return passed_along(outgoing, "sweep", direction)

    return chain_sections(base, inverse, coupling, outgoing_face, backwards, sender)


def local(right_sides, initial, inverse_blocks, couplings, neighbours):
    above = passed_along(face_trace(initial[0], 0, 0), "sweep", -1)
    upper_traces = jnp.concatenate([face_trace(initial[1:], 0, 0), above[None]], 0)
    forward_base = right_sides.astype(jnp.float32) - cross_terms(initial, couplings, neighbours)
    forward_base = forward_base - apply_faces(couplings[:, :, 1], upper_traces)
    middle, below = run_chain(forward_base, inverse_blocks, couplings[:, :, 0], 2, False, 1)
    lower_traces = jnp.concatenate([below[None], face_trace(middle[:-1], 0, 2)], 0)
    backward_base = right_sides.astype(jnp.float32) - cross_terms(middle, couplings, neighbours)
    backward_base = backward_base - apply_faces(couplings[:, :, 0], lower_traces)
    result, _unused = run_chain(backward_base, inverse_blocks, couplings[:, :, 1], 0, True, -1)
    return result


def solution(mesh):
    return jax.shard_map(
        local,
        mesh=mesh,
        in_specs=(
            P("sweep", "cross", None, None),
            P("sweep", "cross", None, None),
            P("sweep", "cross", None, None),
            P("sweep", "cross", None, None, None),
            P("cross", None),
        ),
        out_specs=P("sweep", "cross", None, None),
        check_vma=False,
    )
```

profile of v0, /device:TPU:1, one launch (start us, length us, event | category | flops | bytes accessed | tf_op | source)
XLA Modules:
  0.0 187.6 jit_solution(8205950323143776815)
XLA Ops:
  1.5 2.1 %collective-permute-start = (bf16[4,8,32,90]{3,2,1,0:T(8,128)(2,1)S(1)}, bf16[4,8,32,90]{3,2,1,0:T(8,128)(2,1)}, u32[]{:S(2)}, u32[]{:S(2)}) collective-permute-start(bf16[4,8,32,90]{3,2,1,0:T(8,128)(2,1)S(1)} %fusion.2), channel_id=1, source_target_pairs={{0,1},{1,2},{2,3},{3,4},{4,5},{5,6},{6,7},{7,0},{8,9},{9,10},{10,1... | collective-permute-start | bytes 552968 | tf_op jit(solution)/shard_map/ppermute | solution.py:9
  3.7 2.1 %fusion.3 = bf16[4,8,32,90]{3,2,1,0:T(8,128)(2,1)} fusion(bf16[4,8,32,135]{3,2,1,0:T(8,128)(2,1)} %param.8, pred[135,45]{1,0:T(8,128)(4,1)S(1)} %get-tuple-element.56, pred[135,45]{1,0:T(8,128)(4,1)S(1)} %get-tuple-element.57), kind=kOutput, calls=%fused_computation.57 | convolution fusion | flops 24987510 | bytes 472950 | tf_op jit(solution)/shard_map/dot_general | solution.py:41
  5.8 3.1 %collective-permute-start.1 = (bf16[4,8,32,90]{3,2,1,0:T(8,128)(2,1)}, bf16[4,8,32,90]{3,2,1,0:T(8,128)(2,1)}, u32[]{:S(2)}, u32[]{:S(2)}) collective-permute-start(bf16[4,8,32,90]{3,2,1,0:T(8,128)(2,1)} %fusion.3), channel_id=1, source_target_pairs={{0,7},{1,0},{2,1},{3,2},{4,3},{5,4},{6,5},{7,6},{8,15},{9,8},{10,9... | collective-permute-start | bytes 552968 | tf_op jit(solution)/shard_map/ppermute | solution.py:9
  8.9 1.8 fusion.87
  10.7 2.8 %collective-permute-start.2 = (bf16[8,32,45]{2,1,0:T(8,128)(2,1)}, bf16[8,32,45]{2,1,0:T(8,128)(2,1)S(1)}, u32[]{:S(2)}, u32[]{:S(2)}) collective-permute-start(bf16[8,32,45]{2,1,0:T(8,128)(2,1)} %fusion.87), channel_id=1, source_target_pairs={{8,0},{16,8},{24,16},{9,1},{17,9},{25,17},{10,2},{18,10},{26,18},{... | collective-permute-start | bytes 69128 | tf_op jit(solution)/shard_map/ppermute | solution.py:15
  14.4 1.9 %fusion.242 = (bf16[4,8,32,45]{3,2,1,0:T(8,128)(2,1)}, bf16[4,8,32,45]{3,2,1,0:T(8,128)(2,1)}) fusion(bf16[4,8,32,90]{3,2,1,0:T(8,128)(2,1)} %fusion.3), kind=kLoop, calls=%fused_computation.379 | loop fusion | bytes 368640 | tf_op jit(solution)/shard_map/slice | solution.py:63
  16.3 3.7 %fusion.236 = (bf16[4,8,1,45,135]{4,1,3,2,0:T(8,128)(2,1)}, bf16[4,8,1,45,135]{4,1,3,2,0:T(8,128)(2,1)}, bf16[4,8,1,45,135]{4,1,3,2,0:T(8,128)(2,1)S(1)}, bf16[4...) fusion(bf16[4,8,6,45,135]{4,1,3,2,0:T(8,128)(2,1)} %param.10), kind=kLoop, calls=%fused_computation.373 | loop fusion | bytes 4665600 | tf_op jit(solution)/shard_map/slice | solution.py:115
  20.0 2.8 %slice_bitcast_fusion.16 = (bf16[8,45,135]{2,0,1:T(8,128)(2,1)S(1)}, bf16[8,45,135]{2,0,1:T(8,128)(2,1)}, bf16[8,45,135]{2,0,1:T(8,128)(2,1)}, bf16[8,45,135]{2,...) fusion(bf16[4,8,6,45,135]{4,1,3,2,0:T(8,128)(2,1)} %param.10), kind=kLoop, calls=%fused_computation.239 | loop fusion | bytes 1555200 | tf_op jit(solution)/shard_map/squeeze | solution.py:80
  23.6 3.1 %fusion.237 = (bf16[1,8,135,135]{3,1,2,0:T(8,128)(2,1)}, bf16[1,8,135,135]{3,1,2,0:T(8,128)(2,1)}, bf16[1,8,135,135]{3,1,2,0:T(8,128)(2,1)}, bf16[1,8,135,135]{3,1,2,0:T(8,128)(2,1)}) fusion(bf16[4,8,135,135]{3,1,2,0:T(8,128)(2,1)} %param.9), kind=kLoop, calls=%fused_computation.374 | loop fusion | bytes 2332800 | tf_op jit(solution)/shard_map/slice | solution.py:84
  27.6 1.9 %fusion.244 = (bf16[4,8,32,45]{3,2,1,0:T(8,128)(2,1)}, bf16[4,8,32,45]{3,2,1,0:T(8,128)(2,1)S(1)}) fusion(bf16[4,8,32,90]{3,2,1,0:T(8,128)(2,1)} %collective-permute-done), kind=kLoop, calls=%fused_computation.381 | loop fusion | bytes 368640 | tf_op jit(solution)/shard_map/slice | solution.py:62
  30.4 1.6 gather_fusion
  32.1 1.9 %fusion.243 = (bf16[4,8,32,45]{3,2,1,0:T(8,128)(2,1)}, bf16[4,8,32,45]{3,2,1,0:T(8,128)(2,1)S(1)}) fusion(bf16[4,8,32,90]{3,2,1,0:T(8,128)(2,1)} %collective-permute-done.1), kind=kLoop, calls=%fused_computation.380 | loop fusion | bytes 368640 | tf_op jit(solution)/shard_map/slice | solution.py:63
  34.0 1.8 pad_maximum_fusion.1
  35.8 2.3 %gather_fusion.1 = bf16[8,4,32,45]{3,2,1,0:T(8,128)(2,1)} fusion(bf16[4,16,32,45]{3,2,1,0:T(8,128)(2,1)} %pad_maximum_fusion.1, s32[1024]{0:T(1024)S(1)} %pad_clamp_fusion.2), kind=kCustom, calls=%fused_computation.1.clone | custom fusion | bytes 184352 | tf_op jit(solution)/shard_map/jit(_take)/gather | solution.py:66
  38.2 1.9 %pad_maximum_fusion.2 = bf16[4,16,32,45]{3,2,1,0:T(8,128)(2,1)} fusion(bf16[4,8,32,45]{3,2,1,0:T(8,128)(2,1)} %get-tuple-element.46, bf16[4,8,32,45]{3,2,1,0:T(8,128)(2,1)} %get-tuple-element.44), kind=kLoop, calls=%fused_computation.195 | loop fusion | flops 92160 | bytes 368640 | tf_op jit(solution)/shard_map/concatenate | solution.py:62
  40.1 2.3 %gather_fusion.2 = bf16[8,4,32,45]{3,2,1,0:T(8,128)(2,1)} fusion(bf16[4,16,32,45]{3,2,1,0:T(8,128)(2,1)} %pad_maximum_fusion.2, s32[1024]{0:T(1024)S(1)} %pad_clamp_fusion.1), kind=kCustom, calls=%fused_computation.2.clone | custom fusion | bytes 184352 | tf_op jit(solution)/shard_map/jit(_take)/gather | solution.py:66
  42.4 1.9 %pad_maximum_fusion.3 = bf16[4,16,32,45]{3,2,1,0:T(8,128)(2,1)} fusion(bf16[4,8,32,45]{3,2,1,0:T(8,128)(2,1)} %get-tuple-element.42, bf16[4,8,32,45]{3,2,1,0:T(8,128)(2,1)} %get-tuple-element.40), kind=kLoop, calls=%fused_computation.196 | loop fusion | flops 92160 | bytes 368640 | tf_op jit(solution)/shard_map/concatenate | solution.py:63
  44.3 2.3 %gather_fusion.3 = bf16[8,4,32,45]{3,2,1,0:T(8,128)(2,1)} fusion(bf16[4,16,32,45]{3,2,1,0:T(8,128)(2,1)} %pad_maximum_fusion.3, s32[1024]{0:T(1024)S(1)} %pad_clamp_fusion), kind=kCustom, calls=%fused_computation.3.clone | custom fusion | bytes 184352 | tf_op jit(solution)/shard_map/jit(_take)/gather | solution.py:66
  51.9 1.8 fusion.5
  53.7 1.5 fusion.85
  55.2 1.8 fusion.6
  56.9 1.5 fusion.84
  58.4 1.8 fusion.7
  60.2 2.1 %fusion.83 = bf16[8,32,45]{2,1,0:T(8,128)(2,1)} fusion(bf16[8,32,135]{2,1,0:T(8,128)(2,1)} %fusion.7, bf16[1,8,135,135]{3,1,2,0:T(8,128)(2,1)} %get-tuple-element.28, s32[45]{0:T(128)} %add_add_fusion), kind=kOutput, calls=%fused_computation.169 | convolution fusion | flops 12493755 | bytes 383940 | tf_op jit(solution)/shard_map/dot_general | solution.py:34
  62.3 3.1 %collective-permute-start.3 = (bf16[8,32,45]{2,1,0:T(8,128)(2,1)}, bf16[8,32,45]{2,1,0:T(8,128)(2,1)S(1)}, u32[]{:S(2)}, u32[]{:S(2)}) collective-permute-start(bf16[8,32,45]{2,1,0:T(8,128)(2,1)} %fusion.83), channel_id=1, source_target_pairs={{0,8},{8,16},{16,24},{1,9},{9,17},{17,25},{2,10},{10,18},{18,26},{... | collective-permute-start | bytes 69128 | tf_op jit(solution)/shard_map/ppermute | solution.py:15
  65.5 1.6 collective-permute-done.3
  67.1 1.7 fusion.8
  70.3 1.8 fusion.9
  73.6 1.8 fusion.10
  76.8 1.8 fusion.11
  78.5 2.1 %fusion.79 = bf16[8,32,45]{2,1,0:T(8,128)(2,1)} fusion(bf16[8,32,135]{2,1,0:T(8,128)(2,1)} %fusion.11, bf16[1,8,135,135]{3,1,2,0:T(8,128)(2,1)} %get-tuple-element.28, s32[45]{0:T(128)} %add_add_fusion), kind=kOutput, calls=%fused_computation.165 | convolution fusion | flops 12493755 | bytes 383940 | tf_op jit(solution)/shard_map/dot_general | solution.py:34
  80.7 4.2 %collective-permute-start.4 = (bf16[8,32,45]{2,1,0:T(8,128)(2,1)}, bf16[8,32,45]{2,1,0:T(8,128)(2,1)S(1)}, u32[]{:S(2)}, u32[]{:S(2)}) collective-permute-start(bf16[8,32,45]{2,1,0:T(8,128)(2,1)} %fusion.79), channel_id=1, source_target_pairs={{0,8},{8,16},{16,24},{1,9},{9,17},{17,25},{2,10},{10,18},{18,26},{... | collective-permute-start | bytes 69128 | tf_op jit(solution)/shard_map/ppermute | solution.py:15
  84.8 1.6 collective-permute-done.4
  86.5 1.7 fusion.12
  89.7 1.8 fusion.13
  92.9 1.8 fusion.14
  96.2 1.8 fusion.15
  97.9 2.1 %fusion.75 = bf16[8,32,45]{2,1,0:T(8,128)(2,1)} fusion(bf16[8,32,135]{2,1,0:T(8,128)(2,1)} %fusion.15, bf16[1,8,135,135]{3,1,2,0:T(8,128)(2,1)} %get-tuple-element.28, s32[45]{0:T(128)} %add_add_fusion), kind=kOutput, calls=%fused_computation.161 | convolution fusion | flops 12493755 | bytes 383940 | tf_op jit(solution)/shard_map/dot_general | solution.py:34
  100.1 4.1 %collective-permute-start.5 = (bf16[8,32,45]{2,1,0:T(8,128)(2,1)}, bf16[8,32,45]{2,1,0:T(8,128)(2,1)S(1)}, u32[]{:S(2)}, u32[]{:S(2)}) collective-permute-start(bf16[8,32,45]{2,1,0:T(8,128)(2,1)} %fusion.75), channel_id=1, source_target_pairs={{0,8},{8,16},{16,24},{1,9},{9,17},{17,25},{2,10},{10,18},{18,26},{... | collective-permute-start | bytes 69128 | tf_op jit(solution)/shard_map/ppermute | solution.py:15
  104.2 1.6 collective-permute-done.5
  105.8 2.2 %convolution_convert_fusion.25 = bf16[8,32,135]{2,1,0:T(8,128)(2,1)} fusion(bf16[8,32,45]{2,1,0:T(8,128)(2,1)S(1)} %collective-permute-done.5, f32[4,8,32,135]{3,2,1,0:T(8,128)S(1)} %convolution_subtract_fusion.1, bf16[8,45,135]{2,0,1:T(8,128)(2,1)} %get-tuple-element.16, bf16[1,8,135,135]{3,1,2,0:T(8,128)(2,1)} %get-tuple-element.31), kind=kOutput, calls=%fused_computation.110 | convolution fusion | flops 12545280 | bytes 785600 | tf_op jit(solution)/shard_map/crj,cij->cri/dot_general | solution.py:83
  108.0 1.8 convolution_convert_fusion.43
  109.8 2.2 %convolution_convert_fusion.24 = bf16[8,32,135]{2,1,0:T(8,128)(2,1)} fusion(bf16[8,32,45]{2,1,0:T(8,128)(2,1)} %convolution_convert_fusion.43, f32[4,8,32,135]{3,2,1,0:T(8,128)S(1)} %convolution_subtract_fusion.1, bf16[8,45,135]{2,0,1:T(8,128)(2,1)} %get-tuple-element.15, bf16[1,8,135,135]{3,1,2,0:T(8,128)(2,1)} %get-tuple-element.30), kind=kOutput, calls=%fused_computation.109 | convolution fusion | flops 12545280 | bytes 743104 | tf_op jit(solution)/shard_map/crj,cij->cri/dot_general | solution.py:83
  112.0 1.8 convolution_convert_fusion.42
  113.8 2.2 %convolution_convert_fusion.23 = bf16[8,32,135]{2,1,0:T(8,128)(2,1)} fusion(bf16[8,32,45]{2,1,0:T(8,128)(2,1)} %convolution_convert_fusion.42, f32[4,8,32,135]{3,2,1,0:T(8,128)S(1)} %convolution_subtract_fusion.1, bf16[8,45,135]{2,0,1:T(8,128)(2,1)} %get-tuple-element.18, bf16[1,8,135,135]{3,1,2,0:T(8,128)(2,1)} %get-tuple-element.29), kind=kOutput, calls=%fused_computation.108 | convolution fusion | flops 12545280 | bytes 743104 | tf_op jit(solution)/shard_map/crj,cij->cri/dot_general | solution.py:83
  116.0 1.8 convolution_convert_fusion.41
  117.8 2.2 %fusion.49 = bf16[1,8,32,135]{3,2,1,0:T(8,128)(2,1)} fusion(bf16[8,32,45]{2,1,0:T(8,128)(2,1)} %convolution_convert_fusion.41, f32[4,8,32,135]{3,2,1,0:T(8,128)S(1)} %convolution_subtract_fusion.1, bf16[8,45,135]{2,0,1:T(8,128)(2,1)} %get-tuple-element.17, bf16[1,8,135,135]{3,1,2,0:T(8,128)(2,1)} %get-tuple-element.28), kind=kOutput, calls=%fused_computation.135 | convolution fusion | flops 12545280 | bytes 743104 | tf_op jit(solution)/shard_map/crj,cij->cri/dot_general | solution.py:83
  120.0 1.5 convolution_convert_fusion
  121.6 1.6 collective-permute-start.7
  126.6 1.6 convolution_convert_fusion.4
  130.0 2.5 %gather_fusion.7 = bf16[8,4,32,45]{3,2,1,0:T(8,128)(2,1)} fusion(bf16[4,16,32,45]{3,2,1,0:T(8,128)(2,1)} %pad_maximum_fusion.8, s32[1024]{0:T(1024)} %copy-done.27), kind=kCustom, calls=%fused_computation.7.clone | custom fusion | bytes 184352 | tf_op jit(solution)/shard_map/jit(_take)/gather | solution.py:66
  132.5 2.5 %collective-permute-done.6 = bf16[4,8,32,90]{3,2,1,0:T(8,128)(2,1)} collective-permute-done((bf16[4,8,32,90]{3,2,1,0:T(8,128)(2,1)S(1)}, bf16[4,8,32,90]{3,2,1,0:T(8,128)(2,1)}, u32[]{:S(2)}, u32[]{:S(2)}) %collective-permute-start.6) | collective-permute-done | bytes 184352 | tf_op jit(solution)/shard_map/ppermute | solution.py:9
  136.2 1.9 pad_maximum_fusion.7
  138.0 2.5 %gather_fusion.6 = bf16[8,4,32,45]{3,2,1,0:T(8,128)(2,1)} fusion(bf16[4,16,32,45]{3,2,1,0:T(8,128)(2,1)} %pad_maximum_fusion.7, s32[1024]{0:T(1024)} %copy-done.26), kind=kCustom, calls=%fused_computation.6.clone | custom fusion | bytes 184352 | tf_op jit(solution)/shard_map/jit(_take)/gather | solution.py:66
  140.5 1.9 %pad_maximum_fusion.6 = bf16[4,16,32,45]{3,2,1,0:T(8,128)(2,1)} fusion(bf16[4,8,32,45]{3,2,1,0:T(8,128)(2,1)} %get-tuple-element.35, bf16[4,8,32,45]{3,2,1,0:T(8,128)(2,1)} %get-tuple-element.33), kind=kLoop, calls=%fused_computation.199 | loop fusion | flops 92160 | bytes 368640 | tf_op jit(solution)/shard_map/concatenate | solution.py:61
  142.4 2.5 %gather_fusion.5 = bf16[8,4,32,45]{3,2,1,0:T(8,128)(2,1)} fusion(bf16[4,16,32,45]{3,2,1,0:T(8,128)(2,1)} %pad_maximum_fusion.6, s32[1024]{0:T(1024)} %copy-done.25), kind=kCustom, calls=%fused_computation.5.clone | custom fusion | bytes 184352 | tf_op jit(solution)/shard_map/jit(_take)/gather | solution.py:66
  144.9 1.8 pad_maximum_fusion.5
  146.7 1.6 gather_fusion.4
  155.9 1.9 %collective-permute-start.8 = (bf16[8,32,45]{2,1,0:T(8,128)(2,1)S(1)}, bf16[8,32,45]{2,1,0:T(8,128)(2,1)S(1)}, u32[]{:S(2)}, u32[]{:S(2)}) collective-permute-start(bf16[8,32,45]{2,1,0:T(8,128)(2,1)S(1)} %fusion.71), channel_id=1, source_target_pairs={{8,0},{16,8},{24,16},{9,1},{17,9},{25,17},{10,2},{18,10},{26,18},{... | collective-permute-start | bytes 69128 | tf_op jit(solution)/shard_map/ppermute | solution.py:15
  157.8 4.3 %collective-permute-done.8 = bf16[8,32,45]{2,1,0:T(8,128)(2,1)S(1)} collective-permute-done((bf16[8,32,45]{2,1,0:T(8,128)(2,1)S(1)}, bf16[8,32,45]{2,1,0:T(8,128)(2,1)S(1)}, u32[]{:S(2)}, u32[]{:S(2)}) %collective-permute-start.8) | collective-permute-done | bytes 23072 | tf_op jit(solution)/shard_map/ppermute | solution.py:15
  166.6 1.9 %collective-permute-start.9 = (bf16[8,32,45]{2,1,0:T(8,128)(2,1)S(1)}, bf16[8,32,45]{2,1,0:T(8,128)(2,1)S(1)}, u32[]{:S(2)}, u32[]{:S(2)}) collective-permute-start(bf16[8,32,45]{2,1,0:T(8,128)(2,1)S(1)} %fusion.67), channel_id=1, source_target_pairs={{8,0},{16,8},{24,16},{9,1},{17,9},{25,17},{10,2},{18,10},{26,18},{... | collective-permute-start | bytes 69128 | tf_op jit(solution)/shard_map/ppermute | solution.py:15
  168.6 3.7 %collective-permute-done.9 = bf16[8,32,45]{2,1,0:T(8,128)(2,1)S(1)} collective-permute-done((bf16[8,32,45]{2,1,0:T(8,128)(2,1)S(1)}, bf16[8,32,45]{2,1,0:T(8,128)(2,1)S(1)}, u32[]{:S(2)}, u32[]{:S(2)}) %collective-permute-start.9) | collective-permute-done | bytes 23072 | tf_op jit(solution)/shard_map/ppermute | solution.py:15
  176.7 1.9 %collective-permute-start.10 = (bf16[8,32,45]{2,1,0:T(8,128)(2,1)S(1)}, bf16[8,32,45]{2,1,0:T(8,128)(2,1)S(1)}, u32[]{:S(2)}, u32[]{:S(2)}) collective-permute-start(bf16[8,32,45]{2,1,0:T(8,128)(2,1)S(1)} %fusion.63), channel_id=1, source_target_pairs={{8,0},{16,8},{24,16},{9,1},{17,9},{25,17},{10,2},{18,10},{26,18},{... | collective-permute-start | bytes 69128 | tf_op jit(solution)/shard_map/ppermute | solution.py:15
  178.6 3.7 %collective-permute-done.10 = bf16[8,32,45]{2,1,0:T(8,128)(2,1)S(1)} collective-permute-done((bf16[8,32,45]{2,1,0:T(8,128)(2,1)S(1)}, bf16[8,32,45]{2,1,0:T(8,128)(2,1)S(1)}, u32[]{:S(2)}, u32[]{:S(2)}) %collective-permute-start.10) | collective-permute-done | bytes 23072 | tf_op jit(solution)/shard_map/ppermute | solution.py:15
  (157 shorter events, 46.8 us)
Async XLA Ops:
  1.5 26.1 %collective-permute-start = (bf16[4,8,32,90]{3,2,1,0:T(8,128)(2,1)S(1)}, bf16[4,8,32,90]{3,2,1,0:T(8,128)(2,1)}, u32[]{:S(2)}, u32[]{:S(2)}) collective-permute-start(bf16[4,8,32,90]{3,2,1,0:T(8,128)(2,1)S(1)} %fusion.2), channel_id=1, source_target_pairs={{0,1},{1,2},{2,3},{3,4},{4,5},{5,6},{6,7},{7,0},{8,9},{9,10},{10,1... | collective-permute-start | bytes 552968 | tf_op jit(solution)/shard_map/ppermute | solution.py:9
  3.7 16.3 %copy-start.23 = (pred[135,45]{1,0:T(8,128)(4,1)}, pred[135,45]{1,0:T(8,128)(4,1)S(1)}, u32[]{:S(2)}) copy-start(pred[135,45]{1,0:T(8,128)(4,1)S(1)} %get-tuple-element.56) | copy-start | bytes 18229
  3.7 16.3 %copy-start.24 = (pred[135,45]{1,0:T(8,128)(4,1)}, pred[135,45]{1,0:T(8,128)(4,1)S(1)}, u32[]{:S(2)}) copy-start(pred[135,45]{1,0:T(8,128)(4,1)S(1)} %get-tuple-element.57) | copy-start | bytes 18229
  5.8 26.2 %collective-permute-start.1 = (bf16[4,8,32,90]{3,2,1,0:T(8,128)(2,1)}, bf16[4,8,32,90]{3,2,1,0:T(8,128)(2,1)}, u32[]{:S(2)}, u32[]{:S(2)}) collective-permute-start(bf16[4,8,32,90]{3,2,1,0:T(8,128)(2,1)} %fusion.3), channel_id=1, source_target_pairs={{0,7},{1,0},{2,1},{3,2},{4,3},{5,4},{6,5},{7,6},{8,15},{9,8},{10,9... | collective-permute-start | bytes 552968 | tf_op jit(solution)/shard_map/ppermute | solution.py:9
  8.9 17.7 %copy-start.28 = (s32[45]{0:T(128)}, s32[45]{0:T(128)S(1)}, u32[]{:S(2)}) copy-start(s32[45]{0:T(128)S(1)} %add_add_fusion.1) | copy-start | bytes 544
  10.7 38.6 %collective-permute-start.2 = (bf16[8,32,45]{2,1,0:T(8,128)(2,1)}, bf16[8,32,45]{2,1,0:T(8,128)(2,1)S(1)}, u32[]{:S(2)}, u32[]{:S(2)}) collective-permute-start(bf16[8,32,45]{2,1,0:T(8,128)(2,1)} %fusion.87), channel_id=1, source_target_pairs={{8,0},{16,8},{24,16},{9,1},{17,9},{25,17},{10,2},{18,10},{26,18},{... | collective-permute-start | bytes 69128 | tf_op jit(solution)/shard_map/ppermute | solution.py:15
  16.3 7.1 %copy-start.38 = (s32[8,4]{0,1:T(4,128)S(1)}, s32[8,4]{0,1:T(4,128)}, u32[]{:S(2)}) copy-start(s32[8,4]{0,1:T(4,128)} %param.11) | copy-start | bytes 388
  20.0 27.1 %copy-start = (bf16[4,8,1,45,135]{4,1,3,2,0:T(8,128)(2,1)}, bf16[4,8,1,45,135]{4,1,3,2,0:T(8,128)(2,1)S(1)}, u32[]{:S(2)}) copy-start(bf16[4,8,1,45,135]{4,1,3,2,0:T(8,128)(2,1)S(1)} %get-tuple-element.26) | copy-start | bytes 1166404
  23.4 3.2 %copy-start.10 = (bf16[4,8,32,135]{3,2,1,0:T(8,128)(2,1)S(1)}, bf16[4,8,32,135]{3,2,1,0:T(8,128)(2,1)}, u32[]{:S(2)}) copy-start(bf16[4,8,32,135]{3,2,1,0:T(8,128)(2,1)} %param.8) | copy-start | bytes 829444
  23.4 6.1 %copy-start.13 = (bf16[4,8,32,45]{3,2,1,0:T(8,128)(2,1)S(1)}, bf16[4,8,32,45]{3,2,1,0:T(8,128)(2,1)}, u32[]{:S(2)}) copy-start(bf16[4,8,32,45]{3,2,1,0:T(8,128)(2,1)} %get-tuple-element.47) | copy-start | bytes 276484
  23.4 23.3 %copy-start.30 = (pred[8]{0:T(512)(128)(4,1)}, pred[8]{0:T(512)(128)(4,1)S(1)}, u32[]{:S(2)}) copy-start(pred[8]{0:T(512)(128)(4,1)S(1)} %get-tuple-element.58) | copy-start | bytes 28
  23.4 23.6 %copy-start.34 = (pred[8]{0:T(512)(128)(4,1)}, pred[8]{0:T(512)(128)(4,1)S(1)}, u32[]{:S(2)}) copy-start(pred[8]{0:T(512)(128)(4,1)S(1)} %get-tuple-element.48) | copy-start | bytes 28
  23.5 25.0 %copy-start.32 = (pred[8]{0:T(512)(128)(4,1)}, pred[8]{0:T(512)(128)(4,1)S(1)}, u32[]{:S(2)}) copy-start(pred[8]{0:T(512)(128)(4,1)S(1)} %get-tuple-element.60) | copy-start | bytes 28
  23.5 25.4 %copy-start.36 = (pred[8]{0:T(512)(128)(4,1)}, pred[8]{0:T(512)(128)(4,1)S(1)}, u32[]{:S(2)}) copy-start(pred[8]{0:T(512)(128)(4,1)S(1)} %get-tuple-element.6) | copy-start | bytes 28
  23.5 12.3 %copy-start.25 = (s32[1024]{0:T(1024)}, s32[1024]{0:T(1024)S(1)}, u32[]{:S(2)}) copy-start(s32[1024]{0:T(1024)S(1)} %pad_clamp_fusion.2) | copy-start | bytes 12292
  23.5 16.6 %copy-start.26 = (s32[1024]{0:T(1024)}, s32[1024]{0:T(1024)S(1)}, u32[]{:S(2)}) copy-start(s32[1024]{0:T(1024)S(1)} %pad_clamp_fusion.1) | copy-start | bytes 12292
  23.6 20.8 %copy-start.27 = (s32[1024]{0:T(1024)}, s32[1024]{0:T(1024)S(1)}, u32[]{:S(2)}) copy-start(s32[1024]{0:T(1024)S(1)} %pad_clamp_fusion) | copy-start | bytes 12292
  46.7 1.8 copy-start.16
  46.7 2.2 %copy-start.11 = (bf16[4,8,32,135]{3,2,1,0:T(8,128)(2,1)S(1)}, bf16[4,8,32,135]{3,2,1,0:T(8,128)(2,1)}, u32[]{:S(2)}) copy-start(bf16[4,8,32,135]{3,2,1,0:T(8,128)(2,1)} %param.7) | copy-start | bytes 829444
  46.7 2.2 %copy-start.17 = (bf16[8,4,32,45]{3,2,1,0:T(8,128)(2,1)S(1)}, bf16[8,4,32,45]{3,2,1,0:T(8,128)(2,1)}, u32[]{:S(2)}) copy-start(bf16[8,4,32,45]{3,2,1,0:T(8,128)(2,1)} %gather_fusion.3) | copy-start | bytes 276484
  47.1 2.2 %copy-start.9 = (bf16[4,8,1,45,135]{4,1,3,2,0:T(8,128)(2,1)S(1)}, bf16[4,8,1,45,135]{4,1,3,2,0:T(8,128)(2,1)}, u32[]{:S(2)}) copy-start(bf16[4,8,1,45,135]{4,1,3,2,0:T(8,128)(2,1)} %get-tuple-element.23) | copy-start | bytes 1166404
  47.1 2.2 %copy-start.22 = (bf16[3,8,32,45]{3,2,1,0:T(8,128)(2,1)S(1)}, bf16[3,8,32,45]{3,2,1,0:T(8,128)(2,1)}, u32[]{:S(2)}) copy-start(bf16[3,8,32,45]{3,2,1,0:T(8,128)(2,1)} %fusion.36) | copy-start | bytes 207364
  48.5 1.1 copy-start.5
  62.3 4.8 %collective-permute-start.3 = (bf16[8,32,45]{2,1,0:T(8,128)(2,1)}, bf16[8,32,45]{2,1,0:T(8,128)(2,1)S(1)}, u32[]{:S(2)}, u32[]{:S(2)}) collective-permute-start(bf16[8,32,45]{2,1,0:T(8,128)(2,1)} %fusion.83), channel_id=1, source_target_pairs={{0,8},{8,16},{16,24},{1,9},{9,17},{17,25},{2,10},{10,18},{18,26},{... | collective-permute-start | bytes 69128 | tf_op jit(solution)/shard_map/ppermute | solution.py:15
  80.7 5.8 %collective-permute-start.4 = (bf16[8,32,45]{2,1,0:T(8,128)(2,1)}, bf16[8,32,45]{2,1,0:T(8,128)(2,1)S(1)}, u32[]{:S(2)}, u32[]{:S(2)}) collective-permute-start(bf16[8,32,45]{2,1,0:T(8,128)(2,1)} %fusion.79), channel_id=1, source_target_pairs={{0,8},{8,16},{16,24},{1,9},{9,17},{17,25},{2,10},{10,18},{18,26},{... | collective-permute-start | bytes 69128 | tf_op jit(solution)/shard_map/ppermute | solution.py:15
  100.1 5.8 %collective-permute-start.5 = (bf16[8,32,45]{2,1,0:T(8,128)(2,1)}, bf16[8,32,45]{2,1,0:T(8,128)(2,1)S(1)}, u32[]{:S(2)}, u32[]{:S(2)}) collective-permute-start(bf16[8,32,45]{2,1,0:T(8,128)(2,1)} %fusion.75), channel_id=1, source_target_pairs={{0,8},{8,16},{16,24},{1,9},{9,17},{17,25},{2,10},{10,18},{18,26},{... | collective-permute-start | bytes 69128 | tf_op jit(solution)/shard_map/ppermute | solution.py:15
  120.0 6.6 %copy-start.18 = (bf16[8,32,135]{2,1,0:T(8,128)(2,1)S(1)}, bf16[8,32,135]{2,1,0:T(8,128)(2,1)}, u32[]{:S(2)}) copy-start(bf16[8,32,135]{2,1,0:T(8,128)(2,1)} %convolution_convert_fusion.25) | copy-start | bytes 207364
  120.0 6.6 %copy-start.19 = (bf16[8,32,135]{2,1,0:T(8,128)(2,1)S(1)}, bf16[8,32,135]{2,1,0:T(8,128)(2,1)}, u32[]{:S(2)}) copy-start(bf16[8,32,135]{2,1,0:T(8,128)(2,1)} %convolution_convert_fusion.24) | copy-start | bytes 207364
  120.0 6.6 %copy-start.20 = (bf16[8,32,135]{2,1,0:T(8,128)(2,1)S(1)}, bf16[8,32,135]{2,1,0:T(8,128)(2,1)}, u32[]{:S(2)}) copy-start(bf16[8,32,135]{2,1,0:T(8,128)(2,1)} %convolution_convert_fusion.23) | copy-start | bytes 207364
  121.6 6.7 %collective-permute-start.7 = (bf16[4,8,32,90]{3,2,1,0:T(8,128)(2,1)S(1)}, bf16[4,8,32,90]{3,2,1,0:T(8,128)(2,1)S(1)}, u32[]{:S(2)}, u32[]{:S(2)}) collective-permute-start(bf16[4,8,32,90]{3,2,1,0:T(8,128)(2,1)S(1)} %convolution_convert_fusion), channel_id=1, source_target_pairs={{0,7},{1,0},{2,1},{3,2},{4,3},{5,4},{6,5},{7,6},{8,15},{9,8},{10,9... | collective-permute-start | bytes 552968 | tf_op jit(solution)/shard_map/ppermute | solution.py:9
  125.5 9.5 %collective-permute-start.6 = (bf16[4,8,32,90]{3,2,1,0:T(8,128)(2,1)S(1)}, bf16[4,8,32,90]{3,2,1,0:T(8,128)(2,1)}, u32[]{:S(2)}, u32[]{:S(2)}) collective-permute-start(bf16[4,8,32,90]{3,2,1,0:T(8,128)(2,1)S(1)} %convolution_convert_fusion.1), channel_id=1, source_target_pairs={{0,1},{1,2},{2,3},{3,4},{4,5},{5,6},{6,7},{7,0},{8,9},{9,10},{10,1... | collective-permute-start | bytes 552968 | tf_op jit(solution)/shard_map/ppermute | solution.py:9
  128.3 20.1 %copy-start.31 = (pred[8]{0:T(512)(128)(4,1)S(1)}, pred[8]{0:T(512)(128)(4,1)}, u32[]{:S(2)}) copy-start(pred[8]{0:T(512)(128)(4,1)} %copy-done.30) | copy-start | bytes 28
  130.0 18.8 %copy-start.1 = (bf16[4,8,1,45,135]{4,1,3,2,0:T(8,128)(2,1)S(1)}, bf16[4,8,1,45,135]{4,1,3,2,0:T(8,128)(2,1)}, u32[]{:S(2)}) copy-start(bf16[4,8,1,45,135]{4,1,3,2,0:T(8,128)(2,1)} %copy-done) | copy-start | bytes 1166404
  130.0 18.8 %copy-start.35 = (pred[8]{0:T(512)(128)(4,1)S(1)}, pred[8]{0:T(512)(128)(4,1)}, u32[]{:S(2)}) copy-start(pred[8]{0:T(512)(128)(4,1)} %copy-done.34) | copy-start | bytes 28
  138.0 12.2 %copy-start.33 = (pred[8]{0:T(512)(128)(4,1)S(1)}, pred[8]{0:T(512)(128)(4,1)}, u32[]{:S(2)}) copy-start(pred[8]{0:T(512)(128)(4,1)} %copy-done.32) | copy-start | bytes 28
  146.7 3.9 %copy-start.37 = (pred[8]{0:T(512)(128)(4,1)S(1)}, pred[8]{0:T(512)(128)(4,1)}, u32[]{:S(2)}) copy-start(pred[8]{0:T(512)(128)(4,1)} %copy-done.36) | copy-start | bytes 28
  148.4 1.8 copy-start.15
  148.4 2.2 %copy-start.12 = (bf16[4,8,32,135]{3,2,1,0:T(8,128)(2,1)S(1)}, bf16[4,8,32,135]{3,2,1,0:T(8,128)(2,1)}, u32[]{:S(2)}) copy-start(bf16[4,8,32,135]{3,2,1,0:T(8,128)(2,1)} %param.7) | copy-start | bytes 829444
  148.4 2.2 %copy-start.14 = (bf16[8,4,32,45]{3,2,1,0:T(8,128)(2,1)S(1)}, bf16[8,4,32,45]{3,2,1,0:T(8,128)(2,1)}, u32[]{:S(2)}) copy-start(bf16[8,4,32,45]{3,2,1,0:T(8,128)(2,1)} %gather_fusion.7) | copy-start | bytes 276484
  148.8 2.2 %copy-start.8 = (bf16[4,8,1,45,135]{4,1,3,2,0:T(8,128)(2,1)S(1)}, bf16[4,8,1,45,135]{4,1,3,2,0:T(8,128)(2,1)}, u32[]{:S(2)}) copy-start(bf16[4,8,1,45,135]{4,1,3,2,0:T(8,128)(2,1)} %get-tuple-element.22) | copy-start | bytes 1166404
  148.8 2.2 %copy-start.21 = (bf16[3,8,32,45]{3,2,1,0:T(8,128)(2,1)S(1)}, bf16[3,8,32,45]{3,2,1,0:T(8,128)(2,1)}, u32[]{:S(2)}) copy-start(bf16[3,8,32,45]{3,2,1,0:T(8,128)(2,1)} %convolution_convert_fusion.4) | copy-start | bytes 207364
  150.2 1.1 copy-start.4
  150.6 0.9 copy-start.29
  150.6 2.4 %copy-start.3 = (bf16[8,45,135]{2,0,1:T(8,128)(2,1)S(1)}, bf16[8,45,135]{2,0,1:T(8,128)(2,1)}, u32[]{:S(2)}) copy-start(bf16[8,45,135]{2,0,1:T(8,128)(2,1)} %get-tuple-element.20) | copy-start | bytes 291604
  150.6 4.0 %copy-start.2 = (bf16[8,45,135]{2,0,1:T(8,128)(2,1)S(1)}, bf16[8,45,135]{2,0,1:T(8,128)(2,1)}, u32[]{:S(2)}) copy-start(bf16[8,45,135]{2,0,1:T(8,128)(2,1)} %get-tuple-element.21) | copy-start | bytes 291604
  150.7 4.2 %copy-start.7 = (bf16[1,8,135,135]{3,1,2,0:T(8,128)(2,1)S(1)}, bf16[1,8,135,135]{3,1,2,0:T(8,128)(2,1)}, u32[]{:S(2)}) copy-start(bf16[1,8,135,135]{3,1,2,0:T(8,128)(2,1)} %get-tuple-element.30) | copy-start | bytes 874804
  151.0 4.4 %copy-start.6 = (bf16[1,8,135,135]{3,1,2,0:T(8,128)(2,1)S(1)}, bf16[1,8,135,135]{3,1,2,0:T(8,128)(2,1)}, u32[]{:S(2)}) copy-start(bf16[1,8,135,135]{3,1,2,0:T(8,128)(2,1)} %get-tuple-element.31) | copy-start | bytes 874804
  155.9 6.3 %collective-permute-start.8 = (bf16[8,32,45]{2,1,0:T(8,128)(2,1)S(1)}, bf16[8,32,45]{2,1,0:T(8,128)(2,1)S(1)}, u32[]{:S(2)}, u32[]{:S(2)}) collective-permute-start(bf16[8,32,45]{2,1,0:T(8,128)(2,1)S(1)} %fusion.71), channel_id=1, source_target_pairs={{8,0},{16,8},{24,16},{9,1},{17,9},{25,17},{10,2},{18,10},{26,18},{... | collective-permute-start | bytes 69128 | tf_op jit(solution)/shard_map/ppermute | solution.py:15
  166.6 5.6 %collective-permute-start.9 = (bf16[8,32,45]{2,1,0:T(8,128)(2,1)S(1)}, bf16[8,32,45]{2,1,0:T(8,128)(2,1)S(1)}, u32[]{:S(2)}, u32[]{:S(2)}) collective-permute-start(bf16[8,32,45]{2,1,0:T(8,128)(2,1)S(1)} %fusion.67), channel_id=1, source_target_pairs={{8,0},{16,8},{24,16},{9,1},{17,9},{25,17},{10,2},{18,10},{26,18},{... | collective-permute-start | bytes 69128 | tf_op jit(solution)/shard_map/ppermute | solution.py:15
  176.7 5.6 %collective-permute-start.10 = (bf16[8,32,45]{2,1,0:T(8,128)(2,1)S(1)}, bf16[8,32,45]{2,1,0:T(8,128)(2,1)S(1)}, u32[]{:S(2)}, u32[]{:S(2)}) collective-permute-start(bf16[8,32,45]{2,1,0:T(8,128)(2,1)S(1)} %fusion.63), channel_id=1, source_target_pairs={{8,0},{16,8},{24,16},{9,1},{17,9},{25,17},{10,2},{18,10},{26,18},{... | collective-permute-start | bytes 69128 | tf_op jit(solution)/shard_map/ppermute | solution.py:15
where the time goes:
time: 190 us; the launch traced here: 188 us
  matrix products  88.2 us (46%)
  local copies, waits for them, and re-layouts  37.6 us (20%)
  starting transfers between devices  27.1 us (14%)
  waiting for transfers between devices  19.1 us (10%)
  other arithmetic  14.8 us (8%)
    dot_general x33, matrix products, face_trace(): jnp.dot(field, selector(axis_place, which), preferred_element_type=jnp.fl...  41.5 us
    dot_general x24, matrix products, plane_chain(): jnp.einsum('crt,cti->cri', trace_in, coupling[plane], preferred_element_t...  22.2 us
    ppermute x7, starting transfers between devices, passed_along(): return lax.ppermute(block, axis, route)  20 us
    gather x8, local copies, waits for them, and re-layouts, cross_terms(): gathered = jnp.take(pools[face][0], pools[face][1], axis=1)  17.7 us
    ppermute x7, waiting for transfers between devices, passed_along(): return lax.ppermute(block, axis, route)  16.5 us
    dot_general x8, matrix products, plane_chain(): jnp.einsum('crj,cij->cri', residue, inverse[plane], preferred_element_typ...  12.5 us
    ppermute x4, starting transfers between devices, from_behind(): lax.ppermute(shard, axis, [(i, (i + by) % peers) for i in range(peers)])  7.06 us
    dot_general x4, matrix products, pair_trace(): jnp.dot(field, table, preferred_element_type=jnp.float32)  6.53 us
  transfers between devices with their start and end apart: 11, of which 7 were waited for; matrix products, arithmetic and copies ran while one was open for 26% of the time, Pallas kernels for 0%

commit v1 on v0

v1 whole, which is shorter than its diff:
```python
import functools

import jax
import jax.numpy as jnp
import numpy as np
from jax import lax
from jax.experimental import pallas as pl
from jax.experimental.pallas import tpu as pltpu
from jax.sharding import PartitionSpec as P

BF = jnp.bfloat16
F32 = jnp.float32
NT = 45
FACE = 48
SLOT = 64
ROWS = 3 * FACE
SHARED = 80
MIB = 1 << 20


def natural(v, a, b, c):
    return v * 27 + a * 9 + b * 3 + c


def inner(v, a, b, c):
    return a * FACE + v * 9 + b * 3 + c


NODES = [(v, a, b, c) for v in range(5) for a in range(3) for b in range(3) for c in range(3)]


def face_nodes(place, which):
    return [n for n in NODES if n[1 + place] == which]


def union_nodes(which):
    return [n for n in NODES if n[2] == which or n[3] == which]


def table(height, width, rows, column_of, value=1.0):
    out = np.zeros((height, width), np.float32)
    for row, node in rows:
        out[row, column_of(*node)] = value
    return out


def block(nodes, start=0):
    return [(start + i, n) for i, n in enumerate(nodes)]


def send_table(width, column_of):
    rows = block(union_nodes(2)) + block(union_nodes(0), SHARED)
    return table(2 * SHARED, width, rows, column_of)


def own_table(width, column_of):
    rows = block(face_nodes(2, 2)) + block(face_nodes(2, 0), FACE)
    return table(2 * FACE, width, rows, column_of)


def receive_table(which):
    place = {n: i for i, n in enumerate(union_nodes(which))}
    rows = block(face_nodes(1, which)) + block(face_nodes(2, which), FACE)
    return table(2 * FACE, SHARED, rows, lambda *n: place[n])


def mm(a, b):
    return lax.dot_general(a, b, (((1,), (0,)), ((), ())), preferred_element_type=F32)


def mt(a, b):
    return lax.dot_general(a, b, (((1,), (1,)), ((), ())), preferred_element_type=F32)


def split_lanes(value, width):
    lanes = value.shape[1]
    value = value.astype(F32)
    owner = lax.broadcasted_iota(jnp.int32, value.shape, 1) // width
    pad = jnp.zeros((SLOT - FACE, lanes), BF)
    parts = []
    for c in range(lanes // width):
        parts += [jnp.where(owner == c, value, 0.0).astype(BF), pad]
    return jnp.concatenate(parts, 0)


def own_lanes(values, width):
    owner = lax.broadcasted_iota(jnp.int32, values[0].shape, 1) // width
    out = values[0]
    for c in range(1, len(values)):
        out = jnp.where(owner == c, values[c], out)
    return out


def one_hot(source, start, height):
    row = lax.broadcasted_iota(jnp.int32, (height, source.shape[1]), 0) + start
    return jnp.where(row == source, 1.0, 0.0).astype(BF)


def chain_step(matrix, trace, rhs):
    half = trace.shape[1] // 2
    return jnp.concatenate(
        [mm(matrix[h], split_lanes(trace[:, h * half : (h + 1) * half], rhs)) for h in range(2)], 1
    )


def first_kernel(initial, send, first_face, up, down, above):
    planes, columns, rhs, width = initial.shape
    for p in range(planes):
        x = initial[p].reshape(columns * rhs, width)
        out = mt(send[...], x).astype(BF)
        up[p] = out[:SHARED]
        down[p] = out[SHARED:]
        if p == 0:
            above[...] = mt(first_face[...], x).astype(BF)


def weight_kernel(
    inverse, couplings, right, initial, source, perm, own_sel, first_face,
    known0, known1, known2, lower0, lower1, lower2, upper0, upper1, upper2, base0, base1, base2,
    own, cum_f, cum_b, faces, prev, backs,
):
    known, lower, upper = (known0, known1, known2), (lower0, lower1, lower2), (upper0, upper1, upper2)
    base = (base0, base1, base2)
    p = pl.program_id(0)
    planes, columns, rhs, width = initial.shape
    half = columns // 2

    @pl.when(p == 0)
    def _():
        faces[...] = jnp.zeros(faces.shape, BF)

    pairs_lower, pairs_upper, bases = [], [], []
    rights = [right[0, h * half : (h + 1) * half].reshape(half * rhs, width) for h in range(2)]
    lane = lax.broadcasted_iota(jnp.int32, (ROWS, 2 * SLOT), 1)
    before = None
    for c in range(columns):
        solve = mm(perm[...], inverse[0, c]).astype(BF)
        for f in range(4):
            faces[c, f * FACE : f * FACE + NT] = couplings[0, c, 2 + f]
        faces[c, 4 * FACE : 4 * FACE + NT] = couplings[0, c, 1]
        faces[c, 256 : 256 + NT] = couplings[0, c, 0]
        faces[c, 256 + SLOT : 256 + SLOT + NT] = couplings[0, c, 1]
        all_known = mt(solve, faces[c, :256]).astype(BF)
        for a in range(3):
            known[a][0, c] = all_known[a * FACE : (a + 1) * FACE]
        both = mt(solve, faces[c, 256:])
        if c % 2 == 0:
            before = both
        else:
            pairs_lower.append(jnp.where(lane < SLOT, before, pltpu.roll(both, SLOT, 1)).astype(BF))
            pairs_upper.append(jnp.where(lane < SLOT, pltpu.roll(before, SLOT, 1), both).astype(BF))
        bases.append(mt(solve, rights[c // half]))
    for h in range(2):
        down = jnp.concatenate(pairs_lower[2 * h : 2 * h + 2], 1)
        up = jnp.concatenate(pairs_upper[2 * h : 2 * h + 2], 1)
        backs[p, h] = up[:FACE]
        here = -own_lanes(bases[h * half : (h + 1) * half], rhs)
        for a in range(3):
            lower[a][0, h] = down[a * FACE : (a + 1) * FACE]
            upper[a][0, h] = up[a * FACE : (a + 1) * FACE]
            base[a][0, :, h * half * rhs : (h + 1) * half * rhs] = here[a * FACE : (a + 1) * FACE]
        step = down[2 * FACE :]

        @pl.when(p == 0)
        def _():
            prev[h] = step.astype(F32)

        @pl.when(p > 0)
        def _():
            prev[h] = mm(step, split_lanes(prev[h], SLOT))

        cum_f[0, h] = prev[h].astype(BF)

    x = initial[p].reshape(columns * rhs, width)
    mine = mt(own_sel[...], x).astype(BF)
    size = columns * rhs
    own[0, :FACE] = mm(mine[:FACE], one_hot(source[0:1], size, size)).astype(BF)
    own[0, FACE : 2 * FACE] = mm(mine[FACE:], one_hot(source[1:2], 0, size)).astype(BF)
    beyond = initial[jnp.minimum(p + 1, planes - 1)].reshape(columns * rhs, width)
    own[0, 2 * FACE :] = mt(first_face[...], beyond).astype(BF)

    @pl.when(p == planes - 1)
    def _():
        for h in range(2):
            total = backs[planes - 1, h].astype(F32)
            cum_b[planes - 1, h] = total.astype(BF)
            for q in range(planes - 2, -1, -1):
                total = mm(backs[q, h], split_lanes(total, SLOT))
                cum_b[q, h] = total.astype(BF)


def gathered(received_up, received_down, own, p, up_sel, down_sel, low_pick, high_pick):
    low = mm(up_sel, received_up[p]).astype(BF)
    high = mm(down_sel, received_down[p]).astype(BF)
    c_low = mm(low[FACE:], low_pick).astype(BF) + own[p, :FACE]
    c_high = mm(high[FACE:], high_pick).astype(BF) + own[p, FACE : 2 * FACE]
    return [low[:FACE], high[:FACE], c_low, c_high]


def known_part(known_c, operand, columns, rhs):
    half = columns // 2
    out = []
    for h in range(2):
        side = operand[:, h * half * rhs : (h + 1) * half * rhs]
        out.append(own_lanes([mm(known_c(h * half + c), side) for c in range(half)], rhs))
    return jnp.concatenate(out, 1)


def forward_chain_kernel(
    up, down, above, own, source, up_sel, down_sel, known, lower, base, operand, part, traces, last, *, rhs
):
    planes = up.shape[0]
    columns = known.shape[1]
    size = columns * rhs
    low_pick = one_hot(source[0:1], 0, size)
    high_pick = one_hot(source[1:2], size, size)
    starts = []
    for p in range(planes):
        parts = gathered(up, down, own, p, up_sel[...], down_sel[...], low_pick, high_pick)
        parts.append(own[p, 2 * FACE :] if p + 1 < planes else above[...])
        parts.append(jnp.zeros((256 - 5 * FACE, size), BF))
        whole = jnp.concatenate(parts, 0)
        operand[p] = whole
        starts.append(base[p] + known_part(lambda c: known[p, c], whole, columns, rhs))
    for p in range(planes):
        part[p] = starts[p]
    trace = starts[0]
    traces[0] = trace
    for p in range(1, planes):
        trace = starts[p] + chain_step(lower[p], trace, rhs)
        traces[p] = trace
    last[...] = trace.astype(BF)


def backward_chain_kernel(
    up, down, own, source, up_sel, down_sel, known, upper, base, operand, part, traces, last, *, rhs
):
    planes = up.shape[0]
    columns = known.shape[1]
    size = columns * rhs
    low_pick = one_hot(source[0:1], 0, size)
    high_pick = one_hot(source[1:2], size, size)
    starts = []
    for p in range(planes):
        parts = gathered(up, down, own, p, up_sel[...], down_sel[...], low_pick, high_pick)
        parts.append(jnp.zeros((256 - 4 * FACE, size), BF))
        whole = jnp.concatenate(parts, 0)
        operand[p] = whole
        starts.append(base[p] + known_part(lambda c: known[p, c], whole, columns, rhs))
    for p in range(planes):
        part[p] = starts[p]
    trace = starts[planes - 1]
    traces[planes - 1] = trace
    for p in range(planes - 2, -1, -1):
        trace = starts[p] + chain_step(upper[p], trace, rhs)
        traces[p] = trace
    last[...] = trace.astype(BF)


def base_kernel(known_one, known_two, operand, base_one, base_two, one, two, *, rhs):
    planes, columns = known_one.shape[:2]
    for p in range(planes):
        for known, base, out in ((known_one, base_one, one), (known_two, base_two, two)):
            out[p] = base[p] + known_part(lambda c: known[p, c], operand[p], columns, rhs)


def incoming(one, two, three, first, second, rhs):
    trace = two[...].astype(F32) + chain_step(second, three[...].astype(F32), rhs)
    return one[...].astype(F32) + chain_step(first, trace, rhs)


def forward_finish_kernel(
    one, two, three, first, second, cum, traces, part0, part1, part2, lower0, lower1, lower2, send, middle, change, up, down, *, rhs
):
    planes = traces.shape[0]
    entry = incoming(one, two, three, first, second, rhs)
    trace = entry
    for p in range(planes):
        matrix = [jnp.concatenate([x[p, h] for x in (lower0, lower1, lower2)], 0) for h in range(2)]
        delta = chain_step(matrix, trace, rhs)
        whole = jnp.concatenate([x[p] for x in (part0, part1, part2)], 0) + delta
        change[p] = delta
        whole = whole.astype(BF)
        middle[p] = whole
        out = mm(send[...], whole).astype(BF)
        up[p] = out[:SHARED]
        down[p] = out[SHARED:]
        if p + 1 < planes:
            trace = traces[p] + chain_step(cum[p], entry, rhs)


def middle_kernel(middle, change, base0, base1, base2, source, own_sel, own, out0, out1, out2):
    planes = middle.shape[0]
    size = middle.shape[2]
    low_pick = one_hot(source[0:1], size, size)
    high_pick = one_hot(source[1:2], 0, size)
    for p in range(planes):
        mine = mm(own_sel[...], middle[p]).astype(BF)
        own[p, :FACE] = mm(mine[:FACE], low_pick).astype(BF)
        own[p, FACE:] = mm(mine[FACE:], high_pick).astype(BF)
        for a, (base, out) in enumerate(((base0, out0), (base1, out1), (base2, out2))):
            out[p] = base[p] + change[p, a * FACE : (a + 1) * FACE]


def backward_finish_kernel(
    one, two, three, first, second, cum, traces, part0, part1, part2, upper0, upper1, upper2, back, result, *, rhs
):
    planes = traces.shape[0]
    entry = incoming(one, two, three, first, second, rhs)
    size = entry.shape[1]
    row = lax.broadcasted_iota(jnp.int32, (size, size), 0)
    column = lax.broadcasted_iota(jnp.int32, (size, size), 1)
    unit = jnp.where(row == column, 1.0, 0.0).astype(BF)
    columns, _, width = result.shape[1:]
    for p in range(planes - 1, -1, -1):
        trace = entry if p + 1 == planes else traces[p + 1] + chain_step(cum[p + 1], entry, rhs)
        matrix = [jnp.concatenate([x[p, h] for x in (upper0, upper1, upper2)], 0) for h in range(2)]
        whole = jnp.concatenate([x[p] for x in (part0, part1, part2)], 0) + chain_step(matrix, trace, rhs)
        turned = mm(back[...], whole.astype(BF)).astype(BF)
        result[p] = mt(unit, turned).astype(BF).reshape(columns, rhs, width)


def cost(flops, nbytes):
    return pl.CostEstimate(flops=int(flops), bytes_accessed=int(nbytes), transcendentals=0)


def call(kernel, outs, operands, name, flops=2e8):
    shapes = [jax.ShapeDtypeStruct(s, d) for s, d in outs]
    nbytes = sum(x.size * x.dtype.itemsize for x in list(operands) + shapes)
    return pl.pallas_call(
        kernel,
        out_shape=shapes,
        in_specs=[pl.BlockSpec(memory_space=pltpu.VMEM)] * len(operands),
        out_specs=[pl.BlockSpec(memory_space=pltpu.VMEM)] * len(shapes),
        compiler_params=pltpu.CompilerParams(vmem_limit_bytes=24 * MIB),
        cost_estimate=cost(flops, nbytes),
        name=name,
    )(*operands)


def weights(inverse, couplings, right, initial, source, perm, own_sel, first_face):
    planes, columns, rhs, width = initial.shape
    size = columns * rhs
    whole = lambda x: pl.BlockSpec(x.shape, lambda p, n=x.ndim: (0,) * n)
    lead = lambda s: pl.BlockSpec((1,) + s[1:], lambda p, n=len(s): (p,) + (0,) * (n - 1))
    known = (planes, columns, FACE, 256)
    pack = (planes, 2, FACE, 256)
    base = (planes, FACE, size)
    own = (planes, ROWS, size)
    outs = [(known, BF)] * 3 + [(pack, BF)] * 6 + [(base, F32)] * 3 + [(own, BF), (pack, BF), (pack, BF)]
    outs = [jax.ShapeDtypeStruct(s, d) for s, d in outs]
    return pl.pallas_call(
        weight_kernel,
        grid=(planes,),
        out_shape=outs,
        in_specs=[lead(x.shape) for x in (inverse, couplings, right)]
        + [whole(x) for x in (initial, source, perm, own_sel, first_face)],
        out_specs=[lead(x.shape) for x in outs[:-1]] + [whole(outs[-1])],
        scratch_shapes=[
            pltpu.VMEM((columns, 256 + 2 * SLOT, width), BF),
            pltpu.VMEM((2, FACE, 256), F32),
            pltpu.VMEM((planes, 2, FACE, 256), BF),
        ],
        compiler_params=pltpu.CompilerParams(
            vmem_limit_bytes=24 * MIB, dimension_semantics=("arbitrary",)
        ),
        cost_estimate=cost(6e9, 12e6),
        name="weights",
    )(inverse, couplings, right, initial, source, perm, own_sel, first_face)


def ring(x, axis, by):
    n = lax.axis_size(axis)
    return lax.ppermute(x, axis, [(i, (i + by) % n) for i in range(n)])


def shift(x, axis, by):
    n = lax.axis_size(axis)
    return lax.ppermute(x, axis, [(i, i + by) for i in range(n) if 0 <= i + by < n])


def local(right_sides, initial, inverse_blocks, couplings, neighbours):
    planes, columns, rhs, width = initial.shape
    size = columns * rhs
    const = lambda x: jnp.asarray(x, BF)
    send_nat = const(send_table(width, natural))
    send_in = const(send_table(ROWS, inner))
    own_nat = const(own_table(width, natural))
    own_in = const(own_table(ROWS, inner))
    first_face = const(table(FACE, width, block(face_nodes(0, 0)), natural))
    perm = const(table(ROWS, width, [(inner(*n), n) for n in NODES], natural, -1.0))
    back = const(table(width, ROWS, [(natural(*n), n) for n in NODES], inner))
    up_sel = const(receive_table(2))
    down_sel = const(receive_table(0))

    place = lax.axis_index("cross")
    total = columns * lax.axis_size("cross")
    low = (neighbours[:, 2] - (place - 1) * columns) % total
    high = (neighbours[:, 3] - place * columns) % total
    lane = jnp.arange(size, dtype=jnp.int32)
    which = jnp.stack([low, high])
    source = jnp.repeat(which, rhs, axis=1) * rhs + lane[None] % rhs

    share = (planes, SHARED, size)
    up, down, above = call(
        first_kernel,
        [(share, BF), (share, BF), ((FACE, size), BF)],
        (initial, send_nat, first_face),
        "initial_traces",
    )
    up, down, above, initial = lax.optimization_barrier((up, down, above, initial))
    from_low = ring(up, "cross", 1)
    from_high = ring(down, "cross", -1)
    from_above = shift(above, "sweep", -1)
    *parts, own, cum_f, cum_b = weights(
        inverse_blocks, couplings, right_sides, initial, source, perm, own_nat, first_face
    )
    known, lower, upper, base = parts[:3], parts[3:6], parts[6:9], parts[9:]
    pass_f, pass_b = cum_f[planes - 1], cum_b[0]
    first_f, second_f = shift(pass_f, "sweep", 1), shift(pass_f, "sweep", 2)
    first_b, second_b = shift(pass_b, "sweep", -1), shift(pass_b, "sweep", -2)

    trace = (planes, FACE, size)
    deep = (planes, ROWS, size)
    chain_outs = [((planes, 256, size), BF), (trace, F32), (trace, F32), ((FACE, size), BF)]
    operand, part2, traces, last = call(
        functools.partial(forward_chain_kernel, rhs=rhs),
        chain_outs,
        (from_low, from_high, from_above, own, source, up_sel, down_sel, known[2], lower[2], base[2]),
        "forward_chain",
    )
    one, two, three = (shift(last, "sweep", by) for by in (1, 2, 3))
    part0, part1 = call(
        functools.partial(base_kernel, rhs=rhs),
        [(trace, F32)] * 2,
        (known[0], known[1], operand, base[0], base[1]),
        "forward_base",
        2e9,
    )
    middle, change, up, down = call(
        functools.partial(forward_finish_kernel, rhs=rhs),
        [(deep, BF), (deep, F32), (share, BF), (share, BF)],
        (one, two, three, first_f, second_f, cum_f, traces, part0, part1, part2, *lower, send_in),
        "forward_finish",
    )
    from_low = ring(up, "cross", 1)
    from_high = ring(down, "cross", -1)
    own, *base = call(
        middle_kernel,
        [((planes, 2 * FACE, size), BF)] + [(trace, F32)] * 3,
        (middle, change, *base, source, own_in),
        "middle",
        2e9,
    )
    operand, part0, traces, last = call(
        functools.partial(backward_chain_kernel, rhs=rhs),
        chain_outs,
        (from_low, from_high, own, source, up_sel, down_sel, known[0], upper[0], base[0]),
        "backward_chain",
    )
    one, two, three = (shift(last, "sweep", -by) for by in (1, 2, 3))
    part1, part2 = call(
        functools.partial(base_kernel, rhs=rhs),
        [(trace, F32)] * 2,
        (known[1], known[2], operand, base[1], base[2]),
        "backward_base",
        2e9,
    )
    (result,) = call(
        functools.partial(backward_finish_kernel, rhs=rhs),
        [(right_sides.shape, BF)],
        (one, two, three, first_b, second_b, cum_b, traces, part0, part1, part2, *upper, back),
        "backward_finish",
    )
    return result


def solution(mesh):
    return jax.shard_map(
        local,
        mesh=mesh,
        in_specs=(
            P("sweep", "cross", None, None),
            P("sweep", "cross", None, None),
            P("sweep", "cross", None, None),
            P("sweep", "cross", None, None, None),
            P("cross", None),
        ),
        out_specs=P("sweep", "cross", None, None),
        check_vma=False,
    )
```

time: 190 us -> 73.7 us (0.39)
  matrix products: 88.2 us -> 0 us
  local copies, waits for them, and re-layouts: 37.6 us -> 6.57 us
  Pallas kernels: 0 us -> 21.1 us
  other arithmetic: 14.8 us -> 0.79 us
  waiting for transfers between devices: 19.1 us -> 15 us
  starting transfers between devices: 27.1 us -> 29.4 us
    dot_general x79 -> x0, matrix products: 88.2 us -> none  [the longest x33 41.5 us: face_trace(): jnp.dot(field, selector(axis_place, which), preferred_element_type=jnp.fl...]
    pallas_call x0 -> x9, Pallas kernels: none -> 21.1 us  [the longest x8 11.2 us: call(): pl.pallas_call(kernel, out_shape=shapes, in_specs=[pl.BlockSpec(memory_sp...]
    gather x8 -> x0, local copies, waits for them, and re-layouts: 17.7 us -> none  [cross_terms(): gathered = jnp.take(pools[face][0], pools[face][1], axis=1)]
    slice x10 -> x0, local copies, waits for them, and re-layouts: 16.9 us -> none  [the longest x1 3.66 us: local(): couplings[:, :, 0]]
    concatenate x8 -> x0, other arithmetic: 13.1 us -> none  [the longest x2 3.78 us: cross_terms(): jnp.concatenate([from_lower[..., 45:], toward_upper[..., 45:]], 1)]
    unnamed x78 -> x30, local copies, waits for them, and re-layouts: 0.16 us -> 6.41 us
    ppermute x11 -> x15, waiting for transfers between devices: 19.1 us -> 15 us  [the longest x4 12 us: ring(): return lax.ppermute(x, axis, [(i, (i + by) % n) for i in range(n)])]
    squeeze x1 -> x2, local copies, waits for them, and re-layouts: 2.85 us -> 0.01 us  [local(): pass_f, pass_b = (cum_f[planes - 1], cum_b[0])]
  transfers between devices with their start and end apart: 11 -> 15, of which waited for: 7 -> 6; matrix products, arithmetic and copies ran while one was open for 26% -> 0% of each run, Pallas kernels for 0% -> 11%
where the time goes in v1:
time: 73.7 us; the launch traced here: 73.2 us
  starting transfers between devices  29.4 us (40%)
  Pallas kernels  21.1 us (29%)
  waiting for transfers between devices  15 us (20%)
  local copies, waits for them, and re-layouts  6.57 us (9%)
  other arithmetic  0.79 us (1%)
    ppermute x11, starting transfers between devices, shift(): lax.ppermute(x, axis, [(i, i + by) for i in range(n) if 0 <= i + by < n])  20.7 us
    ppermute x4, waiting for transfers between devices, ring(): return lax.ppermute(x, axis, [(i, (i + by) % n) for i in range(n)])  12 us
    pallas_call x8, Pallas kernels, call(): pl.pallas_call(kernel, out_shape=shapes, in_specs=[pl.BlockSpec(memory_sp...  11.2 us
    pallas_call x1, Pallas kernels, weights(): pl.pallas_call(weight_kernel, grid=(planes,), out_shape=outs, in_specs=[l...  9.89 us
    ppermute x4, starting transfers between devices, ring(): return lax.ppermute(x, axis, [(i, (i + by) % n) for i in range(n)])  8.61 us
    unnamed x30, local copies, waits for them, and re-layouts  6.41 us
    ppermute x11, waiting for transfers between devices, shift(): lax.ppermute(x, axis, [(i, i + by) for i in range(n) if 0 <= i + by < n])  3.03 us
  transfers between devices with their start and end apart: 15, of which 6 were waited for; matrix products, arithmetic and copies ran while one was open for 0% of the time, Pallas kernels for 11%

profile of v1, /device:TPU:1, one launch (start us, length us, event | category | flops | bytes accessed | tf_op | source)
XLA Modules:
  0.0 73.2 jit_solution(14514585171844961966)
XLA Ops:
  0.0 0.8 %and_select_fusion.2 = (s32[1,8]{1,0:T(1,128)S(1)}, s32[1,8]{1,0:T(1,128)S(1)}) fusion(s32[8,4]{0,1:T(4,128)} %param.18, s32[]{:T(128)S(6)} %mul.16, s32[]{:T(128)S(6)} %mul.17), kind=kLoop, calls=%fused_computation.8 | loop fusion | flops 192 | bytes 136 | tf_op jit(solution)/shard_map/jit(remainder)/select_n | solution.py:398
  0.8 0.1 broadcast_in_dim.4
  0.9 0.1 mul.20
  0.9 0.0 copy-start.4
  0.9 1.0 %copy-done.4 = bf16[4,8,32,135]{3,2,1,0:T(8,128)(2,1)S(1)} copy-done((bf16[4,8,32,135]{3,2,1,0:T(8,128)(2,1)S(1)}, bf16[4,8,32,135]{3,2,1,0:T(8,128)(2,1)}, u32[]{:S(2)}) %copy-start.4) | copy-done | bytes 276504
  2.0 0.0 copy-start.7
  2.0 0.9 %copy-done.7 = bf16[160,135]{1,0:T(8,128)(2,1)S(1)} copy-done((bf16[160,135]{1,0:T(8,128)(2,1)S(1)}, bf16[160,135]{1,0:T(8,128)(2,1)}, u32[]{:S(2)}) %copy-start.7) | copy-done | bytes 43224
  2.9 0.0 copy-start.11
  2.9 0.7 %copy-done.11 = bf16[48,135]{1,0:T(8,128)(2,1)S(1)} copy-done((bf16[48,135]{1,0:T(8,128)(2,1)S(1)}, bf16[48,135]{1,0:T(8,128)(2,1)}, u32[]{:S(2)}) %copy-start.11) | copy-done | bytes 12984
  3.6 0.4 initial_traces.1
  4.0 2.3 %copy.15.inverse = bf16[4,8,135,135]{3,2,1,0:T(8,128)(2,1)S(1)} copy(bf16[4,8,135,135]{3,1,2,0:T(8,128)(2,1)} %param.16) | data formatting | bytes 2332800 | tf_op args[2]
  6.2 0.3 copy-done.13
  6.5 0.0 copy-start.12
  6.6 1.1 %copy.16.couplings = bf16[4,8,6,45,135]{4,3,2,1,0:T(8,128)(2,1)S(1)} copy(bf16[4,8,6,45,135]{4,1,3,2,0:T(8,128)(2,1)S(1)} %copy-done.13) | data formatting | bytes 4665600 | tf_op args[3]
  7.7 0.0 copy-done.5
  7.7 0.0 copy-done.6
  7.7 0.0 copy-done.8
  7.7 0.0 copy-done.10
  7.7 0.0 copy-done.12
  7.7 0.0 copy-start.1
  7.8 9.9 %weights.1 = (bf16[4,8,48,256]{3,2,1,0:T(8,128)(2,1)S(1)}, bf16[4,8,48,256]{3,2,1,0:T(8,128)(2,1)S(1)}, bf16[4,8,48,256]{3,2,1,0:T(8,128)(2,1)S(1)}, bf16[4,2,48...) custom-call(bf16[4,8,135,135]{3,2,1,0:T(8,128)(2,1)S(1)} %copy.15.in, ...), custom_call_target="tpu_custom_call" | custom-call | flops 6000000000 | bytes 12000000 | tf_op jit(solution)/shard_map/weights/pallas_call | solution.py:352
  17.7 3.9 %collective-permute-start.7 = (bf16[2,48,256]{2,1,0:T(8,128)(2,1)S(1)}, bf16[2,48,256]{2,1,0:T(8,128)(2,1)S(1)}, u32[]{:S(2)}, u32[]{:S(2)}) collective-permute-start(bf16[2,48,256]{2,1,0:T(8,128)(2,1)S(1)} %slice_bitcast_fusion.1), channel_id=1, source_target_pairs={{0,16},{8,24},{1,17},{9,25},{2,18},{10,26},{3,19},{11,27},{4,20},{... | collective-permute-start | bytes 147464 | tf_op jit(solution)/shard_map/ppermute | solution.py:379
  21.6 1.9 %collective-permute-start.6 = (bf16[2,48,256]{2,1,0:T(8,128)(2,1)S(1)}, bf16[2,48,256]{2,1,0:T(8,128)(2,1)S(1)}, u32[]{:S(2)}, u32[]{:S(2)}) collective-permute-start(bf16[2,48,256]{2,1,0:T(8,128)(2,1)S(1)} %slice_bitcast_fusion.1), channel_id=1, source_target_pairs={{0,8},{8,16},{16,24},{1,9},{9,17},{17,25},{2,10},{10,18},{18,26},{... | collective-permute-start | bytes 147464 | tf_op jit(solution)/shard_map/ppermute | solution.py:379
  23.6 2.4 %collective-permute-start.2 = (bf16[48,256]{1,0:T(8,128)(2,1)S(1)}, bf16[48,256]{1,0:T(8,128)(2,1)S(1)}, u32[]{:S(2)}, u32[]{:S(2)}) collective-permute-start(bf16[48,256]{1,0:T(8,128)(2,1)S(1)} %get-tuple-element.52), channel_id=1, source_target_pairs={{8,0},{16,8},{24,16},{9,1},{17,9},{25,17},{10,2},{18,10},{26,18},{... | collective-permute-start | bytes 73736 | tf_op jit(solution)/shard_map/ppermute | solution.py:379
  26.0 1.3 %collective-permute-start = (bf16[4,80,256]{2,1,0:T(8,128)(2,1)S(1)}, bf16[4,80,256]{2,1,0:T(8,128)(2,1)S(1)}, u32[]{:S(2)}, u32[]{:S(2)}) collective-permute-start(bf16[4,80,256]{2,1,0:T(8,128)(2,1)S(1)} %get-tuple-element.50), channel_id=1, source_target_pairs={{0,1},{1,2},{2,3},{3,4},{4,5},{5,6},{6,7},{7,0},{8,9},{9,10},{10,1... | collective-permute-start | bytes 491528 | tf_op jit(solution)/shard_map/ppermute | solution.py:374
  27.3 3.1 %collective-permute-start.1 = (bf16[4,80,256]{2,1,0:T(8,128)(2,1)S(1)}, bf16[4,80,256]{2,1,0:T(8,128)(2,1)S(1)}, u32[]{:S(2)}, u32[]{:S(2)}) collective-permute-start(bf16[4,80,256]{2,1,0:T(8,128)(2,1)S(1)} %get-tuple-element.51), channel_id=1, source_target_pairs={{0,7},{1,0},{2,1},{3,2},{4,3},{5,4},{6,5},{7,6},{8,15},{9,8},{10,9... | collective-permute-start | bytes 491528 | tf_op jit(solution)/shard_map/ppermute | solution.py:374
  30.4 0.0 collective-permute-done.2.above
  30.4 4.3 %collective-permute-done.up = bf16[4,80,256]{2,1,0:T(8,128)(2,1)S(1)} collective-permute-done((bf16[4,80,256]{2,1,0:T(8,128)(2,1)S(1)}, bf16[4,80,256]{2,1,0:T(8,128)(2,1)S(1)}, u32[]{:S(2)}, u32[]{:S(2)}) %collective-permute-start) | collective-permute-done | bytes 163872 | tf_op jit(solution)/shard_map/ppermute | solution.py:374
  34.7 2.2 %collective-permute-done.1.down = bf16[4,80,256]{2,1,0:T(8,128)(2,1)S(1)} collective-permute-done((bf16[4,80,256]{2,1,0:T(8,128)(2,1)S(1)}, bf16[4,80,256]{2,1,0:T(8,128)(2,1)S(1)}, u32[]{:S(2)}, u32[]{:S(2)}) %collective-permute-start.1) | collective-permute-done | bytes 163872 | tf_op jit(solution)/shard_map/ppermute | solution.py:374
  36.9 0.0 copy-done
  36.9 0.0 copy-done.1
  36.9 2.1 %forward_chain.1 = (bf16[4,256,256]{2,1,0:T(8,128)(2,1)S(1)}, f32[4,48,256]{2,1,0:T(8,128)S(1)}, f32[4,48,256]{2,1,0:T(8,128)S(1)}, bf16[48,256]{1,0:T(8,128)(2,1)S(1)}) custom-call(bf16[4,80,256]{2,1,0:T(8,128)(2,1)S(1)} %collective-permute-done.up, bf16[4,80,256]{2,1,0:T(8,128)(2,1)S(1)} %collective-permute-done.1.down, ...), custom_call_target="tpu_custom_call" | custom-call | flops 200000000 | bytes 2801664 | tf_op jit(solution)/shard_map/forward_chain/pallas_call | solution.py:330
  39.0 0.7 collective-permute-start.5
  39.7 1.3 %collective-permute-start.4 = (bf16[48,256]{1,0:T(8,128)(2,1)S(1)}, bf16[48,256]{1,0:T(8,128)(2,1)S(1)}, u32[]{:S(2)}, u32[]{:S(2)}) collective-permute-start(bf16[48,256]{1,0:T(8,128)(2,1)S(1)} %get-tuple-element.58), channel_id=1, source_target_pairs={{0,16},{8,24},{1,17},{9,25},{2,18},{10,26},{3,19},{11,27},{4,20},{... | collective-permute-start | bytes 73736 | tf_op jit(solution)/shard_map/ppermute | solution.py:379
  41.0 1.9 %collective-permute-start.3 = (bf16[48,256]{1,0:T(8,128)(2,1)S(1)}, bf16[48,256]{1,0:T(8,128)(2,1)S(1)}, u32[]{:S(2)}, u32[]{:S(2)}) collective-permute-start(bf16[48,256]{1,0:T(8,128)(2,1)S(1)} %get-tuple-element.58), channel_id=1, source_target_pairs={{0,8},{8,16},{16,24},{1,9},{9,17},{17,25},{2,10},{10,18},{18,26},{... | collective-permute-start | bytes 73736 | tf_op jit(solution)/shard_map/ppermute | solution.py:379
  42.9 0.0 copy-start.9
  42.9 0.7 forward_base.1
  43.7 0.0 collective-permute-done.7.second
  43.7 1.3 %collective-permute-start.14 = (bf16[2,48,256]{2,1,0:T(8,128)(2,1)S(1)}, bf16[2,48,256]{2,1,0:T(8,128)(2,1)S(1)}, u32[]{:S(2)}, u32[]{:S(2)}) collective-permute-start(bf16[2,48,256]{2,1,0:T(8,128)(2,1)S(1)} %slice_bitcast_fusion), channel_id=1, source_target_pairs={{16,0},{24,8},{17,1},{25,9},{18,2},{26,10},{19,3},{27,11},{20,4},{... | collective-permute-start | bytes 147464 | tf_op jit(solution)/shard_map/ppermute | solution.py:379
  45.0 0.0 collective-permute-done.6.first
  45.0 2.4 %collective-permute-start.13 = (bf16[2,48,256]{2,1,0:T(8,128)(2,1)S(1)}, bf16[2,48,256]{2,1,0:T(8,128)(2,1)S(1)}, u32[]{:S(2)}, u32[]{:S(2)}) collective-permute-start(bf16[2,48,256]{2,1,0:T(8,128)(2,1)S(1)} %slice_bitcast_fusion), channel_id=1, source_target_pairs={{8,0},{16,8},{24,16},{9,1},{17,9},{25,17},{10,2},{18,10},{26,18},{... | collective-permute-start | bytes 147464 | tf_op jit(solution)/shard_map/ppermute | solution.py:379
  47.4 0.0 collective-permute-done.5.three
  47.4 0.0 collective-permute-done.4.two
  47.4 0.0 collective-permute-done.3.one
  47.4 0.0 copy-done.2
  47.5 1.6 %forward_finish.1 = (bf16[4,144,256]{2,1,0:T(8,128)(2,1)S(1)}, f32[4,144,256]{2,1,0:T(8,128)S(1)}, bf16[4,80,256]{2,1,0:T(8,128)(2,1)S(1)}, bf16[4,80,256]{2,1,0:T(8,128)(2,1)S(1)}) custom-call(bf16[48,256]{1,0:T(8,128)(2,1)S(1)} %collective-permute-done.3.one, bf16[48,256]{1,0:T(8,128)(2,1)S(1)} %collective-permute-done.4.two, ...), custom_call_target="tpu_custom_call" | custom-call | flops 200000000 | bytes 3003392 | tf_op jit(solution)/shard_map/forward_finish/pallas_call | solution.py:330
  49.0 0.3 collective-permute-start.8
  49.3 3.9 %collective-permute-start.9 = (bf16[4,80,256]{2,1,0:T(8,128)(2,1)S(1)}, bf16[4,80,256]{2,1,0:T(8,128)(2,1)S(1)}, u32[]{:S(2)}, u32[]{:S(2)}) collective-permute-start(bf16[4,80,256]{2,1,0:T(8,128)(2,1)S(1)} %get-tuple-element.72), channel_id=1, source_target_pairs={{0,7},{1,0},{2,1},{3,2},{4,3},{5,4},{6,5},{7,6},{8,15},{9,8},{10,9... | collective-permute-start | bytes 491528 | tf_op jit(solution)/shard_map/ppermute | solution.py:374
  53.3 0.0 copy-done.9
  53.3 0.7 middle.1
  54.0 3.7 %collective-permute-done.8.up = bf16[4,80,256]{2,1,0:T(8,128)(2,1)S(1)} collective-permute-done((bf16[4,80,256]{2,1,0:T(8,128)(2,1)S(1)}, bf16[4,80,256]{2,1,0:T(8,128)(2,1)S(1)}, u32[]{:S(2)}, u32[]{:S(2)}) %collective-permute-start.8) | collective-permute-done | bytes 163872 | tf_op jit(solution)/shard_map/ppermute | solution.py:374
  57.7 1.8 %collective-permute-done.9.down = bf16[4,80,256]{2,1,0:T(8,128)(2,1)S(1)} collective-permute-done((bf16[4,80,256]{2,1,0:T(8,128)(2,1)S(1)}, bf16[4,80,256]{2,1,0:T(8,128)(2,1)S(1)}, u32[]{:S(2)}, u32[]{:S(2)}) %collective-permute-start.9) | collective-permute-done | bytes 163872 | tf_op jit(solution)/shard_map/ppermute | solution.py:374
  59.5 2.1 %backward_chain.1 = (bf16[4,256,256]{2,1,0:T(8,128)(2,1)S(1)}, f32[4,48,256]{2,1,0:T(8,128)S(1)}, f32[4,48,256]{2,1,0:T(8,128)S(1)}, bf16[48,256]{1,0:T(8,128)(2,1)S(1)}) custom-call(bf16[4,80,256]{2,1,0:T(8,128)(2,1)S(1)} %collective-permute-done.8.up, bf16[4,80,256]{2,1,0:T(8,128)(2,1)S(1)} %collective-permute-done.9.down, ...), custom_call_target="tpu_custom_call" | custom-call | flops 200000000 | bytes 2678784 | tf_op jit(solution)/shard_map/backward_chain/pallas_call | solution.py:330
  61.6 0.7 collective-permute-start.12
  62.3 1.3 %collective-permute-start.11 = (bf16[48,256]{1,0:T(8,128)(2,1)S(1)}, bf16[48,256]{1,0:T(8,128)(2,1)S(1)}, u32[]{:S(2)}, u32[]{:S(2)}) collective-permute-start(bf16[48,256]{1,0:T(8,128)(2,1)S(1)} %get-tuple-element.78), channel_id=1, source_target_pairs={{16,0},{24,8},{17,1},{25,9},{18,2},{26,10},{19,3},{27,11},{20,4},{... | collective-permute-start | bytes 73736 | tf_op jit(solution)/shard_map/ppermute | solution.py:379
  63.6 2.9 %collective-permute-start.10 = (bf16[48,256]{1,0:T(8,128)(2,1)S(1)}, bf16[48,256]{1,0:T(8,128)(2,1)S(1)}, u32[]{:S(2)}, u32[]{:S(2)}) collective-permute-start(bf16[48,256]{1,0:T(8,128)(2,1)S(1)} %get-tuple-element.78), channel_id=1, source_target_pairs={{8,0},{16,8},{24,16},{9,1},{17,9},{25,17},{10,2},{18,10},{26,18},{... | collective-permute-start | bytes 73736 | tf_op jit(solution)/shard_map/ppermute | solution.py:379
  66.5 0.7 backward_base.1
  67.2 0.0 collective-permute-done.14.second
  67.2 0.0 collective-permute-done.13.first
  67.2 0.0 collective-permute-done.12.three
  67.3 0.5 collective-permute-done.11.two
  67.8 2.5 %collective-permute-done.10.one = bf16[48,256]{1,0:T(8,128)(2,1)S(1)} collective-permute-done((bf16[48,256]{1,0:T(8,128)(2,1)S(1)}, bf16[48,256]{1,0:T(8,128)(2,1)S(1)}, u32[]{:S(2)}, u32[]{:S(2)}) %collective-permute-start.10) | collective-permute-done | bytes 24608 | tf_op jit(solution)/shard_map/ppermute | solution.py:379
  70.3 0.0 copy-done.3
  70.3 2.9 %backward_finish.1 = bf16[4,8,32,135]{3,2,1,0:T(8,128)(2,1)} custom-call(bf16[48,256]{1,0:T(8,128)(2,1)S(1)} %collective-permute-done.10.one, bf16[48,256]{1,0:T(8,128)(2,1)S(1)} %collective-permute-done.11.two, bf16[48,256]{1,0:T(8,128)(2,1)S(1)} %collective-permute-done.12.three, bf16[2,48,256]{2,1,0:T(8,128)(2,1)S(1)} %collective-permute-done.13.first, ...), custom_call_target="tpu_custom_call" | custom-call | flops 200000000 | bytes 2060256 | tf_op jit(solution)/shard_map/backward_finish/pallas_call | solution.py:330
  (13 shorter events, 0.0 us)
Async XLA Ops:
  0.9 1.0 %copy-start.4 = (bf16[4,8,32,135]{3,2,1,0:T(8,128)(2,1)S(1)}, bf16[4,8,32,135]{3,2,1,0:T(8,128)(2,1)}, u32[]{:S(2)}) copy-start(bf16[4,8,32,135]{3,2,1,0:T(8,128)(2,1)} %initial.2) | copy-start | bytes 829444
  2.0 0.9 %copy-start.7 = (bf16[160,135]{1,0:T(8,128)(2,1)S(1)}, bf16[160,135]{1,0:T(8,128)(2,1)}, u32[]{:S(2)}) copy-start(bf16[160,135]{1,0:T(8,128)(2,1)} %constant.63.clone.send) | copy-start | bytes 129604
  2.9 0.7 %copy-start.11 = (bf16[48,135]{1,0:T(8,128)(2,1)S(1)}, bf16[48,135]{1,0:T(8,128)(2,1)}, u32[]{:S(2)}) copy-start(bf16[48,135]{1,0:T(8,128)(2,1)} %constant.67.clone.first_face) | copy-start | bytes 38884
  3.6 2.9 %copy-start.13 = (bf16[4,8,6,45,135]{4,1,3,2,0:T(8,128)(2,1)S(1)}, bf16[4,8,6,45,135]{4,1,3,2,0:T(8,128)(2,1)}, u32[]{:S(2)}) copy-start(bf16[4,8,6,45,135]{4,1,3,2,0:T(8,128)(2,1)} %param.17) | copy-start | bytes 6998404
  6.5 1.1 %copy-start.5 = (bf16[4,8,32,135]{3,2,1,0:T(8,128)(2,1)S(1)}, bf16[4,8,32,135]{3,2,1,0:T(8,128)(2,1)}, u32[]{:S(2)}) copy-start(bf16[4,8,32,135]{3,2,1,0:T(8,128)(2,1)} %initial.2) | copy-start | bytes 829444
  6.5 1.2 %copy-start.6 = (bf16[4,8,32,135]{3,2,1,0:T(8,128)(2,1)S(1)}, bf16[4,8,32,135]{3,2,1,0:T(8,128)(2,1)}, u32[]{:S(2)}) copy-start(bf16[4,8,32,135]{3,2,1,0:T(8,128)(2,1)} %right.1) | copy-start | bytes 829444
  6.5 1.2 %copy-start.8 = (bf16[144,135]{1,0:T(8,128)(2,1)S(1)}, bf16[144,135]{1,0:T(8,128)(2,1)}, u32[]{:S(2)}) copy-start(bf16[144,135]{1,0:T(8,128)(2,1)} %constant.68.clone.perm) | copy-start | bytes 116644
  6.5 1.2 %copy-start.10 = (bf16[96,135]{1,0:T(8,128)(2,1)S(1)}, bf16[96,135]{1,0:T(8,128)(2,1)}, u32[]{:S(2)}) copy-start(bf16[96,135]{1,0:T(8,128)(2,1)} %constant.65.clone.own_sel) | copy-start | bytes 77764
  6.5 1.2 %copy-start.12 = (bf16[48,135]{1,0:T(8,128)(2,1)S(1)}, bf16[48,135]{1,0:T(8,128)(2,1)}, u32[]{:S(2)}) copy-start(bf16[48,135]{1,0:T(8,128)(2,1)} %constant.67.clone.first_face) | copy-start | bytes 38884
  7.7 29.1 %copy-start = (bf16[96,80]{1,0:T(8,128)(2,1)S(1)}, bf16[96,80]{1,0:T(8,128)(2,1)}, u32[]{:S(2)}) copy-start(bf16[96,80]{1,0:T(8,128)(2,1)} %constant.71.clone.down_sel) | copy-start | bytes 46084
  7.7 29.1 %copy-start.1 = (bf16[96,80]{1,0:T(8,128)(2,1)S(1)}, bf16[96,80]{1,0:T(8,128)(2,1)}, u32[]{:S(2)}) copy-start(bf16[96,80]{1,0:T(8,128)(2,1)} %constant.70.clone.up_sel) | copy-start | bytes 46084
  17.7 26.0 %collective-permute-start.7 = (bf16[2,48,256]{2,1,0:T(8,128)(2,1)S(1)}, bf16[2,48,256]{2,1,0:T(8,128)(2,1)S(1)}, u32[]{:S(2)}, u32[]{:S(2)}) collective-permute-start(bf16[2,48,256]{2,1,0:T(8,128)(2,1)S(1)} %slice_bitcast_fusion.1), channel_id=1, source_target_pairs={{0,16},{8,24},{1,17},{9,25},{2,18},{10,26},{3,19},{11,27},{4,20},{... | collective-permute-start | bytes 147464 | tf_op jit(solution)/shard_map/ppermute | solution.py:379
  21.6 23.3 %collective-permute-start.6 = (bf16[2,48,256]{2,1,0:T(8,128)(2,1)S(1)}, bf16[2,48,256]{2,1,0:T(8,128)(2,1)S(1)}, u32[]{:S(2)}, u32[]{:S(2)}) collective-permute-start(bf16[2,48,256]{2,1,0:T(8,128)(2,1)S(1)} %slice_bitcast_fusion.1), channel_id=1, source_target_pairs={{0,8},{8,16},{16,24},{1,9},{9,17},{17,25},{2,10},{10,18},{18,26},{... | collective-permute-start | bytes 147464 | tf_op jit(solution)/shard_map/ppermute | solution.py:379
  23.6 6.8 %collective-permute-start.2 = (bf16[48,256]{1,0:T(8,128)(2,1)S(1)}, bf16[48,256]{1,0:T(8,128)(2,1)S(1)}, u32[]{:S(2)}, u32[]{:S(2)}) collective-permute-start(bf16[48,256]{1,0:T(8,128)(2,1)S(1)} %get-tuple-element.52), channel_id=1, source_target_pairs={{8,0},{16,8},{24,16},{9,1},{17,9},{25,17},{10,2},{18,10},{26,18},{... | collective-permute-start | bytes 73736 | tf_op jit(solution)/shard_map/ppermute | solution.py:379
  26.0 8.7 %collective-permute-start = (bf16[4,80,256]{2,1,0:T(8,128)(2,1)S(1)}, bf16[4,80,256]{2,1,0:T(8,128)(2,1)S(1)}, u32[]{:S(2)}, u32[]{:S(2)}) collective-permute-start(bf16[4,80,256]{2,1,0:T(8,128)(2,1)S(1)} %get-tuple-element.50), channel_id=1, source_target_pairs={{0,1},{1,2},{2,3},{3,4},{4,5},{5,6},{6,7},{7,0},{8,9},{9,10},{10,1... | collective-permute-start | bytes 491528 | tf_op jit(solution)/shard_map/ppermute | solution.py:374
  27.3 9.6 %collective-permute-start.1 = (bf16[4,80,256]{2,1,0:T(8,128)(2,1)S(1)}, bf16[4,80,256]{2,1,0:T(8,128)(2,1)S(1)}, u32[]{:S(2)}, u32[]{:S(2)}) collective-permute-start(bf16[4,80,256]{2,1,0:T(8,128)(2,1)S(1)} %get-tuple-element.51), channel_id=1, source_target_pairs={{0,7},{1,0},{2,1},{3,2},{4,3},{5,4},{6,5},{7,6},{8,15},{9,8},{10,9... | collective-permute-start | bytes 491528 | tf_op jit(solution)/shard_map/ppermute | solution.py:374
  36.9 10.6 %copy-start.2 = (bf16[160,144]{1,0:T(8,128)(2,1)S(1)}, bf16[160,144]{1,0:T(8,128)(2,1)}, u32[]{:S(2)}) copy-start(bf16[160,144]{1,0:T(8,128)(2,1)} %constant.64.clone.send) | copy-start | bytes 138244
  39.0 8.4 %collective-permute-start.5 = (bf16[48,256]{1,0:T(8,128)(2,1)S(1)}, bf16[48,256]{1,0:T(8,128)(2,1)S(1)}, u32[]{:S(2)}, u32[]{:S(2)}) collective-permute-start(bf16[48,256]{1,0:T(8,128)(2,1)S(1)} %get-tuple-element.58), channel_id=1, source_target_pairs={{0,24},{1,25},{2,26},{3,27},{4,28},{5,29},{6,30},{7,31}} | collective-permute-start | bytes 73736 | tf_op jit(solution)/shard_map/ppermute | solution.py:379
  39.7 7.7 %collective-permute-start.4 = (bf16[48,256]{1,0:T(8,128)(2,1)S(1)}, bf16[48,256]{1,0:T(8,128)(2,1)S(1)}, u32[]{:S(2)}, u32[]{:S(2)}) collective-permute-start(bf16[48,256]{1,0:T(8,128)(2,1)S(1)} %get-tuple-element.58), channel_id=1, source_target_pairs={{0,16},{8,24},{1,17},{9,25},{2,18},{10,26},{3,19},{11,27},{4,20},{... | collective-permute-start | bytes 73736 | tf_op jit(solution)/shard_map/ppermute | solution.py:379
  41.0 6.4 %collective-permute-start.3 = (bf16[48,256]{1,0:T(8,128)(2,1)S(1)}, bf16[48,256]{1,0:T(8,128)(2,1)S(1)}, u32[]{:S(2)}, u32[]{:S(2)}) collective-permute-start(bf16[48,256]{1,0:T(8,128)(2,1)S(1)} %get-tuple-element.58), channel_id=1, source_target_pairs={{0,8},{8,16},{16,24},{1,9},{9,17},{17,25},{2,10},{10,18},{18,26},{... | collective-permute-start | bytes 73736 | tf_op jit(solution)/shard_map/ppermute | solution.py:379
  42.9 10.3 %copy-start.9 = (bf16[96,144]{1,0:T(8,128)(2,1)S(1)}, bf16[96,144]{1,0:T(8,128)(2,1)}, u32[]{:S(2)}) copy-start(bf16[96,144]{1,0:T(8,128)(2,1)} %constant.66.clone.own_sel) | copy-start | bytes 82948
  43.7 23.6 %collective-permute-start.14 = (bf16[2,48,256]{2,1,0:T(8,128)(2,1)S(1)}, bf16[2,48,256]{2,1,0:T(8,128)(2,1)S(1)}, u32[]{:S(2)}, u32[]{:S(2)}) collective-permute-start(bf16[2,48,256]{2,1,0:T(8,128)(2,1)S(1)} %slice_bitcast_fusion), channel_id=1, source_target_pairs={{16,0},{24,8},{17,1},{25,9},{18,2},{26,10},{19,3},{27,11},{20,4},{... | collective-permute-start | bytes 147464 | tf_op jit(solution)/shard_map/ppermute | solution.py:379
  45.0 22.3 %collective-permute-start.13 = (bf16[2,48,256]{2,1,0:T(8,128)(2,1)S(1)}, bf16[2,48,256]{2,1,0:T(8,128)(2,1)S(1)}, u32[]{:S(2)}, u32[]{:S(2)}) collective-permute-start(bf16[2,48,256]{2,1,0:T(8,128)(2,1)S(1)} %slice_bitcast_fusion), channel_id=1, source_target_pairs={{8,0},{16,8},{24,16},{9,1},{17,9},{25,17},{10,2},{18,10},{26,18},{... | collective-permute-start | bytes 147464 | tf_op jit(solution)/shard_map/ppermute | solution.py:379
  49.0 8.7 %collective-permute-start.8 = (bf16[4,80,256]{2,1,0:T(8,128)(2,1)S(1)}, bf16[4,80,256]{2,1,0:T(8,128)(2,1)S(1)}, u32[]{:S(2)}, u32[]{:S(2)}) collective-permute-start(bf16[4,80,256]{2,1,0:T(8,128)(2,1)S(1)} %get-tuple-element.71), channel_id=1, source_target_pairs={{0,1},{1,2},{2,3},{3,4},{4,5},{5,6},{6,7},{7,0},{8,9},{9,10},{10,1... | collective-permute-start | bytes 491528 | tf_op jit(solution)/shard_map/ppermute | solution.py:374
  49.3 10.1 %collective-permute-start.9 = (bf16[4,80,256]{2,1,0:T(8,128)(2,1)S(1)}, bf16[4,80,256]{2,1,0:T(8,128)(2,1)S(1)}, u32[]{:S(2)}, u32[]{:S(2)}) collective-permute-start(bf16[4,80,256]{2,1,0:T(8,128)(2,1)S(1)} %get-tuple-element.72), channel_id=1, source_target_pairs={{0,7},{1,0},{2,1},{3,2},{4,3},{5,4},{6,5},{7,6},{8,15},{9,8},{10,9... | collective-permute-start | bytes 491528 | tf_op jit(solution)/shard_map/ppermute | solution.py:374
  59.5 10.8 %copy-start.3 = (bf16[135,144]{1,0:T(8,128)(2,1)S(1)}, bf16[135,144]{1,0:T(8,128)(2,1)}, u32[]{:S(2)}) copy-start(bf16[135,144]{1,0:T(8,128)(2,1)} %constant.69.clone.back) | copy-start | bytes 116644
  61.6 5.6 %collective-permute-start.12 = (bf16[48,256]{1,0:T(8,128)(2,1)S(1)}, bf16[48,256]{1,0:T(8,128)(2,1)S(1)}, u32[]{:S(2)}, u32[]{:S(2)}) collective-permute-start(bf16[48,256]{1,0:T(8,128)(2,1)S(1)} %get-tuple-element.78), channel_id=1, source_target_pairs={{24,0},{25,1},{26,2},{27,3},{28,4},{29,5},{30,6},{31,7}} | collective-permute-start | bytes 73736 | tf_op jit(solution)/shard_map/ppermute | solution.py:379
  62.3 5.5 %collective-permute-start.11 = (bf16[48,256]{1,0:T(8,128)(2,1)S(1)}, bf16[48,256]{1,0:T(8,128)(2,1)S(1)}, u32[]{:S(2)}, u32[]{:S(2)}) collective-permute-start(bf16[48,256]{1,0:T(8,128)(2,1)S(1)} %get-tuple-element.78), channel_id=1, source_target_pairs={{16,0},{24,8},{17,1},{25,9},{18,2},{26,10},{19,3},{27,11},{20,4},{... | collective-permute-start | bytes 73736 | tf_op jit(solution)/shard_map/ppermute | solution.py:379
  63.6 6.7 %collective-permute-start.10 = (bf16[48,256]{1,0:T(8,128)(2,1)S(1)}, bf16[48,256]{1,0:T(8,128)(2,1)S(1)}, u32[]{:S(2)}, u32[]{:S(2)}) collective-permute-start(bf16[48,256]{1,0:T(8,128)(2,1)S(1)} %get-tuple-element.78), channel_id=1, source_target_pairs={{8,0},{16,8},{24,16},{9,1},{17,9},{25,17},{10,2},{18,10},{26,18},{... | collective-permute-start | bytes 73736 | tf_op jit(solution)/shard_map/ppermute | solution.py:379

commit v2 on v1

v2 whole, which is shorter than its diff:
```python
import functools

import jax
import jax.numpy as jnp
import numpy as np
from jax import lax
from jax.experimental import pallas as pl
from jax.experimental.pallas import tpu as pltpu
from jax.sharding import PartitionSpec as P

BF = jnp.bfloat16
F32 = jnp.float32
NT = 45
FACE = 48
SLOT = 64
ROWS = 3 * FACE
SHARED = 80
MIB = 1 << 20


def natural(v, a, b, c):
    return v * 27 + a * 9 + b * 3 + c


def inner(v, a, b, c):
    return a * FACE + v * 9 + b * 3 + c


NODES = [(v, a, b, c) for v in range(5) for a in range(3) for b in range(3) for c in range(3)]


def face_nodes(place, which):
    return [n for n in NODES if n[1 + place] == which]


def union_rows(which):
    others = [b for b in range(3) if b != which]
    spots = [(which, c) for c in range(3)] + [(b, which) for b in others]
    return [
        (v * 16 + a * 5 + j, (v, a, b, c)) for v in range(5) for a in range(3) for j, (b, c) in enumerate(spots)
    ]


def table(height, width, rows, column_of, value=1.0):
    out = np.zeros((height, width), np.float32)
    for row, node in rows:
        out[row, column_of(*node)] = value
    return out


def block(nodes, start=0):
    return [(start + i, n) for i, n in enumerate(nodes)]


def send_table(width, column_of):
    rows = union_rows(2) + [(SHARED + i, n) for i, n in union_rows(0)]
    return table(2 * SHARED, width, rows, column_of)


def own_table(width, column_of):
    rows = block(face_nodes(2, 2)) + block(face_nodes(2, 0), FACE)
    return table(2 * FACE, width, rows, column_of)


def receive_table(which):
    place = {n: i for i, n in union_rows(which)}
    rows = block(face_nodes(1, which)) + block(face_nodes(2, which), FACE)
    return table(2 * FACE, SHARED, rows, lambda *n: place[n])


def mm(a, b):
    return lax.dot_general(a, b, (((1,), (0,)), ((), ())), preferred_element_type=F32)


def mt(a, b):
    return lax.dot_general(a, b, (((1,), (1,)), ((), ())), preferred_element_type=F32)


def split_lanes(value, width):
    lanes = value.shape[1]
    value = value.astype(F32)
    owner = lax.broadcasted_iota(jnp.int32, value.shape, 1) // width
    pad = jnp.zeros((SLOT - FACE, lanes), BF)
    parts = []
    for c in range(lanes // width):
        parts += [jnp.where(owner == c, value, 0.0).astype(BF), pad]
    return jnp.concatenate(parts, 0)


def own_lanes(values, width):
    owner = lax.broadcasted_iota(jnp.int32, values[0].shape, 1) // width
    out = values[0]
    for c in range(1, len(values)):
        out = jnp.where(owner == c, values[c], out)
    return out


def one_hot(source, start, height):
    row = lax.broadcasted_iota(jnp.int32, (height, source.shape[1]), 0) + start
    return jnp.where(row == source, 1.0, 0.0).astype(BF)


def chain_step(matrix, trace, rhs):
    half = trace.shape[1] // 2
    return jnp.concatenate(
        [mm(matrix[h], split_lanes(trace[:, h * half : (h + 1) * half], rhs)) for h in range(2)], 1
    )


def shared_target(row, which):
    v, k = row // 16, row % 16
    a = k // 5
    j = k % 5
    b = jnp.where(j < 3, which, j - 3 if which == 2 else j - 2)
    c = jnp.where(j < 3, j, which)
    return jnp.where(k < 15, v * 27 + a * 9 + b * 3 + c, -1)


def picks(target, width):
    lane = lax.broadcasted_iota(jnp.int32, (target.shape[0], width), 1)
    return jnp.where(lane == target, 1.0, 0.0).astype(BF)


def rows_of(height):
    return lax.broadcasted_iota(jnp.int32, (height, 1), 0)


def first_target(row):
    return jnp.where(row < NT, row // 9 * 27 + row % 9, -1)


def c_target(row, which):
    return jnp.where(row < NT, row * 3 + which, -1)


def sources(neighbours, columns, rhs):
    place = lax.axis_index("cross")
    total = columns * lax.axis_size("cross")
    lane = lax.broadcasted_iota(jnp.int32, (1, columns * rhs), 1)
    out = []
    for face, first in ((2, place - 1), (3, place)):
        which = jnp.zeros_like(lane)
        for c in range(columns):
            at = lax.rem(neighbours[face, c] - first * columns + 2 * total, total)
            which = jnp.where(lane // rhs == c, at, which)
        out.append(which * rhs + lane % rhs)
    return out


def first_kernel(initial, up, down, above):
    planes, columns, rhs, width = initial.shape
    shared = rows_of(SHARED)
    tables = [picks(shared_target(shared, which), width) for which in (2, 0)]
    for p in range(planes):
        x = initial[p].reshape(columns * rhs, width)
        up[p] = mt(tables[0], x).astype(BF)
        down[p] = mt(tables[1], x).astype(BF)
        if p == 0:
            above[...] = mt(picks(first_target(rows_of(FACE)), width), x).astype(BF)


def turned(rows):
    pad = jnp.zeros((FACE - NT,) + rows.shape[1:], rows.dtype)
    return jnp.swapaxes(jnp.concatenate([rows, pad], 0), 0, 1)


def weight_kernel(
    inverse, couplings, right, initial, neighbours,
    known0, known1, known2, lower0, lower1, lower2, upper0, upper1, upper2, base0, base1, base2,
    fore0, fore1, fore2, own, cum_f, cum_b, passes, solves, faces, prev, backs, tables,
):
    known, lower, upper = (known0, known1, known2), (lower0, lower1, lower2), (upper0, upper1, upper2)
    base, fore = (base0, base1, base2), (fore0, fore1, fore2)
    p = pl.program_id(0)
    planes, columns, rhs, width = initial.shape
    size = columns * rhs
    half = columns // 2

    @pl.when(p == 0)
    def _():
        faces[...] = jnp.zeros(faces.shape, BF)
        tables[:FACE] = picks(c_target(rows_of(FACE), 2), width)
        tables[FACE : 2 * FACE] = picks(c_target(rows_of(FACE), 0), width)
        tables[2 * FACE :] = picks(first_target(rows_of(FACE)), width)

    for a in range(3):
        rows = [inverse[0, v * 27 + a * 9 : v * 27 + a * 9 + 9] for v in range(5)]
        solves[:, a * FACE : (a + 1) * FACE] = -turned(jnp.concatenate(rows, 0))
    for f in range(4):
        faces[:, f * FACE : (f + 1) * FACE] = turned(couplings[0, 2 + f])
    faces[:, 4 * FACE : 4 * FACE + rhs] = right[0]
    faces[:, 256 : 256 + FACE] = turned(couplings[0, 0])
    faces[:, 256 + SLOT : 256 + SLOT + FACE] = turned(couplings[0, 1])

    pairs_lower, pairs_upper, bases = [], [], []
    lane = lax.broadcasted_iota(jnp.int32, (ROWS, 2 * SLOT), 1)
    before = None
    for c in range(columns):
        solve = solves[c]
        all_known = mt(solve, faces[c, :256])
        side = all_known[:, 128:]
        move = (c % half * rhs - (4 * FACE - 128)) % 128
        bases.append(pltpu.roll(side, move, 1) if move else side)
        all_known = all_known.astype(BF)
        for a in range(3):
            known[a][0, c] = all_known[a * FACE : (a + 1) * FACE]
        both = mt(solve, faces[c, 256:])
        if c % 2 == 0:
            before = both
        else:
            pairs_lower.append(jnp.where(lane < SLOT, before, pltpu.roll(both, SLOT, 1)).astype(BF))
            pairs_upper.append(jnp.where(lane < SLOT, pltpu.roll(before, SLOT, 1), both).astype(BF))
    x = initial[p].reshape(size, width)
    beyond = initial[jnp.minimum(p + 1, planes - 1)].reshape(size, width)
    after = jnp.where(p + 1 < planes, mt(tables[2 * FACE :], beyond), 0.0)
    for h in range(2):
        lanes = slice(h * half * rhs, (h + 1) * half * rhs)
        down = jnp.concatenate(pairs_lower[2 * h : 2 * h + 2], 1)
        up = jnp.concatenate(pairs_upper[2 * h : 2 * h + 2], 1)
        backs[p, h] = up[:FACE]
        here = -own_lanes(bases[h * half : (h + 1) * half], rhs)
        there = here + mm(up, split_lanes(after[:, lanes], rhs))
        for a in range(3):
            rows = slice(a * FACE, (a + 1) * FACE)
            lower[a][0, h] = down[rows]
            upper[a][0, h] = up[rows]
            base[a][0, :, lanes] = here[rows]
            fore[a][0, :, lanes] = there[rows]
        step = down[2 * FACE :]

        @pl.when(p == 0)
        def _():
            prev[h] = step.astype(F32)

        @pl.when(p > 0)
        def _():
            prev[h] = mm(step, split_lanes(prev[h], SLOT))

        cum_f[0, h] = prev[h].astype(BF)

    mine = mt(tables[: 2 * FACE], x).astype(BF)
    source = sources(neighbours, columns, rhs)
    own[0, :FACE] = mm(mine[:FACE], one_hot(source[0], size, size)).astype(BF)
    own[0, FACE:] = mm(mine[FACE:], one_hot(source[1], 0, size)).astype(BF)

    @pl.when(p == planes - 1)
    def _():
        for h in range(2):
            passes[0, h] = prev[h].astype(BF)
            total = backs[planes - 1, h].astype(F32)
            cum_b[planes - 1, h] = total.astype(BF)
            for q in range(planes - 2, -1, -1):
                total = mm(backs[q, h], split_lanes(total, SLOT))
                cum_b[q, h] = total.astype(BF)
            passes[1, h] = total.astype(BF)


def gathered(received_up, received_down, own, p, up_sel, down_sel, low_pick, high_pick):
    low = mm(up_sel, received_up[p]).astype(BF)
    high = mm(down_sel, received_down[p]).astype(BF)
    c_low = mm(low[FACE:], low_pick).astype(BF) + own[p, :FACE]
    c_high = mm(high[FACE:], high_pick).astype(BF) + own[p, FACE : 2 * FACE]
    return [low[:FACE], high[:FACE], c_low, c_high]


def known_part(known_c, operand, columns, rhs):
    half = columns // 2
    out = []
    for h in range(2):
        side = operand[:, h * half * rhs : (h + 1) * half * rhs]
        out.append(own_lanes([mm(known_c(h * half + c), side) for c in range(half)], rhs))
    return jnp.concatenate(out, 1)


def chain_kernel(known, base, matrix, received, own, neighbours, outs, order, rhs, extra=None):
    up, down, up_sel, down_sel = received
    operand, part, traces, last = outs
    planes, columns = known.shape[:2]
    size = columns * rhs
    source = sources(neighbours, columns, rhs)
    low_pick = one_hot(source[0], 0, size)
    high_pick = one_hot(source[1], size, size)
    starts = {}
    for p in order:
        parts = gathered(up, down, own, p, up_sel[...], down_sel[...], low_pick, high_pick)
        parts.append(jnp.zeros((256 - 4 * FACE, size), BF))
        whole = jnp.concatenate(parts, 0)
        operand[p] = whole
        starts[p] = base[p] + known_part(lambda c: known[p, c], whole, columns, rhs)
        if extra is not None and p == planes - 1:
            starts[p] = starts[p] + chain_step(extra[0][p], extra[1][...], rhs)
        part[p] = starts[p]
    trace = None
    for p in order:
        trace = starts[p] if trace is None else starts[p] + chain_step(matrix[p], trace, rhs)
        traces[p] = trace
    for i in range(last.shape[0]):
        last[i] = trace.astype(BF)


def forward_chain_kernel(
    up, down, above, own, neighbours, up_sel, down_sel, known, lower, upper, base, *outs, rhs
):
    order = range(up.shape[0])
    received = (up, down, up_sel, down_sel)
    chain_kernel(known, base, lower, received, own, neighbours, outs, order, rhs, (upper, above))


def backward_chain_kernel(up, down, own, neighbours, up_sel, down_sel, known, upper, base, *outs, rhs):
    order = range(up.shape[0] - 1, -1, -1)
    chain_kernel(known, base, upper, (up, down, up_sel, down_sel), own, neighbours, outs, order, rhs)


def base_kernel(known_one, known_two, operand, base_one, base_two, *rest, rhs):
    planes, columns = known_one.shape[:2]
    extra, (one, two) = rest[:-2], rest[-2:]
    for p in range(planes):
        for i, (known, base, out) in enumerate(((known_one, base_one, one), (known_two, base_two, two))):
            value = base[p] + known_part(lambda c: known[p, c], operand[p], columns, rhs)
            if extra and p == planes - 1:
                value = value + chain_step(extra[1 + i][p], extra[0][...], rhs)
            out[p] = value


def incoming(last, passes, way, rhs):
    here = lax.axis_index("sweep")
    n = last.shape[0]
    trace = None
    for i in range(n - 1) if way == 0 else range(n - 1, 0, -1):
        value = last[i].astype(F32)
        if trace is None:
            trace = jnp.zeros_like(value)
        else:
            value = value + chain_step(passes[i, way], trace, rhs)
        trace = jnp.where(i < here if way == 0 else i > here, value, trace)
    return trace


def forward_finish_kernel(
    last, passes, cum, traces, part0, part1, part2, lower0, lower1, lower2, send, middle, change, up, down, *, rhs
):
    planes = traces.shape[0]
    entry = incoming(last, passes, 0, rhs)
    trace = entry
    for p in range(planes):
        matrix = [jnp.concatenate([x[p, h] for x in (lower0, lower1, lower2)], 0) for h in range(2)]
        delta = chain_step(matrix, trace, rhs)
        whole = jnp.concatenate([x[p] for x in (part0, part1, part2)], 0) + delta
        change[p] = delta
        whole = whole.astype(BF)
        middle[p] = whole
        out = mm(send[...], whole).astype(BF)
        up[p] = out[:SHARED]
        down[p] = out[SHARED:]
        if p + 1 < planes:
            trace = traces[p] + chain_step(cum[p], entry, rhs)


def middle_kernel(middle, change, base0, base1, base2, neighbours, own_sel, own, out0, out1, out2):
    planes, _, size = middle.shape
    columns = neighbours.shape[1]
    source = sources(neighbours, columns, size // columns)
    low_pick = one_hot(source[0], size, size)
    high_pick = one_hot(source[1], 0, size)
    for p in range(planes):
        mine = mm(own_sel[...], middle[p]).astype(BF)
        own[p, :FACE] = mm(mine[:FACE], low_pick).astype(BF)
        own[p, FACE:] = mm(mine[FACE:], high_pick).astype(BF)
        for a, (base, out) in enumerate(((base0, out0), (base1, out1), (base2, out2))):
            out[p] = base[p] + change[p, a * FACE : (a + 1) * FACE]


def backward_finish_kernel(
    last, passes, cum, traces, part0, part1, part2, upper0, upper1, upper2, back, result, *, rhs
):
    planes = traces.shape[0]
    entry = incoming(last, passes, 1, rhs)
    size = entry.shape[1]
    row = lax.broadcasted_iota(jnp.int32, (size, size), 0)
    column = lax.broadcasted_iota(jnp.int32, (size, size), 1)
    unit = jnp.where(row == column, 1.0, 0.0).astype(BF)
    columns, _, width = result.shape[1:]
    for p in range(planes - 1, -1, -1):
        trace = entry if p + 1 == planes else traces[p + 1] + chain_step(cum[p + 1], entry, rhs)
        matrix = [jnp.concatenate([x[p, h] for x in (upper0, upper1, upper2)], 0) for h in range(2)]
        whole = jnp.concatenate([x[p] for x in (part0, part1, part2)], 0) + chain_step(matrix, trace, rhs)
        turned = mm(back[...], whole.astype(BF)).astype(BF)
        result[p] = mt(unit, turned).astype(BF).reshape(columns, rhs, width)


def cost(flops, nbytes):
    return pl.CostEstimate(flops=int(flops), bytes_accessed=int(nbytes), transcendentals=0)


def call(kernel, outs, operands, name, flops=2e8):
    shapes = [jax.ShapeDtypeStruct(s, d) for s, d in outs]
    nbytes = sum(x.size * x.dtype.itemsize for x in list(operands) + shapes)
    return pl.pallas_call(
        kernel,
        out_shape=shapes,
        in_specs=[
            pl.BlockSpec(memory_space=pltpu.SMEM if x.dtype == jnp.int32 else pltpu.VMEM) for x in operands
        ],
        out_specs=[pl.BlockSpec(memory_space=pltpu.VMEM)] * len(shapes),
        compiler_params=pltpu.CompilerParams(vmem_limit_bytes=24 * MIB),
        cost_estimate=cost(flops, nbytes),
        name=name,
    )(*operands)


def weights(inverse, couplings, right, initial, neighbours):
    planes, columns, rhs, width = initial.shape
    size = columns * rhs
    whole = lambda x: pl.BlockSpec(x.shape, lambda p, n=x.ndim: (0,) * n)
    lead = lambda s: pl.BlockSpec((1,) + s[1:], lambda p, n=len(s): (p,) + (0,) * (n - 1))
    known = (planes, columns, FACE, 256)
    pack = (planes, 2, FACE, 256)
    base = (planes, FACE, size)
    own = (planes, 2 * FACE, size)
    outs = [(known, BF)] * 3 + [(pack, BF)] * 6 + [(base, F32)] * 6
    outs += [(own, BF), (pack, BF), (pack, BF), ((2,) + pack[1:], BF)]
    outs = [jax.ShapeDtypeStruct(s, d) for s, d in outs]
    return pl.pallas_call(
        weight_kernel,
        grid=(planes,),
        out_shape=outs,
        in_specs=[lead(x.shape) for x in (inverse, couplings, right)]
        + [whole(initial), pl.BlockSpec(memory_space=pltpu.SMEM)],
        out_specs=[lead(x.shape) for x in outs[:-2]] + [whole(x) for x in outs[-2:]],
        scratch_shapes=[
            pltpu.VMEM((columns, ROWS, width), BF),
            pltpu.VMEM((columns, 256 + 2 * SLOT, width), BF),
            pltpu.VMEM((2, FACE, 256), F32),
            pltpu.VMEM((planes, 2, FACE, 256), BF),
            pltpu.VMEM((3 * FACE, width), BF),
        ],
        compiler_params=pltpu.CompilerParams(
            vmem_limit_bytes=24 * MIB, dimension_semantics=("arbitrary",)
        ),
        cost_estimate=cost(1e10, 12e6),
        name="weights",
    )(inverse, couplings, right, initial, neighbours)


def ring(x, axis, by):
    n = lax.axis_size(axis)
    return lax.ppermute(x, axis, [(i, (i + by) % n) for i in range(n)])


def shift(x, axis, by):
    n = lax.axis_size(axis)
    return lax.ppermute(x, axis, [(i, i + by) for i in range(n) if 0 <= i + by < n])


def local(right_sides, initial, inverse_blocks, couplings, neighbours):
    planes, columns, rhs, width = initial.shape
    size = columns * rhs
    const = lambda x: jnp.asarray(x, BF)
    send_in = const(send_table(ROWS, inner))
    own_in = const(own_table(ROWS, inner))
    back = const(table(width, ROWS, [(natural(*n), n) for n in NODES], inner))
    up_sel = const(receive_table(2))
    down_sel = const(receive_table(0))
    beside = neighbours.T

    share = (planes, SHARED, size)
    up, down, above = call(
        first_kernel, [(share, BF), (share, BF), ((FACE, size), BF)], (initial,), "initial_traces"
    )
    up, down, above, initial = lax.optimization_barrier((up, down, above, initial))
    from_low = ring(up, "cross", 1)
    from_high = ring(down, "cross", -1)
    from_above = shift(above, "sweep", -1)
    *parts, own, cum_f, cum_b, passes = weights(
        inverse_blocks.transpose(0, 2, 1, 3), couplings.transpose(0, 2, 3, 1, 4), right_sides, initial, beside
    )
    known, lower, upper, base, fore = (parts[i : i + 3] for i in range(0, 15, 3))
    from_low, from_high, from_above, passes = lax.optimization_barrier((from_low, from_high, from_above, passes))
    passes = lax.all_gather(passes, "sweep")

    sections = lax.axis_size("sweep")
    trace = (planes, FACE, size)
    deep = (planes, ROWS, size)
    chain_outs = [((planes, 256, size), BF), (trace, F32), (trace, F32), ((sections, FACE, size), BF)]
    operand, part2, traces, last = call(
        functools.partial(forward_chain_kernel, rhs=rhs),
        chain_outs,
        (from_low, from_high, from_above, own, beside, up_sel, down_sel, known[2], lower[2], upper[2], fore[2]),
        "forward_chain",
    )
    last = lax.all_to_all(last, "sweep", 0, 0)
    part0, part1 = call(
        functools.partial(base_kernel, rhs=rhs),
        [(trace, F32)] * 2,
        (known[0], known[1], operand, fore[0], fore[1], from_above, upper[0], upper[1]),
        "forward_base",
        2e9,
    )
    middle, change, up, down = call(
        functools.partial(forward_finish_kernel, rhs=rhs),
        [(deep, BF), (deep, F32), (share, BF), (share, BF)],
        (last, passes, cum_f, traces, part0, part1, part2, *lower, send_in),
        "forward_finish",
    )
    from_low = ring(up, "cross", 1)
    from_high = ring(down, "cross", -1)
    own, *base = call(
        middle_kernel,
        [((planes, 2 * FACE, size), BF)] + [(trace, F32)] * 3,
        (middle, change, *base, beside, own_in),
        "middle",
        2e9,
    )
    operand, part0, traces, last = call(
        functools.partial(backward_chain_kernel, rhs=rhs),
        chain_outs,
        (from_low, from_high, own, beside, up_sel, down_sel, known[0], upper[0], base[0]),
        "backward_chain",
    )
    last = lax.all_to_all(last, "sweep", 0, 0)
    part1, part2 = call(
        functools.partial(base_kernel, rhs=rhs),
        [(trace, F32)] * 2,
        (known[1], known[2], operand, base[1], base[2]),
        "backward_base",
        2e9,
    )
    (result,) = call(
        functools.partial(backward_finish_kernel, rhs=rhs),
        [(right_sides.shape, BF)],
        (last, passes, cum_b, traces, part0, part1, part2, *upper, back),
        "backward_finish",
    )
    return result


def solution(mesh):
    return jax.shard_map(
        local,
        mesh=mesh,
        in_specs=(
            P("sweep", "cross", None, None),
            P("sweep", "cross", None, None),
            P("sweep", "cross", None, None),
            P("sweep", "cross", None, None, None),
            P("cross", None),
        ),
        out_specs=P("sweep", "cross", None, None),
        check_vma=False,
    )
```

time: 73.7 us -> 78.6 us (1.066); the launches traced: 73.2 us -> 77.1 us
  local copies, waits for them, and re-layouts: 6.57 us -> 27.8 us
  waiting for transfers between devices: 15 us -> 0.23 us
  starting transfers between devices: 29.4 us -> 19.5 us
  blocking collectives: 0 us -> 6.67 us
  Pallas kernels: 21.1 us -> 22.6 us
  other arithmetic: 0.79 us -> 0 us
    unnamed x30 -> x88, local copies, waits for them, and re-layouts: 6.41 us -> 27.8 us
    ppermute x11 -> x1, starting transfers between devices: 20.7 us -> 1.97 us  [shift(): lax.ppermute(x, axis, [(i, i + by) for i in range(n) if 0 <= i + by < n])]
    ppermute x4, waiting for transfers between devices: 12 us -> 0.22 us  [ring(): return lax.ppermute(x, axis, [(i, (i + by) % n) for i in range(n)])]
    all_to_all x0 -> x2, starting transfers between devices: none -> 7.53 us  [local(): last = lax.all_to_all(last, 'sweep', 0, 0)]
    all_gather x0 -> x1, blocking collectives: none -> 6.67 us  [local(): passes = lax.all_gather(passes, 'sweep')]
    ppermute x11 -> x1, waiting for transfers between devices: 3.03 us -> 0.01 us  [shift(): lax.ppermute(x, axis, [(i, i + by) for i in range(n) if 0 <= i + by < n])]
    pallas_call x8, Pallas kernels: 11.2 us -> 13.6 us  [call(): pl.pallas_call(kernel, out_shape=shapes, in_specs=[pl.BlockSpec(memory_sp...]
    ppermute x4, starting transfers between devices: 8.61 us -> 10.1 us  [ring(): return lax.ppermute(x, axis, [(i, (i + by) % n) for i in range(n)])]
  transfers between devices with their start and end apart: 15 -> 7, of which waited for: 6 -> 1; matrix products, arithmetic and copies ran while one was open for 0% -> 0% of each run, Pallas kernels for 11% -> 15%
where the time goes in v2:
time: 78.6 us; the launch traced here: 77.1 us
  local copies, waits for them, and re-layouts  27.8 us (35%)
  Pallas kernels  22.6 us (29%)
  starting transfers between devices  19.5 us (25%)
  blocking collectives  6.67 us (8%)
    unnamed x88, local copies, waits for them, and re-layouts  27.8 us
    pallas_call x8, Pallas kernels, call(): pl.pallas_call(kernel, out_shape=shapes, in_specs=[pl.BlockSpec(memory_sp...  13.6 us
    ppermute x4, starting transfers between devices, ring(): return lax.ppermute(x, axis, [(i, (i + by) % n) for i in range(n)])  10.1 us
    pallas_call x1, Pallas kernels, weights(): pl.pallas_call(weight_kernel, grid=(planes,), out_shape=outs, in_specs=[l...  8.99 us
    all_to_all x2, starting transfers between devices, local(): last = lax.all_to_all(last, 'sweep', 0, 0)  7.53 us
    all_gather x1, blocking collectives, local(): passes = lax.all_gather(passes, 'sweep')  6.67 us
    ppermute x1, starting transfers between devices, shift(): lax.ppermute(x, axis, [(i, i + by) for i in range(n) if 0 <= i + by < n])  1.97 us
  transfers between devices with their start and end apart: 7, of which 1 were waited for; matrix products, arithmetic and copies ran while one was open for 0% of the time, Pallas kernels for 15%

profile of v2, /device:TPU:1, one launch (start us, length us, event | category | flops | bytes accessed | tf_op | source)
XLA Modules:
  0.0 77.1 jit_solution(14067724823807413970)
XLA Ops:
  0.0 1.0 %copy-done.21 = bf16[4,8,32,135]{3,2,1,0:T(8,128)(2,1)S(1)} copy-done((bf16[4,8,32,135]{3,2,1,0:T(8,128)(2,1)S(1)}, bf16[4,8,32,135]{3,2,1,0:T(8,128)(2,1)}, u32[]{:S(2)}) %copy-start.21) | copy-done | bytes 276504
  1.0 0.5 initial_traces.1
  1.6 2.0 %collective-permute-start.2 = (bf16[48,256]{1,0:T(8,128)(2,1)S(1)}, bf16[48,256]{1,0:T(8,128)(2,1)S(1)}, u32[]{:S(2)}, u32[]{:S(2)}) collective-permute-start(bf16[48,256]{1,0:T(8,128)(2,1)S(1)} %get-tuple-element.60), channel_id=1, source_target_pairs={{8,0},{16,8},{24,16},{9,1},{17,9},{25,17},{10,2},{18,10},{26,18},{... | collective-permute-start | bytes 73736 | tf_op jit(solution)/shard_map/ppermute | solution.py:452
  3.5 2.7 %collective-permute-start = (bf16[4,80,256]{2,1,0:T(8,128)(2,1)S(1)}, bf16[4,80,256]{2,1,0:T(8,128)(2,1)S(1)}, u32[]{:S(2)}, u32[]{:S(2)}) collective-permute-start(bf16[4,80,256]{2,1,0:T(8,128)(2,1)S(1)} %get-tuple-element.58), channel_id=1, source_target_pairs={{0,1},{1,2},{2,3},{3,4},{4,5},{5,6},{6,7},{7,0},{8,9},{9,10},{10,1... | collective-permute-start | bytes 491528 | tf_op jit(solution)/shard_map/ppermute | solution.py:447
  6.3 3.1 %collective-permute-start.1 = (bf16[4,80,256]{2,1,0:T(8,128)(2,1)S(1)}, bf16[4,80,256]{2,1,0:T(8,128)(2,1)S(1)}, u32[]{:S(2)}, u32[]{:S(2)}) collective-permute-start(bf16[4,80,256]{2,1,0:T(8,128)(2,1)S(1)} %get-tuple-element.59), channel_id=1, source_target_pairs={{0,7},{1,0},{2,1},{3,2},{4,3},{5,4},{6,5},{7,6},{8,15},{9,8},{10,9... | collective-permute-start | bytes 491528 | tf_op jit(solution)/shard_map/ppermute | solution.py:447
  9.4 0.7 copy-done.17
  10.1 2.3 %copy-done.19 = bf16[4,8,6,45,135]{4,1,3,2,0:T(8,128)(2,1)S(1)} copy-done((bf16[4,8,6,45,135]{4,1,3,2,0:T(8,128)(2,1)S(1)}, bf16[4,8,6,45,135]{4,1,3,2,0:T(8,128)(2,1)}, u32[]{:S(2)}) %copy-start.19) | copy-done | bytes 2332824
  12.3 1.6 %copy-done.20 = bf16[4,8,135,135]{3,1,2,0:T(8,128)(2,1)S(1)} copy-done((bf16[4,8,135,135]{3,1,2,0:T(8,128)(2,1)S(1)}, bf16[4,8,135,135]{3,1,2,0:T(8,128)(2,1)}, u32[]{:S(2)}) %copy-start.20) | copy-done | bytes 1166424
  13.9 1.0 %copy-done.22 = bf16[4,8,32,135]{3,2,1,0:T(8,128)(2,1)S(1)} copy-done((bf16[4,8,32,135]{3,2,1,0:T(8,128)(2,1)S(1)}, bf16[4,8,32,135]{3,2,1,0:T(8,128)(2,1)}, u32[]{:S(2)}) %copy-start.22) | copy-done | bytes 276504
  15.0 1.0 %copy-done.23 = bf16[4,8,32,135]{3,2,1,0:T(8,128)(2,1)S(1)} copy-done((bf16[4,8,32,135]{3,2,1,0:T(8,128)(2,1)S(1)}, bf16[4,8,32,135]{3,2,1,0:T(8,128)(2,1)}, u32[]{:S(2)}) %copy-start.23) | copy-done | bytes 276504
  16.0 9.0 %weights.1 = (bf16[4,8,48,256]{3,2,1,0:T(8,128)(2,1)S(1)}, bf16[4,8,48,256]{3,2,1,0:T(8,128)(2,1)S(1)}, bf16[4,8,48,256]{3,2,1,0:T(8,128)(2,1)S(1)}, bf16[4,2,48...) custom-call(bf16[4,135,8,135]{3,2,1,0:T(8,128)(2,1)S(1)} %bitcast.11, ...), custom_call_target="tpu_custom_call" | custom-call | flops 10000000000 | bytes 12000000 | tf_op jit(solution)/shard_map/weights/pallas_call | solution.py:423
  25.0 0.0 copy-start.40
  25.0 0.7 copy-done.40
  25.7 0.7 copy-done.42
  26.4 0.0 collective-permute-done.2.above.rest_0_
  26.4 0.0 collective-permute-done.up
  26.4 0.0 collective-permute-done.1.down
  26.4 0.0 copy-done.10
  26.5 0.0 copy-done.11
  26.5 0.0 copy-done.18
  26.5 2.6 %forward_chain.1 = (bf16[4,256,256]{2,1,0:T(8,128)(2,1)S(1)}, f32[4,48,256]{2,1,0:T(8,128)S(1)}, f32[4,48,256]{2,1,0:T(8,128)S(1)}, bf16[4,48,256]{2,1,0:T(8,128)(2,1)S(1)}) custom-call(bf16[4,80,256]{2,1,0:T(8,128)(2,1)S(1)} %collective-permute-done.up, bf16[4,80,256]{2,1,0:T(8,128)(2,1)S(1)} %collective-permute-done.1.down, ...), custom_call_target="tpu_custom_call" | custom-call | flops 200000000 | bytes 2971776 | tf_op jit(solution)/shard_map/forward_chain/pallas_call | solution.py:398
  29.1 0.0 copy-done.13
  29.1 0.0 copy-done.29
  29.1 0.0 copy-done.32
  29.1 0.0 copy-done.34
  29.2 0.0 copy-done.38
  29.2 0.0 copy-start
  29.2 0.7 copy-done
  29.8 0.7 copy-done.12
  30.5 0.8 %copy-done.26 = bf16[4,256,256]{2,1,0:T(8,128)(2,1)} copy-done((bf16[4,256,256]{2,1,0:T(8,128)(2,1)}, bf16[4,256,256]{2,1,0:T(8,128)(2,1)S(1)}, u32[]{:S(2)}) %copy-start.26) | copy-done | bytes 524312
  31.3 3.3 %all-to-all-start = ((bf16[4,48,256]{2,1,0:T(8,128)(2,1)}), bf16[4,48,256]{2,1,0:T(8,128)(2,1)S(1)}, u32[]{:S(2)}, u32[]{:S(2)}) async-start(bf16[4,48,256]{2,1,0:T(8,128)(2,1)} %copy-done.12), calls=%async_computation | async-start | bytes 196608 | tf_op jit(solution)/shard_map/all_to_all | solution.py:491
  34.6 0.0 copy-start.27
  34.6 1.1 %copy-done.27 = bf16[4,256,256]{2,1,0:T(8,128)(2,1)S(1)} copy-done((bf16[4,256,256]{2,1,0:T(8,128)(2,1)S(1)}, bf16[4,256,256]{2,1,0:T(8,128)(2,1)}, u32[]{:S(2)}) %copy-start.27) | copy-done | bytes 524312
  35.7 1.1 %copy-done.30 = bf16[4,8,48,256]{3,2,1,0:T(8,128)(2,1)S(1)} copy-done((bf16[4,8,48,256]{3,2,1,0:T(8,128)(2,1)S(1)}, bf16[4,8,48,256]{3,2,1,0:T(8,128)(2,1)}, u32[]{:S(2)}) %copy-start.30) | copy-done | bytes 786456
  36.8 0.9 %copy-done.33 = f32[4,48,256]{2,1,0:T(8,128)S(1)} copy-done((f32[4,48,256]{2,1,0:T(8,128)S(1)}, f32[4,48,256]{2,1,0:T(8,128)}, u32[]{:S(2)}) %copy-start.33) | copy-done | bytes 196632
  37.8 0.9 %copy-done.35 = f32[4,48,256]{2,1,0:T(8,128)S(1)} copy-done((f32[4,48,256]{2,1,0:T(8,128)S(1)}, f32[4,48,256]{2,1,0:T(8,128)}, u32[]{:S(2)}) %copy-start.35) | copy-done | bytes 196632
  38.7 0.8 forward_base.1
  39.5 0.7 copy-done.2
  40.1 0.7 copy-done.4
  40.8 6.7 %all-gather = bf16[8,2,48,256]{3,2,1,0:T(8,128)(2,1)S(1)} all-gather(bf16[2,2,48,256]{3,2,1,0:T(8,128)(2,1)S(1)} %copy-done.14), channel_id=2, replica_groups=mesh['sweep'=4,'cross'=8] {'sweep'}, dimensions={0}, use_global_device_ids=true | all-gather | bytes 491520 | tf_op jit(solution)/shard_map/all_gather | solution.py:479
  47.5 0.0 all-to-all-done.last
  47.5 0.9 %copy-done.1 = f32[4,48,256]{2,1,0:T(8,128)S(1)} copy-done((f32[4,48,256]{2,1,0:T(8,128)S(1)}, f32[4,48,256]{2,1,0:T(8,128)}, u32[]{:S(2)}) %copy-start.1) | copy-done | bytes 196632
  48.5 0.9 %copy-done.3 = f32[4,48,256]{2,1,0:T(8,128)S(1)} copy-done((f32[4,48,256]{2,1,0:T(8,128)S(1)}, f32[4,48,256]{2,1,0:T(8,128)}, u32[]{:S(2)}) %copy-start.3) | copy-done | bytes 196632
  49.4 0.9 %copy-done.5 = f32[4,48,256]{2,1,0:T(8,128)S(1)} copy-done((f32[4,48,256]{2,1,0:T(8,128)S(1)}, f32[4,48,256]{2,1,0:T(8,128)}, u32[]{:S(2)}) %copy-start.5) | copy-done | bytes 196632
  50.3 0.9 %copy-done.15 = bf16[160,144]{1,0:T(8,128)(2,1)S(1)} copy-done((bf16[160,144]{1,0:T(8,128)(2,1)S(1)}, bf16[160,144]{1,0:T(8,128)(2,1)}, u32[]{:S(2)}) %copy-start.15) | copy-done | bytes 46104
  51.2 1.6 %forward_finish.1 = (bf16[4,144,256]{2,1,0:T(8,128)(2,1)S(1)}, f32[4,144,256]{2,1,0:T(8,128)S(1)}, bf16[4,80,256]{2,1,0:T(8,128)(2,1)S(1)}, bf16[4,80,256]{2,1,0:T(8,128)(2,1)S(1)}) custom-call(bf16[4,48,256]{2,1,0:T(8,128)(2,1)S(1)} %all-to-all-done.last, bf16[4,2,2,48,256]{4,3,2,1,0:T(8,128)(2,1)S(1)} %bitcast.4, ...), custom_call_target="tpu_custom_call" | custom-call | flops 200000000 | bytes 3322880 | tf_op jit(solution)/shard_map/forward_finish/pallas_call | solution.py:398
  52.8 0.1 collective-permute-start.3
  52.9 4.1 %collective-permute-start.4 = (bf16[4,80,256]{2,1,0:T(8,128)(2,1)S(1)}, bf16[4,80,256]{2,1,0:T(8,128)(2,1)S(1)}, u32[]{:S(2)}, u32[]{:S(2)}) collective-permute-start(bf16[4,80,256]{2,1,0:T(8,128)(2,1)S(1)} %get-tuple-element.88), channel_id=1, source_target_pairs={{0,7},{1,0},{2,1},{3,2},{4,3},{5,4},{6,5},{7,6},{8,15},{9,8},{10,9... | collective-permute-start | bytes 491528 | tf_op jit(solution)/shard_map/ppermute | solution.py:447
  57.0 0.8 %copy-done.28 = bf16[96,144]{1,0:T(8,128)(2,1)S(1)} copy-done((bf16[96,144]{1,0:T(8,128)(2,1)S(1)}, bf16[96,144]{1,0:T(8,128)(2,1)}, u32[]{:S(2)}) %copy-start.28) | copy-done | bytes 27672
  57.8 0.9 %copy-done.39 = f32[4,48,256]{2,1,0:T(8,128)S(1)} copy-done((f32[4,48,256]{2,1,0:T(8,128)S(1)}, f32[4,48,256]{2,1,0:T(8,128)}, u32[]{:S(2)}) %copy-start.39) | copy-done | bytes 196632
  58.7 0.9 %copy-done.41 = f32[4,48,256]{2,1,0:T(8,128)S(1)} copy-done((f32[4,48,256]{2,1,0:T(8,128)S(1)}, f32[4,48,256]{2,1,0:T(8,128)}, u32[]{:S(2)}) %copy-start.41) | copy-done | bytes 196632
  59.7 0.9 %copy-done.43 = f32[4,48,256]{2,1,0:T(8,128)S(1)} copy-done((f32[4,48,256]{2,1,0:T(8,128)S(1)}, f32[4,48,256]{2,1,0:T(8,128)}, u32[]{:S(2)}) %copy-start.43) | copy-done | bytes 196632
  60.6 1.2 %middle.1 = (bf16[4,96,256]{2,1,0:T(8,128)(2,1)S(1)}, f32[4,48,256]{2,1,0:T(8,128)S(1)}, f32[4,48,256]{2,1,0:T(8,128)S(1)}, f32[4,48,256]{2,1,0:T(8,128)S(1)}) custom-call(bf16[4,144,256]{2,1,0:T(8,128)(2,1)S(1)} %get-tuple-element.89.middle, f32[4,144,256]{2,1,0:T(8,128)S(1)} %get-tuple-element.90.change, f32[4,48,256]{2,1,0:T(8,128)S(1)} %copy-done.39, ...), custom_call_target="tpu_custom_call" | custom-call | flops 2000000000 | bytes 2288768 | tf_op jit(solution)/shard_map/middle/pallas_call | solution.py:398
  61.8 0.0 collective-permute-done.3.up
  61.9 0.2 collective-permute-done.4.down
  62.1 3.2 %backward_chain.1 = (bf16[4,256,256]{2,1,0:T(8,128)(2,1)S(1)}, f32[4,48,256]{2,1,0:T(8,128)S(1)}, f32[4,48,256]{2,1,0:T(8,128)S(1)}, bf16[4,48,256]{2,1,0:T(8,128)(2,1)}) custom-call(bf16[4,80,256]{2,1,0:T(8,128)(2,1)S(1)} %collective-permute-done.3.up, bf16[4,80,256]{2,1,0:T(8,128)(2,1)S(1)} %collective-permute-done.4.down, ...), custom_call_target="tpu_custom_call" | custom-call | flops 200000000 | bytes 2750592 | tf_op jit(solution)/shard_map/backward_chain/pallas_call | solution.py:398
  65.3 0.8 %copy-done.24 = bf16[4,256,256]{2,1,0:T(8,128)(2,1)} copy-done((bf16[4,256,256]{2,1,0:T(8,128)(2,1)}, bf16[4,256,256]{2,1,0:T(8,128)(2,1)S(1)}, u32[]{:S(2)}) %copy-start.24) | copy-done | bytes 524312
  66.1 4.2 %all-to-all-start.1 = ((bf16[4,48,256]{2,1,0:T(8,128)(2,1)}), bf16[4,48,256]{2,1,0:T(8,128)(2,1)S(1)}, u32[]{:S(2)}, u32[]{:S(2)}) async-start(bf16[4,48,256]{2,1,0:T(8,128)(2,1)} %get-tuple-element.96), calls=%async_computation.1 | async-start | bytes 196608 | tf_op jit(solution)/shard_map/all_to_all | solution.py:520
  70.3 1.0 %copy-done.25 = bf16[4,256,256]{2,1,0:T(8,128)(2,1)S(1)} copy-done((bf16[4,256,256]{2,1,0:T(8,128)(2,1)S(1)}, bf16[4,256,256]{2,1,0:T(8,128)(2,1)}, u32[]{:S(2)}) %copy-start.25) | copy-done | bytes 524312
  71.4 1.1 %copy-done.31 = bf16[4,8,48,256]{3,2,1,0:T(8,128)(2,1)S(1)} copy-done((bf16[4,8,48,256]{3,2,1,0:T(8,128)(2,1)S(1)}, bf16[4,8,48,256]{3,2,1,0:T(8,128)(2,1)}, u32[]{:S(2)}) %copy-start.31) | copy-done | bytes 786456
  72.5 0.9 %copy-done.37 = f32[4,48,256]{2,1,0:T(8,128)S(1)} copy-done((f32[4,48,256]{2,1,0:T(8,128)S(1)}, f32[4,48,256]{2,1,0:T(8,128)}, u32[]{:S(2)}) %copy-start.37) | copy-done | bytes 196632
  73.5 0.7 backward_base.1
  74.2 0.0 all-to-all-done.1.last
  74.2 2.9 %backward_finish.1 = bf16[4,8,32,135]{3,2,1,0:T(8,128)(2,1)} custom-call(bf16[4,48,256]{2,1,0:T(8,128)(2,1)S(1)} %all-to-all-done.1.last, bf16[4,2,2,48,256]{4,3,2,1,0:T(8,128)(2,1)S(1)} %bitcast.5, bf16[4,2,48,256]{3,2,1,0:T(8,128)(2,1)S(1)} %copy-done.9, f32[4,48,256]{2,1,0:T(8,128)S(1)} %get-tuple-element.98.traces, ...), custom_call_target="tpu_custom_call" | custom-call | flops 200000000 | bytes 2379744 | tf_op jit(solution)/shard_map/backward_finish/pallas_call | solution.py:398
  (48 shorter events, 0.1 us)
Async XLA Ops:
  0.0 1.0 %copy-start.21 = (bf16[4,8,32,135]{3,2,1,0:T(8,128)(2,1)S(1)}, bf16[4,8,32,135]{3,2,1,0:T(8,128)(2,1)}, u32[]{:S(2)}) copy-start(bf16[4,8,32,135]{3,2,1,0:T(8,128)(2,1)} %initial.2) | copy-start | bytes 829444
  1.6 24.9 %collective-permute-start.2 = (bf16[48,256]{1,0:T(8,128)(2,1)S(1)}, bf16[48,256]{1,0:T(8,128)(2,1)S(1)}, u32[]{:S(2)}, u32[]{:S(2)}) collective-permute-start(bf16[48,256]{1,0:T(8,128)(2,1)S(1)} %get-tuple-element.60), channel_id=1, source_target_pairs={{8,0},{16,8},{24,16},{9,1},{17,9},{25,17},{10,2},{18,10},{26,18},{... | collective-permute-start | bytes 73736 | tf_op jit(solution)/shard_map/ppermute | solution.py:452
  3.5 22.9 %collective-permute-start = (bf16[4,80,256]{2,1,0:T(8,128)(2,1)S(1)}, bf16[4,80,256]{2,1,0:T(8,128)(2,1)S(1)}, u32[]{:S(2)}, u32[]{:S(2)}) collective-permute-start(bf16[4,80,256]{2,1,0:T(8,128)(2,1)S(1)} %get-tuple-element.58), channel_id=1, source_target_pairs={{0,1},{1,2},{2,3},{3,4},{4,5},{5,6},{6,7},{7,0},{8,9},{9,10},{10,1... | collective-permute-start | bytes 491528 | tf_op jit(solution)/shard_map/ppermute | solution.py:447
  6.3 20.2 %collective-permute-start.1 = (bf16[4,80,256]{2,1,0:T(8,128)(2,1)S(1)}, bf16[4,80,256]{2,1,0:T(8,128)(2,1)S(1)}, u32[]{:S(2)}, u32[]{:S(2)}) collective-permute-start(bf16[4,80,256]{2,1,0:T(8,128)(2,1)S(1)} %get-tuple-element.59), channel_id=1, source_target_pairs={{0,7},{1,0},{2,1},{3,2},{4,3},{5,4},{6,5},{7,6},{8,15},{9,8},{10,9... | collective-permute-start | bytes 491528 | tf_op jit(solution)/shard_map/ppermute | solution.py:447
  9.4 0.7 copy-start.17
  10.1 2.3 %copy-start.19 = (bf16[4,8,6,45,135]{4,1,3,2,0:T(8,128)(2,1)S(1)}, bf16[4,8,6,45,135]{4,1,3,2,0:T(8,128)(2,1)}, u32[]{:S(2)}) copy-start(bf16[4,8,6,45,135]{4,1,3,2,0:T(8,128)(2,1)} %param.13) | copy-start | bytes 6998404
  12.3 1.6 %copy-start.20 = (bf16[4,8,135,135]{3,1,2,0:T(8,128)(2,1)S(1)}, bf16[4,8,135,135]{3,1,2,0:T(8,128)(2,1)}, u32[]{:S(2)}) copy-start(bf16[4,8,135,135]{3,1,2,0:T(8,128)(2,1)} %param.12) | copy-start | bytes 3499204
  13.9 1.0 %copy-start.22 = (bf16[4,8,32,135]{3,2,1,0:T(8,128)(2,1)S(1)}, bf16[4,8,32,135]{3,2,1,0:T(8,128)(2,1)}, u32[]{:S(2)}) copy-start(bf16[4,8,32,135]{3,2,1,0:T(8,128)(2,1)} %initial.2) | copy-start | bytes 829444
  15.0 1.0 %copy-start.23 = (bf16[4,8,32,135]{3,2,1,0:T(8,128)(2,1)S(1)}, bf16[4,8,32,135]{3,2,1,0:T(8,128)(2,1)}, u32[]{:S(2)}) copy-start(bf16[4,8,32,135]{3,2,1,0:T(8,128)(2,1)} %right.1) | copy-start | bytes 829444
  16.0 10.4 %copy-start.10 = (bf16[96,80]{1,0:T(8,128)(2,1)S(1)}, bf16[96,80]{1,0:T(8,128)(2,1)}, u32[]{:S(2)}) copy-start(bf16[96,80]{1,0:T(8,128)(2,1)} %constant.14.clone.down_sel) | copy-start | bytes 46084
  16.0 10.4 %copy-start.11 = (bf16[96,80]{1,0:T(8,128)(2,1)S(1)}, bf16[96,80]{1,0:T(8,128)(2,1)}, u32[]{:S(2)}) copy-start(bf16[96,80]{1,0:T(8,128)(2,1)} %constant.13.clone.up_sel) | copy-start | bytes 46084
  16.0 10.4 %copy-start.18 = (s32[8,4]{0,1:T(4,128)S(1)}, s32[8,4]{0,1:T(4,128)}, u32[]{:S(2)}) copy-start(s32[8,4]{0,1:T(4,128)} %param.14) | copy-start | bytes 388
  25.0 0.7 copy-start.40
  25.7 0.7 copy-start.42
  26.4 2.7 %copy-start.13 = (bf16[2,2,48,256]{3,2,1,0:T(8,128)(2,1)}, bf16[2,2,48,256]{3,2,1,0:T(8,128)(2,1)S(1)}, u32[]{:S(2)}) copy-start(bf16[2,2,48,256]{3,2,1,0:T(8,128)(2,1)S(1)} %get-tuple-element.72) | copy-start | bytes 294916
  26.4 2.8 %copy-start.29 = (bf16[4,8,48,256]{3,2,1,0:T(8,128)(2,1)}, bf16[4,8,48,256]{3,2,1,0:T(8,128)(2,1)S(1)}, u32[]{:S(2)}) copy-start(bf16[4,8,48,256]{3,2,1,0:T(8,128)(2,1)S(1)} %get-tuple-element.76.known_two.known_one) | copy-start | bytes 2359300
  26.4 2.8 %copy-start.32 = (f32[4,48,256]{2,1,0:T(8,128)}, f32[4,48,256]{2,1,0:T(8,128)S(1)}, u32[]{:S(2)}) copy-start(f32[4,48,256]{2,1,0:T(8,128)S(1)} %get-tuple-element.78.base_one) | copy-start | bytes 589828
  26.4 2.8 %copy-start.34 = (f32[4,48,256]{2,1,0:T(8,128)}, f32[4,48,256]{2,1,0:T(8,128)S(1)}, u32[]{:S(2)}) copy-start(f32[4,48,256]{2,1,0:T(8,128)S(1)} %get-tuple-element.79.base_two) | copy-start | bytes 589828
  26.4 2.8 %copy-start.38 = (f32[4,48,256]{2,1,0:T(8,128)}, f32[4,48,256]{2,1,0:T(8,128)S(1)}, u32[]{:S(2)}) copy-start(f32[4,48,256]{2,1,0:T(8,128)S(1)} %get-tuple-element.91.base0) | copy-start | bytes 589828
  26.4 8.2 %copy-start.6 = (bf16[4,2,48,256]{3,2,1,0:T(8,128)(2,1)}, bf16[4,2,48,256]{3,2,1,0:T(8,128)(2,1)S(1)}, u32[]{:S(2)}) copy-start(bf16[4,2,48,256]{3,2,1,0:T(8,128)(2,1)S(1)} %get-tuple-element.81.rest_2_.upper1) | copy-start | bytes 589828
  26.4 8.2 %copy-start.8 = (bf16[4,2,48,256]{3,2,1,0:T(8,128)(2,1)}, bf16[4,2,48,256]{3,2,1,0:T(8,128)(2,1)S(1)}, u32[]{:S(2)}) copy-start(bf16[4,2,48,256]{3,2,1,0:T(8,128)(2,1)S(1)} %get-tuple-element.97.cum) | copy-start | bytes 589828
  29.2 0.7 copy-start
  29.8 0.7 copy-start.12
  30.5 0.8 %copy-start.26 = (bf16[4,256,256]{2,1,0:T(8,128)(2,1)}, bf16[4,256,256]{2,1,0:T(8,128)(2,1)S(1)}, u32[]{:S(2)}) copy-start(bf16[4,256,256]{2,1,0:T(8,128)(2,1)S(1)} %get-tuple-element.77.operand) | copy-start | bytes 1572868
  31.3 16.2 %all-to-all-start = ((bf16[4,48,256]{2,1,0:T(8,128)(2,1)}), bf16[4,48,256]{2,1,0:T(8,128)(2,1)S(1)}, u32[]{:S(2)}, u32[]{:S(2)}) async-start(bf16[4,48,256]{2,1,0:T(8,128)(2,1)} %copy-done.12), calls=%async_computation | async-start | bytes 196608 | tf_op jit(solution)/shard_map/all_to_all | solution.py:491
  34.6 6.3 %copy-start.14 = (bf16[2,2,48,256]{3,2,1,0:T(8,128)(2,1)S(1)}, bf16[2,2,48,256]{3,2,1,0:T(8,128)(2,1)}, u32[]{:S(2)}) copy-start(bf16[2,2,48,256]{3,2,1,0:T(8,128)(2,1)} %copy-done.13) | copy-start | bytes 294916
  34.6 1.1 %copy-start.27 = (bf16[4,256,256]{2,1,0:T(8,128)(2,1)S(1)}, bf16[4,256,256]{2,1,0:T(8,128)(2,1)}, u32[]{:S(2)}) copy-start(bf16[4,256,256]{2,1,0:T(8,128)(2,1)} %copy-done.26) | copy-start | bytes 1572868
  35.7 1.1 %copy-start.30 = (bf16[4,8,48,256]{3,2,1,0:T(8,128)(2,1)S(1)}, bf16[4,8,48,256]{3,2,1,0:T(8,128)(2,1)}, u32[]{:S(2)}) copy-start(bf16[4,8,48,256]{3,2,1,0:T(8,128)(2,1)} %copy-done.29) | copy-start | bytes 2359300
  36.8 0.9 %copy-start.33 = (f32[4,48,256]{2,1,0:T(8,128)S(1)}, f32[4,48,256]{2,1,0:T(8,128)}, u32[]{:S(2)}) copy-start(f32[4,48,256]{2,1,0:T(8,128)} %copy-done.32) | copy-start | bytes 589828
  37.8 0.9 %copy-start.35 = (f32[4,48,256]{2,1,0:T(8,128)S(1)}, f32[4,48,256]{2,1,0:T(8,128)}, u32[]{:S(2)}) copy-start(f32[4,48,256]{2,1,0:T(8,128)} %copy-done.34) | copy-start | bytes 589828
  39.5 0.7 copy-start.2
  40.1 0.7 copy-start.4
  47.5 0.9 %copy-start.1 = (f32[4,48,256]{2,1,0:T(8,128)S(1)}, f32[4,48,256]{2,1,0:T(8,128)}, u32[]{:S(2)}) copy-start(f32[4,48,256]{2,1,0:T(8,128)} %copy-done) | copy-start | bytes 589828
  48.4 0.9 %copy-start.3 = (f32[4,48,256]{2,1,0:T(8,128)S(1)}, f32[4,48,256]{2,1,0:T(8,128)}, u32[]{:S(2)}) copy-start(f32[4,48,256]{2,1,0:T(8,128)} %copy-done.2) | copy-start | bytes 589828
  49.4 0.9 %copy-start.5 = (f32[4,48,256]{2,1,0:T(8,128)S(1)}, f32[4,48,256]{2,1,0:T(8,128)}, u32[]{:S(2)}) copy-start(f32[4,48,256]{2,1,0:T(8,128)} %copy-done.4) | copy-start | bytes 589828
  50.3 0.9 %copy-start.15 = (bf16[160,144]{1,0:T(8,128)(2,1)S(1)}, bf16[160,144]{1,0:T(8,128)(2,1)}, u32[]{:S(2)}) copy-start(bf16[160,144]{1,0:T(8,128)(2,1)} %constant.10.clone.send) | copy-start | bytes 138244
  52.8 9.1 %collective-permute-start.3 = (bf16[4,80,256]{2,1,0:T(8,128)(2,1)S(1)}, bf16[4,80,256]{2,1,0:T(8,128)(2,1)S(1)}, u32[]{:S(2)}, u32[]{:S(2)}) collective-permute-start(bf16[4,80,256]{2,1,0:T(8,128)(2,1)S(1)} %get-tuple-element.87), channel_id=1, source_target_pairs={{0,1},{1,2},{2,3},{3,4},{4,5},{5,6},{6,7},{7,0},{8,9},{9,10},{10,1... | collective-permute-start | bytes 491528 | tf_op jit(solution)/shard_map/ppermute | solution.py:447
  52.9 9.2 %collective-permute-start.4 = (bf16[4,80,256]{2,1,0:T(8,128)(2,1)S(1)}, bf16[4,80,256]{2,1,0:T(8,128)(2,1)S(1)}, u32[]{:S(2)}, u32[]{:S(2)}) collective-permute-start(bf16[4,80,256]{2,1,0:T(8,128)(2,1)S(1)} %get-tuple-element.88), channel_id=1, source_target_pairs={{0,7},{1,0},{2,1},{3,2},{4,3},{5,4},{6,5},{7,6},{8,15},{9,8},{10,9... | collective-permute-start | bytes 491528 | tf_op jit(solution)/shard_map/ppermute | solution.py:447
  57.0 0.8 %copy-start.28 = (bf16[96,144]{1,0:T(8,128)(2,1)S(1)}, bf16[96,144]{1,0:T(8,128)(2,1)}, u32[]{:S(2)}) copy-start(bf16[96,144]{1,0:T(8,128)(2,1)} %constant.11.clone.own_sel) | copy-start | bytes 82948
  57.8 0.9 %copy-start.39 = (f32[4,48,256]{2,1,0:T(8,128)S(1)}, f32[4,48,256]{2,1,0:T(8,128)}, u32[]{:S(2)}) copy-start(f32[4,48,256]{2,1,0:T(8,128)} %copy-done.38) | copy-start | bytes 589828
  58.7 0.9 %copy-start.41 = (f32[4,48,256]{2,1,0:T(8,128)S(1)}, f32[4,48,256]{2,1,0:T(8,128)}, u32[]{:S(2)}) copy-start(f32[4,48,256]{2,1,0:T(8,128)} %copy-done.40) | copy-start | bytes 589828
  59.7 0.9 %copy-start.43 = (f32[4,48,256]{2,1,0:T(8,128)S(1)}, f32[4,48,256]{2,1,0:T(8,128)}, u32[]{:S(2)}) copy-start(f32[4,48,256]{2,1,0:T(8,128)} %copy-done.42) | copy-start | bytes 589828
  61.8 3.5 %copy-start.36 = (f32[4,48,256]{2,1,0:T(8,128)}, f32[4,48,256]{2,1,0:T(8,128)S(1)}, u32[]{:S(2)}) copy-start(f32[4,48,256]{2,1,0:T(8,128)S(1)} %get-tuple-element.102.base_two) | copy-start | bytes 589828
  62.1 12.1 %copy-start.7 = (bf16[4,2,48,256]{3,2,1,0:T(8,128)(2,1)S(1)}, bf16[4,2,48,256]{3,2,1,0:T(8,128)(2,1)}, u32[]{:S(2)}) copy-start(bf16[4,2,48,256]{3,2,1,0:T(8,128)(2,1)} %copy-done.6) | copy-start | bytes 589828
  62.1 12.1 %copy-start.9 = (bf16[4,2,48,256]{3,2,1,0:T(8,128)(2,1)S(1)}, bf16[4,2,48,256]{3,2,1,0:T(8,128)(2,1)}, u32[]{:S(2)}) copy-start(bf16[4,2,48,256]{3,2,1,0:T(8,128)(2,1)} %copy-done.8) | copy-start | bytes 589828
  62.1 12.1 %copy-start.16 = (bf16[135,144]{1,0:T(8,128)(2,1)S(1)}, bf16[135,144]{1,0:T(8,128)(2,1)}, u32[]{:S(2)}) copy-start(bf16[135,144]{1,0:T(8,128)(2,1)} %constant.12.clone.back) | copy-start | bytes 116644
  65.3 0.8 %copy-start.24 = (bf16[4,256,256]{2,1,0:T(8,128)(2,1)}, bf16[4,256,256]{2,1,0:T(8,128)(2,1)S(1)}, u32[]{:S(2)}) copy-start(bf16[4,256,256]{2,1,0:T(8,128)(2,1)S(1)} %get-tuple-element.100.operand) | copy-start | bytes 1572868
  66.1 8.0 %all-to-all-start.1 = ((bf16[4,48,256]{2,1,0:T(8,128)(2,1)}), bf16[4,48,256]{2,1,0:T(8,128)(2,1)S(1)}, u32[]{:S(2)}, u32[]{:S(2)}) async-start(bf16[4,48,256]{2,1,0:T(8,128)(2,1)} %get-tuple-element.96), calls=%async_computation.1 | async-start | bytes 196608 | tf_op jit(solution)/shard_map/all_to_all | solution.py:520
  70.3 1.0 %copy-start.25 = (bf16[4,256,256]{2,1,0:T(8,128)(2,1)S(1)}, bf16[4,256,256]{2,1,0:T(8,128)(2,1)}, u32[]{:S(2)}) copy-start(bf16[4,256,256]{2,1,0:T(8,128)(2,1)} %copy-done.24) | copy-start | bytes 1572868
  71.4 1.1 %copy-start.31 = (bf16[4,8,48,256]{3,2,1,0:T(8,128)(2,1)S(1)}, bf16[4,8,48,256]{3,2,1,0:T(8,128)(2,1)}, u32[]{:S(2)}) copy-start(bf16[4,8,48,256]{3,2,1,0:T(8,128)(2,1)} %copy-done.29) | copy-start | bytes 2359300
  72.5 0.9 %copy-start.37 = (f32[4,48,256]{2,1,0:T(8,128)S(1)}, f32[4,48,256]{2,1,0:T(8,128)}, u32[]{:S(2)}) copy-start(f32[4,48,256]{2,1,0:T(8,128)} %copy-done.36) | copy-start | bytes 589828

commit v3 on v2

v3 whole, which is shorter than its diff:
```python
import functools

import jax
import jax.numpy as jnp
import numpy as np
from jax import lax
from jax.experimental import pallas as pl
from jax.experimental.pallas import tpu as pltpu
from jax.sharding import PartitionSpec as P

BF = jnp.bfloat16
F32 = jnp.float32
NT = 45
FACE = 48
SLOT = 64
ROWS = 3 * FACE
SHARED = 80
MIB = 1 << 20


def natural(v, a, b, c):
    return v * 27 + a * 9 + b * 3 + c


def inner(v, a, b, c):
    return a * FACE + v * 9 + b * 3 + c


NODES = [(v, a, b, c) for v in range(5) for a in range(3) for b in range(3) for c in range(3)]


def face_nodes(place, which):
    return [n for n in NODES if n[1 + place] == which]


def union_rows(which):
    others = [b for b in range(3) if b != which]
    spots = [(which, c) for c in range(3)] + [(b, which) for b in others]
    return [
        (v * 16 + a * 5 + j, (v, a, b, c)) for v in range(5) for a in range(3) for j, (b, c) in enumerate(spots)
    ]


def table(height, width, rows, column_of, value=1.0):
    out = np.zeros((height, width), np.float32)
    for row, node in rows:
        out[row, column_of(*node)] = value
    return out


def block(nodes, start=0):
    return [(start + i, n) for i, n in enumerate(nodes)]


def send_table(width, column_of):
    rows = union_rows(2) + [(SHARED + i, n) for i, n in union_rows(0)]
    return table(2 * SHARED, width, rows, column_of)


def own_table(width, column_of):
    rows = block(face_nodes(2, 2)) + block(face_nodes(2, 0), FACE)
    return table(2 * FACE, width, rows, column_of)


def receive_table(which):
    place = {n: i for i, n in union_rows(which)}
    rows = block(face_nodes(1, which)) + block(face_nodes(2, which), FACE)
    return table(2 * FACE, SHARED, rows, lambda *n: place[n])


def mm(a, b):
    return lax.dot_general(a, b, (((1,), (0,)), ((), ())), preferred_element_type=F32)


def mt(a, b):
    return lax.dot_general(a, b, (((1,), (1,)), ((), ())), preferred_element_type=F32)


def split_lanes(value, width):
    lanes = value.shape[1]
    value = value.astype(F32)
    owner = lax.broadcasted_iota(jnp.int32, value.shape, 1) // width
    pad = jnp.zeros((SLOT - FACE, lanes), BF)
    parts = []
    for c in range(lanes // width):
        parts += [jnp.where(owner == c, value, 0.0).astype(BF), pad]
    return jnp.concatenate(parts, 0)


def own_lanes(values, width):
    owner = lax.broadcasted_iota(jnp.int32, values[0].shape, 1) // width
    out = values[0]
    for c in range(1, len(values)):
        out = jnp.where(owner == c, values[c], out)
    return out


def one_hot(source, start, height):
    row = lax.broadcasted_iota(jnp.int32, (height, source.shape[1]), 0) + start
    return jnp.where(row == source, 1.0, 0.0).astype(BF)


def chain_step(matrix, trace, rhs, rows=slice(None)):
    half = trace.shape[1] // 2
    return jnp.concatenate(
        [mm(matrix[h, rows], split_lanes(trace[:, h * half : (h + 1) * half], rhs)) for h in range(2)], 1
    )


def shared_target(row, which):
    v, k = row // 16, row % 16
    a = k // 5
    j = k % 5
    b = jnp.where(j < 3, which, j - 3 if which == 2 else j - 2)
    c = jnp.where(j < 3, j, which)
    return jnp.where(k < 15, v * 27 + a * 9 + b * 3 + c, -1)


def picks(target, width):
    lane = lax.broadcasted_iota(jnp.int32, (target.shape[0], width), 1)
    return jnp.where(lane == target, 1.0, 0.0).astype(BF)


def rows_of(height):
    return lax.broadcasted_iota(jnp.int32, (height, 1), 0)


def first_target(row):
    return jnp.where(row < NT, row // 9 * 27 + row % 9, -1)


def c_target(row, which):
    return jnp.where(row < NT, row * 3 + which, -1)


def sources(neighbours, columns, rhs):
    place = lax.axis_index("cross")
    total = columns * lax.axis_size("cross")
    lane = lax.broadcasted_iota(jnp.int32, (1, columns * rhs), 1)
    out = []
    for face, first in ((2, place - 1), (3, place)):
        which = jnp.zeros_like(lane)
        for c in range(columns):
            at = lax.rem(neighbours[face, c] - first * columns + 2 * total, total)
            which = jnp.where(lane // rhs == c, at, which)
        out.append(which * rhs + lane % rhs)
    return out


def first_kernel(initial, up, down, above):
    planes, columns, rhs, width = initial.shape
    shared = rows_of(SHARED)
    tables = [picks(shared_target(shared, which), width) for which in (2, 0)]
    for p in range(planes):
        x = initial[p].reshape(columns * rhs, width)
        up[p] = mt(tables[0], x).astype(BF)
        down[p] = mt(tables[1], x).astype(BF)
        if p == 0:
            above[...] = mt(picks(first_target(rows_of(FACE)), width), x).astype(BF)


def turned(rows):
    pad = jnp.zeros((FACE - NT,) + rows.shape[1:], rows.dtype)
    return jnp.swapaxes(jnp.concatenate([rows, pad], 0), 0, 1)


def weight_kernel(
    inverse, couplings, right, initial, neighbours,
    known, lower, upper, base, fore, own,
    inverse_in, couplings_in, right_in, initial_in, solves, faces, prev, tables, done,
):
    planes, columns, rhs, width = initial.shape
    size = columns * rhs
    half = columns // 2

    def arrivals(p):
        pairs = ((inverse, inverse_in), (couplings, couplings_in), (right, right_in))
        return [pltpu.make_async_copy(x.at[p], y.at[p], done.at[i, p]) for i, (x, y) in enumerate(pairs)]

    start = pltpu.make_async_copy(initial, initial_in, done.at[3, 0])
    for p in range(planes):
        for copy in arrivals(p):
            copy.start()
    start.start()
    faces[...] = jnp.zeros(faces.shape, BF)
    tables[:FACE] = picks(c_target(rows_of(FACE), 2), width)
    tables[FACE : 2 * FACE] = picks(c_target(rows_of(FACE), 0), width)
    tables[2 * FACE :] = picks(first_target(rows_of(FACE)), width)
    source = sources(neighbours, columns, rhs)
    lane = lax.broadcasted_iota(jnp.int32, (ROWS, 2 * SLOT), 1)
    start.wait()

    @pl.loop(0, planes)
    def _(p):
        x = initial_in[p].reshape(size, width)
        beyond = initial_in[jnp.minimum(p + 1, planes - 1)].reshape(size, width)
        after = jnp.where(p + 1 < planes, mt(tables[2 * FACE :], beyond), 0.0)
        mine = mt(tables[: 2 * FACE], x).astype(BF)
        own[p, :FACE] = mm(mine[:FACE], one_hot(source[0], size, size)).astype(BF)
        own[p, FACE:] = mm(mine[FACE:], one_hot(source[1], 0, size)).astype(BF)
        for copy in arrivals(p):
            copy.wait()
        for a in range(3):
            rows = [inverse_in[p, v * 27 + a * 9 : v * 27 + a * 9 + 9] for v in range(5)]
            solves[:, a * FACE : (a + 1) * FACE] = -turned(jnp.concatenate(rows, 0))
        for f in range(4):
            faces[:, f * FACE : (f + 1) * FACE] = turned(couplings_in[p, 2 + f])
        faces[:, 4 * FACE : 4 * FACE + rhs] = right_in[p]
        faces[:, 256 : 256 + FACE] = turned(couplings_in[p, 0])
        faces[:, 256 + SLOT : 256 + SLOT + FACE] = turned(couplings_in[p, 1])

        bases = []
        before = None
        for c in range(columns):
            solve = solves[c]
            all_known = mt(solve, faces[c, :256])
            side = all_known[:, 128:]
            move = (c % half * rhs - (4 * FACE - 128)) % 128
            bases.append(pltpu.roll(side, move, 1) if move else side)
            known[p, c] = all_known.astype(BF)
            both = mt(solve, faces[c, 256:])
            if c % 2 == 0:
                before = both
            else:
                h, at = c // half, c % half // 2 * 2 * SLOT
                lanes = slice(at, at + 2 * SLOT)
                lower[p, h, :ROWS, lanes] = jnp.where(lane < SLOT, before, pltpu.roll(both, SLOT, 1)).astype(BF)
                upper[p, h, :ROWS, lanes] = jnp.where(lane < SLOT, pltpu.roll(before, SLOT, 1), both).astype(BF)
        for h in range(2):
            lanes = slice(h * half * rhs, (h + 1) * half * rhs)
            here = -own_lanes(bases[h * half : (h + 1) * half], rhs)
            base[p, :, lanes] = here
            fore[p, :, lanes] = here + mm(upper[p, h, :ROWS], split_lanes(after[:, lanes], rhs))
            step = lower[p, h, 2 * FACE : ROWS]

            @pl.when(p == 0)
            def _():
                prev[h] = step.astype(F32)

            @pl.when(p > 0)
            def _():
                prev[h] = mm(step, split_lanes(prev[h], SLOT))

            lower[p, h, ROWS:] = prev[h].astype(BF)

    for h in range(2):
        total = upper[planes - 1, h, :FACE].astype(F32)
        upper[planes - 1, h, ROWS:] = total.astype(BF)
        for q in range(planes - 2, -1, -1):
            total = mm(upper[q, h, :FACE], split_lanes(total, SLOT))
            upper[q, h, ROWS:] = total.astype(BF)


def gathered(received_up, received_down, own, p, up_sel, down_sel, low_pick, high_pick):
    low = mm(up_sel, received_up[p]).astype(BF)
    high = mm(down_sel, received_down[p]).astype(BF)
    c_low = mm(low[FACE:], low_pick).astype(BF) + own[p, :FACE]
    c_high = mm(high[FACE:], high_pick).astype(BF) + own[p, FACE : 2 * FACE]
    return [low[:FACE], high[:FACE], c_low, c_high]


def known_part(known_c, operand, columns, rhs):
    half = columns // 2
    out = []
    for h in range(2):
        side = operand[:, h * half * rhs : (h + 1) * half * rhs]
        out.append(own_lanes([mm(known_c(h * half + c), side) for c in range(half)], rhs))
    return jnp.concatenate(out, 1)


FIRST = slice(0, FACE)
LAST = slice(2 * FACE, ROWS)
FULL = slice(0, ROWS)
PRODUCT = slice(ROWS, ROWS + FACE)


def chain_kernel(known, base, matrix, received, own, neighbours, outs, order, rows, rhs, extra=None):
    up, down, up_sel, down_sel = received
    state, message = outs
    planes, columns = known.shape[:2]
    size = columns * rhs
    source = sources(neighbours, columns, rhs)
    low_pick = one_hot(source[0], 0, size)
    high_pick = one_hot(source[1], size, size)
    trace = None
    for p in order:
        parts = gathered(up, down, own, p, up_sel[...], down_sel[...], low_pick, high_pick)
        parts.append(jnp.zeros((256 - 4 * FACE, size), BF))
        whole = jnp.concatenate(parts, 0)
        start = base[p] + known_part(lambda c: known[p, c], whole, columns, rhs)
        if extra is not None and p == planes - 1:
            start = start + chain_step(extra[0].at[p], extra[1][...], rhs, FULL)
        state[p, FULL] = start
        start = start[rows]
        trace = start if trace is None else start + chain_step(matrix.at[p], trace, rhs, rows)
        state[p, PRODUCT] = trace
    for i in range(message.shape[0]):
        message[i, FIRST] = trace.astype(BF)
        for h in range(2):
            message[i, (1 + h) * FACE : (2 + h) * FACE] = matrix[order[-1], h, PRODUCT]


def forward_chain_kernel(
    up, down, above, own, neighbours, up_sel, down_sel, known, lower, upper, base, *outs, rhs
):
    order = range(up.shape[0])
    received = (up, down, up_sel, down_sel)
    chain_kernel(known, base, lower, received, own, neighbours, outs, order, LAST, rhs, (upper, above))


def backward_chain_kernel(up, down, own, neighbours, up_sel, down_sel, known, upper, base, *outs, rhs):
    order = range(up.shape[0] - 1, -1, -1)
    chain_kernel(
        known, base, upper, (up, down, up_sel, down_sel), own, neighbours, outs, order, FIRST, rhs
    )


def incoming(message, forward, rhs):
    here = lax.axis_index("sweep")
    n = message.shape[0]
    trace = None
    for i in range(n - 1) if forward else range(n - 1, 0, -1):
        value = message[i, FIRST].astype(F32)
        if trace is None:
            trace = jnp.zeros_like(value)
        else:
            product = [message[i, (1 + h) * FACE : (2 + h) * FACE] for h in range(2)]
            half = value.shape[1] // 2
            halves = [trace[:, h * half : (h + 1) * half] for h in range(2)]
            value = value + jnp.concatenate([mm(m, split_lanes(t, rhs)) for m, t in zip(product, halves)], 1)
        trace = jnp.where(i < here if forward else i > here, value, trace)
    return trace


def copied(source, target, sem):
    copies = [pltpu.make_async_copy(x, y, sem.at[i]) for i, (x, y) in enumerate(zip(source, target))]
    for copy in copies:
        copy.start()
    return copies


def forward_finish_kernel(
    message, state_there, lower_there, send, middle, change, up, down, state, lower, sem, *, rhs
):
    planes = state.shape[0]
    copies = copied((state_there, lower_there), (state, lower), sem)
    entry = incoming(message, True, rhs)
    for copy in copies:
        copy.wait()
    trace = entry
    for p in range(planes):
        delta = chain_step(lower.at[p], trace, rhs, FULL)
        change[p] = delta
        whole = (state[p, FULL] + delta).astype(BF)
        middle[p] = whole
        out = mm(send[...], whole).astype(BF)
        up[p] = out[:SHARED]
        down[p] = out[SHARED:]
        if p + 1 < planes:
            trace = state[p, PRODUCT] + chain_step(lower.at[p], entry, rhs, PRODUCT)


def middle_kernel(middle, change, base, neighbours, own_sel, own, out):
    planes, _, size = middle.shape
    columns = neighbours.shape[1]
    source = sources(neighbours, columns, size // columns)
    low_pick = one_hot(source[0], size, size)
    high_pick = one_hot(source[1], 0, size)
    for p in range(planes):
        mine = mm(own_sel[...], middle[p]).astype(BF)
        own[p, :FACE] = mm(mine[:FACE], low_pick).astype(BF)
        own[p, FACE:] = mm(mine[FACE:], high_pick).astype(BF)
        out[p] = base[p] + change[p]


def backward_finish_kernel(message, state_there, upper_there, back, result, state, upper, sem, *, rhs):
    planes = state.shape[0]
    copies = copied((state_there, upper_there), (state, upper), sem)
    entry = incoming(message, False, rhs)
    size = entry.shape[1]
    row = lax.broadcasted_iota(jnp.int32, (size, size), 0)
    column = lax.broadcasted_iota(jnp.int32, (size, size), 1)
    unit = jnp.where(row == column, 1.0, 0.0).astype(BF)
    columns, _, width = result.shape[1:]
    for copy in copies:
        copy.wait()
    trace = entry
    for p in range(planes - 1, -1, -1):
        whole = state[p, FULL] + chain_step(upper.at[p], trace, rhs, FULL)
        flat = mm(back[...], whole.astype(BF)).astype(BF)
        result[p] = mt(unit, flat).astype(BF).reshape(columns, rhs, width)
        if p:
            trace = state[p, PRODUCT] + chain_step(upper.at[p], entry, rhs, PRODUCT)


def call(kernel, outs, operands, name, flops=2e8, far=(), scratch=()):
    shapes = [jax.ShapeDtypeStruct(s, d) for s, d in outs]
    nbytes = sum(x.size * x.dtype.itemsize for x in list(operands) + shapes)
    spaces = [pltpu.SMEM if x.dtype == jnp.int32 else pltpu.VMEM for x in operands]
    spaces = [pltpu.HBM if i in far else space for i, space in enumerate(spaces)]
    scratch = list(scratch)
    if far and not scratch:
        scratch = [pltpu.VMEM(operands[i].shape, operands[i].dtype) for i in far]
        scratch.append(pltpu.SemaphoreType.DMA((len(far),)))
    return pl.pallas_call(
        kernel,
        out_shape=shapes,
        in_specs=[pl.BlockSpec(memory_space=space) for space in spaces],
        out_specs=[pl.BlockSpec(memory_space=pltpu.VMEM)] * len(shapes),
        scratch_shapes=scratch,
        compiler_params=pltpu.CompilerParams(vmem_limit_bytes=24 * MIB),
        cost_estimate=pl.CostEstimate(flops=int(flops), bytes_accessed=int(nbytes), transcendentals=0),
        name=name,
    )(*operands)


def weights(inverse, couplings, right, initial, neighbours):
    planes, columns, rhs, width = initial.shape
    size = columns * rhs
    pack = (planes, 2, ROWS + FACE, 256)
    field = (planes, ROWS, size)
    outs = [((planes, columns, ROWS, 256), BF), (pack, BF), (pack, BF), (field, F32), (field, F32)]
    outs.append(((planes, 2 * FACE, size), BF))
    operands = (inverse, couplings, right, initial, neighbours)
    scratch = [pltpu.VMEM(x.shape, x.dtype) for x in operands[:4]] + [
        pltpu.VMEM((columns, ROWS, width), BF),
        pltpu.VMEM((columns, 256 + 2 * SLOT, width), BF),
        pltpu.VMEM((2, FACE, 256), F32),
        pltpu.VMEM((3 * FACE, width), BF),
        pltpu.SemaphoreType.DMA((4, planes)),
    ]
    return call(weight_kernel, outs, operands, "weights", 1e10, (0, 1, 2, 3), scratch)


def ring(x, axis, by):
    n = lax.axis_size(axis)
    return lax.ppermute(x, axis, [(i, (i + by) % n) for i in range(n)])


def shift(x, axis, by):
    n = lax.axis_size(axis)
    return lax.ppermute(x, axis, [(i, i + by) for i in range(n) if 0 <= i + by < n])


def local(right_sides, initial, inverse_blocks, couplings, neighbours):
    planes, columns, rhs, width = initial.shape
    size = columns * rhs
    const = lambda x: jnp.asarray(x, BF)
    send_in = const(send_table(ROWS, inner))
    own_in = const(own_table(ROWS, inner))
    back = const(table(width, ROWS, [(natural(*n), n) for n in NODES], inner))
    up_sel = const(receive_table(2))
    down_sel = const(receive_table(0))
    beside = neighbours.T

    share = (planes, SHARED, size)
    up, down, above = call(
        first_kernel, [(share, BF), (share, BF), ((FACE, size), BF)], (initial,), "initial_traces"
    )
    up, down, above, initial = lax.optimization_barrier((up, down, above, initial))
    from_low = ring(up, "cross", 1)
    from_high = ring(down, "cross", -1)
    from_above = shift(above, "sweep", -1)
    known, lower, upper, base, fore, own = weights(
        inverse_blocks.transpose(0, 2, 1, 3), couplings.transpose(0, 2, 3, 1, 4), right_sides, initial, beside
    )

    field = (planes, ROWS, size)
    chain_outs = [((planes, ROWS + FACE, size), F32), ((lax.axis_size("sweep"), 3 * FACE, size), BF)]
    state, message = call(
        functools.partial(forward_chain_kernel, rhs=rhs),
        chain_outs,
        (from_low, from_high, from_above, own, beside, up_sel, down_sel, known, lower, upper, fore),
        "forward_chain",
    )
    message = lax.all_to_all(message, "sweep", 0, 0)
    middle, change, up, down = call(
        functools.partial(forward_finish_kernel, rhs=rhs),
        [(field, BF), (field, F32), (share, BF), (share, BF)],
        (message, state, lower, send_in),
        "forward_finish",
        far=(1, 2),
    )
    from_low = ring(up, "cross", 1)
    from_high = ring(down, "cross", -1)
    own, base = call(
        middle_kernel,
        [((planes, 2 * FACE, size), BF), (field, F32)],
        (middle, change, base, beside, own_in),
        "middle",
        2e9,
    )
    state, message = call(
        functools.partial(backward_chain_kernel, rhs=rhs),
        chain_outs,
        (from_low, from_high, own, beside, up_sel, down_sel, known, upper, base),
        "backward_chain",
    )
    message = lax.all_to_all(message, "sweep", 0, 0)
    (result,) = call(
        functools.partial(backward_finish_kernel, rhs=rhs),
        [(right_sides.shape, BF)],
        (message, state, upper, back),
        "backward_finish",
        far=(1, 2),
    )
    return result


def solution(mesh):
    return jax.shard_map(
        local,
        mesh=mesh,
        in_specs=(
            P("sweep", "cross", None, None),
            P("sweep", "cross", None, None),
            P("sweep", "cross", None, None),
            P("sweep", "cross", None, None, None),
            P("cross", None),
        ),
        out_specs=P("sweep", "cross", None, None),
        check_vma=False,
    )
```

time: 78.6 us -> 63.2 us (0.80)
  local copies, waits for them, and re-layouts: 27.8 us -> 6.66 us
  blocking collectives: 6.67 us -> 19.4 us
  starting transfers between devices: 19.5 us -> 12 us
  waiting for transfers between devices: 0.23 us -> 2.49 us
  Pallas kernels: 22.6 us -> 21.6 us
    unnamed x88 -> x20, local copies, waits for them, and re-layouts: 27.8 us -> 6.66 us
    all_to_all x0 -> x2, blocking collectives: none -> 19.4 us  [local(): message = lax.all_to_all(message, 'sweep', 0, 0)]
    pallas_call x1 -> x0, Pallas kernels: 8.99 us -> none  [weights(): pl.pallas_call(weight_kernel, grid=(planes,), out_shape=outs, in_specs=[l...]
    pallas_call x8 -> x7, Pallas kernels: 13.6 us -> 21.6 us  [call(): pl.pallas_call(kernel, out_shape=shapes, in_specs=[pl.BlockSpec(memory_sp...]
    all_to_all x2 -> x0, starting transfers between devices: 7.53 us -> none  [local(): last = lax.all_to_all(last, 'sweep', 0, 0)]
    all_gather x1 -> x0, blocking collectives: 6.67 us -> none  [local(): passes = lax.all_gather(passes, 'sweep')]
    ppermute x4, waiting for transfers between devices: 0.22 us -> 2.48 us  [ring(): return lax.ppermute(x, axis, [(i, (i + by) % n) for i in range(n)])]
  transfers between devices with their start and end apart: 7 -> 5, of which waited for: 1 -> 1; matrix products, arithmetic and copies ran while one was open for 0% -> 0% of each run, Pallas kernels for 15% -> 18%
where the time goes in v3:
time: 63.2 us; the launch traced here: 62.3 us
  Pallas kernels  21.6 us (34%)
  blocking collectives  19.4 us (31%)
  starting transfers between devices  12 us (19%)
  local copies, waits for them, and re-layouts  6.66 us (11%)
  waiting for transfers between devices  2.49 us (4%)
    pallas_call x7, Pallas kernels, call(): pl.pallas_call(kernel, out_shape=shapes, in_specs=[pl.BlockSpec(memory_sp...  21.6 us
    all_to_all x2, blocking collectives, local(): message = lax.all_to_all(message, 'sweep', 0, 0)  19.4 us
    ppermute x4, starting transfers between devices, ring(): return lax.ppermute(x, axis, [(i, (i + by) % n) for i in range(n)])  10.1 us
    unnamed x20, local copies, waits for them, and re-layouts  6.66 us
    ppermute x4, waiting for transfers between devices, ring(): return lax.ppermute(x, axis, [(i, (i + by) % n) for i in range(n)])  2.48 us
    ppermute x1, starting transfers between devices, shift(): lax.ppermute(x, axis, [(i, i + by) for i in range(n) if 0 <= i + by < n])  1.97 us
  transfers between devices with their start and end apart: 5, of which 1 were waited for; matrix products, arithmetic and copies ran while one was open for 0% of the time, Pallas kernels for 18%

profile of v3, /device:TPU:1, one launch (start us, length us, event | category | flops | bytes accessed | tf_op | source)
XLA Modules:
  0.0 62.3 jit_solution(11139115360804461399)
XLA Ops:
  0.0 0.0 copy-start.7
  0.0 1.0 %copy-done.7 = bf16[4,8,32,135]{3,2,1,0:T(8,128)(2,1)S(1)} copy-done((bf16[4,8,32,135]{3,2,1,0:T(8,128)(2,1)S(1)}, bf16[4,8,32,135]{3,2,1,0:T(8,128)(2,1)}, u32[]{:S(2)}) %copy-start.7) | copy-done | bytes 276504
  1.0 0.5 initial_traces.1
  1.6 2.0 %collective-permute-start.2 = (bf16[48,256]{1,0:T(8,128)(2,1)S(1)}, bf16[48,256]{1,0:T(8,128)(2,1)S(1)}, u32[]{:S(2)}, u32[]{:S(2)}) collective-permute-start(bf16[48,256]{1,0:T(8,128)(2,1)S(1)} %get-tuple-element.33), channel_id=1, source_target_pairs={{8,0},{16,8},{24,16},{9,1},{17,9},{25,17},{10,2},{18,10},{26,18},{... | collective-permute-start | bytes 73736 | tf_op jit(solution)/shard_map/ppermute | solution.py:442
  3.5 2.7 %collective-permute-start = (bf16[4,80,256]{2,1,0:T(8,128)(2,1)S(1)}, bf16[4,80,256]{2,1,0:T(8,128)(2,1)S(1)}, u32[]{:S(2)}, u32[]{:S(2)}) collective-permute-start(bf16[4,80,256]{2,1,0:T(8,128)(2,1)S(1)} %get-tuple-element.31), channel_id=1, source_target_pairs={{0,1},{1,2},{2,3},{3,4},{4,5},{5,6},{6,7},{7,0},{8,9},{9,10},{10,1... | collective-permute-start | bytes 491528 | tf_op jit(solution)/shard_map/ppermute | solution.py:437
  6.3 3.1 %collective-permute-start.1 = (bf16[4,80,256]{2,1,0:T(8,128)(2,1)S(1)}, bf16[4,80,256]{2,1,0:T(8,128)(2,1)S(1)}, u32[]{:S(2)}, u32[]{:S(2)}) collective-permute-start(bf16[4,80,256]{2,1,0:T(8,128)(2,1)S(1)} %get-tuple-element.32), channel_id=1, source_target_pairs={{0,7},{1,0},{2,1},{3,2},{4,3},{5,4},{6,5},{7,6},{8,15},{9,8},{10,9... | collective-permute-start | bytes 491528 | tf_op jit(solution)/shard_map/ppermute | solution.py:437
  9.4 0.0 copy-start.4
  9.4 0.7 %copy-done.4 = s32[8,4]{0,1:T(4,128)S(1)} copy-done((s32[8,4]{0,1:T(4,128)S(1)}, s32[8,4]{0,1:T(4,128)}, u32[]{:S(2)}) %copy-start.4) | copy-done | bytes 152
  10.1 0.0 copy-start.5
  10.1 2.3 %copy-done.5 = bf16[4,8,6,45,135]{4,1,3,2,0:T(8,128)(2,1)S(1)} copy-done((bf16[4,8,6,45,135]{4,1,3,2,0:T(8,128)(2,1)S(1)}, bf16[4,8,6,45,135]{4,1,3,2,0:T(8,128)(2,1)}, u32[]{:S(2)}) %copy-start.5) | copy-done | bytes 2332824
  12.3 0.0 copy-start.6
  12.3 1.6 %copy-done.6 = bf16[4,8,135,135]{3,1,2,0:T(8,128)(2,1)S(1)} copy-done((bf16[4,8,135,135]{3,1,2,0:T(8,128)(2,1)S(1)}, bf16[4,8,135,135]{3,1,2,0:T(8,128)(2,1)}, u32[]{:S(2)}) %copy-start.6) | copy-done | bytes 1166424
  13.9 0.0 copy-start.8
  13.9 1.0 %copy-done.8 = bf16[4,8,32,135]{3,2,1,0:T(8,128)(2,1)S(1)} copy-done((bf16[4,8,32,135]{3,2,1,0:T(8,128)(2,1)S(1)}, bf16[4,8,32,135]{3,2,1,0:T(8,128)(2,1)}, u32[]{:S(2)}) %copy-start.8) | copy-done | bytes 276504
  15.0 0.0 copy-start
  15.0 0.0 copy-start.1
  15.0 10.1 %weights.1 = (bf16[4,8,144,256]{3,2,1,0:T(8,128)(2,1)S(1)}, bf16[4,2,192,256]{3,2,1,0:T(8,128)(2,1)S(1)}, bf16[4,2,192,256]{3,2,1,0:T(8,128)(2,1)S(1)}, f32[4,14...) custom-call(bf16[4,135,8,135]{3,2,1,0:T(8,128)(2,1)S(1)} %bitcast.8, ...), custom_call_target="tpu_custom_call" | custom-call | flops 10000000000 | bytes 9360704 | tf_op jit(solution)/shard_map/weights/pallas_call | solution.py:405
  25.1 0.0 collective-permute-done.2.above
  25.1 0.0 collective-permute-done.up
  25.1 0.0 collective-permute-done.1.down
  25.1 0.0 copy-done
  25.1 0.0 copy-done.1
  25.1 0.0 copy-start.2
  25.1 2.5 %forward_chain.1 = (f32[4,192,256]{2,1,0:T(8,128)S(1)}, bf16[4,144,256]{2,1,0:T(8,128)(2,1)S(1)}) custom-call(bf16[4,80,256]{2,1,0:T(8,128)(2,1)S(1)} %collective-permute-done.up, bf16[4,80,256]{2,1,0:T(8,128)(2,1)S(1)} %collective-permute-done.1.down, bf16[48,256]{1,0:T(8,128)(2,1)S(1)} %collective-permute-done.2.above, ...), custom_call_target="tpu_custom_call" | custom-call | flops 200000000 | bytes 6183040 | tf_op jit(solution)/shard_map/forward_chain/pallas_call | solution.py:405
  27.7 0.0 copy-start.9
  27.7 8.9 %all_to_all.10.message = bf16[4,144,256]{2,1,0:T(8,128)(2,1)S(1)} all-to-all(bf16[4,144,256]{2,1,0:T(8,128)(2,1)S(1)} %get-tuple-element.40), channel_id=1, replica_groups=mesh['sweep'=4,'cross'=8] {'sweep'}, dimensions={0} | all-to-all | bytes 589824 | tf_op jit(solution)/shard_map/all_to_all | solution.py:476
  36.6 0.0 copy-done.2
  36.6 1.7 %forward_finish.1 = (bf16[4,144,256]{2,1,0:T(8,128)(2,1)S(1)}, f32[4,144,256]{2,1,0:T(8,128)S(1)}, bf16[4,80,256]{2,1,0:T(8,128)(2,1)S(1)}, bf16[4,80,256]{2,1,0:T(8,128)(2,1)S(1)}) custom-call(bf16[4,144,256]{2,1,0:T(8,128)(2,1)S(1)} %all_to_all.10.message, f32[4,192,256]{2,1,0:T(8,128)S(1)} %get-tuple-element.41.state_there, ...), custom_call_target="tpu_custom_call" | custom-call | flops 200000000 | bytes 3126272 | tf_op jit(solution)/shard_map/forward_finish/pallas_call | solution.py:405
  38.3 0.1 collective-permute-start.3
  38.4 4.1 %collective-permute-start.4 = (bf16[4,80,256]{2,1,0:T(8,128)(2,1)S(1)}, bf16[4,80,256]{2,1,0:T(8,128)(2,1)S(1)}, u32[]{:S(2)}, u32[]{:S(2)}) collective-permute-start(bf16[4,80,256]{2,1,0:T(8,128)(2,1)S(1)} %get-tuple-element.43), channel_id=1, source_target_pairs={{0,7},{1,0},{2,1},{3,2},{4,3},{5,4},{6,5},{7,6},{8,15},{9,8},{10,9... | collective-permute-start | bytes 491528 | tf_op jit(solution)/shard_map/ppermute | solution.py:437
  42.5 0.0 copy-done.9
  42.5 1.2 %middle.1 = (bf16[4,96,256]{2,1,0:T(8,128)(2,1)S(1)}, f32[4,144,256]{2,1,0:T(8,128)S(1)}) custom-call(bf16[4,144,256]{2,1,0:T(8,128)(2,1)S(1)} %get-tuple-element.44.middle, f32[4,144,256]{2,1,0:T(8,128)S(1)} %get-tuple-element.45.change, f32[4,144,256]{2,1,0:T(8,128)S(1)} %get-tuple-element.46.base, s32[4,8]{1,0:T(4,128)S(1)} %bitcast.5, ...), custom_call_target="tpu_custom_call" | custom-call | flops 2000000000 | bytes 2288768 | tf_op jit(solution)/shard_map/middle/pallas_call | solution.py:405
  43.8 2.5 %collective-permute-done.3.up = bf16[4,80,256]{2,1,0:T(8,128)(2,1)S(1)} collective-permute-done((bf16[4,80,256]{2,1,0:T(8,128)(2,1)S(1)}, bf16[4,80,256]{2,1,0:T(8,128)(2,1)S(1)}, u32[]{:S(2)}, u32[]{:S(2)}) %collective-permute-start.3) | collective-permute-done | bytes 163872 | tf_op jit(solution)/shard_map/ppermute | solution.py:437
  46.2 0.0 collective-permute-done.4.down
  46.3 0.0 copy-start.3
  46.3 2.5 %backward_chain.1 = (f32[4,192,256]{2,1,0:T(8,128)S(1)}, bf16[4,144,256]{2,1,0:T(8,128)(2,1)S(1)}) custom-call(bf16[4,80,256]{2,1,0:T(8,128)(2,1)S(1)} %collective-permute-done.3.up, bf16[4,80,256]{2,1,0:T(8,128)(2,1)S(1)} %collective-permute-done.4.down, bf16[4,96,256]{2,1,0:T(8,128)(2,1)S(1)} %get-tuple-element.47.own, s32[4,8]{1,0:T(4,128)S(1)} %bitcast.6, ...), custom_call_target="tpu_custom_call" | custom-call | flops 200000000 | bytes 5372032 | tf_op jit(solution)/shard_map/backward_chain/pallas_call | solution.py:405
  48.7 10.5 %all_to_all.11.message = bf16[4,144,256]{2,1,0:T(8,128)(2,1)S(1)} all-to-all(bf16[4,144,256]{2,1,0:T(8,128)(2,1)S(1)} %get-tuple-element.49), channel_id=1, replica_groups=mesh['sweep'=4,'cross'=8] {'sweep'}, dimensions={0} | all-to-all | bytes 589824 | tf_op jit(solution)/shard_map/all_to_all | solution.py:499
  59.2 0.0 copy-done.3
  59.2 3.1 %backward_finish.1 = bf16[4,8,32,135]{3,2,1,0:T(8,128)(2,1)} custom-call(bf16[4,144,256]{2,1,0:T(8,128)(2,1)S(1)} %all_to_all.11.message, f32[4,192,256]{2,1,0:T(8,128)S(1)} %get-tuple-element.50.state_there, bf16[4,2,192,256]{3,2,1,0:T(8,128)(2,1)S(1)} %get-tuple-element.38.upper.upper_there, bf16[135,144]{1,0:T(8,128)(2,1)S(1)} %copy-done.3), custom_call_target="tpu_custom_call" | custom-call | flops 200000000 | bytes 2183136 | tf_op jit(solution)/shard_map/backward_finish/pallas_call | solution.py:405
Async XLA Ops:
  0.0 1.0 %copy-start.7 = (bf16[4,8,32,135]{3,2,1,0:T(8,128)(2,1)S(1)}, bf16[4,8,32,135]{3,2,1,0:T(8,128)(2,1)}, u32[]{:S(2)}) copy-start(bf16[4,8,32,135]{3,2,1,0:T(8,128)(2,1)} %initial.2) | copy-start | bytes 829444
  1.6 23.5 %collective-permute-start.2 = (bf16[48,256]{1,0:T(8,128)(2,1)S(1)}, bf16[48,256]{1,0:T(8,128)(2,1)S(1)}, u32[]{:S(2)}, u32[]{:S(2)}) collective-permute-start(bf16[48,256]{1,0:T(8,128)(2,1)S(1)} %get-tuple-element.33), channel_id=1, source_target_pairs={{8,0},{16,8},{24,16},{9,1},{17,9},{25,17},{10,2},{18,10},{26,18},{... | collective-permute-start | bytes 73736 | tf_op jit(solution)/shard_map/ppermute | solution.py:442
  3.5 21.6 %collective-permute-start = (bf16[4,80,256]{2,1,0:T(8,128)(2,1)S(1)}, bf16[4,80,256]{2,1,0:T(8,128)(2,1)S(1)}, u32[]{:S(2)}, u32[]{:S(2)}) collective-permute-start(bf16[4,80,256]{2,1,0:T(8,128)(2,1)S(1)} %get-tuple-element.31), channel_id=1, source_target_pairs={{0,1},{1,2},{2,3},{3,4},{4,5},{5,6},{6,7},{7,0},{8,9},{9,10},{10,1... | collective-permute-start | bytes 491528 | tf_op jit(solution)/shard_map/ppermute | solution.py:437
  6.3 18.8 %collective-permute-start.1 = (bf16[4,80,256]{2,1,0:T(8,128)(2,1)S(1)}, bf16[4,80,256]{2,1,0:T(8,128)(2,1)S(1)}, u32[]{:S(2)}, u32[]{:S(2)}) collective-permute-start(bf16[4,80,256]{2,1,0:T(8,128)(2,1)S(1)} %get-tuple-element.32), channel_id=1, source_target_pairs={{0,7},{1,0},{2,1},{3,2},{4,3},{5,4},{6,5},{7,6},{8,15},{9,8},{10,9... | collective-permute-start | bytes 491528 | tf_op jit(solution)/shard_map/ppermute | solution.py:437
  9.4 0.7 %copy-start.4 = (s32[8,4]{0,1:T(4,128)S(1)}, s32[8,4]{0,1:T(4,128)}, u32[]{:S(2)}) copy-start(s32[8,4]{0,1:T(4,128)} %param.14) | copy-start | bytes 388
  10.1 2.3 %copy-start.5 = (bf16[4,8,6,45,135]{4,1,3,2,0:T(8,128)(2,1)S(1)}, bf16[4,8,6,45,135]{4,1,3,2,0:T(8,128)(2,1)}, u32[]{:S(2)}) copy-start(bf16[4,8,6,45,135]{4,1,3,2,0:T(8,128)(2,1)} %param.13) | copy-start | bytes 6998404
  12.3 1.6 %copy-start.6 = (bf16[4,8,135,135]{3,1,2,0:T(8,128)(2,1)S(1)}, bf16[4,8,135,135]{3,1,2,0:T(8,128)(2,1)}, u32[]{:S(2)}) copy-start(bf16[4,8,135,135]{3,1,2,0:T(8,128)(2,1)} %param.12) | copy-start | bytes 3499204
  13.9 1.0 %copy-start.8 = (bf16[4,8,32,135]{3,2,1,0:T(8,128)(2,1)S(1)}, bf16[4,8,32,135]{3,2,1,0:T(8,128)(2,1)}, u32[]{:S(2)}) copy-start(bf16[4,8,32,135]{3,2,1,0:T(8,128)(2,1)} %right.1) | copy-start | bytes 829444
  15.0 10.1 %copy-start = (bf16[96,80]{1,0:T(8,128)(2,1)S(1)}, bf16[96,80]{1,0:T(8,128)(2,1)}, u32[]{:S(2)}) copy-start(bf16[96,80]{1,0:T(8,128)(2,1)} %constant.14.clone.down_sel) | copy-start | bytes 46084
  15.0 10.1 %copy-start.1 = (bf16[96,80]{1,0:T(8,128)(2,1)S(1)}, bf16[96,80]{1,0:T(8,128)(2,1)}, u32[]{:S(2)}) copy-start(bf16[96,80]{1,0:T(8,128)(2,1)} %constant.13.clone.up_sel) | copy-start | bytes 46084
  25.1 11.4 %copy-start.2 = (bf16[160,144]{1,0:T(8,128)(2,1)S(1)}, bf16[160,144]{1,0:T(8,128)(2,1)}, u32[]{:S(2)}) copy-start(bf16[160,144]{1,0:T(8,128)(2,1)} %constant.10.clone.send) | copy-start | bytes 138244
  27.7 14.8 %copy-start.9 = (bf16[96,144]{1,0:T(8,128)(2,1)S(1)}, bf16[96,144]{1,0:T(8,128)(2,1)}, u32[]{:S(2)}) copy-start(bf16[96,144]{1,0:T(8,128)(2,1)} %constant.11.clone.own_sel) | copy-start | bytes 82948
  38.3 7.9 %collective-permute-start.3 = (bf16[4,80,256]{2,1,0:T(8,128)(2,1)S(1)}, bf16[4,80,256]{2,1,0:T(8,128)(2,1)S(1)}, u32[]{:S(2)}, u32[]{:S(2)}) collective-permute-start(bf16[4,80,256]{2,1,0:T(8,128)(2,1)S(1)} %get-tuple-element.42), channel_id=1, source_target_pairs={{0,1},{1,2},{2,3},{3,4},{4,5},{5,6},{6,7},{7,0},{8,9},{9,10},{10,1... | collective-permute-start | bytes 491528 | tf_op jit(solution)/shard_map/ppermute | solution.py:437
  38.4 7.9 %collective-permute-start.4 = (bf16[4,80,256]{2,1,0:T(8,128)(2,1)S(1)}, bf16[4,80,256]{2,1,0:T(8,128)(2,1)S(1)}, u32[]{:S(2)}, u32[]{:S(2)}) collective-permute-start(bf16[4,80,256]{2,1,0:T(8,128)(2,1)S(1)} %get-tuple-element.43), channel_id=1, source_target_pairs={{0,7},{1,0},{2,1},{3,2},{4,3},{5,4},{6,5},{7,6},{8,15},{9,8},{10,9... | collective-permute-start | bytes 491528 | tf_op jit(solution)/shard_map/ppermute | solution.py:437
  46.3 13.0 %copy-start.3 = (bf16[135,144]{1,0:T(8,128)(2,1)S(1)}, bf16[135,144]{1,0:T(8,128)(2,1)}, u32[]{:S(2)}) copy-start(bf16[135,144]{1,0:T(8,128)(2,1)} %constant.12.clone.back) | copy-start | bytes 116644

commit v4 on v3

--- a/solution.py
+++ b/solution.py
@@ -295,9 +295,7 @@
         trace = start if trace is None else start + chain_step(matrix.at[p], trace, rhs, rows)
         state[p, PRODUCT] = trace
     for i in range(message.shape[0]):
-        message[i, FIRST] = trace.astype(BF)
-        for h in range(2):
-            message[i, (1 + h) * FACE : (2 + h) * FACE] = matrix[order[-1], h, PRODUCT]
+        message[i] = trace.astype(BF)
 
 
 def forward_chain_kernel(
@@ -315,16 +313,17 @@
     )
 
 
-def incoming(message, forward, rhs):
+def incoming(message, near, next_near, forward, rhs):
     here = lax.axis_index("sweep")
     n = message.shape[0]
     trace = None
     for i in range(n - 1) if forward else range(n - 1, 0, -1):
-        value = message[i, FIRST].astype(F32)
+        value = message[i].astype(F32)
         if trace is None:
             trace = jnp.zeros_like(value)
         else:
-            product = [message[i, (1 + h) * FACE : (2 + h) * FACE] for h in range(2)]
+            step = here - 1 if forward else here + 1
+            product = [jnp.where(step == i, near[h], next_near[h]) for h in range(2)]
             half = value.shape[1] // 2
             halves = [trace[:, h * half : (h + 1) * half] for h in range(2)]
             value = value + jnp.concatenate([mm(m, split_lanes(t, rhs)) for m, t in zip(product, halves)], 1)
@@ -340,11 +339,11 @@
 
 
 def forward_finish_kernel(
-    message, state_there, lower_there, send, middle, change, up, down, state, lower, sem, *, rhs
+    message, near, next_near, state_there, lower_there, send, middle, change, up, down, state, lower, sem, *, rhs
 ):
     planes = state.shape[0]
     copies = copied((state_there, lower_there), (state, lower), sem)
-    entry = incoming(message, True, rhs)
+    entry = incoming(message, near, next_near, True, rhs)
     for copy in copies:
         copy.wait()
     trace = entry
@@ -373,10 +372,12 @@
         out[p] = base[p] + change[p]
 
 
-def backward_finish_kernel(message, state_there, upper_there, back, result, state, upper, sem, *, rhs):
+def backward_finish_kernel(
+    message, near, next_near, state_there, upper_there, back, result, state, upper, sem, *, rhs
+):
     planes = state.shape[0]
     copies = copied((state_there, upper_there), (state, upper), sem)
-    entry = incoming(message, False, rhs)
+    entry = incoming(message, near, next_near, False, rhs)
     size = entry.shape[1]
     row = lax.broadcasted_iota(jnp.int32, (size, size), 0)
     column = lax.broadcasted_iota(jnp.int32, (size, size), 1)
@@ -398,6 +399,9 @@
     nbytes = sum(x.size * x.dtype.itemsize for x in list(operands) + shapes)
     spaces = [pltpu.SMEM if x.dtype == jnp.int32 else pltpu.VMEM for x in operands]
     spaces = [pltpu.HBM if i in far else space for i, space in enumerate(spaces)]
+    operands = [
+        pltpu.with_memory_space_constraint(x, pltpu.HBM) if i in far else x for i, x in enumerate(operands)
+    ]
     scratch = list(scratch)
     if far and not scratch:
         scratch = [pltpu.VMEM(operands[i].shape, operands[i].dtype) for i in far]
@@ -412,6 +416,14 @@
         cost_estimate=pl.CostEstimate(flops=int(flops), bytes_accessed=int(nbytes), transcendentals=0),
         name=name,
     )(*operands)
+
+
+def products(x, by):
+    n = lax.axis_size("sweep")
+    inner = range(1, n - 1)
+    return [
+        lax.ppermute(x, "sweep", [(i, i + step) for i in inner if 0 <= i + step < n]) for step in (by, 2 * by)
+    ]
 
 
 def weights(inverse, couplings, right, initial, neighbours):
@@ -465,8 +477,12 @@
         inverse_blocks.transpose(0, 2, 1, 3), couplings.transpose(0, 2, 3, 1, 4), right_sides, initial, beside
     )
 
+    pass_f = lower[planes - 1, :, PRODUCT]
+    from_low, from_high, from_above, pass_f = lax.optimization_barrier((from_low, from_high, from_above, pass_f))
+    passes = products(pass_f, 1)
+
     field = (planes, ROWS, size)
-    chain_outs = [((planes, ROWS + FACE, size), F32), ((lax.axis_size("sweep"), 3 * FACE, size), BF)]
+    chain_outs = [((planes, ROWS + FACE, size), F32), ((lax.axis_size("sweep"), FACE, size), BF)]
     state, message = call(
         functools.partial(forward_chain_kernel, rhs=rhs),
         chain_outs,
@@ -477,9 +493,9 @@
     middle, change, up, down = call(
         functools.partial(forward_finish_kernel, rhs=rhs),
         [(field, BF), (field, F32), (share, BF), (share, BF)],
-        (message, state, lower, send_in),
+        (message, *passes, state, lower, send_in),
         "forward_finish",
-        far=(1, 2),
+        far=(3, 4),
     )
     from_low = ring(up, "cross", 1)
     from_high = ring(down, "cross", -1)
@@ -490,6 +506,9 @@
         "middle",
         2e9,
     )
+    own, pass_b = lax.optimization_barrier((own, upper[0, :, PRODUCT]))
+    passes = products(pass_b, -1)
+    from_low, from_high, *passes = lax.optimization_barrier((from_low, from_high, *passes))
     state, message = call(
         functools.partial(backward_chain_kernel, rhs=rhs),
         chain_outs,
@@ -500,9 +519,9 @@
     (result,) = call(
         functools.partial(backward_finish_kernel, rhs=rhs),
         [(right_sides.shape, BF)],
-        (message, state, upper, back),
+        (message, *passes, state, upper, back),
         "backward_finish",
-        far=(1, 2),
+        far=(3, 4),
     )
     return result
 

time: 63.2 us -> 69.2 us (1.095)
  the two profiles are of different devices: /device:TPU:1 before, /device:TPU:0 now
where the time goes in v4:
time: 69.2 us; the launch traced here: 68.7 us
  Pallas kernels  25.7 us (37%)
  starting transfers between devices  21.8 us (32%)
  waiting for transfers between devices  8.37 us (12%)
  blocking collectives  6.66 us (10%)
  local copies, waits for them, and re-layouts  5.97 us (9%)
    pallas_call x7, Pallas kernels, call(): pl.pallas_call(kernel, out_shape=shapes, in_specs=[pl.BlockSpec(memory_sp...  25.7 us
    ppermute x4, starting transfers between devices, ring(): return lax.ppermute(x, axis, [(i, (i + by) % n) for i in range(n)])  10.9 us
    all_to_all x1, blocking collectives, local(): message = lax.all_to_all(message, 'sweep', 0, 0)  6.66 us
    all_to_all x1, starting transfers between devices, local(): message = lax.all_to_all(message, 'sweep', 0, 0)  5.56 us
    ppermute x4, waiting for transfers between devices, products(): lax.ppermute(x, 'sweep', [(i, i + step) for i in inner if 0 <= i + step <...  4.69 us
    unnamed x30, local copies, waits for them, and re-layouts  4.67 us
    ppermute x4, starting transfers between devices, products(): lax.ppermute(x, 'sweep', [(i, i + step) for i in inner if 0 <= i + step <...  4.04 us
    all_to_all x1, waiting for transfers between devices, local(): message = lax.all_to_all(message, 'sweep', 0, 0)  3.67 us
  transfers between devices with their start and end apart: 10, of which 3 were waited for; matrix products, arithmetic and copies ran while one was open for 2% of the time, Pallas kernels for 23%

profile of v4, /device:TPU:0, one launch (start us, length us, event | category | flops | bytes accessed | tf_op | source)
XLA Modules:
  0.0 68.7 jit_solution(480260092552976533)
XLA Ops:
  0.0 0.0 copy-start.10
  0.0 1.0 %copy-done.10 = bf16[4,8,32,135]{3,2,1,0:T(8,128)(2,1)S(1)} copy-done((bf16[4,8,32,135]{3,2,1,0:T(8,128)(2,1)S(1)}, bf16[4,8,32,135]{3,2,1,0:T(8,128)(2,1)}, u32[]{:S(2)}) %copy-start.10) | copy-done | bytes 276504
  1.0 0.5 initial_traces.1
  1.6 3.0 %collective-permute-start = (bf16[4,80,256]{2,1,0:T(8,128)(2,1)S(1)}, bf16[4,80,256]{2,1,0:T(8,128)(2,1)S(1)}, u32[]{:S(2)}, u32[]{:S(2)}) collective-permute-start(bf16[4,80,256]{2,1,0:T(8,128)(2,1)S(1)} %get-tuple-element.41), channel_id=1, source_target_pairs={{0,1},{1,2},{2,3},{3,4},{4,5},{5,6},{6,7},{7,0},{8,9},{9,10},{10,1... | collective-permute-start | bytes 491528 | tf_op jit(solution)/shard_map/ppermute | solution.py:449
  4.6 3.1 %collective-permute-start.1 = (bf16[4,80,256]{2,1,0:T(8,128)(2,1)S(1)}, bf16[4,80,256]{2,1,0:T(8,128)(2,1)S(1)}, u32[]{:S(2)}, u32[]{:S(2)}) collective-permute-start(bf16[4,80,256]{2,1,0:T(8,128)(2,1)S(1)} %get-tuple-element.42), channel_id=1, source_target_pairs={{0,7},{1,0},{2,1},{3,2},{4,3},{5,4},{6,5},{7,6},{8,15},{9,8},{10,9... | collective-permute-start | bytes 491528 | tf_op jit(solution)/shard_map/ppermute | solution.py:449
  7.7 1.3 %collective-permute-start.2 = (bf16[48,256]{1,0:T(8,128)(2,1)S(1)}, bf16[48,256]{1,0:T(8,128)(2,1)S(1)}, u32[]{:S(2)}, u32[]{:S(2)}) collective-permute-start(bf16[48,256]{1,0:T(8,128)(2,1)S(1)} %get-tuple-element.43), channel_id=1, source_target_pairs={{8,0},{16,8},{24,16},{9,1},{17,9},{25,17},{10,2},{18,10},{26,18},{... | collective-permute-start | bytes 73736 | tf_op jit(solution)/shard_map/ppermute | solution.py:454
  9.0 0.0 copy-start.8
  9.0 0.7 copy-done.8
  9.6 0.0 copy-start.4
  9.7 0.0 copy-start.5
  9.7 11.6 %weights.1 = (bf16[4,8,144,256]{3,2,1,0:T(8,128)(2,1)S(1)}, bf16[4,2,192,256]{3,2,1,0:T(8,128)(2,1)S(1)}, bf16[4,2,192,256]{3,2,1,0:T(8,128)(2,1)S(1)}, f32[4,14...) custom-call(bf16[4,135,8,135]{3,2,1,0:T(8,128)(2,1)} %bitcast.12, ...), custom_call_target="tpu_custom_call" | custom-call | flops 10000000000 | bytes 9360704 | tf_op jit(solution)/shard_map/weights/pallas_call | solution.py:409
  21.2 0.0 copy-start.1
  21.3 0.0 copy-start.12
  21.3 0.0 copy-start
  21.3 0.7 slice_bitcast_fusion.1
  21.9 0.0 collective-permute-done.2.above
  22.0 0.0 collective-permute-done.up
  22.0 0.0 collective-permute-done.1.down
  22.0 0.7 collective-permute-start.3
  22.6 0.7 collective-permute-start.4
  23.3 0.0 copy-done.4
  23.3 0.0 copy-done.5
  23.3 0.0 copy-start.6
  23.3 0.0 copy-start.9
  23.4 0.0 copy-start.11
  23.4 3.2 %forward_chain.1 = (f32[4,192,256]{2,1,0:T(8,128)S(1)}, bf16[4,48,256]{2,1,0:T(8,128)(2,1)}) custom-call(bf16[4,80,256]{2,1,0:T(8,128)(2,1)S(1)} %collective-permute-done.up, bf16[4,80,256]{2,1,0:T(8,128)(2,1)S(1)} %collective-permute-done.1.down, bf16[48,256]{1,0:T(8,128)(2,1)S(1)} %collective-permute-done.2.above, ...), custom_call_target="tpu_custom_call" | custom-call | flops 200000000 | bytes 5986432 | tf_op jit(solution)/shard_map/forward_chain/pallas_call | solution.py:409
  26.5 0.0 copy-done.1
  26.5 0.0 copy-done.12
  26.5 0.0 copy-start.2
  26.6 0.9 %copy-done.2 = f32[4,192,256]{2,1,0:T(8,128)} copy-done((f32[4,192,256]{2,1,0:T(8,128)}, f32[4,192,256]{2,1,0:T(8,128)S(1)}, u32[]{:S(2)}) %copy-start.2) | copy-done | bytes 786456
  27.5 5.6 %all-to-all-start = ((bf16[4,48,256]{2,1,0:T(8,128)(2,1)}), bf16[4,48,256]{2,1,0:T(8,128)(2,1)S(1)}, u32[]{:S(2)}, u32[]{:S(2)}) async-start(bf16[4,48,256]{2,1,0:T(8,128)(2,1)} %get-tuple-element.53), calls=%async_computation | async-start | bytes 196608 | tf_op jit(solution)/shard_map/all_to_all | solution.py:492
  33.0 0.6 slice_bitcast_fusion
  33.6 0.0 collective-permute-done.3.near
  33.6 0.0 collective-permute-done.4.next_near
  33.6 3.7 %all-to-all-done.message = bf16[4,48,256]{2,1,0:T(8,128)(2,1)S(1)} async-done(((bf16[4,48,256]{2,1,0:T(8,128)(2,1)}), bf16[4,48,256]{2,1,0:T(8,128)(2,1)S(1)}, u32[]{:S(2)}, u32[]{:S(2)}) %all-to-all-start) | async-done | bytes 98336 | tf_op jit(solution)/shard_map/all_to_all | solution.py:492
  37.3 0.0 copy-done.6
  37.3 2.7 %forward_finish.1 = (bf16[4,144,256]{2,1,0:T(8,128)(2,1)S(1)}, f32[4,144,256]{2,1,0:T(8,128)S(1)}, bf16[4,80,256]{2,1,0:T(8,128)(2,1)S(1)}, bf16[4,80,256]{2,1,0:T(8,128)(2,1)S(1)}) custom-call(bf16[4,48,256]{2,1,0:T(8,128)(2,1)S(1)} %all-to-all-done.message, bf16[2,48,256]{2,1,0:T(8,128)(2,1)S(1)} %collective-permute-done.3.near, ...), custom_call_target="tpu_custom_call" | custom-call | flops 200000000 | bytes 3027968 | tf_op jit(solution)/shard_map/forward_finish/pallas_call | solution.py:409
  40.0 0.1 collective-permute-start.5
  40.1 4.7 %collective-permute-start.6 = (bf16[4,80,256]{2,1,0:T(8,128)(2,1)S(1)}, bf16[4,80,256]{2,1,0:T(8,128)(2,1)S(1)}, u32[]{:S(2)}, u32[]{:S(2)}) collective-permute-start(bf16[4,80,256]{2,1,0:T(8,128)(2,1)S(1)} %get-tuple-element.57), channel_id=1, source_target_pairs={{0,7},{1,0},{2,1},{3,2},{4,3},{5,4},{6,5},{7,6},{8,15},{9,8},{10,9... | collective-permute-start | bytes 491528 | tf_op jit(solution)/shard_map/ppermute | solution.py:449
  44.8 0.0 copy-done.9
  44.8 0.0 copy-done.11
  44.8 0.0 copy-start.13
  44.8 1.1 %copy-done.13 = f32[4,144,256]{2,1,0:T(8,128)S(1)} copy-done((f32[4,144,256]{2,1,0:T(8,128)S(1)}, f32[4,144,256]{2,1,0:T(8,128)}, u32[]{:S(2)}) %copy-start.13) | copy-done | bytes 589848
  45.9 0.0 copy-start.14
  45.9 1.2 %middle.1 = (bf16[4,96,256]{2,1,0:T(8,128)(2,1)S(1)}, f32[4,144,256]{2,1,0:T(8,128)S(1)}) custom-call(bf16[4,144,256]{2,1,0:T(8,128)(2,1)S(1)} %get-tuple-element.58.middle, f32[4,144,256]{2,1,0:T(8,128)S(1)} %get-tuple-element.59.change, f32[4,144,256]{2,1,0:T(8,128)S(1)} %copy-done.13, s32[4,8]{1,0:T(4,128)S(1)} %bitcast.9, bf16[96,144]{1,0:T(8,128)(2,1)S(1)} %copy-done.11), custom_call_target="tpu_custom_call" | custom-call | flops 2000000000 | bytes 2288768 | tf_op jit(solution)/shard_map/middle/pallas_call | solution.py:409
  47.1 0.0 copy-start.7
  47.1 0.0 copy-done.14
  47.1 1.4 %collective-permute-start.7 = (bf16[2,48,256]{2,1,0:T(8,128)(2,1)S(1)}, bf16[2,48,256]{2,1,0:T(8,128)(2,1)S(1)}, u32[]{:S(2)}, u32[]{:S(2)}) collective-permute-start(bf16[2,48,256]{2,1,0:T(8,128)(2,1)S(1)} %copy-done.14), channel_id=1, source_target_pairs={{8,0},{16,8},{9,1},{17,9},{10,2},{18,10},{11,3},{19,11},{12,4},{20... | collective-permute-start | bytes 147464 | tf_op jit(solution)/shard_map/ppermute | solution.py:425
  48.6 1.3 %collective-permute-start.8 = (bf16[2,48,256]{2,1,0:T(8,128)(2,1)S(1)}, bf16[2,48,256]{2,1,0:T(8,128)(2,1)S(1)}, u32[]{:S(2)}, u32[]{:S(2)}) collective-permute-start(bf16[2,48,256]{2,1,0:T(8,128)(2,1)S(1)} %copy-done.14), channel_id=1, source_target_pairs={{16,0},{17,1},{18,2},{19,3},{20,4},{21,5},{22,6},{23,7}} | collective-permute-start | bytes 147464 | tf_op jit(solution)/shard_map/ppermute | solution.py:425
  49.9 0.5 collective-permute-done.7.near
  50.4 4.2 %collective-permute-done.8.next_near = bf16[2,48,256]{2,1,0:T(8,128)(2,1)S(1)} collective-permute-done((bf16[2,48,256]{2,1,0:T(8,128)(2,1)S(1)}, bf16[2,48,256]{2,1,0:T(8,128)(2,1)S(1)}, u32[]{:S(2)}, u32[]{:S(2)}) %collective-permute-start.8) | collective-permute-done | bytes 49184 | tf_op jit(solution)/shard_map/ppermute | solution.py:425
  54.5 0.0 collective-permute-done.5.up
  54.5 0.0 collective-permute-done.6.down
  54.6 0.0 copy-done
  54.6 2.5 %backward_chain.1 = (f32[4,192,256]{2,1,0:T(8,128)S(1)}, bf16[4,48,256]{2,1,0:T(8,128)(2,1)S(1)}) custom-call(bf16[4,80,256]{2,1,0:T(8,128)(2,1)S(1)} %collective-permute-done.5.up, bf16[4,80,256]{2,1,0:T(8,128)(2,1)S(1)} %collective-permute-done.6.down, bf16[4,96,256]{2,1,0:T(8,128)(2,1)S(1)} %get-tuple-element.65.own, s32[4,8]{1,0:T(4,128)S(1)} %bitcast.10, ...), custom_call_target="tpu_custom_call" | custom-call | flops 200000000 | bytes 5175424 | tf_op jit(solution)/shard_map/backward_chain/pallas_call | solution.py:409
  57.1 0.0 copy-start.3
  57.1 0.9 %copy-done.3 = f32[4,192,256]{2,1,0:T(8,128)} copy-done((f32[4,192,256]{2,1,0:T(8,128)}, f32[4,192,256]{2,1,0:T(8,128)S(1)}, u32[]{:S(2)}) %copy-start.3) | copy-done | bytes 786456
  58.0 6.7 %all_to_all.10.message = bf16[4,48,256]{2,1,0:T(8,128)(2,1)S(1)} all-to-all(bf16[4,48,256]{2,1,0:T(8,128)(2,1)S(1)} %get-tuple-element.67), channel_id=1, replica_groups=mesh['sweep'=4,'cross'=8] {'sweep'}, dimensions={0} | all-to-all | bytes 196608 | tf_op jit(solution)/shard_map/all_to_all | solution.py:518
  64.7 0.0 copy-done.7
  64.7 4.0 %backward_finish.1 = bf16[4,8,32,135]{3,2,1,0:T(8,128)(2,1)} custom-call(bf16[4,48,256]{2,1,0:T(8,128)(2,1)S(1)} %all_to_all.10.message, bf16[2,48,256]{2,1,0:T(8,128)(2,1)S(1)} %collective-permute-done.7.near, bf16[2,48,256]{2,1,0:T(8,128)(2,1)S(1)} %collective-permute-done.8.next_near, f32[4,192,256]{2,1,0:T(8,128)} %copy-done.3, ...), custom_call_target="tpu_custom_call" | custom-call | flops 200000000 | bytes 2084832 | tf_op jit(solution)/shard_map/backward_finish/pallas_call | solution.py:409
Async XLA Ops:
  0.0 1.0 %copy-start.10 = (bf16[4,8,32,135]{3,2,1,0:T(8,128)(2,1)S(1)}, bf16[4,8,32,135]{3,2,1,0:T(8,128)(2,1)}, u32[]{:S(2)}) copy-start(bf16[4,8,32,135]{3,2,1,0:T(8,128)(2,1)} %initial.2) | copy-start | bytes 829444
  1.6 20.4 %collective-permute-start = (bf16[4,80,256]{2,1,0:T(8,128)(2,1)S(1)}, bf16[4,80,256]{2,1,0:T(8,128)(2,1)S(1)}, u32[]{:S(2)}, u32[]{:S(2)}) collective-permute-start(bf16[4,80,256]{2,1,0:T(8,128)(2,1)S(1)} %get-tuple-element.41), channel_id=1, source_target_pairs={{0,1},{1,2},{2,3},{3,4},{4,5},{5,6},{6,7},{7,0},{8,9},{9,10},{10,1... | collective-permute-start | bytes 491528 | tf_op jit(solution)/shard_map/ppermute | solution.py:449
  4.6 17.4 %collective-permute-start.1 = (bf16[4,80,256]{2,1,0:T(8,128)(2,1)S(1)}, bf16[4,80,256]{2,1,0:T(8,128)(2,1)S(1)}, u32[]{:S(2)}, u32[]{:S(2)}) collective-permute-start(bf16[4,80,256]{2,1,0:T(8,128)(2,1)S(1)} %get-tuple-element.42), channel_id=1, source_target_pairs={{0,7},{1,0},{2,1},{3,2},{4,3},{5,4},{6,5},{7,6},{8,15},{9,8},{10,9... | collective-permute-start | bytes 491528 | tf_op jit(solution)/shard_map/ppermute | solution.py:449
  7.7 14.3 %collective-permute-start.2 = (bf16[48,256]{1,0:T(8,128)(2,1)S(1)}, bf16[48,256]{1,0:T(8,128)(2,1)S(1)}, u32[]{:S(2)}, u32[]{:S(2)}) collective-permute-start(bf16[48,256]{1,0:T(8,128)(2,1)S(1)} %get-tuple-element.43), channel_id=1, source_target_pairs={{8,0},{16,8},{24,16},{9,1},{17,9},{25,17},{10,2},{18,10},{26,18},{... | collective-permute-start | bytes 73736 | tf_op jit(solution)/shard_map/ppermute | solution.py:454
  9.0 0.7 copy-start.8
  9.6 13.7 %copy-start.4 = (bf16[96,80]{1,0:T(8,128)(2,1)S(1)}, bf16[96,80]{1,0:T(8,128)(2,1)}, u32[]{:S(2)}) copy-start(bf16[96,80]{1,0:T(8,128)(2,1)} %constant.13.clone.up_sel) | copy-start | bytes 46084
  9.7 13.7 %copy-start.5 = (bf16[96,80]{1,0:T(8,128)(2,1)S(1)}, bf16[96,80]{1,0:T(8,128)(2,1)}, u32[]{:S(2)}) copy-start(bf16[96,80]{1,0:T(8,128)(2,1)} %constant.14.clone.down_sel) | copy-start | bytes 46084
  21.2 5.3 %copy-start.1 = (bf16[4,2,192,256]{3,2,1,0:T(8,128)(2,1)}, bf16[4,2,192,256]{3,2,1,0:T(8,128)(2,1)S(1)}, u32[]{:S(2)}) copy-start(bf16[4,2,192,256]{3,2,1,0:T(8,128)(2,1)S(1)} %get-tuple-element.45.lower.lower_there) | copy-start | bytes 2359300
  21.3 5.3 %copy-start.12 = (f32[4,144,256]{2,1,0:T(8,128)}, f32[4,144,256]{2,1,0:T(8,128)S(1)}, u32[]{:S(2)}) copy-start(f32[4,144,256]{2,1,0:T(8,128)S(1)} %get-tuple-element.60.base) | copy-start | bytes 1769476
  21.3 33.3 %copy-start = (bf16[4,2,192,256]{3,2,1,0:T(8,128)(2,1)}, bf16[4,2,192,256]{3,2,1,0:T(8,128)(2,1)S(1)}, u32[]{:S(2)}) copy-start(bf16[4,2,192,256]{3,2,1,0:T(8,128)(2,1)S(1)} %get-tuple-element.51.upper.upper_there) | copy-start | bytes 2359300
  22.0 11.7 %collective-permute-start.3 = (bf16[2,48,256]{2,1,0:T(8,128)(2,1)}, bf16[2,48,256]{2,1,0:T(8,128)(2,1)S(1)}, u32[]{:S(2)}, u32[]{:S(2)}) collective-permute-start(bf16[2,48,256]{2,1,0:T(8,128)(2,1)} %slice_bitcast_fusion.1), channel_id=1, source_target_pairs={{8,16},{16,24},{9,17},{17,25},{10,18},{18,26},{11,19},{19,27},{12,... | collective-permute-start | bytes 147464 | tf_op jit(solution)/shard_map/ppermute | solution.py:425
  22.6 11.0 %collective-permute-start.4 = (bf16[2,48,256]{2,1,0:T(8,128)(2,1)}, bf16[2,48,256]{2,1,0:T(8,128)(2,1)S(1)}, u32[]{:S(2)}, u32[]{:S(2)}) collective-permute-start(bf16[2,48,256]{2,1,0:T(8,128)(2,1)} %slice_bitcast_fusion.1), channel_id=1, source_target_pairs={{8,24},{9,25},{10,26},{11,27},{12,28},{13,29},{14,30},{15,31}} | collective-permute-start | bytes 147464 | tf_op jit(solution)/shard_map/ppermute | solution.py:425
  23.3 14.0 %copy-start.6 = (bf16[160,144]{1,0:T(8,128)(2,1)S(1)}, bf16[160,144]{1,0:T(8,128)(2,1)}, u32[]{:S(2)}) copy-start(bf16[160,144]{1,0:T(8,128)(2,1)} %constant.10.clone.send) | copy-start | bytes 138244
  23.3 21.4 %copy-start.9 = (s32[8,4]{0,1:T(4,128)S(1)}, s32[8,4]{0,1:T(4,128)}, u32[]{:S(2)}) copy-start(s32[8,4]{0,1:T(4,128)} %param.14) | copy-start | bytes 388
  23.4 21.4 %copy-start.11 = (bf16[96,144]{1,0:T(8,128)(2,1)S(1)}, bf16[96,144]{1,0:T(8,128)(2,1)}, u32[]{:S(2)}) copy-start(bf16[96,144]{1,0:T(8,128)(2,1)} %constant.11.clone.own_sel) | copy-start | bytes 82948
  26.5 0.9 %copy-start.2 = (f32[4,192,256]{2,1,0:T(8,128)}, f32[4,192,256]{2,1,0:T(8,128)S(1)}, u32[]{:S(2)}) copy-start(f32[4,192,256]{2,1,0:T(8,128)S(1)} %get-tuple-element.55.state_there) | copy-start | bytes 2359300
  27.5 9.9 %all-to-all-start = ((bf16[4,48,256]{2,1,0:T(8,128)(2,1)}), bf16[4,48,256]{2,1,0:T(8,128)(2,1)S(1)}, u32[]{:S(2)}, u32[]{:S(2)}) async-start(bf16[4,48,256]{2,1,0:T(8,128)(2,1)} %get-tuple-element.53), calls=%async_computation | async-start | bytes 196608 | tf_op jit(solution)/shard_map/all_to_all | solution.py:492
  40.0 14.5 %collective-permute-start.5 = (bf16[4,80,256]{2,1,0:T(8,128)(2,1)S(1)}, bf16[4,80,256]{2,1,0:T(8,128)(2,1)S(1)}, u32[]{:S(2)}, u32[]{:S(2)}) collective-permute-start(bf16[4,80,256]{2,1,0:T(8,128)(2,1)S(1)} %get-tuple-element.56), channel_id=1, source_target_pairs={{0,1},{1,2},{2,3},{3,4},{4,5},{5,6},{6,7},{7,0},{8,9},{9,10},{10,1... | collective-permute-start | bytes 491528 | tf_op jit(solution)/shard_map/ppermute | solution.py:449
  40.1 14.5 %collective-permute-start.6 = (bf16[4,80,256]{2,1,0:T(8,128)(2,1)S(1)}, bf16[4,80,256]{2,1,0:T(8,128)(2,1)S(1)}, u32[]{:S(2)}, u32[]{:S(2)}) collective-permute-start(bf16[4,80,256]{2,1,0:T(8,128)(2,1)S(1)} %get-tuple-element.57), channel_id=1, source_target_pairs={{0,7},{1,0},{2,1},{3,2},{4,3},{5,4},{6,5},{7,6},{8,15},{9,8},{10,9... | collective-permute-start | bytes 491528 | tf_op jit(solution)/shard_map/ppermute | solution.py:449
  44.8 1.1 %copy-start.13 = (f32[4,144,256]{2,1,0:T(8,128)S(1)}, f32[4,144,256]{2,1,0:T(8,128)}, u32[]{:S(2)}) copy-start(f32[4,144,256]{2,1,0:T(8,128)} %copy-done.12) | copy-start | bytes 1769476
  45.9 1.3 %copy-start.14 = (bf16[2,48,256]{2,1,0:T(8,128)(2,1)S(1)}, bf16[2,48,256]{2,1,0:T(8,128)(2,1)}, u32[]{:S(2)}) copy-start(bf16[2,48,256]{2,1,0:T(8,128)(2,1)} %slice_bitcast_fusion) | copy-start | bytes 147460
  47.1 17.6 %copy-start.7 = (bf16[135,144]{1,0:T(8,128)(2,1)S(1)}, bf16[135,144]{1,0:T(8,128)(2,1)}, u32[]{:S(2)}) copy-start(bf16[135,144]{1,0:T(8,128)(2,1)} %constant.12.clone.back) | copy-start | bytes 116644
  47.1 3.3 %collective-permute-start.7 = (bf16[2,48,256]{2,1,0:T(8,128)(2,1)S(1)}, bf16[2,48,256]{2,1,0:T(8,128)(2,1)S(1)}, u32[]{:S(2)}, u32[]{:S(2)}) collective-permute-start(bf16[2,48,256]{2,1,0:T(8,128)(2,1)S(1)} %copy-done.14), channel_id=1, source_target_pairs={{8,0},{16,8},{9,1},{17,9},{10,2},{18,10},{11,3},{19,11},{12,4},{20... | collective-permute-start | bytes 147464 | tf_op jit(solution)/shard_map/ppermute | solution.py:425
  48.6 6.0 %collective-permute-start.8 = (bf16[2,48,256]{2,1,0:T(8,128)(2,1)S(1)}, bf16[2,48,256]{2,1,0:T(8,128)(2,1)S(1)}, u32[]{:S(2)}, u32[]{:S(2)}) collective-permute-start(bf16[2,48,256]{2,1,0:T(8,128)(2,1)S(1)} %copy-done.14), channel_id=1, source_target_pairs={{16,0},{17,1},{18,2},{19,3},{20,4},{21,5},{22,6},{23,7}} | collective-permute-start | bytes 147464 | tf_op jit(solution)/shard_map/ppermute | solution.py:425
  57.1 0.9 %copy-start.3 = (f32[4,192,256]{2,1,0:T(8,128)}, f32[4,192,256]{2,1,0:T(8,128)S(1)}, u32[]{:S(2)}) copy-start(f32[4,192,256]{2,1,0:T(8,128)S(1)} %get-tuple-element.70.state_there) | copy-start | bytes 2359300

commit v5 on v4

--- a/solution.py
+++ b/solution.py
@@ -276,7 +276,7 @@
 
 def chain_kernel(known, base, matrix, received, own, neighbours, outs, order, rows, rhs, extra=None):
     up, down, up_sel, down_sel = received
-    state, message = outs
+    operand, start, traces, message = outs
     planes, columns = known.shape[:2]
     size = columns * rhs
     source = sources(neighbours, columns, rhs)
@@ -287,15 +287,27 @@
         parts = gathered(up, down, own, p, up_sel[...], down_sel[...], low_pick, high_pick)
         parts.append(jnp.zeros((256 - 4 * FACE, size), BF))
         whole = jnp.concatenate(parts, 0)
-        start = base[p] + known_part(lambda c: known[p, c], whole, columns, rhs)
+        operand[p] = whole
+        value = base[p, rows] + known_part(lambda c: known[p, c, rows], whole, columns, rhs)
         if extra is not None and p == planes - 1:
-            start = start + chain_step(extra[0].at[p], extra[1][...], rhs, FULL)
-        state[p, FULL] = start
-        start = start[rows]
-        trace = start if trace is None else start + chain_step(matrix.at[p], trace, rhs, rows)
-        state[p, PRODUCT] = trace
-    for i in range(message.shape[0]):
-        message[i] = trace.astype(BF)
+            value = value + chain_step(extra[0].at[p], extra[1][...], rhs, rows)
+        start[p] = value
+        trace = value if trace is None else value + chain_step(matrix.at[p], trace, rhs, rows)
+        traces[p] = trace
+    message[FIRST] = trace.astype(BF)
+    if message.shape[0] > FACE:
+        for h in range(2):
+            message[(1 + h) * FACE : (2 + h) * FACE] = matrix[order[-1], h, PRODUCT]
+
+
+def base_kernel(known, operand, base, *rest, rows, rhs):
+    planes, columns = known.shape[:2]
+    out = rest[-1]
+    for p in range(planes):
+        value = base[p, rows] + known_part(lambda c: known[p, c, rows], operand[p], columns, rhs)
+        if len(rest) > 1 and p == planes - 1:
+            value = value + chain_step(rest[1].at[p], rest[0][...], rhs, rows)
+        out[p] = value
 
 
 def forward_chain_kernel(
@@ -313,50 +325,36 @@
     )
 
 
-def incoming(message, near, next_near, forward, rhs):
-    here = lax.axis_index("sweep")
-    n = message.shape[0]
-    trace = None
-    for i in range(n - 1) if forward else range(n - 1, 0, -1):
-        value = message[i].astype(F32)
-        if trace is None:
-            trace = jnp.zeros_like(value)
-        else:
-            step = here - 1 if forward else here + 1
-            product = [jnp.where(step == i, near[h], next_near[h]) for h in range(2)]
-            half = value.shape[1] // 2
-            halves = [trace[:, h * half : (h + 1) * half] for h in range(2)]
-            value = value + jnp.concatenate([mm(m, split_lanes(t, rhs)) for m, t in zip(product, halves)], 1)
-        trace = jnp.where(i < here if forward else i > here, value, trace)
-    return trace
-
-
-def copied(source, target, sem):
-    copies = [pltpu.make_async_copy(x, y, sem.at[i]) for i, (x, y) in enumerate(zip(source, target))]
-    for copy in copies:
-        copy.start()
-    return copies
+def incoming(one, two, three, near, next_near, rhs):
+    def carried(product, trace):
+        half = trace.shape[1] // 2
+        halves = [trace[:, h * half : (h + 1) * half] for h in range(2)]
+        return jnp.concatenate([mm(m, split_lanes(t, rhs)) for m, t in zip(product, halves)], 1)
+
+    trace = two[FIRST].astype(F32) + carried(next_near, three[FIRST])
+    return one[FIRST].astype(F32) + carried(near, trace)
+
+
+def inside(message):
+    return [message[(1 + h) * FACE : (2 + h) * FACE] for h in range(2)]
 
 
 def forward_finish_kernel(
-    message, near, next_near, state_there, lower_there, send, middle, change, up, down, state, lower, sem, *, rhs
+    one, two, three, start, rest, traces, lower, send, middle, change, up, down, *, rhs
 ):
-    planes = state.shape[0]
-    copies = copied((state_there, lower_there), (state, lower), sem)
-    entry = incoming(message, near, next_near, True, rhs)
-    for copy in copies:
-        copy.wait()
+    planes = start.shape[0]
+    entry = incoming(one, two, three, inside(one), inside(two), rhs)
     trace = entry
     for p in range(planes):
         delta = chain_step(lower.at[p], trace, rhs, FULL)
         change[p] = delta
-        whole = (state[p, FULL] + delta).astype(BF)
+        whole = (jnp.concatenate([rest[p], start[p]], 0) + delta).astype(BF)
         middle[p] = whole
         out = mm(send[...], whole).astype(BF)
         up[p] = out[:SHARED]
         down[p] = out[SHARED:]
         if p + 1 < planes:
-            trace = state[p, PRODUCT] + chain_step(lower.at[p], entry, rhs, PRODUCT)
+            trace = traces[p] + chain_step(lower.at[p], entry, rhs, PRODUCT)
 
 
 def middle_kernel(middle, change, base, neighbours, own_sel, own, out):
@@ -373,25 +371,22 @@
 
 
 def backward_finish_kernel(
-    message, near, next_near, state_there, upper_there, back, result, state, upper, sem, *, rhs
+    one, two, three, near, next_near, start, rest, traces, upper, back, result, *, rhs
 ):
-    planes = state.shape[0]
-    copies = copied((state_there, upper_there), (state, upper), sem)
-    entry = incoming(message, near, next_near, False, rhs)
+    planes = start.shape[0]
+    entry = incoming(one, two, three, [near[0], near[1]], [next_near[0], next_near[1]], rhs)
     size = entry.shape[1]
     row = lax.broadcasted_iota(jnp.int32, (size, size), 0)
     column = lax.broadcasted_iota(jnp.int32, (size, size), 1)
     unit = jnp.where(row == column, 1.0, 0.0).astype(BF)
     columns, _, width = result.shape[1:]
-    for copy in copies:
-        copy.wait()
     trace = entry
     for p in range(planes - 1, -1, -1):
-        whole = state[p, FULL] + chain_step(upper.at[p], trace, rhs, FULL)
+        whole = jnp.concatenate([start[p], rest[p]], 0) + chain_step(upper.at[p], trace, rhs, FULL)
         flat = mm(back[...], whole.astype(BF)).astype(BF)
         result[p] = mt(unit, flat).astype(BF).reshape(columns, rhs, width)
         if p:
-            trace = state[p, PRODUCT] + chain_step(upper.at[p], entry, rhs, PRODUCT)
+            trace = traces[p] + chain_step(upper.at[p], entry, rhs, PRODUCT)
 
 
 def call(kernel, outs, operands, name, flops=2e8, far=(), scratch=()):
@@ -477,25 +472,29 @@
         inverse_blocks.transpose(0, 2, 1, 3), couplings.transpose(0, 2, 3, 1, 4), right_sides, initial, beside
     )
 
-    pass_f = lower[planes - 1, :, PRODUCT]
-    from_low, from_high, from_above, pass_f = lax.optimization_barrier((from_low, from_high, from_above, pass_f))
-    passes = products(pass_f, 1)
-
     field = (planes, ROWS, size)
-    chain_outs = [((planes, ROWS + FACE, size), F32), ((lax.axis_size("sweep"), FACE, size), BF)]
-    state, message = call(
+    trace = (planes, FACE, size)
+    most = (planes, 2 * FACE, size)
+    chain_outs = [((planes, 256, size), BF), (trace, F32), (trace, F32)]
+    operand, start, traces, message = call(
         functools.partial(forward_chain_kernel, rhs=rhs),
-        chain_outs,
+        chain_outs + [((3 * FACE, size), BF)],
         (from_low, from_high, from_above, own, beside, up_sel, down_sel, known, lower, upper, fore),
         "forward_chain",
     )
-    message = lax.all_to_all(message, "sweep", 0, 0)
+    one, two = (shift(message, "sweep", by) for by in (1, 2))
+    three = shift(message[:FACE], "sweep", 3)
+    (rest,) = call(
+        functools.partial(base_kernel, rows=slice(0, 2 * FACE), rhs=rhs),
+        [(most, F32)],
+        (known, operand, fore, from_above, upper),
+        "forward_base",
+    )
     middle, change, up, down = call(
         functools.partial(forward_finish_kernel, rhs=rhs),
         [(field, BF), (field, F32), (share, BF), (share, BF)],
-        (message, *passes, state, lower, send_in),
+        (one, two, three, start, rest, traces, lower, send_in),
         "forward_finish",
-        far=(3, 4),
     )
     from_low = ring(up, "cross", 1)
     from_high = ring(down, "cross", -1)
@@ -509,19 +508,24 @@
     own, pass_b = lax.optimization_barrier((own, upper[0, :, PRODUCT]))
     passes = products(pass_b, -1)
     from_low, from_high, *passes = lax.optimization_barrier((from_low, from_high, *passes))
-    state, message = call(
+    operand, start, traces, message = call(
         functools.partial(backward_chain_kernel, rhs=rhs),
-        chain_outs,
+        chain_outs + [((FACE, size), BF)],
         (from_low, from_high, own, beside, up_sel, down_sel, known, upper, base),
         "backward_chain",
     )
-    message = lax.all_to_all(message, "sweep", 0, 0)
+    one, two, three = (shift(message, "sweep", -by) for by in (1, 2, 3))
+    (rest,) = call(
+        functools.partial(base_kernel, rows=slice(FACE, ROWS), rhs=rhs),
+        [(most, F32)],
+        (known, operand, base),
+        "backward_base",
+    )
     (result,) = call(
         functools.partial(backward_finish_kernel, rhs=rhs),
         [(right_sides.shape, BF)],
-        (message, *passes, state, upper, back),
+        (one, two, three, *passes, start, rest, traces, upper, back),
         "backward_finish",
-        far=(3, 4),
     )
     return result
 

time: 69.2 us -> 62 us (0.90)
  blocking collectives: 6.66 us -> 0 us
  starting transfers between devices: 21.8 us -> 26.3 us
  local copies, waits for them, and re-layouts: 5.97 us -> 1.76 us
  Pallas kernels: 25.7 us -> 23.8 us
  waiting for transfers between devices: 8.37 us -> 9.56 us
    ppermute x1 -> x7, starting transfers between devices: 1.28 us -> 12.8 us  [shift(): lax.ppermute(x, axis, [(i, i + by) for i in range(n) if 0 <= i + by < n])]
    all_to_all x1 -> x0, blocking collectives: 6.66 us -> none  [local(): message = lax.all_to_all(message, 'sweep', 0, 0)]
    all_to_all x1 -> x0, starting transfers between devices: 5.56 us -> none  [local(): message = lax.all_to_all(message, 'sweep', 0, 0)]
    ppermute x1 -> x7, waiting for transfers between devices: 0.01 us -> 4.87 us  [shift(): lax.ppermute(x, axis, [(i, i + by) for i in range(n) if 0 <= i + by < n])]
    all_to_all x1 -> x0, waiting for transfers between devices: 3.67 us -> none  [local(): message = lax.all_to_all(message, 'sweep', 0, 0)]
    unnamed x30 -> x14, local copies, waits for them, and re-layouts: 4.67 us -> 1.75 us
    pallas_call x7 -> x9, Pallas kernels: 25.7 us -> 23.8 us  [call(): pl.pallas_call(kernel, out_shape=shapes, in_specs=[pl.BlockSpec(memory_sp...]
    ppermute x4 -> x2, starting transfers between devices: 4.04 us -> 2.58 us  [products(): lax.ppermute(x, 'sweep', [(i, i + step) for i in inner if 0 <= i + step <...]
  transfers between devices with their start and end apart: 10 -> 13, of which waited for: 3 -> 5; matrix products, arithmetic and copies ran while one was open for 2% -> 0% of each run, Pallas kernels for 23% -> 23%
where the time goes in v5:
time: 62 us; the launch traced here: 61.6 us
  starting transfers between devices  26.3 us (42%)
  Pallas kernels  23.8 us (38%)
  waiting for transfers between devices  9.56 us (15%)
  local copies, waits for them, and re-layouts  1.76 us (3%)
    pallas_call x9, Pallas kernels, call(): pl.pallas_call(kernel, out_shape=shapes, in_specs=[pl.BlockSpec(memory_sp...  23.8 us
    ppermute x7, starting transfers between devices, shift(): lax.ppermute(x, axis, [(i, i + by) for i in range(n) if 0 <= i + by < n])  12.8 us
    ppermute x4, starting transfers between devices, ring(): return lax.ppermute(x, axis, [(i, (i + by) % n) for i in range(n)])  10.9 us
    ppermute x7, waiting for transfers between devices, shift(): lax.ppermute(x, axis, [(i, i + by) for i in range(n) if 0 <= i + by < n])  4.87 us
    ppermute x2, waiting for transfers between devices, products(): lax.ppermute(x, 'sweep', [(i, i + step) for i in inner if 0 <= i + step <...  4.68 us
    ppermute x2, starting transfers between devices, products(): lax.ppermute(x, 'sweep', [(i, i + step) for i in inner if 0 <= i + step <...  2.58 us
    unnamed x14, local copies, waits for them, and re-layouts  1.75 us
  transfers between devices with their start and end apart: 13, of which 5 were waited for; matrix products, arithmetic and copies ran while one was open for 0% of the time, Pallas kernels for 23%

profile of v5, /device:TPU:0, one launch (start us, length us, event | category | flops | bytes accessed | tf_op | source)
XLA Modules:
  0.0 61.6 jit_solution(4962463031139983246)
XLA Ops:
  0.0 0.0 copy-start.5
  0.0 1.0 %copy-done.5 = bf16[4,8,32,135]{3,2,1,0:T(8,128)(2,1)S(1)} copy-done((bf16[4,8,32,135]{3,2,1,0:T(8,128)(2,1)S(1)}, bf16[4,8,32,135]{3,2,1,0:T(8,128)(2,1)}, u32[]{:S(2)}) %copy-start.5) | copy-done | bytes 276504
  1.0 0.5 initial_traces.1
  1.6 1.3 %collective-permute-start.2 = (bf16[48,256]{1,0:T(8,128)(2,1)S(1)}, bf16[48,256]{1,0:T(8,128)(2,1)S(1)}, u32[]{:S(2)}, u32[]{:S(2)}) collective-permute-start(bf16[48,256]{1,0:T(8,128)(2,1)S(1)} %get-tuple-element.43), channel_id=1, source_target_pairs={{8,0},{16,8},{24,16},{9,1},{17,9},{25,17},{10,2},{18,10},{26,18},{... | collective-permute-start | bytes 73736 | tf_op jit(solution)/shard_map/ppermute | solution.py:449
  2.9 3.0 %collective-permute-start = (bf16[4,80,256]{2,1,0:T(8,128)(2,1)S(1)}, bf16[4,80,256]{2,1,0:T(8,128)(2,1)S(1)}, u32[]{:S(2)}, u32[]{:S(2)}) collective-permute-start(bf16[4,80,256]{2,1,0:T(8,128)(2,1)S(1)} %get-tuple-element.41), channel_id=1, source_target_pairs={{0,1},{1,2},{2,3},{3,4},{4,5},{5,6},{6,7},{7,0},{8,9},{9,10},{10,1... | collective-permute-start | bytes 491528 | tf_op jit(solution)/shard_map/ppermute | solution.py:444
  5.9 3.1 %collective-permute-start.1 = (bf16[4,80,256]{2,1,0:T(8,128)(2,1)S(1)}, bf16[4,80,256]{2,1,0:T(8,128)(2,1)S(1)}, u32[]{:S(2)}, u32[]{:S(2)}) collective-permute-start(bf16[4,80,256]{2,1,0:T(8,128)(2,1)S(1)} %get-tuple-element.42), channel_id=1, source_target_pairs={{0,7},{1,0},{2,1},{3,2},{4,3},{5,4},{6,5},{7,6},{8,15},{9,8},{10,9... | collective-permute-start | bytes 491528 | tf_op jit(solution)/shard_map/ppermute | solution.py:444
  9.0 0.0 copy-start.4
  9.0 0.7 %copy-done.4 = s32[8,4]{0,1:T(4,128)S(1)} copy-done((s32[8,4]{0,1:T(4,128)S(1)}, s32[8,4]{0,1:T(4,128)}, u32[]{:S(2)}) %copy-start.4) | copy-done | bytes 152
  9.7 0.0 copy-start
  9.7 0.0 copy-start.1
  9.7 11.6 %weights.1 = (bf16[4,8,144,256]{3,2,1,0:T(8,128)(2,1)S(1)}, bf16[4,2,192,256]{3,2,1,0:T(8,128)(2,1)S(1)}, bf16[4,2,192,256]{3,2,1,0:T(8,128)(2,1)S(1)}, f32[4,14...) custom-call(bf16[4,135,8,135]{3,2,1,0:T(8,128)(2,1)} %bitcast.10, ...), custom_call_target="tpu_custom_call" | custom-call | flops 10000000000 | bytes 9360704 | tf_op jit(solution)/shard_map/weights/pallas_call | solution.py:404
  21.3 0.0 collective-permute-done.2.above.rest_0_
  21.3 0.0 collective-permute-done.up
  21.3 0.0 collective-permute-done.1.down
  21.3 0.0 copy-done
  21.3 0.0 copy-done.1
  21.3 2.4 %forward_chain.1 = (bf16[4,256,256]{2,1,0:T(8,128)(2,1)S(1)}, f32[4,48,256]{2,1,0:T(8,128)S(1)}, f32[4,48,256]{2,1,0:T(8,128)S(1)}, bf16[144,256]{1,0:T(8,128)(2,1)S(1)}) custom-call(bf16[4,80,256]{2,1,0:T(8,128)(2,1)S(1)} %collective-permute-done.up, bf16[4,80,256]{2,1,0:T(8,128)(2,1)S(1)} %collective-permute-done.1.down, ...), custom_call_target="tpu_custom_call" | custom-call | flops 200000000 | bytes 6092928 | tf_op jit(solution)/shard_map/forward_chain/pallas_call | solution.py:404
  23.8 2.8 %collective-permute-start.3 = (bf16[144,256]{1,0:T(8,128)(2,1)S(1)}, bf16[144,256]{1,0:T(8,128)(2,1)S(1)}, u32[]{:S(2)}, u32[]{:S(2)}) collective-permute-start(bf16[144,256]{1,0:T(8,128)(2,1)S(1)} %get-tuple-element.50), channel_id=1, source_target_pairs={{0,8},{8,16},{16,24},{1,9},{9,17},{17,25},{2,10},{10,18},{18,26},{... | collective-permute-start | bytes 221192 | tf_op jit(solution)/shard_map/ppermute | solution.py:449
  26.5 3.4 %collective-permute-start.4 = (bf16[144,256]{1,0:T(8,128)(2,1)S(1)}, bf16[144,256]{1,0:T(8,128)(2,1)S(1)}, u32[]{:S(2)}, u32[]{:S(2)}) collective-permute-start(bf16[144,256]{1,0:T(8,128)(2,1)S(1)} %get-tuple-element.50), channel_id=1, source_target_pairs={{0,16},{8,24},{1,17},{9,25},{2,18},{10,26},{3,19},{11,27},{4,20},{... | collective-permute-start | bytes 221192 | tf_op jit(solution)/shard_map/ppermute | solution.py:449
  30.0 1.3 %collective-permute-start.5 = (bf16[48,256]{1,0:T(8,128)(2,1)S(1)}, bf16[48,256]{1,0:T(8,128)(2,1)S(1)}, u32[]{:S(2)}, u32[]{:S(2)}) collective-permute-start(bf16[48,256]{1,0:T(8,128)(2,1)S(1)} %slice.6), channel_id=1, source_target_pairs={{0,24},{1,25},{2,26},{3,27},{4,28},{5,29},{6,30},{7,31}} | collective-permute-start | bytes 73736 | tf_op jit(solution)/shard_map/ppermute | solution.py:449
  31.3 0.0 copy-start.2
  31.3 0.0 copy-start.6
  31.3 0.6 forward_base.1.rest
  31.9 0.9 %collective-permute-done.5.three = bf16[48,256]{1,0:T(8,128)(2,1)S(1)} collective-permute-done((bf16[48,256]{1,0:T(8,128)(2,1)S(1)}, bf16[48,256]{1,0:T(8,128)(2,1)S(1)}, u32[]{:S(2)}, u32[]{:S(2)}) %collective-permute-start.5) | collective-permute-done | bytes 24608 | tf_op jit(solution)/shard_map/ppermute | solution.py:449
  32.8 0.0 collective-permute-done.3.one
  32.8 0.0 collective-permute-done.4.two
  32.8 0.0 copy-done.2
  32.8 1.6 %forward_finish.1 = (bf16[4,144,256]{2,1,0:T(8,128)(2,1)S(1)}, f32[4,144,256]{2,1,0:T(8,128)S(1)}, bf16[4,80,256]{2,1,0:T(8,128)(2,1)S(1)}, bf16[4,80,256]{2,1,0:T(8,128)(2,1)S(1)}) custom-call(bf16[144,256]{1,0:T(8,128)(2,1)S(1)} %collective-permute-done.3.one, bf16[144,256]{1,0:T(8,128)(2,1)S(1)} %collective-permute-done.4.two, ...), custom_call_target="tpu_custom_call" | custom-call | flops 200000000 | bytes 3003392 | tf_op jit(solution)/shard_map/forward_finish/pallas_call | solution.py:404
  34.4 0.1 collective-permute-start.6
  34.5 4.7 %collective-permute-start.7 = (bf16[4,80,256]{2,1,0:T(8,128)(2,1)S(1)}, bf16[4,80,256]{2,1,0:T(8,128)(2,1)S(1)}, u32[]{:S(2)}, u32[]{:S(2)}) collective-permute-start(bf16[4,80,256]{2,1,0:T(8,128)(2,1)S(1)} %get-tuple-element.55), channel_id=1, source_target_pairs={{0,7},{1,0},{2,1},{3,2},{4,3},{5,4},{6,5},{7,6},{8,15},{9,8},{10,9... | collective-permute-start | bytes 491528 | tf_op jit(solution)/shard_map/ppermute | solution.py:444
  39.2 0.0 copy-done.6
  39.2 1.2 %middle.1 = (bf16[4,96,256]{2,1,0:T(8,128)(2,1)S(1)}, f32[4,144,256]{2,1,0:T(8,128)S(1)}) custom-call(bf16[4,144,256]{2,1,0:T(8,128)(2,1)S(1)} %get-tuple-element.56.middle, f32[4,144,256]{2,1,0:T(8,128)S(1)} %get-tuple-element.57.change, f32[4,144,256]{2,1,0:T(8,128)S(1)} %get-tuple-element.58.base, s32[4,8]{1,0:T(4,128)S(1)} %bitcast.7, ...), custom_call_target="tpu_custom_call" | custom-call | flops 2000000000 | bytes 2288768 | tf_op jit(solution)/shard_map/middle/pallas_call | solution.py:404
  40.4 1.3 %collective-permute-start.8 = (bf16[2,48,256]{2,1,0:T(8,128)(2,1)S(1)}, bf16[2,48,256]{2,1,0:T(8,128)(2,1)S(1)}, u32[]{:S(2)}, u32[]{:S(2)}) collective-permute-start(bf16[2,48,256]{2,1,0:T(8,128)(2,1)S(1)} %slice_bitcast_fusion), channel_id=1, source_target_pairs={{8,0},{16,8},{9,1},{17,9},{10,2},{18,10},{11,3},{19,11},{12,4},{20... | collective-permute-start | bytes 147464 | tf_op jit(solution)/shard_map/ppermute | solution.py:420
  41.7 1.3 %collective-permute-start.9 = (bf16[2,48,256]{2,1,0:T(8,128)(2,1)S(1)}, bf16[2,48,256]{2,1,0:T(8,128)(2,1)S(1)}, u32[]{:S(2)}, u32[]{:S(2)}) collective-permute-start(bf16[2,48,256]{2,1,0:T(8,128)(2,1)S(1)} %slice_bitcast_fusion), channel_id=1, source_target_pairs={{16,0},{17,1},{18,2},{19,3},{20,4},{21,5},{22,6},{23,7}} | collective-permute-start | bytes 147464 | tf_op jit(solution)/shard_map/ppermute | solution.py:420
  43.0 0.5 collective-permute-done.8.near
  43.5 4.2 %collective-permute-done.9.next_near = bf16[2,48,256]{2,1,0:T(8,128)(2,1)S(1)} collective-permute-done((bf16[2,48,256]{2,1,0:T(8,128)(2,1)S(1)}, bf16[2,48,256]{2,1,0:T(8,128)(2,1)S(1)}, u32[]{:S(2)}, u32[]{:S(2)}) %collective-permute-start.9) | collective-permute-done | bytes 49184 | tf_op jit(solution)/shard_map/ppermute | solution.py:420
  47.7 0.0 collective-permute-done.6.up
  47.7 0.0 collective-permute-done.7.down
  47.7 2.4 %backward_chain.1 = (bf16[4,256,256]{2,1,0:T(8,128)(2,1)S(1)}, f32[4,48,256]{2,1,0:T(8,128)S(1)}, f32[4,48,256]{2,1,0:T(8,128)S(1)}, bf16[48,256]{1,0:T(8,128)(2,1)S(1)}) custom-call(bf16[4,80,256]{2,1,0:T(8,128)(2,1)S(1)} %collective-permute-done.6.up, bf16[4,80,256]{2,1,0:T(8,128)(2,1)S(1)} %collective-permute-done.7.down, ...), custom_call_target="tpu_custom_call" | custom-call | flops 200000000 | bytes 5232768 | tf_op jit(solution)/shard_map/backward_chain/pallas_call | solution.py:404
  50.1 0.0 copy-start.3
  50.1 1.4 %collective-permute-start.10 = (bf16[48,256]{1,0:T(8,128)(2,1)S(1)}, bf16[48,256]{1,0:T(8,128)(2,1)S(1)}, u32[]{:S(2)}, u32[]{:S(2)}) collective-permute-start(bf16[48,256]{1,0:T(8,128)(2,1)S(1)} %get-tuple-element.65), channel_id=1, source_target_pairs={{8,0},{16,8},{24,16},{9,1},{17,9},{25,17},{10,2},{18,10},{26,18},{... | collective-permute-start | bytes 73736 | tf_op jit(solution)/shard_map/ppermute | solution.py:449
  51.5 1.3 %collective-permute-start.11 = (bf16[48,256]{1,0:T(8,128)(2,1)S(1)}, bf16[48,256]{1,0:T(8,128)(2,1)S(1)}, u32[]{:S(2)}, u32[]{:S(2)}) collective-permute-start(bf16[48,256]{1,0:T(8,128)(2,1)S(1)} %get-tuple-element.65), channel_id=1, source_target_pairs={{16,0},{24,8},{17,1},{25,9},{18,2},{26,10},{19,3},{27,11},{20,4},{... | collective-permute-start | bytes 73736 | tf_op jit(solution)/shard_map/ppermute | solution.py:449
  52.8 1.3 %collective-permute-start.12 = (bf16[48,256]{1,0:T(8,128)(2,1)S(1)}, bf16[48,256]{1,0:T(8,128)(2,1)S(1)}, u32[]{:S(2)}, u32[]{:S(2)}) collective-permute-start(bf16[48,256]{1,0:T(8,128)(2,1)S(1)} %get-tuple-element.65), channel_id=1, source_target_pairs={{24,0},{25,1},{26,2},{27,3},{28,4},{29,5},{30,6},{31,7}} | collective-permute-start | bytes 73736 | tf_op jit(solution)/shard_map/ppermute | solution.py:449
  54.1 0.6 backward_base.1.rest
  54.7 0.0 collective-permute-done.10.one
  54.7 2.6 %collective-permute-done.11.two = bf16[48,256]{1,0:T(8,128)(2,1)S(1)} collective-permute-done((bf16[48,256]{1,0:T(8,128)(2,1)S(1)}, bf16[48,256]{1,0:T(8,128)(2,1)S(1)}, u32[]{:S(2)}, u32[]{:S(2)}) %collective-permute-start.11) | collective-permute-done | bytes 24608 | tf_op jit(solution)/shard_map/ppermute | solution.py:449
  57.4 1.4 %collective-permute-done.12.three = bf16[48,256]{1,0:T(8,128)(2,1)S(1)} collective-permute-done((bf16[48,256]{1,0:T(8,128)(2,1)S(1)}, bf16[48,256]{1,0:T(8,128)(2,1)S(1)}, u32[]{:S(2)}, u32[]{:S(2)}) %collective-permute-start.12) | collective-permute-done | bytes 24608 | tf_op jit(solution)/shard_map/ppermute | solution.py:449
  58.7 0.0 copy-done.3
  58.7 2.9 %backward_finish.1 = bf16[4,8,32,135]{3,2,1,0:T(8,128)(2,1)} custom-call(bf16[48,256]{1,0:T(8,128)(2,1)S(1)} %collective-permute-done.10.one, bf16[48,256]{1,0:T(8,128)(2,1)S(1)} %collective-permute-done.11.two, bf16[48,256]{1,0:T(8,128)(2,1)S(1)} %collective-permute-done.12.three, bf16[2,48,256]{2,1,0:T(8,128)(2,1)S(1)} %collective-permute-done.8.near, ...), custom_call_target="tpu_custom_call" | custom-call | flops 200000000 | bytes 2060256 | tf_op jit(solution)/shard_map/backward_finish/pallas_call | solution.py:404
  (2 shorter events, 0.0 us)
Async XLA Ops:
  0.0 1.0 %copy-start.5 = (bf16[4,8,32,135]{3,2,1,0:T(8,128)(2,1)S(1)}, bf16[4,8,32,135]{3,2,1,0:T(8,128)(2,1)}, u32[]{:S(2)}) copy-start(bf16[4,8,32,135]{3,2,1,0:T(8,128)(2,1)} %initial.2) | copy-start | bytes 829444
  1.6 19.7 %collective-permute-start.2 = (bf16[48,256]{1,0:T(8,128)(2,1)S(1)}, bf16[48,256]{1,0:T(8,128)(2,1)S(1)}, u32[]{:S(2)}, u32[]{:S(2)}) collective-permute-start(bf16[48,256]{1,0:T(8,128)(2,1)S(1)} %get-tuple-element.43), channel_id=1, source_target_pairs={{8,0},{16,8},{24,16},{9,1},{17,9},{25,17},{10,2},{18,10},{26,18},{... | collective-permute-start | bytes 73736 | tf_op jit(solution)/shard_map/ppermute | solution.py:449
  2.9 18.4 %collective-permute-start = (bf16[4,80,256]{2,1,0:T(8,128)(2,1)S(1)}, bf16[4,80,256]{2,1,0:T(8,128)(2,1)S(1)}, u32[]{:S(2)}, u32[]{:S(2)}) collective-permute-start(bf16[4,80,256]{2,1,0:T(8,128)(2,1)S(1)} %get-tuple-element.41), channel_id=1, source_target_pairs={{0,1},{1,2},{2,3},{3,4},{4,5},{5,6},{6,7},{7,0},{8,9},{9,10},{10,1... | collective-permute-start | bytes 491528 | tf_op jit(solution)/shard_map/ppermute | solution.py:444
  5.9 15.4 %collective-permute-start.1 = (bf16[4,80,256]{2,1,0:T(8,128)(2,1)S(1)}, bf16[4,80,256]{2,1,0:T(8,128)(2,1)S(1)}, u32[]{:S(2)}, u32[]{:S(2)}) collective-permute-start(bf16[4,80,256]{2,1,0:T(8,128)(2,1)S(1)} %get-tuple-element.42), channel_id=1, source_target_pairs={{0,7},{1,0},{2,1},{3,2},{4,3},{5,4},{6,5},{7,6},{8,15},{9,8},{10,9... | collective-permute-start | bytes 491528 | tf_op jit(solution)/shard_map/ppermute | solution.py:444
  9.0 0.7 %copy-start.4 = (s32[8,4]{0,1:T(4,128)S(1)}, s32[8,4]{0,1:T(4,128)}, u32[]{:S(2)}) copy-start(s32[8,4]{0,1:T(4,128)} %param.14) | copy-start | bytes 388
  9.7 11.6 %copy-start = (bf16[96,80]{1,0:T(8,128)(2,1)S(1)}, bf16[96,80]{1,0:T(8,128)(2,1)}, u32[]{:S(2)}) copy-start(bf16[96,80]{1,0:T(8,128)(2,1)} %constant.13.clone.up_sel) | copy-start | bytes 46084
  9.7 11.6 %copy-start.1 = (bf16[96,80]{1,0:T(8,128)(2,1)S(1)}, bf16[96,80]{1,0:T(8,128)(2,1)}, u32[]{:S(2)}) copy-start(bf16[96,80]{1,0:T(8,128)(2,1)} %constant.14.clone.down_sel) | copy-start | bytes 46084
  23.8 9.0 %collective-permute-start.3 = (bf16[144,256]{1,0:T(8,128)(2,1)S(1)}, bf16[144,256]{1,0:T(8,128)(2,1)S(1)}, u32[]{:S(2)}, u32[]{:S(2)}) collective-permute-start(bf16[144,256]{1,0:T(8,128)(2,1)S(1)} %get-tuple-element.50), channel_id=1, source_target_pairs={{0,8},{8,16},{16,24},{1,9},{9,17},{17,25},{2,10},{10,18},{18,26},{... | collective-permute-start | bytes 221192 | tf_op jit(solution)/shard_map/ppermute | solution.py:449
  26.5 6.3 %collective-permute-start.4 = (bf16[144,256]{1,0:T(8,128)(2,1)S(1)}, bf16[144,256]{1,0:T(8,128)(2,1)S(1)}, u32[]{:S(2)}, u32[]{:S(2)}) collective-permute-start(bf16[144,256]{1,0:T(8,128)(2,1)S(1)} %get-tuple-element.50), channel_id=1, source_target_pairs={{0,16},{8,24},{1,17},{9,25},{2,18},{10,26},{3,19},{11,27},{4,20},{... | collective-permute-start | bytes 221192 | tf_op jit(solution)/shard_map/ppermute | solution.py:449
  30.0 2.8 %collective-permute-start.5 = (bf16[48,256]{1,0:T(8,128)(2,1)S(1)}, bf16[48,256]{1,0:T(8,128)(2,1)S(1)}, u32[]{:S(2)}, u32[]{:S(2)}) collective-permute-start(bf16[48,256]{1,0:T(8,128)(2,1)S(1)} %slice.6), channel_id=1, source_target_pairs={{0,24},{1,25},{2,26},{3,27},{4,28},{5,29},{6,30},{7,31}} | collective-permute-start | bytes 73736 | tf_op jit(solution)/shard_map/ppermute | solution.py:449
  31.3 1.5 %copy-start.2 = (bf16[160,144]{1,0:T(8,128)(2,1)S(1)}, bf16[160,144]{1,0:T(8,128)(2,1)}, u32[]{:S(2)}) copy-start(bf16[160,144]{1,0:T(8,128)(2,1)} %constant.10.clone.send) | copy-start | bytes 138244
  31.3 7.9 %copy-start.6 = (bf16[96,144]{1,0:T(8,128)(2,1)S(1)}, bf16[96,144]{1,0:T(8,128)(2,1)}, u32[]{:S(2)}) copy-start(bf16[96,144]{1,0:T(8,128)(2,1)} %constant.11.clone.own_sel) | copy-start | bytes 82948
  34.4 13.3 %collective-permute-start.6 = (bf16[4,80,256]{2,1,0:T(8,128)(2,1)S(1)}, bf16[4,80,256]{2,1,0:T(8,128)(2,1)S(1)}, u32[]{:S(2)}, u32[]{:S(2)}) collective-permute-start(bf16[4,80,256]{2,1,0:T(8,128)(2,1)S(1)} %get-tuple-element.54), channel_id=1, source_target_pairs={{0,1},{1,2},{2,3},{3,4},{4,5},{5,6},{6,7},{7,0},{8,9},{9,10},{10,1... | collective-permute-start | bytes 491528 | tf_op jit(solution)/shard_map/ppermute | solution.py:444
  34.5 13.3 %collective-permute-start.7 = (bf16[4,80,256]{2,1,0:T(8,128)(2,1)S(1)}, bf16[4,80,256]{2,1,0:T(8,128)(2,1)S(1)}, u32[]{:S(2)}, u32[]{:S(2)}) collective-permute-start(bf16[4,80,256]{2,1,0:T(8,128)(2,1)S(1)} %get-tuple-element.55), channel_id=1, source_target_pairs={{0,7},{1,0},{2,1},{3,2},{4,3},{5,4},{6,5},{7,6},{8,15},{9,8},{10,9... | collective-permute-start | bytes 491528 | tf_op jit(solution)/shard_map/ppermute | solution.py:444
  40.4 3.1 %collective-permute-start.8 = (bf16[2,48,256]{2,1,0:T(8,128)(2,1)S(1)}, bf16[2,48,256]{2,1,0:T(8,128)(2,1)S(1)}, u32[]{:S(2)}, u32[]{:S(2)}) collective-permute-start(bf16[2,48,256]{2,1,0:T(8,128)(2,1)S(1)} %slice_bitcast_fusion), channel_id=1, source_target_pairs={{8,0},{16,8},{9,1},{17,9},{10,2},{18,10},{11,3},{19,11},{12,4},{20... | collective-permute-start | bytes 147464 | tf_op jit(solution)/shard_map/ppermute | solution.py:420
  41.7 6.0 %collective-permute-start.9 = (bf16[2,48,256]{2,1,0:T(8,128)(2,1)S(1)}, bf16[2,48,256]{2,1,0:T(8,128)(2,1)S(1)}, u32[]{:S(2)}, u32[]{:S(2)}) collective-permute-start(bf16[2,48,256]{2,1,0:T(8,128)(2,1)S(1)} %slice_bitcast_fusion), channel_id=1, source_target_pairs={{16,0},{17,1},{18,2},{19,3},{20,4},{21,5},{22,6},{23,7}} | collective-permute-start | bytes 147464 | tf_op jit(solution)/shard_map/ppermute | solution.py:420
  50.1 8.6 %copy-start.3 = (bf16[135,144]{1,0:T(8,128)(2,1)S(1)}, bf16[135,144]{1,0:T(8,128)(2,1)}, u32[]{:S(2)}) copy-start(bf16[135,144]{1,0:T(8,128)(2,1)} %constant.12.clone.back) | copy-start | bytes 116644
  50.1 4.6 %collective-permute-start.10 = (bf16[48,256]{1,0:T(8,128)(2,1)S(1)}, bf16[48,256]{1,0:T(8,128)(2,1)S(1)}, u32[]{:S(2)}, u32[]{:S(2)}) collective-permute-start(bf16[48,256]{1,0:T(8,128)(2,1)S(1)} %get-tuple-element.65), channel_id=1, source_target_pairs={{8,0},{16,8},{24,16},{9,1},{17,9},{25,17},{10,2},{18,10},{26,18},{... | collective-permute-start | bytes 73736 | tf_op jit(solution)/shard_map/ppermute | solution.py:449
  51.5 5.8 %collective-permute-start.11 = (bf16[48,256]{1,0:T(8,128)(2,1)S(1)}, bf16[48,256]{1,0:T(8,128)(2,1)S(1)}, u32[]{:S(2)}, u32[]{:S(2)}) collective-permute-start(bf16[48,256]{1,0:T(8,128)(2,1)S(1)} %get-tuple-element.65), channel_id=1, source_target_pairs={{16,0},{24,8},{17,1},{25,9},{18,2},{26,10},{19,3},{27,11},{20,4},{... | collective-permute-start | bytes 73736 | tf_op jit(solution)/shard_map/ppermute | solution.py:449
  52.8 5.9 %collective-permute-start.12 = (bf16[48,256]{1,0:T(8,128)(2,1)S(1)}, bf16[48,256]{1,0:T(8,128)(2,1)S(1)}, u32[]{:S(2)}, u32[]{:S(2)}) collective-permute-start(bf16[48,256]{1,0:T(8,128)(2,1)S(1)} %get-tuple-element.65), channel_id=1, source_target_pairs={{24,0},{25,1},{26,2},{27,3},{28,4},{29,5},{30,6},{31,7}} | collective-permute-start | bytes 73736 | tf_op jit(solution)/shard_map/ppermute | solution.py:449

commit v6 on v5

--- a/solution.py
+++ b/solution.py
@@ -159,15 +159,18 @@
             above[...] = mt(picks(first_target(rows_of(FACE)), width), x).astype(BF)
 
 
-def turned(rows):
-    pad = jnp.zeros((FACE - NT,) + rows.shape[1:], rows.dtype)
-    return jnp.swapaxes(jnp.concatenate([rows, pad], 0), 0, 1)
+def turned(rows, raw, put):
+    count, columns, width = rows.shape
+    raw[0, : count * columns] = rows[:, :, :128].astype(F32).reshape(count * columns, 128)
+    raw[1, : count * columns, : width - 128] = rows[:, :, 128:].astype(F32).reshape(count * columns, width - 128)
+    for c in range(columns):
+        put(c, jnp.concatenate([raw[i, pl.ds(c, FACE, stride=columns), :] for i in range(2)], 1))
 
 
 def weight_kernel(
     inverse, couplings, right, initial, neighbours,
     known, lower, upper, base, fore, own,
-    inverse_in, couplings_in, right_in, initial_in, solves, faces, prev, tables, done,
+    inverse_in, couplings_in, right_in, initial_in, solves, faces, prev, tables, raw, done,
 ):
     planes, columns, rhs, width = initial.shape
     size = columns * rhs
@@ -183,6 +186,7 @@
             copy.start()
     start.start()
     faces[...] = jnp.zeros(faces.shape, BF)
+    raw[...] = jnp.zeros(raw.shape, F32)
     tables[:FACE] = picks(c_target(rows_of(FACE), 2), width)
     tables[FACE : 2 * FACE] = picks(c_target(rows_of(FACE), 0), width)
     tables[2 * FACE :] = picks(first_target(rows_of(FACE)), width)
@@ -202,12 +206,20 @@
             copy.wait()
         for a in range(3):
             rows = [inverse_in[p, v * 27 + a * 9 : v * 27 + a * 9 + 9] for v in range(5)]
-            solves[:, a * FACE : (a + 1) * FACE] = -turned(jnp.concatenate(rows, 0))
-        for f in range(4):
-            faces[:, f * FACE : (f + 1) * FACE] = turned(couplings_in[p, 2 + f])
-        faces[:, 4 * FACE : 4 * FACE + rhs] = right_in[p]
-        faces[:, 256 : 256 + FACE] = turned(couplings_in[p, 0])
-        faces[:, 256 + SLOT : 256 + SLOT + FACE] = turned(couplings_in[p, 1])
+
+
+            def put(c, value):
+                solves[c, a * FACE : (a + 1) * FACE] = (-value).astype(BF)
+
+            turned(jnp.concatenate(rows, 0), raw.at[a], put)
+        places = (256, 256 + SLOT, 0, FACE, 2 * FACE, 3 * FACE)
+        for f, place in enumerate(places):
+
+            def put(c, value):
+                faces[c, place : place + FACE] = value.astype(BF)
+
+            turned(couplings_in[p, f], raw.at[3 + f], put)
+        faces[:, 4 * FACE : 4 * FACE + rhs, :width] = right_in[p]
 
         bases = []
         before = None
@@ -276,7 +288,7 @@
 
 def chain_kernel(known, base, matrix, received, own, neighbours, outs, order, rows, rhs, extra=None):
     up, down, up_sel, down_sel = received
-    operand, start, traces, message = outs
+    operand, start, traces, message, *wide = outs
     planes, columns = known.shape[:2]
     size = columns * rhs
     source = sources(neighbours, columns, rhs)
@@ -294,10 +306,11 @@
         start[p] = value
         trace = value if trace is None else value + chain_step(matrix.at[p], trace, rhs, rows)
         traces[p] = trace
-    message[FIRST] = trace.astype(BF)
-    if message.shape[0] > FACE:
+    message[...] = trace.astype(BF)
+    for both in wide:
+        both[FIRST] = trace.astype(BF)
         for h in range(2):
-            message[(1 + h) * FACE : (2 + h) * FACE] = matrix[order[-1], h, PRODUCT]
+            both[(1 + h) * FACE : (2 + h) * FACE] = matrix[order[-1], h, PRODUCT]
 
 
 def base_kernel(known, operand, base, *rest, rows, rhs):
@@ -430,10 +443,11 @@
     outs.append(((planes, 2 * FACE, size), BF))
     operands = (inverse, couplings, right, initial, neighbours)
     scratch = [pltpu.VMEM(x.shape, x.dtype) for x in operands[:4]] + [
-        pltpu.VMEM((columns, ROWS, width), BF),
-        pltpu.VMEM((columns, 256 + 2 * SLOT, width), BF),
+        pltpu.VMEM((columns, ROWS, 256), BF),
+        pltpu.VMEM((columns, 256 + 2 * SLOT, 256), BF),
         pltpu.VMEM((2, FACE, 256), F32),
         pltpu.VMEM((3 * FACE, width), BF),
+        pltpu.VMEM((9, 2, FACE * columns, 128), F32),
         pltpu.SemaphoreType.DMA((4, planes)),
     ]
     return call(weight_kernel, outs, operands, "weights", 1e10, (0, 1, 2, 3), scratch)
@@ -476,14 +490,14 @@
     trace = (planes, FACE, size)
     most = (planes, 2 * FACE, size)
     chain_outs = [((planes, 256, size), BF), (trace, F32), (trace, F32)]
-    operand, start, traces, message = call(
+    operand, start, traces, message, wide = call(
         functools.partial(forward_chain_kernel, rhs=rhs),
-        chain_outs + [((3 * FACE, size), BF)],
+        chain_outs + [((FACE, size), BF), ((3 * FACE, size), BF)],
         (from_low, from_high, from_above, own, beside, up_sel, down_sel, known, lower, upper, fore),
         "forward_chain",
     )
-    one, two = (shift(message, "sweep", by) for by in (1, 2))
-    three = shift(message[:FACE], "sweep", 3)
+    three = shift(message, "sweep", 3)
+    two, one = (shift(wide, "sweep", by) for by in (2, 1))
     (rest,) = call(
         functools.partial(base_kernel, rows=slice(0, 2 * FACE), rhs=rhs),
         [(most, F32)],
@@ -507,14 +521,13 @@
     )
     own, pass_b = lax.optimization_barrier((own, upper[0, :, PRODUCT]))
     passes = products(pass_b, -1)
-    from_low, from_high, *passes = lax.optimization_barrier((from_low, from_high, *passes))
     operand, start, traces, message = call(
         functools.partial(backward_chain_kernel, rhs=rhs),
         chain_outs + [((FACE, size), BF)],
         (from_low, from_high, own, beside, up_sel, down_sel, known, upper, base),
         "backward_chain",
     )
-    one, two, three = (shift(message, "sweep", -by) for by in (1, 2, 3))
+    three, two, one = (shift(message, "sweep", -by) for by in (3, 2, 1))
     (rest,) = call(
         functools.partial(base_kernel, rows=slice(FACE, ROWS), rhs=rhs),
         [(most, F32)],

time: 62 us -> 58.3 us (0.940)
  the two profiles are of different devices: /device:TPU:0 before, /device:TPU:1 now
where the time goes in v6:
time: 58.3 us; the launch traced here: 57.4 us
  starting transfers between devices  27.6 us (47%)
  Pallas kernels  24.3 us (42%)
  waiting for transfers between devices  3.24 us (6%)
  local copies, waits for them, and re-layouts  1.94 us (3%)
    pallas_call x9, Pallas kernels, call(): pl.pallas_call(kernel, out_shape=shapes, in_specs=[pl.BlockSpec(memory_sp...  24.3 us
    ppermute x7, starting transfers between devices, shift(): lax.ppermute(x, axis, [(i, i + by) for i in range(n) if 0 <= i + by < n])  12 us
    ppermute x4, starting transfers between devices, ring(): return lax.ppermute(x, axis, [(i, (i + by) % n) for i in range(n)])  10.1 us
    ppermute x2, starting transfers between devices, products(): lax.ppermute(x, 'sweep', [(i, i + step) for i in inner if 0 <= i + step <...  5.53 us
    ppermute x7, waiting for transfers between devices, shift(): lax.ppermute(x, axis, [(i, i + by) for i in range(n) if 0 <= i + by < n])  3.22 us
    unnamed x14, local copies, waits for them, and re-layouts  1.93 us
  transfers between devices with their start and end apart: 13, of which 2 were waited for; matrix products, arithmetic and copies ran while one was open for 0% of the time, Pallas kernels for 29%

profile of v6, /device:TPU:1, one launch (start us, length us, event | category | flops | bytes accessed | tf_op | source)
XLA Modules:
  0.0 57.4 jit_solution(12721387330289579813)
XLA Ops:
  0.0 0.0 copy-start.5
  0.0 1.0 %copy-done.5 = bf16[4,8,32,135]{3,2,1,0:T(8,128)(2,1)S(1)} copy-done((bf16[4,8,32,135]{3,2,1,0:T(8,128)(2,1)S(1)}, bf16[4,8,32,135]{3,2,1,0:T(8,128)(2,1)}, u32[]{:S(2)}) %copy-start.5) | copy-done | bytes 276504
  1.0 0.5 initial_traces.1
  1.6 2.0 %collective-permute-start.2 = (bf16[48,256]{1,0:T(8,128)(2,1)S(1)}, bf16[48,256]{1,0:T(8,128)(2,1)S(1)}, u32[]{:S(2)}, u32[]{:S(2)}) collective-permute-start(bf16[48,256]{1,0:T(8,128)(2,1)S(1)} %get-tuple-element.40), channel_id=1, source_target_pairs={{8,0},{16,8},{24,16},{9,1},{17,9},{25,17},{10,2},{18,10},{26,18},{... | collective-permute-start | bytes 73736 | tf_op jit(solution)/shard_map/ppermute | solution.py:463
  3.5 2.7 %collective-permute-start = (bf16[4,80,256]{2,1,0:T(8,128)(2,1)S(1)}, bf16[4,80,256]{2,1,0:T(8,128)(2,1)S(1)}, u32[]{:S(2)}, u32[]{:S(2)}) collective-permute-start(bf16[4,80,256]{2,1,0:T(8,128)(2,1)S(1)} %get-tuple-element.38), channel_id=1, source_target_pairs={{0,1},{1,2},{2,3},{3,4},{4,5},{5,6},{6,7},{7,0},{8,9},{9,10},{10,1... | collective-permute-start | bytes 491528 | tf_op jit(solution)/shard_map/ppermute | solution.py:458
  6.3 3.1 %collective-permute-start.1 = (bf16[4,80,256]{2,1,0:T(8,128)(2,1)S(1)}, bf16[4,80,256]{2,1,0:T(8,128)(2,1)S(1)}, u32[]{:S(2)}, u32[]{:S(2)}) collective-permute-start(bf16[4,80,256]{2,1,0:T(8,128)(2,1)S(1)} %get-tuple-element.39), channel_id=1, source_target_pairs={{0,7},{1,0},{2,1},{3,2},{4,3},{5,4},{6,5},{7,6},{8,15},{9,8},{10,9... | collective-permute-start | bytes 491528 | tf_op jit(solution)/shard_map/ppermute | solution.py:458
  9.4 0.0 copy-start.4
  9.4 0.7 %copy-done.4 = s32[8,4]{0,1:T(4,128)S(1)} copy-done((s32[8,4]{0,1:T(4,128)S(1)}, s32[8,4]{0,1:T(4,128)}, u32[]{:S(2)}) %copy-start.4) | copy-done | bytes 152
  10.1 0.0 copy-start
  10.1 0.0 copy-start.1
  10.1 12.1 %weights.1 = (bf16[4,8,144,256]{3,2,1,0:T(8,128)(2,1)S(1)}, bf16[4,2,192,256]{3,2,1,0:T(8,128)(2,1)S(1)}, bf16[4,2,192,256]{3,2,1,0:T(8,128)(2,1)S(1)}, f32[4,14...) custom-call(bf16[4,135,8,135]{3,2,1,0:T(8,128)(2,1)} %bitcast.10, ...), custom_call_target="tpu_custom_call" | custom-call | flops 10000000000 | bytes 9360704 | tf_op jit(solution)/shard_map/weights/pallas_call | solution.py:417
  22.1 0.0 collective-permute-done.2.above.rest_0_
  22.1 0.0 collective-permute-done.up
  22.2 0.0 collective-permute-done.1.down
  22.2 0.0 copy-done
  22.2 0.0 copy-done.1
  22.2 2.4 %forward_chain.1 = (bf16[4,256,256]{2,1,0:T(8,128)(2,1)S(1)}, f32[4,48,256]{2,1,0:T(8,128)S(1)}, f32[4,48,256]{2,1,0:T(8,128)S(1)}, bf16[48,256]{1,0:T(8,128)(2,1)S(1)}, bf16[144,256]{1,0:T(8,128)(2,1)S(1)}) custom-call(bf16[4,80,256]{2,1,0:T(8,128)(2,1)S(1)} %collective-permute-done.up, bf16[4,80,256]{2,1,0:T(8,128)(2,1)S(1)} %collective-permute-done.1.down, ...), custom_call_target="tpu_custom_call" | custom-call | flops 200000000 | bytes 6117504 | tf_op jit(solution)/shard_map/forward_chain/pallas_call | solution.py:417
  24.6 3.4 %collective-permute-start.3 = (bf16[144,256]{1,0:T(8,128)(2,1)S(1)}, bf16[144,256]{1,0:T(8,128)(2,1)S(1)}, u32[]{:S(2)}, u32[]{:S(2)}) collective-permute-start(bf16[144,256]{1,0:T(8,128)(2,1)S(1)} %get-tuple-element.47), channel_id=1, source_target_pairs={{0,8},{8,16},{16,24},{1,9},{9,17},{17,25},{2,10},{10,18},{18,26},{... | collective-permute-start | bytes 221192 | tf_op jit(solution)/shard_map/ppermute | solution.py:463
  28.0 1.3 %collective-permute-start.4 = (bf16[144,256]{1,0:T(8,128)(2,1)S(1)}, bf16[144,256]{1,0:T(8,128)(2,1)S(1)}, u32[]{:S(2)}, u32[]{:S(2)}) collective-permute-start(bf16[144,256]{1,0:T(8,128)(2,1)S(1)} %get-tuple-element.47), channel_id=1, source_target_pairs={{0,16},{8,24},{1,17},{9,25},{2,18},{10,26},{3,19},{11,27},{4,20},{... | collective-permute-start | bytes 221192 | tf_op jit(solution)/shard_map/ppermute | solution.py:463
  29.3 0.7 %collective-permute-start.5 = (bf16[48,256]{1,0:T(8,128)(2,1)S(1)}, bf16[48,256]{1,0:T(8,128)(2,1)S(1)}, u32[]{:S(2)}, u32[]{:S(2)}) collective-permute-start(bf16[48,256]{1,0:T(8,128)(2,1)S(1)} %get-tuple-element.48), channel_id=1, source_target_pairs={{0,24},{1,25},{2,26},{3,27},{4,28},{5,29},{6,30},{7,31}} | collective-permute-start | bytes 73736 | tf_op jit(solution)/shard_map/ppermute | solution.py:463
  30.0 0.0 copy-start.2
  30.0 0.0 copy-start.6
  30.1 0.6 %forward_base.1.rest = f32[4,96,256]{2,1,0:T(8,128)S(1)} custom-call(bf16[4,8,144,256]{3,2,1,0:T(8,128)(2,1)S(1)} %get-tuple-element.43.known, bf16[4,256,256]{2,1,0:T(8,128)(2,1)S(1)} %get-tuple-element.50.operand, f32[4,144,256]{2,1,0:T(8,128)S(1)} %get-tuple-element.46.base, bf16[48,256]{1,0:T(8,128)(2,1)S(1)} %collective-permute-done.2.above.rest_0_, ...), custom_call_target="tpu_custom_call" | custom-call | flops 200000000 | bytes 4677632 | tf_op jit(solution)/shard_map/forward_base/pallas_call | solution.py:417
  30.7 0.0 collective-permute-done.5.three
  30.7 0.0 collective-permute-done.3.one
  30.7 0.0 collective-permute-done.4.two
  30.7 0.2 copy-done.2
  30.9 1.6 %forward_finish.1 = (bf16[4,144,256]{2,1,0:T(8,128)(2,1)S(1)}, f32[4,144,256]{2,1,0:T(8,128)S(1)}, bf16[4,80,256]{2,1,0:T(8,128)(2,1)S(1)}, bf16[4,80,256]{2,1,0:T(8,128)(2,1)S(1)}) custom-call(bf16[144,256]{1,0:T(8,128)(2,1)S(1)} %collective-permute-done.3.one, bf16[144,256]{1,0:T(8,128)(2,1)S(1)} %collective-permute-done.4.two, ...), custom_call_target="tpu_custom_call" | custom-call | flops 200000000 | bytes 3003392 | tf_op jit(solution)/shard_map/forward_finish/pallas_call | solution.py:417
  32.5 0.1 collective-permute-start.6
  32.6 4.1 %collective-permute-start.7 = (bf16[4,80,256]{2,1,0:T(8,128)(2,1)S(1)}, bf16[4,80,256]{2,1,0:T(8,128)(2,1)S(1)}, u32[]{:S(2)}, u32[]{:S(2)}) collective-permute-start(bf16[4,80,256]{2,1,0:T(8,128)(2,1)S(1)} %get-tuple-element.53), channel_id=1, source_target_pairs={{0,7},{1,0},{2,1},{3,2},{4,3},{5,4},{6,5},{7,6},{8,15},{9,8},{10,9... | collective-permute-start | bytes 491528 | tf_op jit(solution)/shard_map/ppermute | solution.py:458
  36.7 0.0 copy-done.6
  36.7 1.2 %middle.1 = (bf16[4,96,256]{2,1,0:T(8,128)(2,1)S(1)}, f32[4,144,256]{2,1,0:T(8,128)S(1)}) custom-call(bf16[4,144,256]{2,1,0:T(8,128)(2,1)S(1)} %get-tuple-element.54.middle, f32[4,144,256]{2,1,0:T(8,128)S(1)} %get-tuple-element.55.change, f32[4,144,256]{2,1,0:T(8,128)S(1)} %get-tuple-element.56.base, s32[4,8]{1,0:T(4,128)S(1)} %bitcast.7, ...), custom_call_target="tpu_custom_call" | custom-call | flops 2000000000 | bytes 2288768 | tf_op jit(solution)/shard_map/middle/pallas_call | solution.py:417
  38.0 4.9 %collective-permute-start.11 = (bf16[2,48,256]{2,1,0:T(8,128)(2,1)S(1)}, bf16[2,48,256]{2,1,0:T(8,128)(2,1)S(1)}, u32[]{:S(2)}, u32[]{:S(2)}) collective-permute-start(bf16[2,48,256]{2,1,0:T(8,128)(2,1)S(1)} %slice_bitcast_fusion), channel_id=1, source_target_pairs={{8,0},{16,8},{9,1},{17,9},{10,2},{18,10},{11,3},{19,11},{12,4},{20... | collective-permute-start | bytes 147464 | tf_op jit(solution)/shard_map/ppermute | solution.py:433
  42.9 0.7 %collective-permute-start.12 = (bf16[2,48,256]{2,1,0:T(8,128)(2,1)S(1)}, bf16[2,48,256]{2,1,0:T(8,128)(2,1)S(1)}, u32[]{:S(2)}, u32[]{:S(2)}) collective-permute-start(bf16[2,48,256]{2,1,0:T(8,128)(2,1)S(1)} %slice_bitcast_fusion), channel_id=1, source_target_pairs={{16,0},{17,1},{18,2},{19,3},{20,4},{21,5},{22,6},{23,7}} | collective-permute-start | bytes 147464 | tf_op jit(solution)/shard_map/ppermute | solution.py:433
  43.5 0.0 collective-permute-done.6.up
  43.5 0.0 collective-permute-done.7.down
  43.6 2.4 %backward_chain.1 = (bf16[4,256,256]{2,1,0:T(8,128)(2,1)S(1)}, f32[4,48,256]{2,1,0:T(8,128)S(1)}, f32[4,48,256]{2,1,0:T(8,128)S(1)}, bf16[48,256]{1,0:T(8,128)(2,1)S(1)}) custom-call(bf16[4,80,256]{2,1,0:T(8,128)(2,1)S(1)} %collective-permute-done.6.up, bf16[4,80,256]{2,1,0:T(8,128)(2,1)S(1)} %collective-permute-done.7.down, ...), custom_call_target="tpu_custom_call" | custom-call | flops 200000000 | bytes 5232768 | tf_op jit(solution)/shard_map/backward_chain/pallas_call | solution.py:417
  46.0 0.0 copy-start.3
  46.0 0.8 %collective-permute-start.10 = (bf16[48,256]{1,0:T(8,128)(2,1)S(1)}, bf16[48,256]{1,0:T(8,128)(2,1)S(1)}, u32[]{:S(2)}, u32[]{:S(2)}) collective-permute-start(bf16[48,256]{1,0:T(8,128)(2,1)S(1)} %get-tuple-element.60), channel_id=1, source_target_pairs={{24,0},{25,1},{26,2},{27,3},{28,4},{29,5},{30,6},{31,7}} | collective-permute-start | bytes 73736 | tf_op jit(solution)/shard_map/ppermute | solution.py:463
  46.8 2.6 %collective-permute-start.8 = (bf16[48,256]{1,0:T(8,128)(2,1)S(1)}, bf16[48,256]{1,0:T(8,128)(2,1)S(1)}, u32[]{:S(2)}, u32[]{:S(2)}) collective-permute-start(bf16[48,256]{1,0:T(8,128)(2,1)S(1)} %get-tuple-element.60), channel_id=1, source_target_pairs={{8,0},{16,8},{24,16},{9,1},{17,9},{25,17},{10,2},{18,10},{26,18},{... | collective-permute-start | bytes 73736 | tf_op jit(solution)/shard_map/ppermute | solution.py:463
  49.4 1.3 %collective-permute-start.9 = (bf16[48,256]{1,0:T(8,128)(2,1)S(1)}, bf16[48,256]{1,0:T(8,128)(2,1)S(1)}, u32[]{:S(2)}, u32[]{:S(2)}) collective-permute-start(bf16[48,256]{1,0:T(8,128)(2,1)S(1)} %get-tuple-element.60), channel_id=1, source_target_pairs={{16,0},{24,8},{17,1},{25,9},{18,2},{26,10},{19,3},{27,11},{20,4},{... | collective-permute-start | bytes 73736 | tf_op jit(solution)/shard_map/ppermute | solution.py:463
  50.7 0.6 %backward_base.1.rest = f32[4,96,256]{2,1,0:T(8,128)S(1)} custom-call(bf16[4,8,144,256]{3,2,1,0:T(8,128)(2,1)S(1)} %get-tuple-element.43.known, bf16[4,256,256]{2,1,0:T(8,128)(2,1)S(1)} %get-tuple-element.63.operand, f32[4,144,256]{2,1,0:T(8,128)S(1)} %get-tuple-element.59.base), custom_call_target="tpu_custom_call" | custom-call | flops 200000000 | bytes 3866624 | tf_op jit(solution)/shard_map/backward_base/pallas_call | solution.py:417
  51.3 0.0 collective-permute-done.11.near
  51.3 0.0 collective-permute-done.12.next_near
  51.3 0.0 collective-permute-done.10.three
  51.3 1.7 %collective-permute-done.8.one = bf16[48,256]{1,0:T(8,128)(2,1)S(1)} collective-permute-done((bf16[48,256]{1,0:T(8,128)(2,1)S(1)}, bf16[48,256]{1,0:T(8,128)(2,1)S(1)}, u32[]{:S(2)}, u32[]{:S(2)}) %collective-permute-start.8) | collective-permute-done | bytes 24608 | tf_op jit(solution)/shard_map/ppermute | solution.py:463
  53.0 1.5 %collective-permute-done.9.two = bf16[48,256]{1,0:T(8,128)(2,1)S(1)} collective-permute-done((bf16[48,256]{1,0:T(8,128)(2,1)S(1)}, bf16[48,256]{1,0:T(8,128)(2,1)S(1)}, u32[]{:S(2)}, u32[]{:S(2)}) %collective-permute-start.9) | collective-permute-done | bytes 24608 | tf_op jit(solution)/shard_map/ppermute | solution.py:463
  54.5 0.0 copy-done.3
  54.5 2.9 %backward_finish.1 = bf16[4,8,32,135]{3,2,1,0:T(8,128)(2,1)} custom-call(bf16[48,256]{1,0:T(8,128)(2,1)S(1)} %collective-permute-done.8.one, bf16[48,256]{1,0:T(8,128)(2,1)S(1)} %collective-permute-done.9.two, bf16[48,256]{1,0:T(8,128)(2,1)S(1)} %collective-permute-done.10.three, bf16[2,48,256]{2,1,0:T(8,128)(2,1)S(1)} %collective-permute-done.11.near, ...), custom_call_target="tpu_custom_call" | custom-call | flops 200000000 | bytes 2060256 | tf_op jit(solution)/shard_map/backward_finish/pallas_call | solution.py:417
  (1 shorter events, 0.0 us)
Async XLA Ops:
  0.0 1.0 %copy-start.5 = (bf16[4,8,32,135]{3,2,1,0:T(8,128)(2,1)S(1)}, bf16[4,8,32,135]{3,2,1,0:T(8,128)(2,1)}, u32[]{:S(2)}) copy-start(bf16[4,8,32,135]{3,2,1,0:T(8,128)(2,1)} %initial.2) | copy-start | bytes 829444
  1.6 20.6 %collective-permute-start.2 = (bf16[48,256]{1,0:T(8,128)(2,1)S(1)}, bf16[48,256]{1,0:T(8,128)(2,1)S(1)}, u32[]{:S(2)}, u32[]{:S(2)}) collective-permute-start(bf16[48,256]{1,0:T(8,128)(2,1)S(1)} %get-tuple-element.40), channel_id=1, source_target_pairs={{8,0},{16,8},{24,16},{9,1},{17,9},{25,17},{10,2},{18,10},{26,18},{... | collective-permute-start | bytes 73736 | tf_op jit(solution)/shard_map/ppermute | solution.py:463
  3.5 18.6 %collective-permute-start = (bf16[4,80,256]{2,1,0:T(8,128)(2,1)S(1)}, bf16[4,80,256]{2,1,0:T(8,128)(2,1)S(1)}, u32[]{:S(2)}, u32[]{:S(2)}) collective-permute-start(bf16[4,80,256]{2,1,0:T(8,128)(2,1)S(1)} %get-tuple-element.38), channel_id=1, source_target_pairs={{0,1},{1,2},{2,3},{3,4},{4,5},{5,6},{6,7},{7,0},{8,9},{9,10},{10,1... | collective-permute-start | bytes 491528 | tf_op jit(solution)/shard_map/ppermute | solution.py:458
  6.3 15.9 %collective-permute-start.1 = (bf16[4,80,256]{2,1,0:T(8,128)(2,1)S(1)}, bf16[4,80,256]{2,1,0:T(8,128)(2,1)S(1)}, u32[]{:S(2)}, u32[]{:S(2)}) collective-permute-start(bf16[4,80,256]{2,1,0:T(8,128)(2,1)S(1)} %get-tuple-element.39), channel_id=1, source_target_pairs={{0,7},{1,0},{2,1},{3,2},{4,3},{5,4},{6,5},{7,6},{8,15},{9,8},{10,9... | collective-permute-start | bytes 491528 | tf_op jit(solution)/shard_map/ppermute | solution.py:458
  9.4 0.7 %copy-start.4 = (s32[8,4]{0,1:T(4,128)S(1)}, s32[8,4]{0,1:T(4,128)}, u32[]{:S(2)}) copy-start(s32[8,4]{0,1:T(4,128)} %param.14) | copy-start | bytes 388
  10.1 12.1 %copy-start = (bf16[96,80]{1,0:T(8,128)(2,1)S(1)}, bf16[96,80]{1,0:T(8,128)(2,1)}, u32[]{:S(2)}) copy-start(bf16[96,80]{1,0:T(8,128)(2,1)} %constant.13.clone.up_sel) | copy-start | bytes 46084
  10.1 12.1 %copy-start.1 = (bf16[96,80]{1,0:T(8,128)(2,1)S(1)}, bf16[96,80]{1,0:T(8,128)(2,1)}, u32[]{:S(2)}) copy-start(bf16[96,80]{1,0:T(8,128)(2,1)} %constant.14.clone.down_sel) | copy-start | bytes 46084
  24.6 6.0 %collective-permute-start.3 = (bf16[144,256]{1,0:T(8,128)(2,1)S(1)}, bf16[144,256]{1,0:T(8,128)(2,1)S(1)}, u32[]{:S(2)}, u32[]{:S(2)}) collective-permute-start(bf16[144,256]{1,0:T(8,128)(2,1)S(1)} %get-tuple-element.47), channel_id=1, source_target_pairs={{0,8},{8,16},{16,24},{1,9},{9,17},{17,25},{2,10},{10,18},{18,26},{... | collective-permute-start | bytes 221192 | tf_op jit(solution)/shard_map/ppermute | solution.py:463
  28.0 2.7 %collective-permute-start.4 = (bf16[144,256]{1,0:T(8,128)(2,1)S(1)}, bf16[144,256]{1,0:T(8,128)(2,1)S(1)}, u32[]{:S(2)}, u32[]{:S(2)}) collective-permute-start(bf16[144,256]{1,0:T(8,128)(2,1)S(1)} %get-tuple-element.47), channel_id=1, source_target_pairs={{0,16},{8,24},{1,17},{9,25},{2,18},{10,26},{3,19},{11,27},{4,20},{... | collective-permute-start | bytes 221192 | tf_op jit(solution)/shard_map/ppermute | solution.py:463
  29.3 1.3 %collective-permute-start.5 = (bf16[48,256]{1,0:T(8,128)(2,1)S(1)}, bf16[48,256]{1,0:T(8,128)(2,1)S(1)}, u32[]{:S(2)}, u32[]{:S(2)}) collective-permute-start(bf16[48,256]{1,0:T(8,128)(2,1)S(1)} %get-tuple-element.48), channel_id=1, source_target_pairs={{0,24},{1,25},{2,26},{3,27},{4,28},{5,29},{6,30},{7,31}} | collective-permute-start | bytes 73736 | tf_op jit(solution)/shard_map/ppermute | solution.py:463
  30.0 0.9 %copy-start.2 = (bf16[160,144]{1,0:T(8,128)(2,1)S(1)}, bf16[160,144]{1,0:T(8,128)(2,1)}, u32[]{:S(2)}) copy-start(bf16[160,144]{1,0:T(8,128)(2,1)} %constant.10.clone.send) | copy-start | bytes 138244
  30.0 6.7 %copy-start.6 = (bf16[96,144]{1,0:T(8,128)(2,1)S(1)}, bf16[96,144]{1,0:T(8,128)(2,1)}, u32[]{:S(2)}) copy-start(bf16[96,144]{1,0:T(8,128)(2,1)} %constant.11.clone.own_sel) | copy-start | bytes 82948
  32.5 11.0 %collective-permute-start.6 = (bf16[4,80,256]{2,1,0:T(8,128)(2,1)S(1)}, bf16[4,80,256]{2,1,0:T(8,128)(2,1)S(1)}, u32[]{:S(2)}, u32[]{:S(2)}) collective-permute-start(bf16[4,80,256]{2,1,0:T(8,128)(2,1)S(1)} %get-tuple-element.52), channel_id=1, source_target_pairs={{0,1},{1,2},{2,3},{3,4},{4,5},{5,6},{6,7},{7,0},{8,9},{9,10},{10,1... | collective-permute-start | bytes 491528 | tf_op jit(solution)/shard_map/ppermute | solution.py:458
  32.6 11.0 %collective-permute-start.7 = (bf16[4,80,256]{2,1,0:T(8,128)(2,1)S(1)}, bf16[4,80,256]{2,1,0:T(8,128)(2,1)S(1)}, u32[]{:S(2)}, u32[]{:S(2)}) collective-permute-start(bf16[4,80,256]{2,1,0:T(8,128)(2,1)S(1)} %get-tuple-element.53), channel_id=1, source_target_pairs={{0,7},{1,0},{2,1},{3,2},{4,3},{5,4},{6,5},{7,6},{8,15},{9,8},{10,9... | collective-permute-start | bytes 491528 | tf_op jit(solution)/shard_map/ppermute | solution.py:458
  38.0 13.3 %collective-permute-start.11 = (bf16[2,48,256]{2,1,0:T(8,128)(2,1)S(1)}, bf16[2,48,256]{2,1,0:T(8,128)(2,1)S(1)}, u32[]{:S(2)}, u32[]{:S(2)}) collective-permute-start(bf16[2,48,256]{2,1,0:T(8,128)(2,1)S(1)} %slice_bitcast_fusion), channel_id=1, source_target_pairs={{8,0},{16,8},{9,1},{17,9},{10,2},{18,10},{11,3},{19,11},{12,4},{20... | collective-permute-start | bytes 147464 | tf_op jit(solution)/shard_map/ppermute | solution.py:433
  42.9 8.4 %collective-permute-start.12 = (bf16[2,48,256]{2,1,0:T(8,128)(2,1)S(1)}, bf16[2,48,256]{2,1,0:T(8,128)(2,1)S(1)}, u32[]{:S(2)}, u32[]{:S(2)}) collective-permute-start(bf16[2,48,256]{2,1,0:T(8,128)(2,1)S(1)} %slice_bitcast_fusion), channel_id=1, source_target_pairs={{16,0},{17,1},{18,2},{19,3},{20,4},{21,5},{22,6},{23,7}} | collective-permute-start | bytes 147464 | tf_op jit(solution)/shard_map/ppermute | solution.py:433
  46.0 8.5 %copy-start.3 = (bf16[135,144]{1,0:T(8,128)(2,1)S(1)}, bf16[135,144]{1,0:T(8,128)(2,1)}, u32[]{:S(2)}) copy-start(bf16[135,144]{1,0:T(8,128)(2,1)} %constant.12.clone.back) | copy-start | bytes 116644
  46.0 5.3 %collective-permute-start.10 = (bf16[48,256]{1,0:T(8,128)(2,1)S(1)}, bf16[48,256]{1,0:T(8,128)(2,1)S(1)}, u32[]{:S(2)}, u32[]{:S(2)}) collective-permute-start(bf16[48,256]{1,0:T(8,128)(2,1)S(1)} %get-tuple-element.60), channel_id=1, source_target_pairs={{24,0},{25,1},{26,2},{27,3},{28,4},{29,5},{30,6},{31,7}} | collective-permute-start | bytes 73736 | tf_op jit(solution)/shard_map/ppermute | solution.py:463
  46.8 6.2 %collective-permute-start.8 = (bf16[48,256]{1,0:T(8,128)(2,1)S(1)}, bf16[48,256]{1,0:T(8,128)(2,1)S(1)}, u32[]{:S(2)}, u32[]{:S(2)}) collective-permute-start(bf16[48,256]{1,0:T(8,128)(2,1)S(1)} %get-tuple-element.60), channel_id=1, source_target_pairs={{8,0},{16,8},{24,16},{9,1},{17,9},{25,17},{10,2},{18,10},{26,18},{... | collective-permute-start | bytes 73736 | tf_op jit(solution)/shard_map/ppermute | solution.py:463
  49.4 5.1 %collective-permute-start.9 = (bf16[48,256]{1,0:T(8,128)(2,1)S(1)}, bf16[48,256]{1,0:T(8,128)(2,1)S(1)}, u32[]{:S(2)}, u32[]{:S(2)}) collective-permute-start(bf16[48,256]{1,0:T(8,128)(2,1)S(1)} %get-tuple-element.60), channel_id=1, source_target_pairs={{16,0},{24,8},{17,1},{25,9},{18,2},{26,10},{19,3},{27,11},{20,4},{... | collective-permute-start | bytes 73736 | tf_op jit(solution)/shard_map/ppermute | solution.py:463

commit v7 on v6

--- a/solution.py
+++ b/solution.py
@@ -16,6 +16,10 @@
 ROWS = 3 * FACE
 SHARED = 80
 MIB = 1 << 20
+FIRST = slice(0, FACE)
+LAST = slice(2 * FACE, ROWS)
+FULL = slice(0, ROWS)
+PRODUCT = slice(ROWS, ROWS + FACE)
 
 
 def natural(v, a, b, c):
@@ -169,106 +173,94 @@
 
 def weight_kernel(
     inverse, couplings, right, initial, neighbours,
-    known, lower, upper, base, fore, own,
-    inverse_in, couplings_in, right_in, initial_in, solves, faces, prev, tables, raw, done,
+    known, lower, upper, base, fore, own, gathers,
+    inverse_in, right_in, solves, faces, raw, done,
 ):
     planes, columns, rhs, width = initial.shape
     size = columns * rhs
     half = columns // 2
-
-    def arrivals(p):
-        pairs = ((inverse, inverse_in), (couplings, couplings_in), (right, right_in))
-        return [pltpu.make_async_copy(x.at[p], y.at[p], done.at[i, p]) for i, (x, y) in enumerate(pairs)]
-
-    start = pltpu.make_async_copy(initial, initial_in, done.at[3, 0])
+    copies = []
     for p in range(planes):
-        for copy in arrivals(p):
+        pairs = ((inverse, inverse_in), (right, right_in))
+        copies.append([pltpu.make_async_copy(x.at[p], y.at[p], done.at[i, p]) for i, (x, y) in enumerate(pairs)])
+        for copy in copies[p]:
             copy.start()
-    start.start()
     faces[...] = jnp.zeros(faces.shape, BF)
     raw[...] = jnp.zeros(raw.shape, F32)
-    tables[:FACE] = picks(c_target(rows_of(FACE), 2), width)
-    tables[FACE : 2 * FACE] = picks(c_target(rows_of(FACE), 0), width)
-    tables[2 * FACE :] = picks(first_target(rows_of(FACE)), width)
     source = sources(neighbours, columns, rhs)
+    for i, start in enumerate((0, size)):
+        for j in range(2):
+            gathers[i, j] = one_hot(source[j], start, size)
+    own_table = [picks(c_target(rows_of(FACE), which), width) for which in (2, 0)]
+    first_table = picks(first_target(rows_of(FACE)), width)
+    fields = [initial[p].reshape(size, width) for p in range(planes)]
+    for j in range(2):
+        mine = jnp.concatenate([mt(own_table[j], x).astype(BF) for x in fields], 0)
+        mine = mm(mine, gathers[1 - j, j]).astype(BF)
+        for p in range(planes):
+            own[p, j * FACE : (j + 1) * FACE] = mine[p * FACE : (p + 1) * FACE]
     lane = lax.broadcasted_iota(jnp.int32, (ROWS, 2 * SLOT), 1)
-    start.wait()
-
-    @pl.loop(0, planes)
-    def _(p):
-        x = initial_in[p].reshape(size, width)
-        beyond = initial_in[jnp.minimum(p + 1, planes - 1)].reshape(size, width)
-        after = jnp.where(p + 1 < planes, mt(tables[2 * FACE :], beyond), 0.0)
-        mine = mt(tables[: 2 * FACE], x).astype(BF)
-        own[p, :FACE] = mm(mine[:FACE], one_hot(source[0], size, size)).astype(BF)
-        own[p, FACE:] = mm(mine[FACE:], one_hot(source[1], 0, size)).astype(BF)
-        for copy in arrivals(p):
+
+    for p in range(planes):
+        slot = p % 2
+        for c in range(columns):
+            for f, place in enumerate((256, 256 + SLOT, 0, FACE, 2 * FACE, 3 * FACE)):
+                faces[slot, c, place : place + NT, :width] = couplings[p, c, f]
+        for copy in copies[p]:
             copy.wait()
+        faces[slot, :, 4 * FACE : 4 * FACE + rhs, :width] = right_in[p]
         for a in range(3):
             rows = [inverse_in[p, v * 27 + a * 9 : v * 27 + a * 9 + 9] for v in range(5)]
 
-
             def put(c, value):
-                solves[c, a * FACE : (a + 1) * FACE] = (-value).astype(BF)
-
-            turned(jnp.concatenate(rows, 0), raw.at[a], put)
-        places = (256, 256 + SLOT, 0, FACE, 2 * FACE, 3 * FACE)
-        for f, place in enumerate(places):
-
-            def put(c, value):
-                faces[c, place : place + FACE] = value.astype(BF)
-
-            turned(couplings_in[p, f], raw.at[3 + f], put)
-        faces[:, 4 * FACE : 4 * FACE + rhs, :width] = right_in[p]
-
-        bases = []
+                solves[slot, c, a * FACE : (a + 1) * FACE] = (-value).astype(BF)
+
+            turned(jnp.concatenate(rows, 0), raw.at[slot, a], put)
+        bases, lowers, uppers = [], [], []
         before = None
         for c in range(columns):
-            solve = solves[c]
-            all_known = mt(solve, faces[c, :256])
+            solve = solves[slot, c]
+            all_known = mt(solve, faces[slot, c, :256])
             side = all_known[:, 128:]
             move = (c % half * rhs - (4 * FACE - 128)) % 128
             bases.append(pltpu.roll(side, move, 1) if move else side)
             known[p, c] = all_known.astype(BF)
-            both = mt(solve, faces[c, 256:])
+            both = mt(solve, faces[slot, c, 256:])
             if c % 2 == 0:
                 before = both
             else:
-                h, at = c // half, c % half // 2 * 2 * SLOT
-                lanes = slice(at, at + 2 * SLOT)
-                lower[p, h, :ROWS, lanes] = jnp.where(lane < SLOT, before, pltpu.roll(both, SLOT, 1)).astype(BF)
-                upper[p, h, :ROWS, lanes] = jnp.where(lane < SLOT, pltpu.roll(before, SLOT, 1), both).astype(BF)
+                lowers.append(jnp.where(lane < SLOT, before, pltpu.roll(both, SLOT, 1)).astype(BF))
+                uppers.append(jnp.where(lane < SLOT, pltpu.roll(before, SLOT, 1), both).astype(BF))
         for h in range(2):
             lanes = slice(h * half * rhs, (h + 1) * half * rhs)
+            lower[p, h, :ROWS] = jnp.concatenate(lowers[2 * h : 2 * h + 2], 1)
+            up = jnp.concatenate(uppers[2 * h : 2 * h + 2], 1)
+            upper[p, h, :ROWS] = up
             here = -own_lanes(bases[h * half : (h + 1) * half], rhs)
             base[p, :, lanes] = here
-            fore[p, :, lanes] = here + mm(upper[p, h, :ROWS], split_lanes(after[:, lanes], rhs))
-            step = lower[p, h, 2 * FACE : ROWS]
-
-            @pl.when(p == 0)
-            def _():
-                prev[h] = step.astype(F32)
-
-            @pl.when(p > 0)
-            def _():
-                prev[h] = mm(step, split_lanes(prev[h], SLOT))
-
-            lower[p, h, ROWS:] = prev[h].astype(BF)
+            if p + 1 < planes:
+                here = here + mm(up, split_lanes(mt(first_table, fields[p + 1])[:, lanes], rhs))
+            fore[p, :, lanes] = here
 
     for h in range(2):
-        total = upper[planes - 1, h, :FACE].astype(F32)
-        upper[planes - 1, h, ROWS:] = total.astype(BF)
-        for q in range(planes - 2, -1, -1):
-            total = mm(upper[q, h, :FACE], split_lanes(total, SLOT))
-            upper[q, h, ROWS:] = total.astype(BF)
-
-
-def gathered(received_up, received_down, own, p, up_sel, down_sel, low_pick, high_pick):
-    low = mm(up_sel, received_up[p]).astype(BF)
-    high = mm(down_sel, received_down[p]).astype(BF)
-    c_low = mm(low[FACE:], low_pick).astype(BF) + own[p, :FACE]
-    c_high = mm(high[FACE:], high_pick).astype(BF) + own[p, FACE : 2 * FACE]
-    return [low[:FACE], high[:FACE], c_low, c_high]
+        for matrix, rows, order in ((lower, LAST, range(planes)), (upper, FIRST, range(planes - 1, -1, -1))):
+            total = None
+            for q in order:
+                step = matrix[q, h, rows]
+                total = step.astype(F32) if total is None else mm(step, split_lanes(total, SLOT))
+                matrix[q, h, PRODUCT] = total.astype(BF)
+
+
+def gathered(received_up, received_down, own, up_sel, down_sel, gathers):
+    planes, _, size = received_up.shape
+    low = [mm(up_sel[...], received_up[p]).astype(BF) for p in range(planes)]
+    high = [mm(down_sel[...], received_down[p]).astype(BF) for p in range(planes)]
+    sides = []
+    for j, side in enumerate((low, high)):
+        picked = mm(jnp.concatenate([x[FACE:] for x in side], 0), gathers[j, j]).astype(BF)
+        sides.append([picked[p * FACE : (p + 1) * FACE] + own[p, j * FACE : (j + 1) * FACE] for p in range(planes)])
+    pad = jnp.zeros((256 - 4 * FACE, size), BF)
+    return [jnp.concatenate([low[p][:FACE], high[p][:FACE], sides[0][p], sides[1][p], pad], 0) for p in range(planes)]
 
 
 def known_part(known_c, operand, columns, rhs):
@@ -280,25 +272,14 @@
     return jnp.concatenate(out, 1)
 
 
-FIRST = slice(0, FACE)
-LAST = slice(2 * FACE, ROWS)
-FULL = slice(0, ROWS)
-PRODUCT = slice(ROWS, ROWS + FACE)
-
-
-def chain_kernel(known, base, matrix, received, own, neighbours, outs, order, rows, rhs, extra=None):
+def chain_kernel(known, base, matrix, received, own, gathers, outs, order, rows, rhs, extra=None):
     up, down, up_sel, down_sel = received
     operand, start, traces, message, *wide = outs
     planes, columns = known.shape[:2]
-    size = columns * rhs
-    source = sources(neighbours, columns, rhs)
-    low_pick = one_hot(source[0], 0, size)
-    high_pick = one_hot(source[1], size, size)
+    wholes = gathered(up, down, own, up_sel, down_sel, gathers)
     trace = None
     for p in order:
-        parts = gathered(up, down, own, p, up_sel[...], down_sel[...], low_pick, high_pick)
-        parts.append(jnp.zeros((256 - 4 * FACE, size), BF))
-        whole = jnp.concatenate(parts, 0)
+        whole = wholes[p]
         operand[p] = whole
         value = base[p, rows] + known_part(lambda c: known[p, c, rows], whole, columns, rhs)
         if extra is not None and p == planes - 1:
@@ -324,17 +305,17 @@
 
 
 def forward_chain_kernel(
-    up, down, above, own, neighbours, up_sel, down_sel, known, lower, upper, base, *outs, rhs
+    up, down, above, own, gathers, up_sel, down_sel, known, lower, upper, base, *outs, rhs
 ):
     order = range(up.shape[0])
     received = (up, down, up_sel, down_sel)
-    chain_kernel(known, base, lower, received, own, neighbours, outs, order, LAST, rhs, (upper, above))
-
-
-def backward_chain_kernel(up, down, own, neighbours, up_sel, down_sel, known, upper, base, *outs, rhs):
+    chain_kernel(known, base, lower, received, own, gathers, outs, order, LAST, rhs, (upper, above))
+
+
+def backward_chain_kernel(up, down, own, gathers, up_sel, down_sel, known, upper, base, *outs, rhs):
     order = range(up.shape[0] - 1, -1, -1)
     chain_kernel(
-        known, base, upper, (up, down, up_sel, down_sel), own, neighbours, outs, order, FIRST, rhs
+        known, base, upper, (up, down, up_sel, down_sel), own, gathers, outs, order, FIRST, rhs
     )
 
 
@@ -370,16 +351,15 @@
             trace = traces[p] + chain_step(lower.at[p], entry, rhs, PRODUCT)
 
 
-def middle_kernel(middle, change, base, neighbours, own_sel, own, out):
-    planes, _, size = middle.shape
-    columns = neighbours.shape[1]
-    source = sources(neighbours, columns, size // columns)
-    low_pick = one_hot(source[0], size, size)
-    high_pick = one_hot(source[1], 0, size)
+def middle_kernel(middle, change, base, gathers, own_sel, own, out):
+    planes = middle.shape[0]
+    mine = [mm(own_sel[...], middle[p]).astype(BF) for p in range(planes)]
+    for j in range(2):
+        side = jnp.concatenate([x[j * FACE : (j + 1) * FACE] for x in mine], 0)
+        side = mm(side, gathers[1 - j, j]).astype(BF)
+        for p in range(planes):
+            own[p, j * FACE : (j + 1) * FACE] = side[p * FACE : (p + 1) * FACE]
     for p in range(planes):
-        mine = mm(own_sel[...], middle[p]).astype(BF)
-        own[p, :FACE] = mm(mine[:FACE], low_pick).astype(BF)
-        own[p, FACE:] = mm(mine[FACE:], high_pick).astype(BF)
         out[p] = base[p] + change[p]
 
 
@@ -440,17 +420,17 @@
     pack = (planes, 2, ROWS + FACE, 256)
     field = (planes, ROWS, size)
     outs = [((planes, columns, ROWS, 256), BF), (pack, BF), (pack, BF), (field, F32), (field, F32)]
-    outs.append(((planes, 2 * FACE, size), BF))
+    outs += [((planes, 2 * FACE, size), BF), ((2, 2, size, size), BF)]
     operands = (inverse, couplings, right, initial, neighbours)
-    scratch = [pltpu.VMEM(x.shape, x.dtype) for x in operands[:4]] + [
-        pltpu.VMEM((columns, ROWS, 256), BF),
-        pltpu.VMEM((columns, 256 + 2 * SLOT, 256), BF),
-        pltpu.VMEM((2, FACE, 256), F32),
-        pltpu.VMEM((3 * FACE, width), BF),
-        pltpu.VMEM((9, 2, FACE * columns, 128), F32),
-        pltpu.SemaphoreType.DMA((4, planes)),
+    scratch = [
+        pltpu.VMEM(inverse.shape, BF),
+        pltpu.VMEM(right.shape, BF),
+        pltpu.VMEM((2, columns, ROWS, 256), BF),
+        pltpu.VMEM((2, columns, 256 + 2 * SLOT, 256), BF),
+        pltpu.VMEM((2, 3, 2, FACE * columns, 128), F32),
+        pltpu.SemaphoreType.DMA((2, planes)),
     ]
-    return call(weight_kernel, outs, operands, "weights", 1e10, (0, 1, 2, 3), scratch)
+    return call(weight_kernel, outs, operands, "weights", 1e10, (0, 2), scratch)
 
 
 def ring(x, axis, by):
@@ -482,8 +462,8 @@
     from_low = ring(up, "cross", 1)
     from_high = ring(down, "cross", -1)
     from_above = shift(above, "sweep", -1)
-    known, lower, upper, base, fore, own = weights(
-        inverse_blocks.transpose(0, 2, 1, 3), couplings.transpose(0, 2, 3, 1, 4), right_sides, initial, beside
+    known, lower, upper, base, fore, own, gathers = weights(
+        inverse_blocks.transpose(0, 2, 1, 3), couplings, right_sides, initial, beside
     )
 
     field = (planes, ROWS, size)
@@ -493,7 +473,7 @@
     operand, start, traces, message, wide = call(
         functools.partial(forward_chain_kernel, rhs=rhs),
         chain_outs + [((FACE, size), BF), ((3 * FACE, size), BF)],
-        (from_low, from_high, from_above, own, beside, up_sel, down_sel, known, lower, upper, fore),
+        (from_low, from_high, from_above, own, gathers, up_sel, down_sel, known, lower, upper, fore),
         "forward_chain",
     )
     three = shift(message, "sweep", 3)
@@ -515,7 +495,7 @@
     own, base = call(
         middle_kernel,
         [((planes, 2 * FACE, size), BF), (field, F32)],
-        (middle, change, base, beside, own_in),
+        (middle, change, base, gathers, own_in),
         "middle",
         2e9,
     )
@@ -524,7 +504,7 @@
     operand, start, traces, message = call(
         functools.partial(backward_chain_kernel, rhs=rhs),
         chain_outs + [((FACE, size), BF)],
-        (from_low, from_high, own, beside, up_sel, down_sel, known, upper, base),
+        (from_low, from_high, own, gathers, up_sel, down_sel, known, upper, base),
         "backward_chain",
     )
     three, two, one = (shift(message, "sweep", -by) for by in (3, 2, 1))

time: 58.3 us -> 52.6 us (0.902)
  Pallas kernels: 24.3 us -> 15.4 us
  local copies, waits for them, and re-layouts: 1.94 us -> 4.44 us
  starting transfers between devices: 27.6 us -> 28.8 us
    pallas_call x9, Pallas kernels: 24.3 us -> 15.4 us  [call(): pl.pallas_call(kernel, out_shape=shapes, in_specs=[pl.BlockSpec(memory_sp...]
    unnamed x14 -> x17, local copies, waits for them, and re-layouts: 1.93 us -> 4.43 us
    ppermute x7, starting transfers between devices: 12 us -> 12.9 us  [shift(): lax.ppermute(x, axis, [(i, i + by) for i in range(n) if 0 <= i + by < n])]
  transfers between devices with their start and end apart: 13 -> 13, of which waited for: 2 -> 3; matrix products, arithmetic and copies ran while one was open for 0% -> 6% of each run, Pallas kernels for 29% -> 18%
where the time goes in v7:
time: 52.6 us; the launch traced here: 52.2 us
  starting transfers between devices  28.8 us (55%)
  Pallas kernels  15.4 us (29%)
  local copies, waits for them, and re-layouts  4.44 us (8%)
  waiting for transfers between devices  3.24 us (6%)
    pallas_call x9, Pallas kernels, call(): pl.pallas_call(kernel, out_shape=shapes, in_specs=[pl.BlockSpec(memory_sp...  15.4 us
    ppermute x7, starting transfers between devices, shift(): lax.ppermute(x, axis, [(i, i + by) for i in range(n) if 0 <= i + by < n])  12.9 us
    ppermute x4, starting transfers between devices, ring(): return lax.ppermute(x, axis, [(i, (i + by) % n) for i in range(n)])  10.1 us
    ppermute x2, starting transfers between devices, products(): lax.ppermute(x, 'sweep', [(i, i + step) for i in inner if 0 <= i + step <...  5.82 us
    unnamed x17, local copies, waits for them, and re-layouts  4.43 us
    ppermute x7, waiting for transfers between devices, shift(): lax.ppermute(x, axis, [(i, i + by) for i in range(n) if 0 <= i + by < n])  3.22 us
  transfers between devices with their start and end apart: 13, of which 3 were waited for; matrix products, arithmetic and copies ran while one was open for 6% of the time, Pallas kernels for 18%

profile of v7, /device:TPU:1, one launch (start us, length us, event | category | flops | bytes accessed | tf_op | source)
XLA Modules:
  0.0 52.2 jit_solution(8153005394418943057)
XLA Ops:
  0.0 0.0 copy-start.4
  0.0 1.0 %copy-done.4 = bf16[4,8,32,135]{3,2,1,0:T(8,128)(2,1)S(1)} copy-done((bf16[4,8,32,135]{3,2,1,0:T(8,128)(2,1)S(1)}, bf16[4,8,32,135]{3,2,1,0:T(8,128)(2,1)}, u32[]{:S(2)}) %copy-start.4) | copy-done | bytes 276504
  1.0 0.5 initial_traces.1
  1.6 0.0 copy-start.5
  1.6 0.0 copy-start.6
  1.6 2.1 %collective-permute-start.2 = (bf16[48,256]{1,0:T(8,128)(2,1)S(1)}, bf16[48,256]{1,0:T(8,128)(2,1)S(1)}, u32[]{:S(2)}, u32[]{:S(2)}) collective-permute-start(bf16[48,256]{1,0:T(8,128)(2,1)S(1)} %get-tuple-element.41), channel_id=1, source_target_pairs={{8,0},{16,8},{24,16},{9,1},{17,9},{25,17},{10,2},{18,10},{26,18},{... | collective-permute-start | bytes 73736 | tf_op jit(solution)/shard_map/ppermute | solution.py:443
  3.7 2.7 %collective-permute-start = (bf16[4,80,256]{2,1,0:T(8,128)(2,1)S(1)}, bf16[4,80,256]{2,1,0:T(8,128)(2,1)S(1)}, u32[]{:S(2)}, u32[]{:S(2)}) collective-permute-start(bf16[4,80,256]{2,1,0:T(8,128)(2,1)S(1)} %get-tuple-element.39), channel_id=1, source_target_pairs={{0,1},{1,2},{2,3},{3,4},{4,5},{5,6},{6,7},{7,0},{8,9},{9,10},{10,1... | collective-permute-start | bytes 491528 | tf_op jit(solution)/shard_map/ppermute | solution.py:438
  6.4 3.1 %collective-permute-start.1 = (bf16[4,80,256]{2,1,0:T(8,128)(2,1)S(1)}, bf16[4,80,256]{2,1,0:T(8,128)(2,1)S(1)}, u32[]{:S(2)}, u32[]{:S(2)}) collective-permute-start(bf16[4,80,256]{2,1,0:T(8,128)(2,1)S(1)} %get-tuple-element.40), channel_id=1, source_target_pairs={{0,7},{1,0},{2,1},{3,2},{4,3},{5,4},{6,5},{7,6},{8,15},{9,8},{10,9... | collective-permute-start | bytes 491528 | tf_op jit(solution)/shard_map/ppermute | solution.py:438
  9.5 3.3 %copy.11.couplings = bf16[4,8,6,45,135]{4,3,2,1,0:T(8,128)(2,1)S(1)} copy(bf16[4,8,6,45,135]{4,1,3,2,0:T(8,128)(2,1)} %param.13) | data formatting | bytes 4665600 | tf_op args[3]
  12.9 0.0 copy-done.5
  12.9 0.0 copy-done.6
  12.9 0.0 copy-start
  12.9 0.0 copy-start.1
  12.9 6.7 %weights.1 = (bf16[4,8,144,256]{3,2,1,0:T(8,128)(2,1)S(1)}, bf16[4,2,192,256]{3,2,1,0:T(8,128)(2,1)S(1)}, bf16[4,2,192,256]{3,2,1,0:T(8,128)(2,1)S(1)}, f32[4,14...) custom-call(bf16[4,135,8,135]{3,2,1,0:T(8,128)(2,1)} %bitcast.5, ...), custom_call_target="tpu_custom_call" | custom-call | flops 10000000000 | bytes 9884992 | tf_op jit(solution)/shard_map/weights/pallas_call | solution.py:397
  19.7 0.0 collective-permute-done.2.above.rest_0_
  19.7 0.0 collective-permute-done.up
  19.7 0.0 collective-permute-done.1.down
  19.7 0.0 copy-done
  19.7 0.0 copy-done.1
  19.7 0.0 copy-start.2
  19.7 1.1 %forward_chain.1 = (bf16[4,256,256]{2,1,0:T(8,128)(2,1)S(1)}, f32[4,48,256]{2,1,0:T(8,128)S(1)}, f32[4,48,256]{2,1,0:T(8,128)S(1)}, bf16[48,256]{1,0:T(8,128)(2,1)S(1)}, bf16[144,256]{1,0:T(8,128)(2,1)S(1)}) custom-call(bf16[4,80,256]{2,1,0:T(8,128)(2,1)S(1)} %collective-permute-done.up, bf16[4,80,256]{2,1,0:T(8,128)(2,1)S(1)} %collective-permute-done.1.down, ...), custom_call_target="tpu_custom_call" | custom-call | flops 200000000 | bytes 6641664 | tf_op jit(solution)/shard_map/forward_chain/pallas_call | solution.py:397
  20.8 0.0 copy-start.7
  20.8 3.3 %collective-permute-start.4 = (bf16[144,256]{1,0:T(8,128)(2,1)S(1)}, bf16[144,256]{1,0:T(8,128)(2,1)S(1)}, u32[]{:S(2)}, u32[]{:S(2)}) collective-permute-start(bf16[144,256]{1,0:T(8,128)(2,1)S(1)} %get-tuple-element.49), channel_id=1, source_target_pairs={{0,16},{8,24},{1,17},{9,25},{2,18},{10,26},{3,19},{11,27},{4,20},{... | collective-permute-start | bytes 221192 | tf_op jit(solution)/shard_map/ppermute | solution.py:443
  24.1 1.9 %collective-permute-start.3 = (bf16[144,256]{1,0:T(8,128)(2,1)S(1)}, bf16[144,256]{1,0:T(8,128)(2,1)S(1)}, u32[]{:S(2)}, u32[]{:S(2)}) collective-permute-start(bf16[144,256]{1,0:T(8,128)(2,1)S(1)} %get-tuple-element.49), channel_id=1, source_target_pairs={{0,8},{8,16},{16,24},{1,9},{9,17},{17,25},{2,10},{10,18},{18,26},{... | collective-permute-start | bytes 221192 | tf_op jit(solution)/shard_map/ppermute | solution.py:443
  26.0 0.7 %collective-permute-start.5 = (bf16[48,256]{1,0:T(8,128)(2,1)S(1)}, bf16[48,256]{1,0:T(8,128)(2,1)S(1)}, u32[]{:S(2)}, u32[]{:S(2)}) collective-permute-start(bf16[48,256]{1,0:T(8,128)(2,1)S(1)} %get-tuple-element.50), channel_id=1, source_target_pairs={{0,24},{1,25},{2,26},{3,27},{4,28},{5,29},{6,30},{7,31}} | collective-permute-start | bytes 73736 | tf_op jit(solution)/shard_map/ppermute | solution.py:443
  26.7 0.6 %forward_base.1.rest = f32[4,96,256]{2,1,0:T(8,128)S(1)} custom-call(bf16[4,8,144,256]{3,2,1,0:T(8,128)(2,1)S(1)} %get-tuple-element.45.known, bf16[4,256,256]{2,1,0:T(8,128)(2,1)S(1)} %get-tuple-element.52.operand, f32[4,144,256]{2,1,0:T(8,128)S(1)} %get-tuple-element.48.base, bf16[48,256]{1,0:T(8,128)(2,1)S(1)} %collective-permute-done.2.above.rest_0_, ...), custom_call_target="tpu_custom_call" | custom-call | flops 200000000 | bytes 4677632 | tf_op jit(solution)/shard_map/forward_base/pallas_call | solution.py:397
  27.3 0.0 collective-permute-done.5.three
  27.3 0.0 collective-permute-done.4.two
  27.3 0.1 collective-permute-done.3.one
  27.4 0.0 copy-done.2
  27.4 1.6 %forward_finish.1 = (bf16[4,144,256]{2,1,0:T(8,128)(2,1)S(1)}, f32[4,144,256]{2,1,0:T(8,128)S(1)}, bf16[4,80,256]{2,1,0:T(8,128)(2,1)S(1)}, bf16[4,80,256]{2,1,0:T(8,128)(2,1)S(1)}) custom-call(bf16[144,256]{1,0:T(8,128)(2,1)S(1)} %collective-permute-done.3.one, bf16[144,256]{1,0:T(8,128)(2,1)S(1)} %collective-permute-done.4.two, ...), custom_call_target="tpu_custom_call" | custom-call | flops 200000000 | bytes 3003392 | tf_op jit(solution)/shard_map/forward_finish/pallas_call | solution.py:397
  29.0 0.1 collective-permute-start.6
  29.1 4.1 %collective-permute-start.7 = (bf16[4,80,256]{2,1,0:T(8,128)(2,1)S(1)}, bf16[4,80,256]{2,1,0:T(8,128)(2,1)S(1)}, u32[]{:S(2)}, u32[]{:S(2)}) collective-permute-start(bf16[4,80,256]{2,1,0:T(8,128)(2,1)S(1)} %get-tuple-element.55), channel_id=1, source_target_pairs={{0,7},{1,0},{2,1},{3,2},{4,3},{5,4},{6,5},{7,6},{8,15},{9,8},{10,9... | collective-permute-start | bytes 491528 | tf_op jit(solution)/shard_map/ppermute | solution.py:438
  33.2 0.0 copy-done.7
  33.2 0.3 middle.1
  33.6 0.0 copy-start.3
  33.6 0.8 %collective-permute-start.12 = (bf16[2,48,256]{2,1,0:T(8,128)(2,1)S(1)}, bf16[2,48,256]{2,1,0:T(8,128)(2,1)S(1)}, u32[]{:S(2)}, u32[]{:S(2)}) collective-permute-start(bf16[2,48,256]{2,1,0:T(8,128)(2,1)S(1)} %slice_bitcast_fusion), channel_id=1, source_target_pairs={{16,0},{17,1},{18,2},{19,3},{20,4},{21,5},{22,6},{23,7}} | collective-permute-start | bytes 147464 | tf_op jit(solution)/shard_map/ppermute | solution.py:413
  34.4 5.0 %collective-permute-start.11 = (bf16[2,48,256]{2,1,0:T(8,128)(2,1)S(1)}, bf16[2,48,256]{2,1,0:T(8,128)(2,1)S(1)}, u32[]{:S(2)}, u32[]{:S(2)}) collective-permute-start(bf16[2,48,256]{2,1,0:T(8,128)(2,1)S(1)} %slice_bitcast_fusion), channel_id=1, source_target_pairs={{8,0},{16,8},{9,1},{17,9},{10,2},{18,10},{11,3},{19,11},{12,4},{20... | collective-permute-start | bytes 147464 | tf_op jit(solution)/shard_map/ppermute | solution.py:413
  39.4 0.0 collective-permute-done.6.up
  39.4 0.0 collective-permute-done.7.down
  39.4 1.1 %backward_chain.1 = (bf16[4,256,256]{2,1,0:T(8,128)(2,1)S(1)}, f32[4,48,256]{2,1,0:T(8,128)S(1)}, f32[4,48,256]{2,1,0:T(8,128)S(1)}, bf16[48,256]{1,0:T(8,128)(2,1)S(1)}) custom-call(bf16[4,80,256]{2,1,0:T(8,128)(2,1)S(1)} %collective-permute-done.6.up, bf16[4,80,256]{2,1,0:T(8,128)(2,1)S(1)} %collective-permute-done.7.down, ...), custom_call_target="tpu_custom_call" | custom-call | flops 200000000 | bytes 5756928 | tf_op jit(solution)/shard_map/backward_chain/pallas_call | solution.py:397
  40.5 0.7 %collective-permute-start.10 = (bf16[48,256]{1,0:T(8,128)(2,1)S(1)}, bf16[48,256]{1,0:T(8,128)(2,1)S(1)}, u32[]{:S(2)}, u32[]{:S(2)}) collective-permute-start(bf16[48,256]{1,0:T(8,128)(2,1)S(1)} %get-tuple-element.62), channel_id=1, source_target_pairs={{24,0},{25,1},{26,2},{27,3},{28,4},{29,5},{30,6},{31,7}} | collective-permute-start | bytes 73736 | tf_op jit(solution)/shard_map/ppermute | solution.py:443
  41.2 1.3 %collective-permute-start.9 = (bf16[48,256]{1,0:T(8,128)(2,1)S(1)}, bf16[48,256]{1,0:T(8,128)(2,1)S(1)}, u32[]{:S(2)}, u32[]{:S(2)}) collective-permute-start(bf16[48,256]{1,0:T(8,128)(2,1)S(1)} %get-tuple-element.62), channel_id=1, source_target_pairs={{16,0},{24,8},{17,1},{25,9},{18,2},{26,10},{19,3},{27,11},{20,4},{... | collective-permute-start | bytes 73736 | tf_op jit(solution)/shard_map/ppermute | solution.py:443
  42.5 3.0 %collective-permute-start.8 = (bf16[48,256]{1,0:T(8,128)(2,1)S(1)}, bf16[48,256]{1,0:T(8,128)(2,1)S(1)}, u32[]{:S(2)}, u32[]{:S(2)}) collective-permute-start(bf16[48,256]{1,0:T(8,128)(2,1)S(1)} %get-tuple-element.62), channel_id=1, source_target_pairs={{8,0},{16,8},{24,16},{9,1},{17,9},{25,17},{10,2},{18,10},{26,18},{... | collective-permute-start | bytes 73736 | tf_op jit(solution)/shard_map/ppermute | solution.py:443
  45.5 0.6 %backward_base.1.rest = f32[4,96,256]{2,1,0:T(8,128)S(1)} custom-call(bf16[4,8,144,256]{3,2,1,0:T(8,128)(2,1)S(1)} %get-tuple-element.45.known, bf16[4,256,256]{2,1,0:T(8,128)(2,1)S(1)} %get-tuple-element.65.operand, f32[4,144,256]{2,1,0:T(8,128)S(1)} %get-tuple-element.61.base), custom_call_target="tpu_custom_call" | custom-call | flops 200000000 | bytes 3866624 | tf_op jit(solution)/shard_map/backward_base/pallas_call | solution.py:397
  46.1 0.0 collective-permute-done.12.next_near
  46.1 0.0 collective-permute-done.11.near
  46.1 0.0 collective-permute-done.10.three
  46.1 0.6 %collective-permute-done.9.two = bf16[48,256]{1,0:T(8,128)(2,1)S(1)} collective-permute-done((bf16[48,256]{1,0:T(8,128)(2,1)S(1)}, bf16[48,256]{1,0:T(8,128)(2,1)S(1)}, u32[]{:S(2)}, u32[]{:S(2)}) %collective-permute-start.9) | collective-permute-done | bytes 24608 | tf_op jit(solution)/shard_map/ppermute | solution.py:443
  46.7 2.5 %collective-permute-done.8.one = bf16[48,256]{1,0:T(8,128)(2,1)S(1)} collective-permute-done((bf16[48,256]{1,0:T(8,128)(2,1)S(1)}, bf16[48,256]{1,0:T(8,128)(2,1)S(1)}, u32[]{:S(2)}, u32[]{:S(2)}) %collective-permute-start.8) | collective-permute-done | bytes 24608 | tf_op jit(solution)/shard_map/ppermute | solution.py:443
  49.2 0.0 copy-done.3
  49.3 2.9 %backward_finish.1 = bf16[4,8,32,135]{3,2,1,0:T(8,128)(2,1)} custom-call(bf16[48,256]{1,0:T(8,128)(2,1)S(1)} %collective-permute-done.8.one, bf16[48,256]{1,0:T(8,128)(2,1)S(1)} %collective-permute-done.9.two, bf16[48,256]{1,0:T(8,128)(2,1)S(1)} %collective-permute-done.10.three, bf16[2,48,256]{2,1,0:T(8,128)(2,1)S(1)} %collective-permute-done.11.near, ...), custom_call_target="tpu_custom_call" | custom-call | flops 200000000 | bytes 2060256 | tf_op jit(solution)/shard_map/backward_finish/pallas_call | solution.py:397
  (1 shorter events, 0.0 us)
Async XLA Ops:
  0.0 1.0 %copy-start.4 = (bf16[4,8,32,135]{3,2,1,0:T(8,128)(2,1)S(1)}, bf16[4,8,32,135]{3,2,1,0:T(8,128)(2,1)}, u32[]{:S(2)}) copy-start(bf16[4,8,32,135]{3,2,1,0:T(8,128)(2,1)} %initial.2) | copy-start | bytes 829444
  1.6 11.3 %copy-start.5 = (bf16[4,8,32,135]{3,2,1,0:T(8,128)(2,1)S(1)}, bf16[4,8,32,135]{3,2,1,0:T(8,128)(2,1)}, u32[]{:S(2)}) copy-start(bf16[4,8,32,135]{3,2,1,0:T(8,128)(2,1)} %initial.2) | copy-start | bytes 829444
  1.6 11.3 %copy-start.6 = (s32[8,4]{0,1:T(4,128)S(1)}, s32[8,4]{0,1:T(4,128)}, u32[]{:S(2)}) copy-start(s32[8,4]{0,1:T(4,128)} %param.14) | copy-start | bytes 388
  1.6 18.1 %collective-permute-start.2 = (bf16[48,256]{1,0:T(8,128)(2,1)S(1)}, bf16[48,256]{1,0:T(8,128)(2,1)S(1)}, u32[]{:S(2)}, u32[]{:S(2)}) collective-permute-start(bf16[48,256]{1,0:T(8,128)(2,1)S(1)} %get-tuple-element.41), channel_id=1, source_target_pairs={{8,0},{16,8},{24,16},{9,1},{17,9},{25,17},{10,2},{18,10},{26,18},{... | collective-permute-start | bytes 73736 | tf_op jit(solution)/shard_map/ppermute | solution.py:443
  3.7 16.0 %collective-permute-start = (bf16[4,80,256]{2,1,0:T(8,128)(2,1)S(1)}, bf16[4,80,256]{2,1,0:T(8,128)(2,1)S(1)}, u32[]{:S(2)}, u32[]{:S(2)}) collective-permute-start(bf16[4,80,256]{2,1,0:T(8,128)(2,1)S(1)} %get-tuple-element.39), channel_id=1, source_target_pairs={{0,1},{1,2},{2,3},{3,4},{4,5},{5,6},{6,7},{7,0},{8,9},{9,10},{10,1... | collective-permute-start | bytes 491528 | tf_op jit(solution)/shard_map/ppermute | solution.py:438
  6.4 13.3 %collective-permute-start.1 = (bf16[4,80,256]{2,1,0:T(8,128)(2,1)S(1)}, bf16[4,80,256]{2,1,0:T(8,128)(2,1)S(1)}, u32[]{:S(2)}, u32[]{:S(2)}) collective-permute-start(bf16[4,80,256]{2,1,0:T(8,128)(2,1)S(1)} %get-tuple-element.40), channel_id=1, source_target_pairs={{0,7},{1,0},{2,1},{3,2},{4,3},{5,4},{6,5},{7,6},{8,15},{9,8},{10,9... | collective-permute-start | bytes 491528 | tf_op jit(solution)/shard_map/ppermute | solution.py:438
  12.9 6.8 %copy-start = (bf16[96,80]{1,0:T(8,128)(2,1)S(1)}, bf16[96,80]{1,0:T(8,128)(2,1)}, u32[]{:S(2)}) copy-start(bf16[96,80]{1,0:T(8,128)(2,1)} %constant.14.clone.down_sel) | copy-start | bytes 46084
  12.9 6.8 %copy-start.1 = (bf16[96,80]{1,0:T(8,128)(2,1)S(1)}, bf16[96,80]{1,0:T(8,128)(2,1)}, u32[]{:S(2)}) copy-start(bf16[96,80]{1,0:T(8,128)(2,1)} %constant.13.clone.up_sel) | copy-start | bytes 46084
  19.7 7.7 %copy-start.2 = (bf16[160,144]{1,0:T(8,128)(2,1)S(1)}, bf16[160,144]{1,0:T(8,128)(2,1)}, u32[]{:S(2)}) copy-start(bf16[160,144]{1,0:T(8,128)(2,1)} %constant.10.clone.send) | copy-start | bytes 138244
  20.8 12.4 %copy-start.7 = (bf16[96,144]{1,0:T(8,128)(2,1)S(1)}, bf16[96,144]{1,0:T(8,128)(2,1)}, u32[]{:S(2)}) copy-start(bf16[96,144]{1,0:T(8,128)(2,1)} %constant.11.clone.own_sel) | copy-start | bytes 82948
  20.8 6.5 %collective-permute-start.4 = (bf16[144,256]{1,0:T(8,128)(2,1)S(1)}, bf16[144,256]{1,0:T(8,128)(2,1)S(1)}, u32[]{:S(2)}, u32[]{:S(2)}) collective-permute-start(bf16[144,256]{1,0:T(8,128)(2,1)S(1)} %get-tuple-element.49), channel_id=1, source_target_pairs={{0,16},{8,24},{1,17},{9,25},{2,18},{10,26},{3,19},{11,27},{4,20},{... | collective-permute-start | bytes 221192 | tf_op jit(solution)/shard_map/ppermute | solution.py:443
  24.1 3.3 %collective-permute-start.3 = (bf16[144,256]{1,0:T(8,128)(2,1)S(1)}, bf16[144,256]{1,0:T(8,128)(2,1)S(1)}, u32[]{:S(2)}, u32[]{:S(2)}) collective-permute-start(bf16[144,256]{1,0:T(8,128)(2,1)S(1)} %get-tuple-element.49), channel_id=1, source_target_pairs={{0,8},{8,16},{16,24},{1,9},{9,17},{17,25},{2,10},{10,18},{18,26},{... | collective-permute-start | bytes 221192 | tf_op jit(solution)/shard_map/ppermute | solution.py:443
  26.0 1.3 %collective-permute-start.5 = (bf16[48,256]{1,0:T(8,128)(2,1)S(1)}, bf16[48,256]{1,0:T(8,128)(2,1)S(1)}, u32[]{:S(2)}, u32[]{:S(2)}) collective-permute-start(bf16[48,256]{1,0:T(8,128)(2,1)S(1)} %get-tuple-element.50), channel_id=1, source_target_pairs={{0,24},{1,25},{2,26},{3,27},{4,28},{5,29},{6,30},{7,31}} | collective-permute-start | bytes 73736 | tf_op jit(solution)/shard_map/ppermute | solution.py:443
  29.0 10.4 %collective-permute-start.6 = (bf16[4,80,256]{2,1,0:T(8,128)(2,1)S(1)}, bf16[4,80,256]{2,1,0:T(8,128)(2,1)S(1)}, u32[]{:S(2)}, u32[]{:S(2)}) collective-permute-start(bf16[4,80,256]{2,1,0:T(8,128)(2,1)S(1)} %get-tuple-element.54), channel_id=1, source_target_pairs={{0,1},{1,2},{2,3},{3,4},{4,5},{5,6},{6,7},{7,0},{8,9},{9,10},{10,1... | collective-permute-start | bytes 491528 | tf_op jit(solution)/shard_map/ppermute | solution.py:438
  29.1 10.4 %collective-permute-start.7 = (bf16[4,80,256]{2,1,0:T(8,128)(2,1)S(1)}, bf16[4,80,256]{2,1,0:T(8,128)(2,1)S(1)}, u32[]{:S(2)}, u32[]{:S(2)}) collective-permute-start(bf16[4,80,256]{2,1,0:T(8,128)(2,1)S(1)} %get-tuple-element.55), channel_id=1, source_target_pairs={{0,7},{1,0},{2,1},{3,2},{4,3},{5,4},{6,5},{7,6},{8,15},{9,8},{10,9... | collective-permute-start | bytes 491528 | tf_op jit(solution)/shard_map/ppermute | solution.py:438
  33.6 15.7 %copy-start.3 = (bf16[135,144]{1,0:T(8,128)(2,1)S(1)}, bf16[135,144]{1,0:T(8,128)(2,1)}, u32[]{:S(2)}) copy-start(bf16[135,144]{1,0:T(8,128)(2,1)} %constant.12.clone.back) | copy-start | bytes 116644
  33.6 12.5 %collective-permute-start.12 = (bf16[2,48,256]{2,1,0:T(8,128)(2,1)S(1)}, bf16[2,48,256]{2,1,0:T(8,128)(2,1)S(1)}, u32[]{:S(2)}, u32[]{:S(2)}) collective-permute-start(bf16[2,48,256]{2,1,0:T(8,128)(2,1)S(1)} %slice_bitcast_fusion), channel_id=1, source_target_pairs={{16,0},{17,1},{18,2},{19,3},{20,4},{21,5},{22,6},{23,7}} | collective-permute-start | bytes 147464 | tf_op jit(solution)/shard_map/ppermute | solution.py:413
  34.4 11.7 %collective-permute-start.11 = (bf16[2,48,256]{2,1,0:T(8,128)(2,1)S(1)}, bf16[2,48,256]{2,1,0:T(8,128)(2,1)S(1)}, u32[]{:S(2)}, u32[]{:S(2)}) collective-permute-start(bf16[2,48,256]{2,1,0:T(8,128)(2,1)S(1)} %slice_bitcast_fusion), channel_id=1, source_target_pairs={{8,0},{16,8},{9,1},{17,9},{10,2},{18,10},{11,3},{19,11},{12,4},{20... | collective-permute-start | bytes 147464 | tf_op jit(solution)/shard_map/ppermute | solution.py:413
  40.5 5.6 %collective-permute-start.10 = (bf16[48,256]{1,0:T(8,128)(2,1)S(1)}, bf16[48,256]{1,0:T(8,128)(2,1)S(1)}, u32[]{:S(2)}, u32[]{:S(2)}) collective-permute-start(bf16[48,256]{1,0:T(8,128)(2,1)S(1)} %get-tuple-element.62), channel_id=1, source_target_pairs={{24,0},{25,1},{26,2},{27,3},{28,4},{29,5},{30,6},{31,7}} | collective-permute-start | bytes 73736 | tf_op jit(solution)/shard_map/ppermute | solution.py:443
  41.2 5.5 %collective-permute-start.9 = (bf16[48,256]{1,0:T(8,128)(2,1)S(1)}, bf16[48,256]{1,0:T(8,128)(2,1)S(1)}, u32[]{:S(2)}, u32[]{:S(2)}) collective-permute-start(bf16[48,256]{1,0:T(8,128)(2,1)S(1)} %get-tuple-element.62), channel_id=1, source_target_pairs={{16,0},{24,8},{17,1},{25,9},{18,2},{26,10},{19,3},{27,11},{20,4},{... | collective-permute-start | bytes 73736 | tf_op jit(solution)/shard_map/ppermute | solution.py:443
  42.5 6.7 %collective-permute-start.8 = (bf16[48,256]{1,0:T(8,128)(2,1)S(1)}, bf16[48,256]{1,0:T(8,128)(2,1)S(1)}, u32[]{:S(2)}, u32[]{:S(2)}) collective-permute-start(bf16[48,256]{1,0:T(8,128)(2,1)S(1)} %get-tuple-element.62), channel_id=1, source_target_pairs={{8,0},{16,8},{24,16},{9,1},{17,9},{25,17},{10,2},{18,10},{26,18},{... | collective-permute-start | bytes 73736 | tf_op jit(solution)/shard_map/ppermute | solution.py:443

commit v8 on v7

--- a/solution.py
+++ b/solution.py
@@ -80,22 +80,25 @@
     return lax.dot_general(a, b, (((1,), (1,)), ((), ())), preferred_element_type=F32)
 
 
+def group(shape, width, at):
+    lane = lax.broadcasted_iota(jnp.int32, shape, 1)
+    return (lane >= at * width) & (lane < (at + 1) * width)
+
+
 def split_lanes(value, width):
     lanes = value.shape[1]
     value = value.astype(F32)
-    owner = lax.broadcasted_iota(jnp.int32, value.shape, 1) // width
     pad = jnp.zeros((SLOT - FACE, lanes), BF)
     parts = []
     for c in range(lanes // width):
-        parts += [jnp.where(owner == c, value, 0.0).astype(BF), pad]
+        parts += [jnp.where(group(value.shape, width, c), value, 0.0).astype(BF), pad]
     return jnp.concatenate(parts, 0)
 
 
 def own_lanes(values, width):
-    owner = lax.broadcasted_iota(jnp.int32, values[0].shape, 1) // width
     out = values[0]
     for c in range(1, len(values)):
-        out = jnp.where(owner == c, values[c], out)
+        out = jnp.where(group(out.shape, width, c), values[c], out)
     return out
 
 
@@ -143,11 +146,13 @@
     lane = lax.broadcasted_iota(jnp.int32, (1, columns * rhs), 1)
     out = []
     for face, first in ((2, place - 1), (3, place)):
-        which = jnp.zeros_like(lane)
+        source = lane
         for c in range(columns):
-            at = lax.rem(neighbours[face, c] - first * columns + 2 * total, total)
-            which = jnp.where(lane // rhs == c, at, which)
-        out.append(which * rhs + lane % rhs)
+            at = neighbours[face, c] - first * columns
+            at = jnp.where(at < 0, at + total, at)
+            at = jnp.where(at >= total, at - total, at)
+            source = jnp.where(lane >= c * rhs, lane + (at - c) * rhs, source)
+        out.append(source)
     return out
 
 
@@ -173,15 +178,15 @@
 
 def weight_kernel(
     inverse, couplings, right, initial, neighbours,
-    known, lower, upper, base, fore, own, gathers,
-    inverse_in, right_in, solves, faces, raw, done,
+    known, lower, base, own, gathers,
+    inverse_in, couplings_in, right_in, solves, faces, raw, done,
 ):
     planes, columns, rhs, width = initial.shape
     size = columns * rhs
     half = columns // 2
     copies = []
     for p in range(planes):
-        pairs = ((inverse, inverse_in), (right, right_in))
+        pairs = ((inverse, inverse_in), (couplings, couplings_in), (right, right_in))
         copies.append([pltpu.make_async_copy(x.at[p], y.at[p], done.at[i, p]) for i, (x, y) in enumerate(pairs)])
         for copy in copies[p]:
             copy.start()
@@ -199,16 +204,15 @@
         mine = mm(mine, gathers[1 - j, j]).astype(BF)
         for p in range(planes):
             own[p, j * FACE : (j + 1) * FACE] = mine[p * FACE : (p + 1) * FACE]
+    for p in range(planes):
+        own[p, LAST] = mt(first_table, fields[min(p + 1, planes - 1)]).astype(BF)
     lane = lax.broadcasted_iota(jnp.int32, (ROWS, 2 * SLOT), 1)
 
     for p in range(planes):
         slot = p % 2
-        for c in range(columns):
-            for f, place in enumerate((256, 256 + SLOT, 0, FACE, 2 * FACE, 3 * FACE)):
-                faces[slot, c, place : place + NT, :width] = couplings[p, c, f]
         for copy in copies[p]:
             copy.wait()
-        faces[slot, :, 4 * FACE : 4 * FACE + rhs, :width] = right_in[p]
+        faces[slot, :, 256 + SLOT : 256 + SLOT + rhs, :width] = right_in[p]
         for a in range(3):
             rows = [inverse_in[p, v * 27 + a * 9 : v * 27 + a * 9 + 9] for v in range(5)]
 
@@ -216,51 +220,49 @@
                 solves[slot, c, a * FACE : (a + 1) * FACE] = (-value).astype(BF)
 
             turned(jnp.concatenate(rows, 0), raw.at[slot, a], put)
-        bases, lowers, uppers = [], [], []
+        for f, place in enumerate((256, 4 * FACE, 0, FACE, 2 * FACE, 3 * FACE)):
+
+            def put(c, value):
+                faces[slot, c, place : place + FACE] = value.astype(BF)
+
+            turned(couplings_in[p, f], raw.at[slot, 3 + f], put)
+        bases, lowers = [], []
         before = None
         for c in range(columns):
             solve = solves[slot, c]
-            all_known = mt(solve, faces[slot, c, :256])
-            side = all_known[:, 128:]
-            move = (c % half * rhs - (4 * FACE - 128)) % 128
-            bases.append(pltpu.roll(side, move, 1) if move else side)
-            known[p, c] = all_known.astype(BF)
+            known[p, c] = mt(solve, faces[slot, c, :256]).astype(BF)
             both = mt(solve, faces[slot, c, 256:])
+            move = (c % half * rhs - SLOT) % 128
+            bases.append(pltpu.roll(both, move, 1) if move else both)
             if c % 2 == 0:
                 before = both
             else:
                 lowers.append(jnp.where(lane < SLOT, before, pltpu.roll(both, SLOT, 1)).astype(BF))
-                uppers.append(jnp.where(lane < SLOT, pltpu.roll(before, SLOT, 1), both).astype(BF))
         for h in range(2):
             lanes = slice(h * half * rhs, (h + 1) * half * rhs)
             lower[p, h, :ROWS] = jnp.concatenate(lowers[2 * h : 2 * h + 2], 1)
-            up = jnp.concatenate(uppers[2 * h : 2 * h + 2], 1)
-            upper[p, h, :ROWS] = up
-            here = -own_lanes(bases[h * half : (h + 1) * half], rhs)
-            base[p, :, lanes] = here
-            if p + 1 < planes:
-                here = here + mm(up, split_lanes(mt(first_table, fields[p + 1])[:, lanes], rhs))
-            fore[p, :, lanes] = here
-
+            base[p, :, lanes] = -own_lanes(bases[h * half : (h + 1) * half], rhs)
+    chain_products(lower, LAST, range(planes))
+
+
+def chain_products(matrix, rows, order):
     for h in range(2):
-        for matrix, rows, order in ((lower, LAST, range(planes)), (upper, FIRST, range(planes - 1, -1, -1))):
-            total = None
-            for q in order:
-                step = matrix[q, h, rows]
-                total = step.astype(F32) if total is None else mm(step, split_lanes(total, SLOT))
-                matrix[q, h, PRODUCT] = total.astype(BF)
+        total = None
+        for q in order:
+            step = matrix[q, h, rows]
+            total = step.astype(F32) if total is None else mm(step, split_lanes(total, SLOT))
+            matrix[q, h, PRODUCT] = total.astype(BF)
 
 
 def gathered(received_up, received_down, own, up_sel, down_sel, gathers):
-    planes, _, size = received_up.shape
+    planes = received_up.shape[0]
     low = [mm(up_sel[...], received_up[p]).astype(BF) for p in range(planes)]
     high = [mm(down_sel[...], received_down[p]).astype(BF) for p in range(planes)]
     sides = []
     for j, side in enumerate((low, high)):
         picked = mm(jnp.concatenate([x[FACE:] for x in side], 0), gathers[j, j]).astype(BF)
         sides.append([picked[p * FACE : (p + 1) * FACE] + own[p, j * FACE : (j + 1) * FACE] for p in range(planes)])
-    pad = jnp.zeros((256 - 4 * FACE, size), BF)
-    return [jnp.concatenate([low[p][:FACE], high[p][:FACE], sides[0][p], sides[1][p], pad], 0) for p in range(planes)]
+    return [[low[p][:FACE], high[p][:FACE], sides[0][p], sides[1][p]] for p in range(planes)]
 
 
 def known_part(known_c, operand, columns, rhs):
@@ -272,18 +274,22 @@
     return jnp.concatenate(out, 1)
 
 
-def chain_kernel(known, base, matrix, received, own, gathers, outs, order, rows, rhs, extra=None):
+def chain_kernel(known, base, matrix, received, own, gathers, outs, order, rows, rhs, above=None):
     up, down, up_sel, down_sel = received
     operand, start, traces, message, *wide = outs
     planes, columns = known.shape[:2]
+    size = operand.shape[2]
     wholes = gathered(up, down, own, up_sel, down_sel, gathers)
     trace = None
     for p in order:
-        whole = wholes[p]
+        if above is None:
+            last_face = jnp.zeros((256 - 4 * FACE, size), BF)
+        else:
+            face = own[p, LAST] if p + 1 < planes else above[...]
+            last_face = jnp.concatenate([face, jnp.zeros((256 - 5 * FACE, size), BF)], 0)
+        whole = jnp.concatenate(wholes[p] + [last_face], 0)
         operand[p] = whole
         value = base[p, rows] + known_part(lambda c: known[p, c, rows], whole, columns, rhs)
-        if extra is not None and p == planes - 1:
-            value = value + chain_step(extra[0].at[p], extra[1][...], rhs, rows)
         start[p] = value
         trace = value if trace is None else value + chain_step(matrix.at[p], trace, rhs, rows)
         traces[p] = trace
@@ -294,29 +300,22 @@
             both[(1 + h) * FACE : (2 + h) * FACE] = matrix[order[-1], h, PRODUCT]
 
 
-def base_kernel(known, operand, base, *rest, rows, rhs):
+def base_kernel(known, operand, base, out, *, rows, rhs):
     planes, columns = known.shape[:2]
-    out = rest[-1]
-    for p in range(planes):
-        value = base[p, rows] + known_part(lambda c: known[p, c, rows], operand[p], columns, rhs)
-        if len(rest) > 1 and p == planes - 1:
-            value = value + chain_step(rest[1].at[p], rest[0][...], rhs, rows)
-        out[p] = value
-
-
-def forward_chain_kernel(
-    up, down, above, own, gathers, up_sel, down_sel, known, lower, upper, base, *outs, rhs
-):
+    for p in range(planes):
+        out[p] = base[p, rows] + known_part(lambda c: known[p, c, rows], operand[p], columns, rhs)
+
+
+def forward_chain_kernel(up, down, above, own, gathers, up_sel, down_sel, known, lower, base, *outs, rhs):
     order = range(up.shape[0])
     received = (up, down, up_sel, down_sel)
-    chain_kernel(known, base, lower, received, own, gathers, outs, order, LAST, rhs, (upper, above))
+    chain_kernel(known, base, lower, received, own, gathers, outs, order, LAST, rhs, above)
 
 
 def backward_chain_kernel(up, down, own, gathers, up_sel, down_sel, known, upper, base, *outs, rhs):
     order = range(up.shape[0] - 1, -1, -1)
-    chain_kernel(
-        known, base, upper, (up, down, up_sel, down_sel), own, gathers, outs, order, FIRST, rhs
-    )
+    received = (up, down, up_sel, down_sel)
+    chain_kernel(known, base, upper, received, own, gathers, outs, order, FIRST, rhs)
 
 
 def incoming(one, two, three, near, next_near, rhs):
@@ -351,7 +350,7 @@
             trace = traces[p] + chain_step(lower.at[p], entry, rhs, PRODUCT)
 
 
-def middle_kernel(middle, change, base, gathers, own_sel, own, out):
+def middle_kernel(middle, change, base, gathers, own_sel, known, own, out, upper):
     planes = middle.shape[0]
     mine = [mm(own_sel[...], middle[p]).astype(BF) for p in range(planes)]
     for j in range(2):
@@ -361,10 +360,20 @@
             own[p, j * FACE : (j + 1) * FACE] = side[p * FACE : (p + 1) * FACE]
     for p in range(planes):
         out[p] = base[p] + change[p]
+    columns = known.shape[1]
+    lane = lax.broadcasted_iota(jnp.int32, (ROWS, 2 * SLOT), 1)
+    for p in range(planes):
+        pairs = []
+        for c in range(0, columns, 2):
+            one, two = (known[p, c + i, :, 128:].astype(F32) for i in range(2))
+            pairs.append(jnp.where(lane < SLOT, pltpu.roll(one, SLOT, 1), two).astype(BF))
+        for h in range(2):
+            upper[p, h, :ROWS] = jnp.concatenate(pairs[2 * h : 2 * h + 2], 1)
+    chain_products(upper, FIRST, range(planes - 1, -1, -1))
 
 
 def backward_finish_kernel(
-    one, two, three, near, next_near, start, rest, traces, upper, back, result, *, rhs
+    one, two, three, near, next_near, start, rest, traces, upper, back, result, results, sem, *, rhs
 ):
     planes = start.shape[0]
     entry = incoming(one, two, three, [near[0], near[1]], [next_near[0], next_near[1]], rhs)
@@ -373,16 +382,21 @@
     column = lax.broadcasted_iota(jnp.int32, (size, size), 1)
     unit = jnp.where(row == column, 1.0, 0.0).astype(BF)
     columns, _, width = result.shape[1:]
+    copies = []
     trace = entry
     for p in range(planes - 1, -1, -1):
         whole = jnp.concatenate([start[p], rest[p]], 0) + chain_step(upper.at[p], trace, rhs, FULL)
         flat = mm(back[...], whole.astype(BF)).astype(BF)
-        result[p] = mt(unit, flat).astype(BF).reshape(columns, rhs, width)
+        results[p] = mt(unit, flat).astype(BF).reshape(columns, rhs, width)
+        copies.append(pltpu.make_async_copy(results.at[p], result.at[p], sem.at[p]))
+        copies[-1].start()
         if p:
             trace = traces[p] + chain_step(upper.at[p], entry, rhs, PRODUCT)
-
-
-def call(kernel, outs, operands, name, flops=2e8, far=(), scratch=()):
+    for copy in copies:
+        copy.wait()
+
+
+def call(kernel, outs, operands, name, flops=2e8, far=(), scratch=(), out_space=pltpu.VMEM):
     shapes = [jax.ShapeDtypeStruct(s, d) for s, d in outs]
     nbytes = sum(x.size * x.dtype.itemsize for x in list(operands) + shapes)
     spaces = [pltpu.SMEM if x.dtype == jnp.int32 else pltpu.VMEM for x in operands]
@@ -390,16 +404,12 @@
     operands = [
         pltpu.with_memory_space_constraint(x, pltpu.HBM) if i in far else x for i, x in enumerate(operands)
     ]
-    scratch = list(scratch)
-    if far and not scratch:
-        scratch = [pltpu.VMEM(operands[i].shape, operands[i].dtype) for i in far]
-        scratch.append(pltpu.SemaphoreType.DMA((len(far),)))
     return pl.pallas_call(
         kernel,
         out_shape=shapes,
         in_specs=[pl.BlockSpec(memory_space=space) for space in spaces],
-        out_specs=[pl.BlockSpec(memory_space=pltpu.VMEM)] * len(shapes),
-        scratch_shapes=scratch,
+        out_specs=[pl.BlockSpec(memory_space=out_space)] * len(shapes),
+        scratch_shapes=list(scratch),
         compiler_params=pltpu.CompilerParams(vmem_limit_bytes=24 * MIB),
         cost_estimate=pl.CostEstimate(flops=int(flops), bytes_accessed=int(nbytes), transcendentals=0),
         name=name,
@@ -419,18 +429,15 @@
     size = columns * rhs
     pack = (planes, 2, ROWS + FACE, 256)
     field = (planes, ROWS, size)
-    outs = [((planes, columns, ROWS, 256), BF), (pack, BF), (pack, BF), (field, F32), (field, F32)]
-    outs += [((planes, 2 * FACE, size), BF), ((2, 2, size, size), BF)]
+    outs = [((planes, columns, ROWS, 256), BF), (pack, BF), (field, F32), (field, BF), ((2, 2, size, size), BF)]
     operands = (inverse, couplings, right, initial, neighbours)
-    scratch = [
-        pltpu.VMEM(inverse.shape, BF),
-        pltpu.VMEM(right.shape, BF),
+    scratch = [pltpu.VMEM(x.shape, BF) for x in operands[:3]] + [
         pltpu.VMEM((2, columns, ROWS, 256), BF),
         pltpu.VMEM((2, columns, 256 + 2 * SLOT, 256), BF),
-        pltpu.VMEM((2, 3, 2, FACE * columns, 128), F32),
-        pltpu.SemaphoreType.DMA((2, planes)),
+        pltpu.VMEM((2, 9, 2, FACE * columns, 128), F32),
+        pltpu.SemaphoreType.DMA((3, planes)),
     ]
-    return call(weight_kernel, outs, operands, "weights", 1e10, (0, 2), scratch)
+    return call(weight_kernel, outs, operands, "weights", 1e10, (0, 1, 2), scratch)
 
 
 def ring(x, axis, by):
@@ -462,8 +469,8 @@
     from_low = ring(up, "cross", 1)
     from_high = ring(down, "cross", -1)
     from_above = shift(above, "sweep", -1)
-    known, lower, upper, base, fore, own, gathers = weights(
-        inverse_blocks.transpose(0, 2, 1, 3), couplings, right_sides, initial, beside
+    known, lower, base, own, gathers = weights(
+        inverse_blocks.transpose(0, 2, 1, 3), couplings.transpose(0, 2, 3, 1, 4), right_sides, initial, beside
     )
 
     field = (planes, ROWS, size)
@@ -473,7 +480,7 @@
     operand, start, traces, message, wide = call(
         functools.partial(forward_chain_kernel, rhs=rhs),
         chain_outs + [((FACE, size), BF), ((3 * FACE, size), BF)],
-        (from_low, from_high, from_above, own, gathers, up_sel, down_sel, known, lower, upper, fore),
+        (from_low, from_high, from_above, own, gathers, up_sel, down_sel, known, lower, base),
         "forward_chain",
     )
     three = shift(message, "sweep", 3)
@@ -481,7 +488,7 @@
     (rest,) = call(
         functools.partial(base_kernel, rows=slice(0, 2 * FACE), rhs=rhs),
         [(most, F32)],
-        (known, operand, fore, from_above, upper),
+        (known, operand, base),
         "forward_base",
     )
     middle, change, up, down = call(
@@ -492,10 +499,10 @@
     )
     from_low = ring(up, "cross", 1)
     from_high = ring(down, "cross", -1)
-    own, base = call(
+    own, base, upper = call(
         middle_kernel,
-        [((planes, 2 * FACE, size), BF), (field, F32)],
-        (middle, change, base, gathers, own_in),
+        [((planes, 2 * FACE, size), BF), (field, F32), (lower.shape, BF)],
+        (middle, change, base, gathers, own_in, known),
         "middle",
         2e9,
     )
@@ -519,6 +526,8 @@
         [(right_sides.shape, BF)],
         (one, two, three, *passes, start, rest, traces, upper, back),
         "backward_finish",
+        scratch=[pltpu.VMEM(right_sides.shape, BF), pltpu.SemaphoreType.DMA((planes,))],
+        out_space=pltpu.HBM,
     )
     return result
 

time: 52.6 us -> 50.4 us (0.958)
  local copies, waits for them, and re-layouts: 4.44 us -> 1.76 us
  Pallas kernels: 15.4 us -> 16.4 us
    unnamed x17 -> x14, local copies, waits for them, and re-layouts: 4.43 us -> 1.75 us
    pallas_call x9, Pallas kernels: 15.4 us -> 16.4 us  [call(): pl.pallas_call(kernel, out_shape=shapes, in_specs=[pl.BlockSpec(memory_sp...]
  transfers between devices with their start and end apart: 13 -> 13, of which waited for: 3 -> 3; matrix products, arithmetic and copies ran while one was open for 6% -> 0% of each run, Pallas kernels for 18% -> 21%
where the time goes in v8:
time: 50.4 us; the launch traced here: 50 us
  starting transfers between devices  28.3 us (56%)
  Pallas kernels  16.4 us (33%)
  waiting for transfers between devices  3.27 us (6%)
  local copies, waits for them, and re-layouts  1.76 us (3%)
    pallas_call x9, Pallas kernels, call(): pl.pallas_call(kernel, out_shape=shapes, in_specs=[pl.BlockSpec(memory_sp...  16.4 us
    ppermute x7, starting transfers between devices, shift(): lax.ppermute(x, axis, [(i, i + by) for i in range(n) if 0 <= i + by < n])  12.6 us
    ppermute x4, starting transfers between devices, ring(): return lax.ppermute(x, axis, [(i, (i + by) % n) for i in range(n)])  10.1 us
    ppermute x2, starting transfers between devices, products(): lax.ppermute(x, 'sweep', [(i, i + step) for i in inner if 0 <= i + step <...  5.68 us
    ppermute x7, waiting for transfers between devices, shift(): lax.ppermute(x, axis, [(i, i + by) for i in range(n) if 0 <= i + by < n])  3.25 us
    unnamed x14, local copies, waits for them, and re-layouts  1.75 us
  transfers between devices with their start and end apart: 13, of which 3 were waited for; matrix products, arithmetic and copies ran while one was open for 0% of the time, Pallas kernels for 21%

profile of v8, /device:TPU:1, one launch (start us, length us, event | category | flops | bytes accessed | tf_op | source)
XLA Modules:
  0.0 50.0 jit_solution(3555744095513606414)
XLA Ops:
  0.0 0.0 copy-start.4
  0.0 1.0 %copy-done.4 = bf16[4,8,32,135]{3,2,1,0:T(8,128)(2,1)S(1)} copy-done((bf16[4,8,32,135]{3,2,1,0:T(8,128)(2,1)S(1)}, bf16[4,8,32,135]{3,2,1,0:T(8,128)(2,1)}, u32[]{:S(2)}) %copy-start.4) | copy-done | bytes 276504
  1.0 0.5 %initial_traces.1 = (bf16[4,80,256]{2,1,0:T(8,128)(2,1)S(1)}, bf16[4,80,256]{2,1,0:T(8,128)(2,1)S(1)}, bf16[48,256]{1,0:T(8,128)(2,1)S(1)}) custom-call(bf16[4,8,32,135]{3,2,1,0:T(8,128)(2,1)S(1)} %copy-done.4), custom_call_target="tpu_custom_call" | custom-call | flops 200000000 | bytes 628736 | tf_op jit(solution)/shard_map/initial_traces/pallas_call | solution.py:407
  1.6 2.0 %collective-permute-start.2 = (bf16[48,256]{1,0:T(8,128)(2,1)S(1)}, bf16[48,256]{1,0:T(8,128)(2,1)S(1)}, u32[]{:S(2)}, u32[]{:S(2)}) collective-permute-start(bf16[48,256]{1,0:T(8,128)(2,1)S(1)} %get-tuple-element.40), channel_id=1, source_target_pairs={{8,0},{16,8},{24,16},{9,1},{17,9},{25,17},{10,2},{18,10},{26,18},{... | collective-permute-start | bytes 73736 | tf_op jit(solution)/shard_map/ppermute | solution.py:450
  3.5 2.7 %collective-permute-start = (bf16[4,80,256]{2,1,0:T(8,128)(2,1)S(1)}, bf16[4,80,256]{2,1,0:T(8,128)(2,1)S(1)}, u32[]{:S(2)}, u32[]{:S(2)}) collective-permute-start(bf16[4,80,256]{2,1,0:T(8,128)(2,1)S(1)} %get-tuple-element.38), channel_id=1, source_target_pairs={{0,1},{1,2},{2,3},{3,4},{4,5},{5,6},{6,7},{7,0},{8,9},{9,10},{10,1... | collective-permute-start | bytes 491528 | tf_op jit(solution)/shard_map/ppermute | solution.py:445
  6.3 3.1 %collective-permute-start.1 = (bf16[4,80,256]{2,1,0:T(8,128)(2,1)S(1)}, bf16[4,80,256]{2,1,0:T(8,128)(2,1)S(1)}, u32[]{:S(2)}, u32[]{:S(2)}) collective-permute-start(bf16[4,80,256]{2,1,0:T(8,128)(2,1)S(1)} %get-tuple-element.39), channel_id=1, source_target_pairs={{0,7},{1,0},{2,1},{3,2},{4,3},{5,4},{6,5},{7,6},{8,15},{9,8},{10,9... | collective-permute-start | bytes 491528 | tf_op jit(solution)/shard_map/ppermute | solution.py:445
  9.4 0.0 copy-start.5
  9.4 0.7 %copy-done.5 = s32[8,4]{0,1:T(4,128)S(1)} copy-done((s32[8,4]{0,1:T(4,128)S(1)}, s32[8,4]{0,1:T(4,128)}, u32[]{:S(2)}) %copy-start.5) | copy-done | bytes 152
  10.1 0.0 copy-start
  10.1 0.0 copy-start.1
  10.1 7.3 %weights.1 = (bf16[4,8,144,256]{3,2,1,0:T(8,128)(2,1)S(1)}, bf16[4,2,192,256]{3,2,1,0:T(8,128)(2,1)S(1)}, f32[4,144,256]{2,1,0:T(8,128)S(1)}, bf16[4,144,256]{2,...) custom-call(bf16[4,135,8,135]{3,2,1,0:T(8,128)(2,1)} %bitcast.7, bf16[4,6,45,8,135]{4,3,2,1,0:T(8,128)(2,1)} %bitcast.6, ...), custom_call_target="tpu_custom_call" | custom-call | flops 10000000000 | bytes 8607040 | tf_op jit(solution)/shard_map/weights/pallas_call | solution.py:407
  17.3 0.0 collective-permute-done.2.above
  17.3 0.0 collective-permute-done.up
  17.4 0.0 collective-permute-done.1.down
  17.4 0.0 copy-done
  17.4 0.0 copy-done.1
  17.4 1.2 %forward_chain.1 = (bf16[4,256,256]{2,1,0:T(8,128)(2,1)S(1)}, f32[4,48,256]{2,1,0:T(8,128)S(1)}, f32[4,48,256]{2,1,0:T(8,128)S(1)}, bf16[48,256]{1,0:T(8,128)(2,1)S(1)}, bf16[144,256]{1,0:T(8,128)(2,1)S(1)}) custom-call(bf16[4,80,256]{2,1,0:T(8,128)(2,1)S(1)} %collective-permute-done.up, bf16[4,80,256]{2,1,0:T(8,128)(2,1)S(1)} %collective-permute-done.1.down, ...), custom_call_target="tpu_custom_call" | custom-call | flops 200000000 | bytes 5953536 | tf_op jit(solution)/shard_map/forward_chain/pallas_call | solution.py:407
  18.6 0.0 copy-start.2
  18.6 3.3 %collective-permute-start.4 = (bf16[144,256]{1,0:T(8,128)(2,1)S(1)}, bf16[144,256]{1,0:T(8,128)(2,1)S(1)}, u32[]{:S(2)}, u32[]{:S(2)}) collective-permute-start(bf16[144,256]{1,0:T(8,128)(2,1)S(1)} %get-tuple-element.47), channel_id=1, source_target_pairs={{0,16},{8,24},{1,17},{9,25},{2,18},{10,26},{3,19},{11,27},{4,20},{... | collective-permute-start | bytes 221192 | tf_op jit(solution)/shard_map/ppermute | solution.py:450
  21.9 1.9 %collective-permute-start.3 = (bf16[144,256]{1,0:T(8,128)(2,1)S(1)}, bf16[144,256]{1,0:T(8,128)(2,1)S(1)}, u32[]{:S(2)}, u32[]{:S(2)}) collective-permute-start(bf16[144,256]{1,0:T(8,128)(2,1)S(1)} %get-tuple-element.47), channel_id=1, source_target_pairs={{0,8},{8,16},{16,24},{1,9},{9,17},{17,25},{2,10},{10,18},{18,26},{... | collective-permute-start | bytes 221192 | tf_op jit(solution)/shard_map/ppermute | solution.py:450
  23.9 0.7 %collective-permute-start.5 = (bf16[48,256]{1,0:T(8,128)(2,1)S(1)}, bf16[48,256]{1,0:T(8,128)(2,1)S(1)}, u32[]{:S(2)}, u32[]{:S(2)}) collective-permute-start(bf16[48,256]{1,0:T(8,128)(2,1)S(1)} %get-tuple-element.48), channel_id=1, source_target_pairs={{0,24},{1,25},{2,26},{3,27},{4,28},{5,29},{6,30},{7,31}} | collective-permute-start | bytes 73736 | tf_op jit(solution)/shard_map/ppermute | solution.py:450
  24.5 0.0 copy-start.6
  24.5 0.6 %forward_base.1.rest = f32[4,96,256]{2,1,0:T(8,128)S(1)} custom-call(bf16[4,8,144,256]{3,2,1,0:T(8,128)(2,1)S(1)} %get-tuple-element.44.known, bf16[4,256,256]{2,1,0:T(8,128)(2,1)S(1)} %get-tuple-element.50.operand, f32[4,144,256]{2,1,0:T(8,128)S(1)} %get-tuple-element.46.base), custom_call_target="tpu_custom_call" | custom-call | flops 200000000 | bytes 3866624 | tf_op jit(solution)/shard_map/forward_base/pallas_call | solution.py:407
  25.1 0.0 collective-permute-done.5.three
  25.1 0.0 collective-permute-done.4.two
  25.1 0.1 collective-permute-done.3.one
  25.2 0.0 copy-done.2
  25.2 1.6 %forward_finish.1 = (bf16[4,144,256]{2,1,0:T(8,128)(2,1)S(1)}, f32[4,144,256]{2,1,0:T(8,128)S(1)}, bf16[4,80,256]{2,1,0:T(8,128)(2,1)S(1)}, bf16[4,80,256]{2,1,0:T(8,128)(2,1)S(1)}) custom-call(bf16[144,256]{1,0:T(8,128)(2,1)S(1)} %collective-permute-done.3.one, bf16[144,256]{1,0:T(8,128)(2,1)S(1)} %collective-permute-done.4.two, ...), custom_call_target="tpu_custom_call" | custom-call | flops 200000000 | bytes 3003392 | tf_op jit(solution)/shard_map/forward_finish/pallas_call | solution.py:407
  26.8 0.1 collective-permute-start.6
  26.9 4.1 %collective-permute-start.7 = (bf16[4,80,256]{2,1,0:T(8,128)(2,1)S(1)}, bf16[4,80,256]{2,1,0:T(8,128)(2,1)S(1)}, u32[]{:S(2)}, u32[]{:S(2)}) collective-permute-start(bf16[4,80,256]{2,1,0:T(8,128)(2,1)S(1)} %get-tuple-element.53), channel_id=1, source_target_pairs={{0,7},{1,0},{2,1},{3,2},{4,3},{5,4},{6,5},{7,6},{8,15},{9,8},{10,9... | collective-permute-start | bytes 491528 | tf_op jit(solution)/shard_map/ppermute | solution.py:445
  31.1 0.0 copy-done.6
  31.1 0.8 %middle.1 = (bf16[4,96,256]{2,1,0:T(8,128)(2,1)S(1)}, f32[4,144,256]{2,1,0:T(8,128)S(1)}, bf16[4,2,192,256]{3,2,1,0:T(8,128)(2,1)S(1)}) custom-call(bf16[4,144,256]{2,1,0:T(8,128)(2,1)S(1)} %get-tuple-element.54.middle, f32[4,144,256]{2,1,0:T(8,128)S(1)} %get-tuple-element.55.change, f32[4,144,256]{2,1,0:T(8,128)S(1)} %get-tuple-element.46.base, ...), custom_call_target="tpu_custom_call" | custom-call | flops 2000000000 | bytes 5958656 | tf_op jit(solution)/shard_map/middle/pallas_call | solution.py:407
  31.9 0.7 %collective-permute-start.12 = (bf16[2,48,256]{2,1,0:T(8,128)(2,1)S(1)}, bf16[2,48,256]{2,1,0:T(8,128)(2,1)S(1)}, u32[]{:S(2)}, u32[]{:S(2)}) collective-permute-start(bf16[2,48,256]{2,1,0:T(8,128)(2,1)S(1)} %slice_bitcast_fusion), channel_id=1, source_target_pairs={{16,0},{17,1},{18,2},{19,3},{20,4},{21,5},{22,6},{23,7}} | collective-permute-start | bytes 147464 | tf_op jit(solution)/shard_map/ppermute | solution.py:423
  32.6 5.0 %collective-permute-start.11 = (bf16[2,48,256]{2,1,0:T(8,128)(2,1)S(1)}, bf16[2,48,256]{2,1,0:T(8,128)(2,1)S(1)}, u32[]{:S(2)}, u32[]{:S(2)}) collective-permute-start(bf16[2,48,256]{2,1,0:T(8,128)(2,1)S(1)} %slice_bitcast_fusion), channel_id=1, source_target_pairs={{8,0},{16,8},{9,1},{17,9},{10,2},{18,10},{11,3},{19,11},{12,4},{20... | collective-permute-start | bytes 147464 | tf_op jit(solution)/shard_map/ppermute | solution.py:423
  37.6 0.0 collective-permute-done.6.up
  37.6 0.0 collective-permute-done.7.down
  37.6 1.1 %backward_chain.1 = (bf16[4,256,256]{2,1,0:T(8,128)(2,1)S(1)}, f32[4,48,256]{2,1,0:T(8,128)S(1)}, f32[4,48,256]{2,1,0:T(8,128)S(1)}, bf16[48,256]{1,0:T(8,128)(2,1)S(1)}) custom-call(bf16[4,80,256]{2,1,0:T(8,128)(2,1)S(1)} %collective-permute-done.6.up, bf16[4,80,256]{2,1,0:T(8,128)(2,1)S(1)} %collective-permute-done.7.down, ...), custom_call_target="tpu_custom_call" | custom-call | flops 200000000 | bytes 5756928 | tf_op jit(solution)/shard_map/backward_chain/pallas_call | solution.py:407
  38.7 0.0 copy-start.3
  38.7 0.8 %collective-permute-start.10 = (bf16[48,256]{1,0:T(8,128)(2,1)S(1)}, bf16[48,256]{1,0:T(8,128)(2,1)S(1)}, u32[]{:S(2)}, u32[]{:S(2)}) collective-permute-start(bf16[48,256]{1,0:T(8,128)(2,1)S(1)} %get-tuple-element.60), channel_id=1, source_target_pairs={{24,0},{25,1},{26,2},{27,3},{28,4},{29,5},{30,6},{31,7}} | collective-permute-start | bytes 73736 | tf_op jit(solution)/shard_map/ppermute | solution.py:450
  39.5 1.3 %collective-permute-start.9 = (bf16[48,256]{1,0:T(8,128)(2,1)S(1)}, bf16[48,256]{1,0:T(8,128)(2,1)S(1)}, u32[]{:S(2)}, u32[]{:S(2)}) collective-permute-start(bf16[48,256]{1,0:T(8,128)(2,1)S(1)} %get-tuple-element.60), channel_id=1, source_target_pairs={{16,0},{24,8},{17,1},{25,9},{18,2},{26,10},{19,3},{27,11},{20,4},{... | collective-permute-start | bytes 73736 | tf_op jit(solution)/shard_map/ppermute | solution.py:450
  40.8 2.6 %collective-permute-start.8 = (bf16[48,256]{1,0:T(8,128)(2,1)S(1)}, bf16[48,256]{1,0:T(8,128)(2,1)S(1)}, u32[]{:S(2)}, u32[]{:S(2)}) collective-permute-start(bf16[48,256]{1,0:T(8,128)(2,1)S(1)} %get-tuple-element.60), channel_id=1, source_target_pairs={{8,0},{16,8},{24,16},{9,1},{17,9},{25,17},{10,2},{18,10},{26,18},{... | collective-permute-start | bytes 73736 | tf_op jit(solution)/shard_map/ppermute | solution.py:450
  43.5 0.6 %backward_base.1.rest = f32[4,96,256]{2,1,0:T(8,128)S(1)} custom-call(bf16[4,8,144,256]{3,2,1,0:T(8,128)(2,1)S(1)} %get-tuple-element.44.known, bf16[4,256,256]{2,1,0:T(8,128)(2,1)S(1)} %get-tuple-element.63.operand, f32[4,144,256]{2,1,0:T(8,128)S(1)} %get-tuple-element.59.base), custom_call_target="tpu_custom_call" | custom-call | flops 200000000 | bytes 3866624 | tf_op jit(solution)/shard_map/backward_base/pallas_call | solution.py:407
  44.0 0.0 collective-permute-done.12.next_near
  44.1 0.0 collective-permute-done.11.near
  44.1 0.0 collective-permute-done.10.three
  44.1 0.6 %collective-permute-done.9.two = bf16[48,256]{1,0:T(8,128)(2,1)S(1)} collective-permute-done((bf16[48,256]{1,0:T(8,128)(2,1)S(1)}, bf16[48,256]{1,0:T(8,128)(2,1)S(1)}, u32[]{:S(2)}, u32[]{:S(2)}) %collective-permute-start.9) | collective-permute-done | bytes 24608 | tf_op jit(solution)/shard_map/ppermute | solution.py:450
  44.7 2.5 %collective-permute-done.8.one = bf16[48,256]{1,0:T(8,128)(2,1)S(1)} collective-permute-done((bf16[48,256]{1,0:T(8,128)(2,1)S(1)}, bf16[48,256]{1,0:T(8,128)(2,1)S(1)}, u32[]{:S(2)}, u32[]{:S(2)}) %collective-permute-start.8) | collective-permute-done | bytes 24608 | tf_op jit(solution)/shard_map/ppermute | solution.py:450
  47.2 0.0 copy-done.3
  47.2 2.8 %backward_finish.1 = bf16[4,8,32,135]{3,2,1,0:T(8,128)(2,1)} custom-call(bf16[48,256]{1,0:T(8,128)(2,1)S(1)} %collective-permute-done.8.one, bf16[48,256]{1,0:T(8,128)(2,1)S(1)} %collective-permute-done.9.two, bf16[48,256]{1,0:T(8,128)(2,1)S(1)} %collective-permute-done.10.three, bf16[2,48,256]{2,1,0:T(8,128)(2,1)S(1)} %collective-permute-done.11.near, ...), custom_call_target="tpu_custom_call" | custom-call | flops 200000000 | bytes 2060256 | tf_op jit(solution)/shard_map/backward_finish/pallas_call | solution.py:407
  (1 shorter events, 0.0 us)
Async XLA Ops:
  0.0 1.0 %copy-start.4 = (bf16[4,8,32,135]{3,2,1,0:T(8,128)(2,1)S(1)}, bf16[4,8,32,135]{3,2,1,0:T(8,128)(2,1)}, u32[]{:S(2)}) copy-start(bf16[4,8,32,135]{3,2,1,0:T(8,128)(2,1)} %initial.2) | copy-start | bytes 829444
  1.6 15.8 %collective-permute-start.2 = (bf16[48,256]{1,0:T(8,128)(2,1)S(1)}, bf16[48,256]{1,0:T(8,128)(2,1)S(1)}, u32[]{:S(2)}, u32[]{:S(2)}) collective-permute-start(bf16[48,256]{1,0:T(8,128)(2,1)S(1)} %get-tuple-element.40), channel_id=1, source_target_pairs={{8,0},{16,8},{24,16},{9,1},{17,9},{25,17},{10,2},{18,10},{26,18},{... | collective-permute-start | bytes 73736 | tf_op jit(solution)/shard_map/ppermute | solution.py:450
  3.5 13.8 %collective-permute-start = (bf16[4,80,256]{2,1,0:T(8,128)(2,1)S(1)}, bf16[4,80,256]{2,1,0:T(8,128)(2,1)S(1)}, u32[]{:S(2)}, u32[]{:S(2)}) collective-permute-start(bf16[4,80,256]{2,1,0:T(8,128)(2,1)S(1)} %get-tuple-element.38), channel_id=1, source_target_pairs={{0,1},{1,2},{2,3},{3,4},{4,5},{5,6},{6,7},{7,0},{8,9},{9,10},{10,1... | collective-permute-start | bytes 491528 | tf_op jit(solution)/shard_map/ppermute | solution.py:445
  6.3 11.1 %collective-permute-start.1 = (bf16[4,80,256]{2,1,0:T(8,128)(2,1)S(1)}, bf16[4,80,256]{2,1,0:T(8,128)(2,1)S(1)}, u32[]{:S(2)}, u32[]{:S(2)}) collective-permute-start(bf16[4,80,256]{2,1,0:T(8,128)(2,1)S(1)} %get-tuple-element.39), channel_id=1, source_target_pairs={{0,7},{1,0},{2,1},{3,2},{4,3},{5,4},{6,5},{7,6},{8,15},{9,8},{10,9... | collective-permute-start | bytes 491528 | tf_op jit(solution)/shard_map/ppermute | solution.py:445
  9.4 0.7 %copy-start.5 = (s32[8,4]{0,1:T(4,128)S(1)}, s32[8,4]{0,1:T(4,128)}, u32[]{:S(2)}) copy-start(s32[8,4]{0,1:T(4,128)} %param.14) | copy-start | bytes 388
  10.1 7.3 %copy-start = (bf16[96,80]{1,0:T(8,128)(2,1)S(1)}, bf16[96,80]{1,0:T(8,128)(2,1)}, u32[]{:S(2)}) copy-start(bf16[96,80]{1,0:T(8,128)(2,1)} %constant.14.clone.down_sel) | copy-start | bytes 46084
  10.1 7.3 %copy-start.1 = (bf16[96,80]{1,0:T(8,128)(2,1)S(1)}, bf16[96,80]{1,0:T(8,128)(2,1)}, u32[]{:S(2)}) copy-start(bf16[96,80]{1,0:T(8,128)(2,1)} %constant.13.clone.up_sel) | copy-start | bytes 46084
  18.6 6.6 %copy-start.2 = (bf16[160,144]{1,0:T(8,128)(2,1)S(1)}, bf16[160,144]{1,0:T(8,128)(2,1)}, u32[]{:S(2)}) copy-start(bf16[160,144]{1,0:T(8,128)(2,1)} %constant.10.clone.send) | copy-start | bytes 138244
  18.6 6.5 %collective-permute-start.4 = (bf16[144,256]{1,0:T(8,128)(2,1)S(1)}, bf16[144,256]{1,0:T(8,128)(2,1)S(1)}, u32[]{:S(2)}, u32[]{:S(2)}) collective-permute-start(bf16[144,256]{1,0:T(8,128)(2,1)S(1)} %get-tuple-element.47), channel_id=1, source_target_pairs={{0,16},{8,24},{1,17},{9,25},{2,18},{10,26},{3,19},{11,27},{4,20},{... | collective-permute-start | bytes 221192 | tf_op jit(solution)/shard_map/ppermute | solution.py:450
  21.9 3.3 %collective-permute-start.3 = (bf16[144,256]{1,0:T(8,128)(2,1)S(1)}, bf16[144,256]{1,0:T(8,128)(2,1)S(1)}, u32[]{:S(2)}, u32[]{:S(2)}) collective-permute-start(bf16[144,256]{1,0:T(8,128)(2,1)S(1)} %get-tuple-element.47), channel_id=1, source_target_pairs={{0,8},{8,16},{16,24},{1,9},{9,17},{17,25},{2,10},{10,18},{18,26},{... | collective-permute-start | bytes 221192 | tf_op jit(solution)/shard_map/ppermute | solution.py:450
  23.9 1.3 %collective-permute-start.5 = (bf16[48,256]{1,0:T(8,128)(2,1)S(1)}, bf16[48,256]{1,0:T(8,128)(2,1)S(1)}, u32[]{:S(2)}, u32[]{:S(2)}) collective-permute-start(bf16[48,256]{1,0:T(8,128)(2,1)S(1)} %get-tuple-element.48), channel_id=1, source_target_pairs={{0,24},{1,25},{2,26},{3,27},{4,28},{5,29},{6,30},{7,31}} | collective-permute-start | bytes 73736 | tf_op jit(solution)/shard_map/ppermute | solution.py:450
  24.5 6.5 %copy-start.6 = (bf16[96,144]{1,0:T(8,128)(2,1)S(1)}, bf16[96,144]{1,0:T(8,128)(2,1)}, u32[]{:S(2)}) copy-start(bf16[96,144]{1,0:T(8,128)(2,1)} %constant.11.clone.own_sel) | copy-start | bytes 82948
  26.8 10.7 %collective-permute-start.6 = (bf16[4,80,256]{2,1,0:T(8,128)(2,1)S(1)}, bf16[4,80,256]{2,1,0:T(8,128)(2,1)S(1)}, u32[]{:S(2)}, u32[]{:S(2)}) collective-permute-start(bf16[4,80,256]{2,1,0:T(8,128)(2,1)S(1)} %get-tuple-element.52), channel_id=1, source_target_pairs={{0,1},{1,2},{2,3},{3,4},{4,5},{5,6},{6,7},{7,0},{8,9},{9,10},{10,1... | collective-permute-start | bytes 491528 | tf_op jit(solution)/shard_map/ppermute | solution.py:445
  26.9 10.7 %collective-permute-start.7 = (bf16[4,80,256]{2,1,0:T(8,128)(2,1)S(1)}, bf16[4,80,256]{2,1,0:T(8,128)(2,1)S(1)}, u32[]{:S(2)}, u32[]{:S(2)}) collective-permute-start(bf16[4,80,256]{2,1,0:T(8,128)(2,1)S(1)} %get-tuple-element.53), channel_id=1, source_target_pairs={{0,7},{1,0},{2,1},{3,2},{4,3},{5,4},{6,5},{7,6},{8,15},{9,8},{10,9... | collective-permute-start | bytes 491528 | tf_op jit(solution)/shard_map/ppermute | solution.py:445
  31.9 12.2 %collective-permute-start.12 = (bf16[2,48,256]{2,1,0:T(8,128)(2,1)S(1)}, bf16[2,48,256]{2,1,0:T(8,128)(2,1)S(1)}, u32[]{:S(2)}, u32[]{:S(2)}) collective-permute-start(bf16[2,48,256]{2,1,0:T(8,128)(2,1)S(1)} %slice_bitcast_fusion), channel_id=1, source_target_pairs={{16,0},{17,1},{18,2},{19,3},{20,4},{21,5},{22,6},{23,7}} | collective-permute-start | bytes 147464 | tf_op jit(solution)/shard_map/ppermute | solution.py:423
  32.6 11.5 %collective-permute-start.11 = (bf16[2,48,256]{2,1,0:T(8,128)(2,1)S(1)}, bf16[2,48,256]{2,1,0:T(8,128)(2,1)S(1)}, u32[]{:S(2)}, u32[]{:S(2)}) collective-permute-start(bf16[2,48,256]{2,1,0:T(8,128)(2,1)S(1)} %slice_bitcast_fusion), channel_id=1, source_target_pairs={{8,0},{16,8},{9,1},{17,9},{10,2},{18,10},{11,3},{19,11},{12,4},{20... | collective-permute-start | bytes 147464 | tf_op jit(solution)/shard_map/ppermute | solution.py:423
  38.7 8.5 %copy-start.3 = (bf16[135,144]{1,0:T(8,128)(2,1)S(1)}, bf16[135,144]{1,0:T(8,128)(2,1)}, u32[]{:S(2)}) copy-start(bf16[135,144]{1,0:T(8,128)(2,1)} %constant.12.clone.back) | copy-start | bytes 116644
  38.7 5.3 %collective-permute-start.10 = (bf16[48,256]{1,0:T(8,128)(2,1)S(1)}, bf16[48,256]{1,0:T(8,128)(2,1)S(1)}, u32[]{:S(2)}, u32[]{:S(2)}) collective-permute-start(bf16[48,256]{1,0:T(8,128)(2,1)S(1)} %get-tuple-element.60), channel_id=1, source_target_pairs={{24,0},{25,1},{26,2},{27,3},{28,4},{29,5},{30,6},{31,7}} | collective-permute-start | bytes 73736 | tf_op jit(solution)/shard_map/ppermute | solution.py:450
  39.5 5.2 %collective-permute-start.9 = (bf16[48,256]{1,0:T(8,128)(2,1)S(1)}, bf16[48,256]{1,0:T(8,128)(2,1)S(1)}, u32[]{:S(2)}, u32[]{:S(2)}) collective-permute-start(bf16[48,256]{1,0:T(8,128)(2,1)S(1)} %get-tuple-element.60), channel_id=1, source_target_pairs={{16,0},{24,8},{17,1},{25,9},{18,2},{26,10},{19,3},{27,11},{20,4},{... | collective-permute-start | bytes 73736 | tf_op jit(solution)/shard_map/ppermute | solution.py:450
  40.8 6.4 %collective-permute-start.8 = (bf16[48,256]{1,0:T(8,128)(2,1)S(1)}, bf16[48,256]{1,0:T(8,128)(2,1)S(1)}, u32[]{:S(2)}, u32[]{:S(2)}) collective-permute-start(bf16[48,256]{1,0:T(8,128)(2,1)S(1)} %get-tuple-element.60), channel_id=1, source_target_pairs={{8,0},{16,8},{24,16},{9,1},{17,9},{25,17},{10,2},{18,10},{26,18},{... | collective-permute-start | bytes 73736 | tf_op jit(solution)/shard_map/ppermute | solution.py:450

commit v9 on v8

--- a/solution.py
+++ b/solution.py
@@ -276,7 +276,7 @@
 
 def chain_kernel(known, base, matrix, received, own, gathers, outs, order, rows, rhs, above=None):
     up, down, up_sel, down_sel = received
-    operand, start, traces, message, *wide = outs
+    operand, start, traces, message = outs
     planes, columns = known.shape[:2]
     size = operand.shape[2]
     wholes = gathered(up, down, own, up_sel, down_sel, gathers)
@@ -293,11 +293,10 @@
         start[p] = value
         trace = value if trace is None else value + chain_step(matrix.at[p], trace, rhs, rows)
         traces[p] = trace
-    message[...] = trace.astype(BF)
-    for both in wide:
-        both[FIRST] = trace.astype(BF)
+    message[FIRST] = trace.astype(BF)
+    if message.shape[0] > FACE:
         for h in range(2):
-            both[(1 + h) * FACE : (2 + h) * FACE] = matrix[order[-1], h, PRODUCT]
+            message[(1 + h) * FACE : (2 + h) * FACE] = matrix[order[-1], h, PRODUCT]
 
 
 def base_kernel(known, operand, base, out, *, rows, rhs):
@@ -318,25 +317,28 @@
     chain_kernel(known, base, upper, received, own, gathers, outs, order, FIRST, rhs)
 
 
-def incoming(one, two, three, near, next_near, rhs):
-    def carried(product, trace):
-        half = trace.shape[1] // 2
-        halves = [trace[:, h * half : (h + 1) * half] for h in range(2)]
-        return jnp.concatenate([mm(m, split_lanes(t, rhs)) for m, t in zip(product, halves)], 1)
-
-    trace = two[FIRST].astype(F32) + carried(next_near, three[FIRST])
-    return one[FIRST].astype(F32) + carried(near, trace)
-
-
-def inside(message):
-    return [message[(1 + h) * FACE : (2 + h) * FACE] for h in range(2)]
+def incoming(messages, products, forward, rhs):
+    here = lax.axis_index("sweep")
+    n = messages.shape[0]
+    trace = None
+    for i in range(n - 1) if forward else range(n - 1, 0, -1):
+        value = messages[i, FIRST].astype(F32)
+        if trace is None:
+            trace = jnp.zeros_like(value)
+        else:
+            half = value.shape[1] // 2
+            halves = [trace[:, h * half : (h + 1) * half] for h in range(2)]
+            value = value + jnp.concatenate([mm(m, split_lanes(t, rhs)) for m, t in zip(products(i), halves)], 1)
+        trace = jnp.where(i < here if forward else i > here, value, trace)
+    return trace
 
 
 def forward_finish_kernel(
-    one, two, three, start, rest, traces, lower, send, middle, change, up, down, *, rhs
+    messages, start, rest, traces, lower, send, middle, change, up, down, *, rhs
 ):
     planes = start.shape[0]
-    entry = incoming(one, two, three, inside(one), inside(two), rhs)
+    inside = lambda i: [messages[i, (1 + h) * FACE : (2 + h) * FACE] for h in range(2)]
+    entry = incoming(messages, inside, True, rhs)
     trace = entry
     for p in range(planes):
         delta = chain_step(lower.at[p], trace, rhs, FULL)
@@ -373,10 +375,12 @@
 
 
 def backward_finish_kernel(
-    one, two, three, near, next_near, start, rest, traces, upper, back, result, results, sem, *, rhs
+    messages, near, next_near, start, rest, traces, upper, back, result, results, sem, *, rhs
 ):
     planes = start.shape[0]
-    entry = incoming(one, two, three, [near[0], near[1]], [next_near[0], next_near[1]], rhs)
+    here = lax.axis_index("sweep")
+    beside = lambda i: [jnp.where(here + 1 == i, near[h], next_near[h]) for h in range(2)]
+    entry = incoming(messages, beside, False, rhs)
     size = entry.shape[1]
     row = lax.broadcasted_iota(jnp.int32, (size, size), 0)
     column = lax.broadcasted_iota(jnp.int32, (size, size), 1)
@@ -477,14 +481,13 @@
     trace = (planes, FACE, size)
     most = (planes, 2 * FACE, size)
     chain_outs = [((planes, 256, size), BF), (trace, F32), (trace, F32)]
-    operand, start, traces, message, wide = call(
+    operand, start, traces, message = call(
         functools.partial(forward_chain_kernel, rhs=rhs),
-        chain_outs + [((FACE, size), BF), ((3 * FACE, size), BF)],
+        chain_outs + [((3 * FACE, size), BF)],
         (from_low, from_high, from_above, own, gathers, up_sel, down_sel, known, lower, base),
         "forward_chain",
     )
-    three = shift(message, "sweep", 3)
-    two, one = (shift(wide, "sweep", by) for by in (2, 1))
+    messages = lax.all_gather(message, "sweep")
     (rest,) = call(
         functools.partial(base_kernel, rows=slice(0, 2 * FACE), rhs=rhs),
         [(most, F32)],
@@ -494,7 +497,7 @@
     middle, change, up, down = call(
         functools.partial(forward_finish_kernel, rhs=rhs),
         [(field, BF), (field, F32), (share, BF), (share, BF)],
-        (one, two, three, start, rest, traces, lower, send_in),
+        (messages, start, rest, traces, lower, send_in),
         "forward_finish",
     )
     from_low = ring(up, "cross", 1)
@@ -514,7 +517,7 @@
         (from_low, from_high, own, gathers, up_sel, down_sel, known, upper, base),
         "backward_chain",
     )
-    three, two, one = (shift(message, "sweep", -by) for by in (3, 2, 1))
+    messages = lax.all_gather(message, "sweep")
     (rest,) = call(
         functools.partial(base_kernel, rows=slice(FACE, ROWS), rhs=rhs),
         [(most, F32)],
@@ -524,7 +527,7 @@
     (result,) = call(
         functools.partial(backward_finish_kernel, rhs=rhs),
         [(right_sides.shape, BF)],
-        (one, two, three, *passes, start, rest, traces, upper, back),
+        (messages, *passes, start, rest, traces, upper, back),
         "backward_finish",
         scratch=[pltpu.VMEM(right_sides.shape, BF), pltpu.SemaphoreType.DMA((planes,))],
         out_space=pltpu.HBM,

time: 50.4 us -> 47.4 us (0.940)
  blocking collectives: 0 us -> 12.4 us
  starting transfers between devices: 28.3 us -> 15.9 us
  waiting for transfers between devices: 3.27 us -> 0.28 us
    all_gather x0 -> x2, blocking collectives: none -> 12.4 us  [local(): messages = lax.all_gather(message, 'sweep')]
    ppermute x7 -> x1, starting transfers between devices: 12.6 us -> 1.97 us  [shift(): lax.ppermute(x, axis, [(i, i + by) for i in range(n) if 0 <= i + by < n])]
    ppermute x7 -> x1, waiting for transfers between devices: 3.25 us -> 0.01 us  [shift(): lax.ppermute(x, axis, [(i, i + by) for i in range(n) if 0 <= i + by < n])]
    ppermute x2, starting transfers between devices: 5.68 us -> 3.93 us  [products(): lax.ppermute(x, 'sweep', [(i, i + step) for i in inner if 0 <= i + step <...]
  transfers between devices with their start and end apart: 13 -> 7, of which waited for: 3 -> 1; matrix products, arithmetic and copies ran while one was open for 0% -> 0% of each run, Pallas kernels for 21% -> 21%
where the time goes in v9:
time: 47.4 us; the launch traced here: 47 us
  Pallas kernels  16.5 us (35%)
  starting transfers between devices  15.9 us (34%)
  blocking collectives  12.4 us (26%)
  local copies, waits for them, and re-layouts  1.75 us (4%)
    pallas_call x9, Pallas kernels, call(): pl.pallas_call(kernel, out_shape=shapes, in_specs=[pl.BlockSpec(memory_sp...  16.5 us
    all_gather x2, blocking collectives, local(): messages = lax.all_gather(message, 'sweep')  12.4 us
    ppermute x4, starting transfers between devices, ring(): return lax.ppermute(x, axis, [(i, (i + by) % n) for i in range(n)])  10.1 us
    ppermute x2, starting transfers between devices, products(): lax.ppermute(x, 'sweep', [(i, i + step) for i in inner if 0 <= i + step <...  3.93 us
    ppermute x1, starting transfers between devices, shift(): lax.ppermute(x, axis, [(i, i + by) for i in range(n) if 0 <= i + by < n])  1.97 us
    unnamed x14, local copies, waits for them, and re-layouts  1.75 us
  transfers between devices with their start and end apart: 7, of which 1 were waited for; matrix products, arithmetic and copies ran while one was open for 0% of the time, Pallas kernels for 21%

profile of v9, /device:TPU:1, one launch (start us, length us, event | category | flops | bytes accessed | tf_op | source)
XLA Modules:
  0.0 47.0 jit_solution(16936855332978157728)
XLA Ops:
  0.0 0.0 copy-start.4
  0.0 1.0 %copy-done.4 = bf16[4,8,32,135]{3,2,1,0:T(8,128)(2,1)S(1)} copy-done((bf16[4,8,32,135]{3,2,1,0:T(8,128)(2,1)S(1)}, bf16[4,8,32,135]{3,2,1,0:T(8,128)(2,1)}, u32[]{:S(2)}) %copy-start.4) | copy-done | bytes 276504
  1.0 0.5 %initial_traces.1 = (bf16[4,80,256]{2,1,0:T(8,128)(2,1)S(1)}, bf16[4,80,256]{2,1,0:T(8,128)(2,1)S(1)}, bf16[48,256]{1,0:T(8,128)(2,1)S(1)}) custom-call(bf16[4,8,32,135]{3,2,1,0:T(8,128)(2,1)S(1)} %copy-done.4), custom_call_target="tpu_custom_call" | custom-call | flops 200000000 | bytes 628736 | tf_op jit(solution)/shard_map/initial_traces/pallas_call | solution.py:411
  1.6 2.0 %collective-permute-start.2 = (bf16[48,256]{1,0:T(8,128)(2,1)S(1)}, bf16[48,256]{1,0:T(8,128)(2,1)S(1)}, u32[]{:S(2)}, u32[]{:S(2)}) collective-permute-start(bf16[48,256]{1,0:T(8,128)(2,1)S(1)} %get-tuple-element.39), channel_id=1, source_target_pairs={{8,0},{16,8},{24,16},{9,1},{17,9},{25,17},{10,2},{18,10},{26,18},{... | collective-permute-start | bytes 73736 | tf_op jit(solution)/shard_map/ppermute | solution.py:454
  3.5 2.7 %collective-permute-start = (bf16[4,80,256]{2,1,0:T(8,128)(2,1)S(1)}, bf16[4,80,256]{2,1,0:T(8,128)(2,1)S(1)}, u32[]{:S(2)}, u32[]{:S(2)}) collective-permute-start(bf16[4,80,256]{2,1,0:T(8,128)(2,1)S(1)} %get-tuple-element.37), channel_id=1, source_target_pairs={{0,1},{1,2},{2,3},{3,4},{4,5},{5,6},{6,7},{7,0},{8,9},{9,10},{10,1... | collective-permute-start | bytes 491528 | tf_op jit(solution)/shard_map/ppermute | solution.py:449
  6.3 3.1 %collective-permute-start.1 = (bf16[4,80,256]{2,1,0:T(8,128)(2,1)S(1)}, bf16[4,80,256]{2,1,0:T(8,128)(2,1)S(1)}, u32[]{:S(2)}, u32[]{:S(2)}) collective-permute-start(bf16[4,80,256]{2,1,0:T(8,128)(2,1)S(1)} %get-tuple-element.38), channel_id=1, source_target_pairs={{0,7},{1,0},{2,1},{3,2},{4,3},{5,4},{6,5},{7,6},{8,15},{9,8},{10,9... | collective-permute-start | bytes 491528 | tf_op jit(solution)/shard_map/ppermute | solution.py:449
  9.4 0.0 copy-start.5
  9.4 0.7 %copy-done.5 = s32[8,4]{0,1:T(4,128)S(1)} copy-done((s32[8,4]{0,1:T(4,128)S(1)}, s32[8,4]{0,1:T(4,128)}, u32[]{:S(2)}) %copy-start.5) | copy-done | bytes 152
  10.1 0.0 copy-start
  10.1 0.0 copy-start.1
  10.1 7.3 %weights.1 = (bf16[4,8,144,256]{3,2,1,0:T(8,128)(2,1)S(1)}, bf16[4,2,192,256]{3,2,1,0:T(8,128)(2,1)S(1)}, f32[4,144,256]{2,1,0:T(8,128)S(1)}, bf16[4,144,256]{2,...) custom-call(bf16[4,135,8,135]{3,2,1,0:T(8,128)(2,1)} %bitcast.11, bf16[4,6,45,8,135]{4,3,2,1,0:T(8,128)(2,1)} %bitcast.10, ...), custom_call_target="tpu_custom_call" | custom-call | flops 10000000000 | bytes 8607040 | tf_op jit(solution)/shard_map/weights/pallas_call | solution.py:411
  17.3 0.0 collective-permute-done.2.above
  17.3 0.0 collective-permute-done.up
  17.4 0.0 collective-permute-done.1.down
  17.4 0.0 copy-done
  17.4 0.0 copy-done.1
  17.4 1.2 %forward_chain.1 = (bf16[4,256,256]{2,1,0:T(8,128)(2,1)S(1)}, f32[4,48,256]{2,1,0:T(8,128)S(1)}, f32[4,48,256]{2,1,0:T(8,128)S(1)}, bf16[144,256]{1,0:T(8,128)(2,1)S(1)}) custom-call(bf16[4,80,256]{2,1,0:T(8,128)(2,1)S(1)} %collective-permute-done.up, bf16[4,80,256]{2,1,0:T(8,128)(2,1)S(1)} %collective-permute-done.1.down, ...), custom_call_target="tpu_custom_call" | custom-call | flops 200000000 | bytes 5928960 | tf_op jit(solution)/shard_map/forward_chain/pallas_call | solution.py:411
  18.6 0.0 copy-start.2
  18.6 6.3 %all-gather = bf16[576,256]{1,0:T(8,128)(2,1)S(1)} all-gather(bf16[144,256]{1,0:T(8,128)(2,1)S(1)} %get-tuple-element.46), channel_id=2, replica_groups=mesh['sweep'=4,'cross'=8] {'sweep'}, dimensions={0}, use_global_device_ids=true | all-gather | bytes 368640 | tf_op jit(solution)/shard_map/all_gather | solution.py:490
  24.9 0.0 copy-start.6
  24.9 0.6 %forward_base.1.rest = f32[4,96,256]{2,1,0:T(8,128)S(1)} custom-call(bf16[4,8,144,256]{3,2,1,0:T(8,128)(2,1)S(1)} %get-tuple-element.43.known, bf16[4,256,256]{2,1,0:T(8,128)(2,1)S(1)} %get-tuple-element.48.operand, f32[4,144,256]{2,1,0:T(8,128)S(1)} %get-tuple-element.45.base), custom_call_target="tpu_custom_call" | custom-call | flops 200000000 | bytes 3866624 | tf_op jit(solution)/shard_map/forward_base/pallas_call | solution.py:411
  25.5 0.0 copy-done.2
  25.5 1.6 %forward_finish.1 = (bf16[4,144,256]{2,1,0:T(8,128)(2,1)S(1)}, f32[4,144,256]{2,1,0:T(8,128)S(1)}, bf16[4,80,256]{2,1,0:T(8,128)(2,1)S(1)}, bf16[4,80,256]{2,1,0:T(8,128)(2,1)S(1)}) custom-call(bf16[4,144,256]{2,1,0:T(8,128)(2,1)S(1)} %bitcast.7, f32[4,48,256]{2,1,0:T(8,128)S(1)} %get-tuple-element.47.start, f32[4,96,256]{2,1,0:T(8,128)S(1)} %forward_base.1.rest, ...), custom_call_target="tpu_custom_call" | custom-call | flops 200000000 | bytes 3126272 | tf_op jit(solution)/shard_map/forward_finish/pallas_call | solution.py:411
  27.1 0.1 collective-permute-start.3
  27.2 4.1 %collective-permute-start.4 = (bf16[4,80,256]{2,1,0:T(8,128)(2,1)S(1)}, bf16[4,80,256]{2,1,0:T(8,128)(2,1)S(1)}, u32[]{:S(2)}, u32[]{:S(2)}) collective-permute-start(bf16[4,80,256]{2,1,0:T(8,128)(2,1)S(1)} %get-tuple-element.51), channel_id=1, source_target_pairs={{0,7},{1,0},{2,1},{3,2},{4,3},{5,4},{6,5},{7,6},{8,15},{9,8},{10,9... | collective-permute-start | bytes 491528 | tf_op jit(solution)/shard_map/ppermute | solution.py:449
  31.3 0.0 copy-done.6
  31.3 0.8 %middle.1 = (bf16[4,96,256]{2,1,0:T(8,128)(2,1)S(1)}, f32[4,144,256]{2,1,0:T(8,128)S(1)}, bf16[4,2,192,256]{3,2,1,0:T(8,128)(2,1)S(1)}) custom-call(bf16[4,144,256]{2,1,0:T(8,128)(2,1)S(1)} %get-tuple-element.52.middle, f32[4,144,256]{2,1,0:T(8,128)S(1)} %get-tuple-element.53.change, f32[4,144,256]{2,1,0:T(8,128)S(1)} %get-tuple-element.45.base, ...), custom_call_target="tpu_custom_call" | custom-call | flops 2000000000 | bytes 5958656 | tf_op jit(solution)/shard_map/middle/pallas_call | solution.py:411
  32.1 0.7 %collective-permute-start.6 = (bf16[2,48,256]{2,1,0:T(8,128)(2,1)S(1)}, bf16[2,48,256]{2,1,0:T(8,128)(2,1)S(1)}, u32[]{:S(2)}, u32[]{:S(2)}) collective-permute-start(bf16[2,48,256]{2,1,0:T(8,128)(2,1)S(1)} %slice_bitcast_fusion), channel_id=1, source_target_pairs={{16,0},{17,1},{18,2},{19,3},{20,4},{21,5},{22,6},{23,7}} | collective-permute-start | bytes 147464 | tf_op jit(solution)/shard_map/ppermute | solution.py:427
  32.8 3.3 %collective-permute-start.5 = (bf16[2,48,256]{2,1,0:T(8,128)(2,1)S(1)}, bf16[2,48,256]{2,1,0:T(8,128)(2,1)S(1)}, u32[]{:S(2)}, u32[]{:S(2)}) collective-permute-start(bf16[2,48,256]{2,1,0:T(8,128)(2,1)S(1)} %slice_bitcast_fusion), channel_id=1, source_target_pairs={{8,0},{16,8},{9,1},{17,9},{10,2},{18,10},{11,3},{19,11},{12,4},{20... | collective-permute-start | bytes 147464 | tf_op jit(solution)/shard_map/ppermute | solution.py:427
  36.1 0.0 collective-permute-done.3.up
  36.1 0.3 collective-permute-done.4.down
  36.4 1.1 %backward_chain.1 = (bf16[4,256,256]{2,1,0:T(8,128)(2,1)S(1)}, f32[4,48,256]{2,1,0:T(8,128)S(1)}, f32[4,48,256]{2,1,0:T(8,128)S(1)}, bf16[48,256]{1,0:T(8,128)(2,1)S(1)}) custom-call(bf16[4,80,256]{2,1,0:T(8,128)(2,1)S(1)} %collective-permute-done.3.up, bf16[4,80,256]{2,1,0:T(8,128)(2,1)S(1)} %collective-permute-done.4.down, ...), custom_call_target="tpu_custom_call" | custom-call | flops 200000000 | bytes 5756928 | tf_op jit(solution)/shard_map/backward_chain/pallas_call | solution.py:411
  37.5 0.0 copy-start.3
  37.5 0.6 %backward_base.1.rest = f32[4,96,256]{2,1,0:T(8,128)S(1)} custom-call(bf16[4,8,144,256]{3,2,1,0:T(8,128)(2,1)S(1)} %get-tuple-element.43.known, bf16[4,256,256]{2,1,0:T(8,128)(2,1)S(1)} %get-tuple-element.61.operand, f32[4,144,256]{2,1,0:T(8,128)S(1)} %get-tuple-element.57.base), custom_call_target="tpu_custom_call" | custom-call | flops 200000000 | bytes 3866624 | tf_op jit(solution)/shard_map/backward_base/pallas_call | solution.py:411
  38.1 6.1 %all-gather.1 = bf16[192,256]{1,0:T(8,128)(2,1)S(1)} all-gather(bf16[48,256]{1,0:T(8,128)(2,1)S(1)} %get-tuple-element.58), channel_id=3, replica_groups=mesh['sweep'=4,'cross'=8] {'sweep'}, dimensions={0}, use_global_device_ids=true | all-gather | bytes 122880 | tf_op jit(solution)/shard_map/all_gather | solution.py:520
  44.2 0.0 collective-permute-done.6.next_near
  44.2 0.0 collective-permute-done.5.near
  44.2 0.0 copy-done.3
  44.2 2.8 %backward_finish.1 = bf16[4,8,32,135]{3,2,1,0:T(8,128)(2,1)} custom-call(bf16[4,48,256]{2,1,0:T(8,128)(2,1)S(1)} %bitcast.8, bf16[2,48,256]{2,1,0:T(8,128)(2,1)S(1)} %collective-permute-done.5.near, bf16[2,48,256]{2,1,0:T(8,128)(2,1)S(1)} %collective-permute-done.6.next_near, f32[4,48,256]{2,1,0:T(8,128)S(1)} %get-tuple-element.60.start, ...), custom_call_target="tpu_custom_call" | custom-call | flops 200000000 | bytes 2084832 | tf_op jit(solution)/shard_map/backward_finish/pallas_call | solution.py:411
  (1 shorter events, 0.0 us)
Async XLA Ops:
  0.0 1.0 %copy-start.4 = (bf16[4,8,32,135]{3,2,1,0:T(8,128)(2,1)S(1)}, bf16[4,8,32,135]{3,2,1,0:T(8,128)(2,1)}, u32[]{:S(2)}) copy-start(bf16[4,8,32,135]{3,2,1,0:T(8,128)(2,1)} %initial.2) | copy-start | bytes 829444
  1.6 15.8 %collective-permute-start.2 = (bf16[48,256]{1,0:T(8,128)(2,1)S(1)}, bf16[48,256]{1,0:T(8,128)(2,1)S(1)}, u32[]{:S(2)}, u32[]{:S(2)}) collective-permute-start(bf16[48,256]{1,0:T(8,128)(2,1)S(1)} %get-tuple-element.39), channel_id=1, source_target_pairs={{8,0},{16,8},{24,16},{9,1},{17,9},{25,17},{10,2},{18,10},{26,18},{... | collective-permute-start | bytes 73736 | tf_op jit(solution)/shard_map/ppermute | solution.py:454
  3.5 13.8 %collective-permute-start = (bf16[4,80,256]{2,1,0:T(8,128)(2,1)S(1)}, bf16[4,80,256]{2,1,0:T(8,128)(2,1)S(1)}, u32[]{:S(2)}, u32[]{:S(2)}) collective-permute-start(bf16[4,80,256]{2,1,0:T(8,128)(2,1)S(1)} %get-tuple-element.37), channel_id=1, source_target_pairs={{0,1},{1,2},{2,3},{3,4},{4,5},{5,6},{6,7},{7,0},{8,9},{9,10},{10,1... | collective-permute-start | bytes 491528 | tf_op jit(solution)/shard_map/ppermute | solution.py:449
  6.3 11.1 %collective-permute-start.1 = (bf16[4,80,256]{2,1,0:T(8,128)(2,1)S(1)}, bf16[4,80,256]{2,1,0:T(8,128)(2,1)S(1)}, u32[]{:S(2)}, u32[]{:S(2)}) collective-permute-start(bf16[4,80,256]{2,1,0:T(8,128)(2,1)S(1)} %get-tuple-element.38), channel_id=1, source_target_pairs={{0,7},{1,0},{2,1},{3,2},{4,3},{5,4},{6,5},{7,6},{8,15},{9,8},{10,9... | collective-permute-start | bytes 491528 | tf_op jit(solution)/shard_map/ppermute | solution.py:449
  9.4 0.7 %copy-start.5 = (s32[8,4]{0,1:T(4,128)S(1)}, s32[8,4]{0,1:T(4,128)}, u32[]{:S(2)}) copy-start(s32[8,4]{0,1:T(4,128)} %param.14) | copy-start | bytes 388
  10.1 7.3 %copy-start = (bf16[96,80]{1,0:T(8,128)(2,1)S(1)}, bf16[96,80]{1,0:T(8,128)(2,1)}, u32[]{:S(2)}) copy-start(bf16[96,80]{1,0:T(8,128)(2,1)} %constant.14.clone.down_sel) | copy-start | bytes 46084
  10.1 7.3 %copy-start.1 = (bf16[96,80]{1,0:T(8,128)(2,1)S(1)}, bf16[96,80]{1,0:T(8,128)(2,1)}, u32[]{:S(2)}) copy-start(bf16[96,80]{1,0:T(8,128)(2,1)} %constant.13.clone.up_sel) | copy-start | bytes 46084
  18.6 6.9 %copy-start.2 = (bf16[160,144]{1,0:T(8,128)(2,1)S(1)}, bf16[160,144]{1,0:T(8,128)(2,1)}, u32[]{:S(2)}) copy-start(bf16[160,144]{1,0:T(8,128)(2,1)} %constant.10.clone.send) | copy-start | bytes 138244
  24.9 6.4 %copy-start.6 = (bf16[96,144]{1,0:T(8,128)(2,1)S(1)}, bf16[96,144]{1,0:T(8,128)(2,1)}, u32[]{:S(2)}) copy-start(bf16[96,144]{1,0:T(8,128)(2,1)} %constant.11.clone.own_sel) | copy-start | bytes 82948
  27.1 9.0 %collective-permute-start.3 = (bf16[4,80,256]{2,1,0:T(8,128)(2,1)S(1)}, bf16[4,80,256]{2,1,0:T(8,128)(2,1)S(1)}, u32[]{:S(2)}, u32[]{:S(2)}) collective-permute-start(bf16[4,80,256]{2,1,0:T(8,128)(2,1)S(1)} %get-tuple-element.50), channel_id=1, source_target_pairs={{0,1},{1,2},{2,3},{3,4},{4,5},{5,6},{6,7},{7,0},{8,9},{9,10},{10,1... | collective-permute-start | bytes 491528 | tf_op jit(solution)/shard_map/ppermute | solution.py:449
  27.2 9.2 %collective-permute-start.4 = (bf16[4,80,256]{2,1,0:T(8,128)(2,1)S(1)}, bf16[4,80,256]{2,1,0:T(8,128)(2,1)S(1)}, u32[]{:S(2)}, u32[]{:S(2)}) collective-permute-start(bf16[4,80,256]{2,1,0:T(8,128)(2,1)S(1)} %get-tuple-element.51), channel_id=1, source_target_pairs={{0,7},{1,0},{2,1},{3,2},{4,3},{5,4},{6,5},{7,6},{8,15},{9,8},{10,9... | collective-permute-start | bytes 491528 | tf_op jit(solution)/shard_map/ppermute | solution.py:449
  32.1 12.0 %collective-permute-start.6 = (bf16[2,48,256]{2,1,0:T(8,128)(2,1)S(1)}, bf16[2,48,256]{2,1,0:T(8,128)(2,1)S(1)}, u32[]{:S(2)}, u32[]{:S(2)}) collective-permute-start(bf16[2,48,256]{2,1,0:T(8,128)(2,1)S(1)} %slice_bitcast_fusion), channel_id=1, source_target_pairs={{16,0},{17,1},{18,2},{19,3},{20,4},{21,5},{22,6},{23,7}} | collective-permute-start | bytes 147464 | tf_op jit(solution)/shard_map/ppermute | solution.py:427
  32.8 11.4 %collective-permute-start.5 = (bf16[2,48,256]{2,1,0:T(8,128)(2,1)S(1)}, bf16[2,48,256]{2,1,0:T(8,128)(2,1)S(1)}, u32[]{:S(2)}, u32[]{:S(2)}) collective-permute-start(bf16[2,48,256]{2,1,0:T(8,128)(2,1)S(1)} %slice_bitcast_fusion), channel_id=1, source_target_pairs={{8,0},{16,8},{9,1},{17,9},{10,2},{18,10},{11,3},{19,11},{12,4},{20... | collective-permute-start | bytes 147464 | tf_op jit(solution)/shard_map/ppermute | solution.py:427
  37.5 6.7 %copy-start.3 = (bf16[135,144]{1,0:T(8,128)(2,1)S(1)}, bf16[135,144]{1,0:T(8,128)(2,1)}, u32[]{:S(2)}) copy-start(bf16[135,144]{1,0:T(8,128)(2,1)} %constant.12.clone.back) | copy-start | bytes 116644

commit v10 on v9

--- a/solution.py
+++ b/solution.py
@@ -156,16 +156,21 @@
     return out
 
 
-def first_kernel(initial, up, down, above):
+def first_kernel(initial, up, down, above, initial_in, sem):
     planes, columns, rhs, width = initial.shape
+    copies = [pltpu.make_async_copy(initial.at[p], initial_in.at[p], sem.at[p]) for p in range(planes)]
+    for copy in copies:
+        copy.start()
     shared = rows_of(SHARED)
     tables = [picks(shared_target(shared, which), width) for which in (2, 0)]
-    for p in range(planes):
-        x = initial[p].reshape(columns * rhs, width)
+    first_table = picks(first_target(rows_of(FACE)), width)
+    for p in range(planes):
+        copies[p].wait()
+        x = initial_in[p].reshape(columns * rhs, width)
         up[p] = mt(tables[0], x).astype(BF)
         down[p] = mt(tables[1], x).astype(BF)
         if p == 0:
-            above[...] = mt(picks(first_target(rows_of(FACE)), width), x).astype(BF)
+            above[...] = mt(first_table, x).astype(BF)
 
 
 def turned(rows, raw, put):
@@ -177,13 +182,19 @@
 
 
 def weight_kernel(
-    inverse, couplings, right, initial, neighbours,
+    inverse, couplings, right, initial_there, neighbours_there,
     known, lower, base, own, gathers,
-    inverse_in, couplings_in, right_in, solves, faces, raw, done,
+    inverse_in, couplings_in, right_in, initial, neighbours, solves, faces, raw, done,
 ):
     planes, columns, rhs, width = initial.shape
     size = columns * rhs
     half = columns // 2
+    early = [
+        pltpu.make_async_copy(neighbours_there, neighbours, done.at[3, 0]),
+        pltpu.make_async_copy(initial_there, initial, done.at[3, 1]),
+    ]
+    for copy in early:
+        copy.start()
     copies = []
     for p in range(planes):
         pairs = ((inverse, inverse_in), (couplings, couplings_in), (right, right_in))
@@ -192,6 +203,8 @@
             copy.start()
     faces[...] = jnp.zeros(faces.shape, BF)
     raw[...] = jnp.zeros(raw.shape, F32)
+    for copy in early:
+        copy.wait()
     source = sources(neighbours, columns, rhs)
     for i, start in enumerate((0, size)):
         for j in range(2):
@@ -276,9 +289,9 @@
 
 def chain_kernel(known, base, matrix, received, own, gathers, outs, order, rows, rhs, above=None):
     up, down, up_sel, down_sel = received
-    operand, start, traces, message = outs
+    part, traces, message = outs
     planes, columns = known.shape[:2]
-    size = operand.shape[2]
+    size = part.shape[2]
     wholes = gathered(up, down, own, up_sel, down_sel, gathers)
     trace = None
     for p in order:
@@ -288,21 +301,15 @@
             face = own[p, LAST] if p + 1 < planes else above[...]
             last_face = jnp.concatenate([face, jnp.zeros((256 - 5 * FACE, size), BF)], 0)
         whole = jnp.concatenate(wholes[p] + [last_face], 0)
-        operand[p] = whole
-        value = base[p, rows] + known_part(lambda c: known[p, c, rows], whole, columns, rhs)
-        start[p] = value
+        value = base[p] + known_part(lambda c: known[p, c], whole, columns, rhs)
+        part[p] = value
+        value = value[rows]
         trace = value if trace is None else value + chain_step(matrix.at[p], trace, rhs, rows)
         traces[p] = trace
     message[FIRST] = trace.astype(BF)
     if message.shape[0] > FACE:
         for h in range(2):
             message[(1 + h) * FACE : (2 + h) * FACE] = matrix[order[-1], h, PRODUCT]
-
-
-def base_kernel(known, operand, base, out, *, rows, rhs):
-    planes, columns = known.shape[:2]
-    for p in range(planes):
-        out[p] = base[p, rows] + known_part(lambda c: known[p, c, rows], operand[p], columns, rhs)
 
 
 def forward_chain_kernel(up, down, above, own, gathers, up_sel, down_sel, known, lower, base, *outs, rhs):
@@ -334,16 +341,16 @@
 
 
 def forward_finish_kernel(
-    messages, start, rest, traces, lower, send, middle, change, up, down, *, rhs
+    messages, part, traces, lower, send, middle, change, up, down, *, rhs
 ):
-    planes = start.shape[0]
+    planes = part.shape[0]
     inside = lambda i: [messages[i, (1 + h) * FACE : (2 + h) * FACE] for h in range(2)]
     entry = incoming(messages, inside, True, rhs)
     trace = entry
     for p in range(planes):
         delta = chain_step(lower.at[p], trace, rhs, FULL)
         change[p] = delta
-        whole = (jnp.concatenate([rest[p], start[p]], 0) + delta).astype(BF)
+        whole = (part[p] + delta).astype(BF)
         middle[p] = whole
         out = mm(send[...], whole).astype(BF)
         up[p] = out[:SHARED]
@@ -375,9 +382,9 @@
 
 
 def backward_finish_kernel(
-    messages, near, next_near, start, rest, traces, upper, back, result, results, sem, *, rhs
+    messages, near, next_near, part, traces, upper, back, result, results, sem, *, rhs
 ):
-    planes = start.shape[0]
+    planes = part.shape[0]
     here = lax.axis_index("sweep")
     beside = lambda i: [jnp.where(here + 1 == i, near[h], next_near[h]) for h in range(2)]
     entry = incoming(messages, beside, False, rhs)
@@ -389,7 +396,7 @@
     copies = []
     trace = entry
     for p in range(planes - 1, -1, -1):
-        whole = jnp.concatenate([start[p], rest[p]], 0) + chain_step(upper.at[p], trace, rhs, FULL)
+        whole = part[p] + chain_step(upper.at[p], trace, rhs, FULL)
         flat = mm(back[...], whole.astype(BF)).astype(BF)
         results[p] = mt(unit, flat).astype(BF).reshape(columns, rhs, width)
         copies.append(pltpu.make_async_copy(results.at[p], result.at[p], sem.at[p]))
@@ -435,13 +442,14 @@
     field = (planes, ROWS, size)
     outs = [((planes, columns, ROWS, 256), BF), (pack, BF), (field, F32), (field, BF), ((2, 2, size, size), BF)]
     operands = (inverse, couplings, right, initial, neighbours)
-    scratch = [pltpu.VMEM(x.shape, BF) for x in operands[:3]] + [
+    scratch = [pltpu.VMEM(x.shape, BF) for x in operands[:4]] + [
+        pltpu.SMEM(neighbours.shape, jnp.int32),
         pltpu.VMEM((2, columns, ROWS, 256), BF),
         pltpu.VMEM((2, columns, 256 + 2 * SLOT, 256), BF),
         pltpu.VMEM((2, 9, 2, FACE * columns, 128), F32),
-        pltpu.SemaphoreType.DMA((3, planes)),
+        pltpu.SemaphoreType.DMA((4, planes)),
     ]
-    return call(weight_kernel, outs, operands, "weights", 1e10, (0, 1, 2), scratch)
+    return call(weight_kernel, outs, operands, "weights", 1e10, (0, 1, 2, 3, 4), scratch)
 
 
 def ring(x, axis, by):
@@ -467,7 +475,12 @@
 
     share = (planes, SHARED, size)
     up, down, above = call(
-        first_kernel, [(share, BF), (share, BF), ((FACE, size), BF)], (initial,), "initial_traces"
+        first_kernel,
+        [(share, BF), (share, BF), ((FACE, size), BF)],
+        (initial,),
+        "initial_traces",
+        far=(0,),
+        scratch=[pltpu.VMEM(initial.shape, BF), pltpu.SemaphoreType.DMA((planes,))],
     )
     up, down, above, initial = lax.optimization_barrier((up, down, above, initial))
     from_low = ring(up, "cross", 1)
@@ -479,25 +492,18 @@
 
     field = (planes, ROWS, size)
     trace = (planes, FACE, size)
-    most = (planes, 2 * FACE, size)
-    chain_outs = [((planes, 256, size), BF), (trace, F32), (trace, F32)]
-    operand, start, traces, message = call(
+    chain_outs = [(field, F32), (trace, F32)]
+    part, traces, message = call(
         functools.partial(forward_chain_kernel, rhs=rhs),
         chain_outs + [((3 * FACE, size), BF)],
         (from_low, from_high, from_above, own, gathers, up_sel, down_sel, known, lower, base),
         "forward_chain",
     )
     messages = lax.all_gather(message, "sweep")
-    (rest,) = call(
-        functools.partial(base_kernel, rows=slice(0, 2 * FACE), rhs=rhs),
-        [(most, F32)],
-        (known, operand, base),
-        "forward_base",
-    )
     middle, change, up, down = call(
         functools.partial(forward_finish_kernel, rhs=rhs),
         [(field, BF), (field, F32), (share, BF), (share, BF)],
-        (messages, start, rest, traces, lower, send_in),
+        (messages, part, traces, lower, send_in),
         "forward_finish",
     )
     from_low = ring(up, "cross", 1)
@@ -511,23 +517,17 @@
     )
     own, pass_b = lax.optimization_barrier((own, upper[0, :, PRODUCT]))
     passes = products(pass_b, -1)
-    operand, start, traces, message = call(
+    part, traces, message = call(
         functools.partial(backward_chain_kernel, rhs=rhs),
         chain_outs + [((FACE, size), BF)],
         (from_low, from_high, own, gathers, up_sel, down_sel, known, upper, base),
         "backward_chain",
     )
     messages = lax.all_gather(message, "sweep")
-    (rest,) = call(
-        functools.partial(base_kernel, rows=slice(FACE, ROWS), rhs=rhs),
-        [(most, F32)],
-        (known, operand, base),
-        "backward_base",
-    )
     (result,) = call(
         functools.partial(backward_finish_kernel, rhs=rhs),
         [(right_sides.shape, BF)],
-        (messages, *passes, start, rest, traces, upper, back),
+        (messages, *passes, part, traces, upper, back),
         "backward_finish",
         scratch=[pltpu.VMEM(right_sides.shape, BF), pltpu.SemaphoreType.DMA((planes,))],
         out_space=pltpu.HBM,

time: 47.4 us -> 45.8 us (0.966)
  local copies, waits for them, and re-layouts: 1.75 us -> 0.03 us
    unnamed x14 -> x10, local copies, waits for them, and re-layouts: 1.75 us -> 0.02 us
    pallas_call x9 -> x7, Pallas kernels: 16.5 us -> 16.8 us  [call(): pl.pallas_call(kernel, out_shape=shapes, in_specs=[pl.BlockSpec(memory_sp...]
  transfers between devices with their start and end apart: 7 -> 7, of which waited for: 1 -> 1; matrix products, arithmetic and copies ran while one was open for 0% -> 0% of each run, Pallas kernels for 21% -> 20%
where the time goes in v10:
time: 45.8 us; the launch traced here: 45.5 us
  Pallas kernels  16.8 us (37%)
  starting transfers between devices  15.9 us (35%)
  blocking collectives  12.3 us (27%)
    pallas_call x7, Pallas kernels, call(): pl.pallas_call(kernel, out_shape=shapes, in_specs=[pl.BlockSpec(memory_sp...  16.8 us
    all_gather x2, blocking collectives, local(): messages = lax.all_gather(message, 'sweep')  12.3 us
    ppermute x4, starting transfers between devices, ring(): return lax.ppermute(x, axis, [(i, (i + by) % n) for i in range(n)])  10.1 us
    ppermute x2, starting transfers between devices, products(): lax.ppermute(x, 'sweep', [(i, i + step) for i in inner if 0 <= i + step <...  3.92 us
    ppermute x1, starting transfers between devices, shift(): lax.ppermute(x, axis, [(i, i + by) for i in range(n) if 0 <= i + by < n])  1.97 us
  transfers between devices with their start and end apart: 7, of which 1 were waited for; matrix products, arithmetic and copies ran while one was open for 0% of the time, Pallas kernels for 20%

profile of v10, /device:TPU:1, one launch (start us, length us, event | category | flops | bytes accessed | tf_op | source)
XLA Modules:
  0.0 45.5 jit_solution(13623412784657762514)
XLA Ops:
  0.0 1.9 %initial_traces.1 = (bf16[4,80,256]{2,1,0:T(8,128)(2,1)S(1)}, bf16[4,80,256]{2,1,0:T(8,128)(2,1)S(1)}, bf16[48,256]{1,0:T(8,128)(2,1)S(1)}) custom-call(bf16[4,8,32,135]{3,2,1,0:T(8,128)(2,1)} %initial_there), custom_call_target="tpu_custom_call" | custom-call | flops 200000000 | bytes 628736 | tf_op jit(solution)/shard_map/initial_traces/pallas_call | solution.py:418
  1.9 2.0 %collective-permute-start.2 = (bf16[48,256]{1,0:T(8,128)(2,1)S(1)}, bf16[48,256]{1,0:T(8,128)(2,1)S(1)}, u32[]{:S(2)}, u32[]{:S(2)}) collective-permute-start(bf16[48,256]{1,0:T(8,128)(2,1)S(1)} %get-tuple-element.37), channel_id=1, source_target_pairs={{8,0},{16,8},{24,16},{9,1},{17,9},{25,17},{10,2},{18,10},{26,18},{... | collective-permute-start | bytes 73736 | tf_op jit(solution)/shard_map/ppermute | solution.py:462
  3.9 2.7 %collective-permute-start = (bf16[4,80,256]{2,1,0:T(8,128)(2,1)S(1)}, bf16[4,80,256]{2,1,0:T(8,128)(2,1)S(1)}, u32[]{:S(2)}, u32[]{:S(2)}) collective-permute-start(bf16[4,80,256]{2,1,0:T(8,128)(2,1)S(1)} %get-tuple-element.35), channel_id=1, source_target_pairs={{0,1},{1,2},{2,3},{3,4},{4,5},{5,6},{6,7},{7,0},{8,9},{9,10},{10,1... | collective-permute-start | bytes 491528 | tf_op jit(solution)/shard_map/ppermute | solution.py:457
  6.6 3.1 %collective-permute-start.1 = (bf16[4,80,256]{2,1,0:T(8,128)(2,1)S(1)}, bf16[4,80,256]{2,1,0:T(8,128)(2,1)S(1)}, u32[]{:S(2)}, u32[]{:S(2)}) collective-permute-start(bf16[4,80,256]{2,1,0:T(8,128)(2,1)S(1)} %get-tuple-element.36), channel_id=1, source_target_pairs={{0,7},{1,0},{2,1},{3,2},{4,3},{5,4},{6,5},{7,6},{8,15},{9,8},{10,9... | collective-permute-start | bytes 491528 | tf_op jit(solution)/shard_map/ppermute | solution.py:457
  9.7 0.0 copy-start
  9.7 0.0 copy-start.1
  9.7 7.2 %weights.1 = (bf16[4,8,144,256]{3,2,1,0:T(8,128)(2,1)S(1)}, bf16[4,2,192,256]{3,2,1,0:T(8,128)(2,1)S(1)}, f32[4,144,256]{2,1,0:T(8,128)S(1)}, bf16[4,144,256]{2,...) custom-call(bf16[4,135,8,135]{3,2,1,0:T(8,128)(2,1)} %bitcast.10, bf16[4,6,45,8,135]{4,3,2,1,0:T(8,128)(2,1)} %bitcast.9, ...), custom_call_target="tpu_custom_call" | custom-call | flops 10000000000 | bytes 8607040 | tf_op jit(solution)/shard_map/weights/pallas_call | solution.py:418
  16.9 0.0 collective-permute-done.2.above
  16.9 0.0 collective-permute-done.up
  17.0 0.0 collective-permute-done.1.down
  17.0 0.0 copy-done
  17.0 0.0 copy-done.1
  17.0 0.0 copy-start.2
  17.0 0.0 copy-start.4
  17.0 1.2 %forward_chain.1 = (f32[4,144,256]{2,1,0:T(8,128)S(1)}, f32[4,48,256]{2,1,0:T(8,128)S(1)}, bf16[144,256]{1,0:T(8,128)(2,1)S(1)}) custom-call(bf16[4,80,256]{2,1,0:T(8,128)(2,1)S(1)} %collective-permute-done.up, bf16[4,80,256]{2,1,0:T(8,128)(2,1)S(1)} %collective-permute-done.1.down, bf16[48,256]{1,0:T(8,128)(2,1)S(1)} %collective-permute-done.2.above, ...), custom_call_target="tpu_custom_call" | custom-call | flops 200000000 | bytes 5797888 | tf_op jit(solution)/shard_map/forward_chain/pallas_call | solution.py:418
  18.2 6.1 %all-gather = bf16[576,256]{1,0:T(8,128)(2,1)S(1)} all-gather(bf16[144,256]{1,0:T(8,128)(2,1)S(1)} %get-tuple-element.44), channel_id=2, replica_groups=mesh['sweep'=4,'cross'=8] {'sweep'}, dimensions={0}, use_global_device_ids=true | all-gather | bytes 368640 | tf_op jit(solution)/shard_map/all_gather | solution.py:502
  24.4 0.0 copy-done.2
  24.4 1.6 %forward_finish.1 = (bf16[4,144,256]{2,1,0:T(8,128)(2,1)S(1)}, f32[4,144,256]{2,1,0:T(8,128)S(1)}, bf16[4,80,256]{2,1,0:T(8,128)(2,1)S(1)}, bf16[4,80,256]{2,1,0:T(8,128)(2,1)S(1)}) custom-call(bf16[4,144,256]{2,1,0:T(8,128)(2,1)S(1)} %bitcast.7, f32[4,144,256]{2,1,0:T(8,128)S(1)} %get-tuple-element.45.part, f32[4,48,256]{2,1,0:T(8,128)S(1)} %get-tuple-element.46.traces, ...), custom_call_target="tpu_custom_call" | custom-call | flops 200000000 | bytes 3126272 | tf_op jit(solution)/shard_map/forward_finish/pallas_call | solution.py:418
  26.0 0.1 collective-permute-start.3
  26.1 4.1 %collective-permute-start.4 = (bf16[4,80,256]{2,1,0:T(8,128)(2,1)S(1)}, bf16[4,80,256]{2,1,0:T(8,128)(2,1)S(1)}, u32[]{:S(2)}, u32[]{:S(2)}) collective-permute-start(bf16[4,80,256]{2,1,0:T(8,128)(2,1)S(1)} %get-tuple-element.48), channel_id=1, source_target_pairs={{0,7},{1,0},{2,1},{3,2},{4,3},{5,4},{6,5},{7,6},{8,15},{9,8},{10,9... | collective-permute-start | bytes 491528 | tf_op jit(solution)/shard_map/ppermute | solution.py:457
  30.2 0.0 copy-done.4
  30.2 0.8 %middle.1 = (bf16[4,96,256]{2,1,0:T(8,128)(2,1)S(1)}, f32[4,144,256]{2,1,0:T(8,128)S(1)}, bf16[4,2,192,256]{3,2,1,0:T(8,128)(2,1)S(1)}) custom-call(bf16[4,144,256]{2,1,0:T(8,128)(2,1)S(1)} %get-tuple-element.49.middle, f32[4,144,256]{2,1,0:T(8,128)S(1)} %get-tuple-element.50.change, f32[4,144,256]{2,1,0:T(8,128)S(1)} %get-tuple-element.43.base, ...), custom_call_target="tpu_custom_call" | custom-call | flops 2000000000 | bytes 5958656 | tf_op jit(solution)/shard_map/middle/pallas_call | solution.py:418
  31.0 0.7 %collective-permute-start.6 = (bf16[2,48,256]{2,1,0:T(8,128)(2,1)S(1)}, bf16[2,48,256]{2,1,0:T(8,128)(2,1)S(1)}, u32[]{:S(2)}, u32[]{:S(2)}) collective-permute-start(bf16[2,48,256]{2,1,0:T(8,128)(2,1)S(1)} %slice_bitcast_fusion), channel_id=1, source_target_pairs={{16,0},{17,1},{18,2},{19,3},{20,4},{21,5},{22,6},{23,7}} | collective-permute-start | bytes 147464 | tf_op jit(solution)/shard_map/ppermute | solution.py:434
  31.7 3.3 %collective-permute-start.5 = (bf16[2,48,256]{2,1,0:T(8,128)(2,1)S(1)}, bf16[2,48,256]{2,1,0:T(8,128)(2,1)S(1)}, u32[]{:S(2)}, u32[]{:S(2)}) collective-permute-start(bf16[2,48,256]{2,1,0:T(8,128)(2,1)S(1)} %slice_bitcast_fusion), channel_id=1, source_target_pairs={{8,0},{16,8},{9,1},{17,9},{10,2},{18,10},{11,3},{19,11},{12,4},{20... | collective-permute-start | bytes 147464 | tf_op jit(solution)/shard_map/ppermute | solution.py:434
  35.0 0.0 collective-permute-done.3.up
  35.0 0.3 collective-permute-done.4.down
  35.3 0.0 copy-start.3
  35.3 1.2 %backward_chain.1 = (f32[4,144,256]{2,1,0:T(8,128)S(1)}, f32[4,48,256]{2,1,0:T(8,128)S(1)}, bf16[48,256]{1,0:T(8,128)(2,1)S(1)}) custom-call(bf16[4,80,256]{2,1,0:T(8,128)(2,1)S(1)} %collective-permute-done.3.up, bf16[4,80,256]{2,1,0:T(8,128)(2,1)S(1)} %collective-permute-done.4.down, bf16[4,96,256]{2,1,0:T(8,128)(2,1)S(1)} %get-tuple-element.53.own, ...), custom_call_target="tpu_custom_call" | custom-call | flops 200000000 | bytes 5625856 | tf_op jit(solution)/shard_map/backward_chain/pallas_call | solution.py:418
  36.5 6.1 %all-gather.1 = bf16[192,256]{1,0:T(8,128)(2,1)S(1)} all-gather(bf16[48,256]{1,0:T(8,128)(2,1)S(1)} %get-tuple-element.55), channel_id=3, replica_groups=mesh['sweep'=4,'cross'=8] {'sweep'}, dimensions={0}, use_global_device_ids=true | all-gather | bytes 122880 | tf_op jit(solution)/shard_map/all_gather | solution.py:526
  42.6 0.0 collective-permute-done.6.next_near
  42.6 0.0 collective-permute-done.5.near
  42.6 0.0 copy-done.3
  42.7 2.8 %backward_finish.1 = bf16[4,8,32,135]{3,2,1,0:T(8,128)(2,1)} custom-call(bf16[4,48,256]{2,1,0:T(8,128)(2,1)S(1)} %bitcast.8, bf16[2,48,256]{2,1,0:T(8,128)(2,1)S(1)} %collective-permute-done.5.near, bf16[2,48,256]{2,1,0:T(8,128)(2,1)S(1)} %collective-permute-done.6.next_near, f32[4,144,256]{2,1,0:T(8,128)S(1)} %get-tuple-element.57.part, ...), custom_call_target="tpu_custom_call" | custom-call | flops 200000000 | bytes 2084832 | tf_op jit(solution)/shard_map/backward_finish/pallas_call | solution.py:418
  (1 shorter events, 0.0 us)
Async XLA Ops:
  1.9 15.0 %collective-permute-start.2 = (bf16[48,256]{1,0:T(8,128)(2,1)S(1)}, bf16[48,256]{1,0:T(8,128)(2,1)S(1)}, u32[]{:S(2)}, u32[]{:S(2)}) collective-permute-start(bf16[48,256]{1,0:T(8,128)(2,1)S(1)} %get-tuple-element.37), channel_id=1, source_target_pairs={{8,0},{16,8},{24,16},{9,1},{17,9},{25,17},{10,2},{18,10},{26,18},{... | collective-permute-start | bytes 73736 | tf_op jit(solution)/shard_map/ppermute | solution.py:462
  3.9 13.1 %collective-permute-start = (bf16[4,80,256]{2,1,0:T(8,128)(2,1)S(1)}, bf16[4,80,256]{2,1,0:T(8,128)(2,1)S(1)}, u32[]{:S(2)}, u32[]{:S(2)}) collective-permute-start(bf16[4,80,256]{2,1,0:T(8,128)(2,1)S(1)} %get-tuple-element.35), channel_id=1, source_target_pairs={{0,1},{1,2},{2,3},{3,4},{4,5},{5,6},{6,7},{7,0},{8,9},{9,10},{10,1... | collective-permute-start | bytes 491528 | tf_op jit(solution)/shard_map/ppermute | solution.py:457
  6.6 10.3 %collective-permute-start.1 = (bf16[4,80,256]{2,1,0:T(8,128)(2,1)S(1)}, bf16[4,80,256]{2,1,0:T(8,128)(2,1)S(1)}, u32[]{:S(2)}, u32[]{:S(2)}) collective-permute-start(bf16[4,80,256]{2,1,0:T(8,128)(2,1)S(1)} %get-tuple-element.36), channel_id=1, source_target_pairs={{0,7},{1,0},{2,1},{3,2},{4,3},{5,4},{6,5},{7,6},{8,15},{9,8},{10,9... | collective-permute-start | bytes 491528 | tf_op jit(solution)/shard_map/ppermute | solution.py:457
  9.7 7.2 %copy-start = (bf16[96,80]{1,0:T(8,128)(2,1)S(1)}, bf16[96,80]{1,0:T(8,128)(2,1)}, u32[]{:S(2)}) copy-start(bf16[96,80]{1,0:T(8,128)(2,1)} %constant.14.clone.down_sel) | copy-start | bytes 46084
  9.7 7.2 %copy-start.1 = (bf16[96,80]{1,0:T(8,128)(2,1)S(1)}, bf16[96,80]{1,0:T(8,128)(2,1)}, u32[]{:S(2)}) copy-start(bf16[96,80]{1,0:T(8,128)(2,1)} %constant.13.clone.up_sel) | copy-start | bytes 46084
  17.0 7.4 %copy-start.2 = (bf16[160,144]{1,0:T(8,128)(2,1)S(1)}, bf16[160,144]{1,0:T(8,128)(2,1)}, u32[]{:S(2)}) copy-start(bf16[160,144]{1,0:T(8,128)(2,1)} %constant.10.clone.send) | copy-start | bytes 138244
  17.0 13.2 %copy-start.4 = (bf16[96,144]{1,0:T(8,128)(2,1)S(1)}, bf16[96,144]{1,0:T(8,128)(2,1)}, u32[]{:S(2)}) copy-start(bf16[96,144]{1,0:T(8,128)(2,1)} %constant.11.clone.own_sel) | copy-start | bytes 82948
  26.0 9.0 %collective-permute-start.3 = (bf16[4,80,256]{2,1,0:T(8,128)(2,1)S(1)}, bf16[4,80,256]{2,1,0:T(8,128)(2,1)S(1)}, u32[]{:S(2)}, u32[]{:S(2)}) collective-permute-start(bf16[4,80,256]{2,1,0:T(8,128)(2,1)S(1)} %get-tuple-element.47), channel_id=1, source_target_pairs={{0,1},{1,2},{2,3},{3,4},{4,5},{5,6},{6,7},{7,0},{8,9},{9,10},{10,1... | collective-permute-start | bytes 491528 | tf_op jit(solution)/shard_map/ppermute | solution.py:457
  26.1 9.2 %collective-permute-start.4 = (bf16[4,80,256]{2,1,0:T(8,128)(2,1)S(1)}, bf16[4,80,256]{2,1,0:T(8,128)(2,1)S(1)}, u32[]{:S(2)}, u32[]{:S(2)}) collective-permute-start(bf16[4,80,256]{2,1,0:T(8,128)(2,1)S(1)} %get-tuple-element.48), channel_id=1, source_target_pairs={{0,7},{1,0},{2,1},{3,2},{4,3},{5,4},{6,5},{7,6},{8,15},{9,8},{10,9... | collective-permute-start | bytes 491528 | tf_op jit(solution)/shard_map/ppermute | solution.py:457
  31.0 11.6 %collective-permute-start.6 = (bf16[2,48,256]{2,1,0:T(8,128)(2,1)S(1)}, bf16[2,48,256]{2,1,0:T(8,128)(2,1)S(1)}, u32[]{:S(2)}, u32[]{:S(2)}) collective-permute-start(bf16[2,48,256]{2,1,0:T(8,128)(2,1)S(1)} %slice_bitcast_fusion), channel_id=1, source_target_pairs={{16,0},{17,1},{18,2},{19,3},{20,4},{21,5},{22,6},{23,7}} | collective-permute-start | bytes 147464 | tf_op jit(solution)/shard_map/ppermute | solution.py:434
  31.7 10.9 %collective-permute-start.5 = (bf16[2,48,256]{2,1,0:T(8,128)(2,1)S(1)}, bf16[2,48,256]{2,1,0:T(8,128)(2,1)S(1)}, u32[]{:S(2)}, u32[]{:S(2)}) collective-permute-start(bf16[2,48,256]{2,1,0:T(8,128)(2,1)S(1)} %slice_bitcast_fusion), channel_id=1, source_target_pairs={{8,0},{16,8},{9,1},{17,9},{10,2},{18,10},{11,3},{19,11},{12,4},{20... | collective-permute-start | bytes 147464 | tf_op jit(solution)/shard_map/ppermute | solution.py:434
  35.3 7.4 %copy-start.3 = (bf16[135,144]{1,0:T(8,128)(2,1)S(1)}, bf16[135,144]{1,0:T(8,128)(2,1)}, u32[]{:S(2)}) copy-start(bf16[135,144]{1,0:T(8,128)(2,1)} %constant.12.clone.back) | copy-start | bytes 116644

commit v11 on v10

--- a/solution.py
+++ b/solution.py
@@ -14,7 +14,8 @@
 FACE = 48
 SLOT = 64
 ROWS = 3 * FACE
-SHARED = 80
+SHARED = 75
+MAIN = 64
 MIB = 1 << 20
 FIRST = slice(0, FACE)
 LAST = slice(2 * FACE, ROWS)
@@ -37,28 +38,39 @@
     return [n for n in NODES if n[1 + place] == which]
 
 
-def union_rows(which):
+def table(height, width, rows, column_of):
+    out = np.zeros((height, width), np.float32)
+    for row, node in rows:
+        out[row, column_of(*node)] = 1
+    return out
+
+
+def block(nodes, start=0):
+    return [(start + i, n) for i, n in enumerate(nodes)]
+
+
+def tail_rows(planes):
+    return -(-planes * (SHARED - MAIN) // 16) * 16
+
+
+def union_nodes(which):
     others = [b for b in range(3) if b != which]
     spots = [(which, c) for c in range(3)] + [(b, which) for b in others]
-    return [
-        (v * 16 + a * 5 + j, (v, a, b, c)) for v in range(5) for a in range(3) for j, (b, c) in enumerate(spots)
-    ]
-
-
-def table(height, width, rows, column_of, value=1.0):
-    out = np.zeros((height, width), np.float32)
-    for row, node in rows:
-        out[row, column_of(*node)] = value
-    return out
-
-
-def block(nodes, start=0):
-    return [(start + i, n) for i, n in enumerate(nodes)]
-
-
-def send_table(width, column_of):
-    rows = union_rows(2) + [(SHARED + i, n) for i, n in union_rows(0)]
-    return table(2 * SHARED, width, rows, column_of)
+    return [(v, a, b, c) for v in range(5) for a in range(3) for b, c in spots]
+
+
+def place_of(i, plane):
+    return i if i < MAIN else i + plane * (SHARED - MAIN)
+
+
+def send_table(width, column_of, planes):
+    height = MAIN + tail_rows(planes)
+    out = []
+    for p in range(planes):
+        rows = [(place_of(i, p), n) for i, n in enumerate(union_nodes(2))]
+        rows += [(height + place_of(i, p), n) for i, n in enumerate(union_nodes(0))]
+        out.append(table(2 * height, width, rows, column_of))
+    return np.stack(out)
 
 
 def own_table(width, column_of):
@@ -66,10 +78,13 @@
     return table(2 * FACE, width, rows, column_of)
 
 
-def receive_table(which):
-    place = {n: i for i, n in union_rows(which)}
+def receive_table(which, planes):
     rows = block(face_nodes(1, which)) + block(face_nodes(2, which), FACE)
-    return table(2 * FACE, SHARED, rows, lambda *n: place[n])
+    out = []
+    for p in range(planes):
+        place = {n: place_of(i, p) for i, n in enumerate(union_nodes(which))}
+        out.append(table(2 * FACE, MAIN + tail_rows(planes), rows, lambda *n: place[n]))
+    return np.stack(out)
 
 
 def mm(a, b):
@@ -114,13 +129,16 @@
     )
 
 
-def shared_target(row, which):
-    v, k = row // 16, row % 16
+def shared_target(row, which, plane, planes):
+    rest = SHARED - MAIN
+    i = jnp.where(row < MAIN, row, row - plane * rest)
+    k = i % 15
     a = k // 5
     j = k % 5
     b = jnp.where(j < 3, which, j - 3 if which == 2 else j - 2)
     c = jnp.where(j < 3, j, which)
-    return jnp.where(k < 15, v * 27 + a * 9 + b * 3 + c, -1)
+    inside = (row < MAIN) | ((i >= MAIN) & (i < SHARED))
+    return jnp.where(inside, i // 15 * 27 + a * 9 + b * 3 + c, -1)
 
 
 def picks(target, width):
@@ -156,21 +174,27 @@
     return out
 
 
-def first_kernel(initial, up, down, above, initial_in, sem):
+def put_shared(out, ups, downs):
+    planes = len(out)
+    height = out[0].shape[0] // 2
+    for target, start in ((ups, 0), (downs, height)):
+        for p in range(planes):
+            target[p * MAIN : (p + 1) * MAIN] = out[p][start : start + MAIN].astype(BF)
+        tails = [x[start + MAIN : start + height] for x in out]
+        target[planes * MAIN :] = sum(tails[1:], tails[0]).astype(BF)
+
+
+def first_kernel(initial, up, down, above):
     planes, columns, rhs, width = initial.shape
-    copies = [pltpu.make_async_copy(initial.at[p], initial_in.at[p], sem.at[p]) for p in range(planes)]
-    for copy in copies:
-        copy.start()
-    shared = rows_of(SHARED)
-    tables = [picks(shared_target(shared, which), width) for which in (2, 0)]
-    first_table = picks(first_target(rows_of(FACE)), width)
-    for p in range(planes):
-        copies[p].wait()
-        x = initial_in[p].reshape(columns * rhs, width)
-        up[p] = mt(tables[0], x).astype(BF)
-        down[p] = mt(tables[1], x).astype(BF)
+    row = rows_of(MAIN + tail_rows(planes))
+    out = []
+    for p in range(planes):
+        x = initial[p].reshape(columns * rhs, width)
+        tables = [picks(shared_target(row, which, p, planes), width) for which in (2, 0)]
+        out.append(mt(jnp.concatenate(tables, 0), x))
         if p == 0:
-            above[...] = mt(first_table, x).astype(BF)
+            above[...] = mt(picks(first_target(rows_of(FACE)), width), x).astype(BF)
+    put_shared(out, up, down)
 
 
 def turned(rows, raw, put):
@@ -268,14 +292,24 @@
 
 
 def gathered(received_up, received_down, own, up_sel, down_sel, gathers):
-    planes = received_up.shape[0]
-    low = [mm(up_sel[...], received_up[p]).astype(BF) for p in range(planes)]
-    high = [mm(down_sel[...], received_down[p]).astype(BF) for p in range(planes)]
+    planes = up_sel.shape[0]
+
+    def faces(received, select):
+        tail = received[planes * MAIN :]
+        wholes = [jnp.concatenate([received[p * MAIN : (p + 1) * MAIN], tail], 0) for p in range(planes)]
+        return [mm(select[p], wholes[p]).astype(BF) for p in range(planes)]
+
+    low, high = faces(received_up, up_sel), faces(received_down, down_sel)
     sides = []
     for j, side in enumerate((low, high)):
         picked = mm(jnp.concatenate([x[FACE:] for x in side], 0), gathers[j, j]).astype(BF)
         sides.append([picked[p * FACE : (p + 1) * FACE] + own[p, j * FACE : (j + 1) * FACE] for p in range(planes)])
-    return [[low[p][:FACE], high[p][:FACE], sides[0][p], sides[1][p]] for p in range(planes)]
+    return [jnp.concatenate([low[p][:FACE], high[p][:FACE], sides[0][p], sides[1][p]], 0) for p in range(planes)]
+
+
+def gather_kernel(up, down, own, gathers, up_sel, down_sel, operand):
+    for p, whole in enumerate(gathered(up, down, own, up_sel, down_sel, gathers)):
+        operand[p] = whole
 
 
 def known_part(known_c, operand, columns, rhs):
@@ -287,20 +321,12 @@
     return jnp.concatenate(out, 1)
 
 
-def chain_kernel(known, base, matrix, received, own, gathers, outs, order, rows, rhs, above=None):
-    up, down, up_sel, down_sel = received
+def chain_kernel(known, base, matrix, wholes, outs, order, rows, rhs, last_face):
     part, traces, message = outs
     planes, columns = known.shape[:2]
-    size = part.shape[2]
-    wholes = gathered(up, down, own, up_sel, down_sel, gathers)
     trace = None
     for p in order:
-        if above is None:
-            last_face = jnp.zeros((256 - 4 * FACE, size), BF)
-        else:
-            face = own[p, LAST] if p + 1 < planes else above[...]
-            last_face = jnp.concatenate([face, jnp.zeros((256 - 5 * FACE, size), BF)], 0)
-        whole = jnp.concatenate(wholes[p] + [last_face], 0)
+        whole = jnp.concatenate([wholes[p], last_face(p)], 0)
         value = base[p] + known_part(lambda c: known[p, c], whole, columns, rhs)
         part[p] = value
         value = value[rows]
@@ -312,16 +338,17 @@
             message[(1 + h) * FACE : (2 + h) * FACE] = matrix[order[-1], h, PRODUCT]
 
 
-def forward_chain_kernel(up, down, above, own, gathers, up_sel, down_sel, known, lower, base, *outs, rhs):
-    order = range(up.shape[0])
-    received = (up, down, up_sel, down_sel)
-    chain_kernel(known, base, lower, received, own, gathers, outs, order, LAST, rhs, above)
+def forward_chain_kernel(operand, above, own, known, lower, base, *outs, rhs):
+    planes, _, size = operand.shape
+    pad = jnp.zeros((256 - 5 * FACE, size), BF)
+    last_face = lambda p: jnp.concatenate([own[p, LAST] if p + 1 < planes else above[...], pad], 0)
+    chain_kernel(known, base, lower, operand, outs, range(planes), LAST, rhs, last_face)
 
 
 def backward_chain_kernel(up, down, own, gathers, up_sel, down_sel, known, upper, base, *outs, rhs):
-    order = range(up.shape[0] - 1, -1, -1)
-    received = (up, down, up_sel, down_sel)
-    chain_kernel(known, base, upper, received, own, gathers, outs, order, FIRST, rhs)
+    wholes = gathered(up, down, own, up_sel, down_sel, gathers)
+    last_face = lambda p: jnp.zeros((256 - 4 * FACE, up.shape[1]), BF)
+    chain_kernel(known, base, upper, wholes, outs, range(len(wholes) - 1, -1, -1), FIRST, rhs, last_face)
 
 
 def incoming(messages, products, forward, rhs):
@@ -346,17 +373,17 @@
     planes = part.shape[0]
     inside = lambda i: [messages[i, (1 + h) * FACE : (2 + h) * FACE] for h in range(2)]
     entry = incoming(messages, inside, True, rhs)
+    out = []
     trace = entry
     for p in range(planes):
         delta = chain_step(lower.at[p], trace, rhs, FULL)
         change[p] = delta
         whole = (part[p] + delta).astype(BF)
         middle[p] = whole
-        out = mm(send[...], whole).astype(BF)
-        up[p] = out[:SHARED]
-        down[p] = out[SHARED:]
+        out.append(mm(send[p], whole))
         if p + 1 < planes:
             trace = traces[p] + chain_step(lower.at[p], entry, rhs, PRODUCT)
+    put_shared(out, up, down)
 
 
 def middle_kernel(middle, change, base, gathers, own_sel, known, own, out, upper):
@@ -466,21 +493,19 @@
     planes, columns, rhs, width = initial.shape
     size = columns * rhs
     const = lambda x: jnp.asarray(x, BF)
-    send_in = const(send_table(ROWS, inner))
+    send_in = const(send_table(ROWS, inner, planes))
     own_in = const(own_table(ROWS, inner))
     back = const(table(width, ROWS, [(natural(*n), n) for n in NODES], inner))
-    up_sel = const(receive_table(2))
-    down_sel = const(receive_table(0))
+    up_sel = const(receive_table(2, planes))
+    down_sel = const(receive_table(0, planes))
     beside = neighbours.T
 
-    share = (planes, SHARED, size)
+    share = (planes * MAIN + tail_rows(planes), size)
     up, down, above = call(
         first_kernel,
         [(share, BF), (share, BF), ((FACE, size), BF)],
         (initial,),
         "initial_traces",
-        far=(0,),
-        scratch=[pltpu.VMEM(initial.shape, BF), pltpu.SemaphoreType.DMA((planes,))],
     )
     up, down, above, initial = lax.optimization_barrier((up, down, above, initial))
     from_low = ring(up, "cross", 1)
@@ -493,10 +518,16 @@
     field = (planes, ROWS, size)
     trace = (planes, FACE, size)
     chain_outs = [(field, F32), (trace, F32)]
+    (operand,) = call(
+        gather_kernel,
+        [((planes, 4 * FACE, size), BF)],
+        (from_low, from_high, own, gathers, up_sel, down_sel),
+        "forward_gather",
+    )
     part, traces, message = call(
         functools.partial(forward_chain_kernel, rhs=rhs),
         chain_outs + [((3 * FACE, size), BF)],
-        (from_low, from_high, from_above, own, gathers, up_sel, down_sel, known, lower, base),
+        (operand, from_above, own, known, lower, base),
         "forward_chain",
     )
     messages = lax.all_gather(message, "sweep")

time: 45.8 us -> 44.9 us (0.980)
  Pallas kernels: 16.8 us -> 15.1 us
  local copies, waits for them, and re-layouts: 0.03 us -> 1.07 us
    pallas_call x7 -> x8, Pallas kernels: 16.8 us -> 15.1 us  [call(): pl.pallas_call(kernel, out_shape=shapes, in_specs=[pl.BlockSpec(memory_sp...]
    unnamed x10 -> x12, local copies, waits for them, and re-layouts: 0.02 us -> 1.07 us
  transfers between devices with their start and end apart: 7 -> 7, of which waited for: 1 -> 0; matrix products, arithmetic and copies ran while one was open for 0% -> 0% of each run, Pallas kernels for 20% -> 22%
where the time goes in v11:
time: 44.9 us; the launch traced here: 44.5 us
  starting transfers between devices  15.9 us (35%)
  Pallas kernels  15.1 us (34%)
  blocking collectives  12.2 us (27%)
  local copies, waits for them, and re-layouts  1.07 us (2%)
    pallas_call x8, Pallas kernels, call(): pl.pallas_call(kernel, out_shape=shapes, in_specs=[pl.BlockSpec(memory_sp...  15.1 us
    all_gather x2, blocking collectives, local(): messages = lax.all_gather(message, 'sweep')  12.2 us
    ppermute x4, starting transfers between devices, ring(): return lax.ppermute(x, axis, [(i, (i + by) % n) for i in range(n)])  10.1 us
    ppermute x2, starting transfers between devices, products(): lax.ppermute(x, 'sweep', [(i, i + step) for i in inner if 0 <= i + step <...  3.92 us
    ppermute x1, starting transfers between devices, shift(): lax.ppermute(x, axis, [(i, i + by) for i in range(n) if 0 <= i + by < n])  1.97 us
    unnamed x12, local copies, waits for them, and re-layouts  1.07 us
  transfers between devices with their start and end apart: 7, of which 0 were waited for; matrix products, arithmetic and copies ran while one was open for 0% of the time, Pallas kernels for 22%

profile of v11, /device:TPU:1, one launch (start us, length us, event | category | flops | bytes accessed | tf_op | source)
XLA Modules:
  0.0 44.5 jit_solution(11588263245547001727)
XLA Ops:
  0.0 0.0 copy-start.4
  0.0 1.0 %copy-done.4 = bf16[4,8,32,135]{3,2,1,0:T(8,128)(2,1)S(1)} copy-done((bf16[4,8,32,135]{3,2,1,0:T(8,128)(2,1)S(1)}, bf16[4,8,32,135]{3,2,1,0:T(8,128)(2,1)}, u32[]{:S(2)}) %copy-start.4) | copy-done | bytes 276504
  1.0 0.4 initial_traces.1
  1.4 2.0 %collective-permute-start.2 = (bf16[48,256]{1,0:T(8,128)(2,1)S(1)}, bf16[48,256]{1,0:T(8,128)(2,1)S(1)}, u32[]{:S(2)}, u32[]{:S(2)}) collective-permute-start(bf16[48,256]{1,0:T(8,128)(2,1)S(1)} %get-tuple-element.40), channel_id=1, source_target_pairs={{8,0},{16,8},{24,16},{9,1},{17,9},{25,17},{10,2},{18,10},{26,18},{... | collective-permute-start | bytes 73736 | tf_op jit(solution)/shard_map/ppermute | solution.py:489
  3.4 2.7 %collective-permute-start = (bf16[304,256]{1,0:T(8,128)(2,1)S(1)}, bf16[304,256]{1,0:T(8,128)(2,1)S(1)}, u32[]{:S(2)}, u32[]{:S(2)}) collective-permute-start(bf16[304,256]{1,0:T(8,128)(2,1)S(1)} %get-tuple-element.35), channel_id=1, source_target_pairs={{0,1},{1,2},{2,3},{3,4},{4,5},{5,6},{6,7},{7,0},{8,9},{9,10},{10,1... | collective-permute-start | bytes 466952 | tf_op jit(solution)/shard_map/ppermute | solution.py:484
  6.1 3.1 %collective-permute-start.1 = (bf16[304,256]{1,0:T(8,128)(2,1)S(1)}, bf16[304,256]{1,0:T(8,128)(2,1)S(1)}, u32[]{:S(2)}, u32[]{:S(2)}) collective-permute-start(bf16[304,256]{1,0:T(8,128)(2,1)S(1)} %get-tuple-element.36), channel_id=1, source_target_pairs={{0,7},{1,0},{2,1},{3,2},{4,3},{5,4},{6,5},{7,6},{8,15},{9,8},{10,9... | collective-permute-start | bytes 466952 | tf_op jit(solution)/shard_map/ppermute | solution.py:484
  9.2 0.0 copy-start.1
  9.2 0.0 copy-start.2
  9.2 7.2 %weights.1 = (bf16[4,8,144,256]{3,2,1,0:T(8,128)(2,1)S(1)}, bf16[4,2,192,256]{3,2,1,0:T(8,128)(2,1)S(1)}, f32[4,144,256]{2,1,0:T(8,128)S(1)}, bf16[4,144,256]{2,...) custom-call(bf16[4,135,8,135]{3,2,1,0:T(8,128)(2,1)} %bitcast.10, bf16[4,6,45,8,135]{4,3,2,1,0:T(8,128)(2,1)} %bitcast.9, ...), custom_call_target="tpu_custom_call" | custom-call | flops 10000000000 | bytes 8607040 | tf_op jit(solution)/shard_map/weights/pallas_call | solution.py:445
  16.5 0.0 collective-permute-done.up
  16.5 0.0 collective-permute-done.1.down
  16.5 0.0 copy-done.1
  16.5 0.0 copy-done.2
  16.5 0.4 forward_gather.1.operand
  16.9 0.0 collective-permute-done.2.above
  16.9 0.0 copy-start
  16.9 0.9 %forward_chain.1 = (f32[4,144,256]{2,1,0:T(8,128)S(1)}, f32[4,48,256]{2,1,0:T(8,128)S(1)}, bf16[144,256]{1,0:T(8,128)(2,1)S(1)}) custom-call(bf16[4,192,256]{2,1,0:T(8,128)(2,1)S(1)} %forward_gather.1.operand, bf16[48,256]{1,0:T(8,128)(2,1)S(1)} %collective-permute-done.2.above, bf16[4,144,256]{2,1,0:T(8,128)(2,1)S(1)} %get-tuple-element.38.own, ...), custom_call_target="tpu_custom_call" | custom-call | flops 200000000 | bytes 5308416 | tf_op jit(solution)/shard_map/forward_chain/pallas_call | solution.py:445
  17.8 0.0 copy-start.5
  17.8 6.2 %all-gather = bf16[576,256]{1,0:T(8,128)(2,1)S(1)} all-gather(bf16[144,256]{1,0:T(8,128)(2,1)S(1)} %get-tuple-element.44), channel_id=2, replica_groups=mesh['sweep'=4,'cross'=8] {'sweep'}, dimensions={0}, use_global_device_ids=true | all-gather | bytes 368640 | tf_op jit(solution)/shard_map/all_gather | solution.py:533
  24.0 0.0 copy-done
  24.0 1.4 %forward_finish.1 = (bf16[4,144,256]{2,1,0:T(8,128)(2,1)S(1)}, f32[4,144,256]{2,1,0:T(8,128)S(1)}, bf16[304,256]{1,0:T(8,128)(2,1)S(1)}, bf16[304,256]{1,0:T(8,128)(2,1)S(1)}) custom-call(bf16[4,144,256]{2,1,0:T(8,128)(2,1)S(1)} %bitcast.7, f32[4,144,256]{2,1,0:T(8,128)S(1)} %get-tuple-element.45.part, f32[4,48,256]{2,1,0:T(8,128)S(1)} %get-tuple-element.46.traces, ...), custom_call_target="tpu_custom_call" | custom-call | flops 200000000 | bytes 3321856 | tf_op jit(solution)/shard_map/forward_finish/pallas_call | solution.py:445
  25.4 0.1 collective-permute-start.3
  25.4 4.1 %collective-permute-start.4 = (bf16[304,256]{1,0:T(8,128)(2,1)S(1)}, bf16[304,256]{1,0:T(8,128)(2,1)S(1)}, u32[]{:S(2)}, u32[]{:S(2)}) collective-permute-start(bf16[304,256]{1,0:T(8,128)(2,1)S(1)} %get-tuple-element.48), channel_id=1, source_target_pairs={{0,7},{1,0},{2,1},{3,2},{4,3},{5,4},{6,5},{7,6},{8,15},{9,8},{10,9... | collective-permute-start | bytes 466952 | tf_op jit(solution)/shard_map/ppermute | solution.py:484
  29.6 0.0 copy-done.5
  29.6 0.8 %middle.1 = (bf16[4,96,256]{2,1,0:T(8,128)(2,1)S(1)}, f32[4,144,256]{2,1,0:T(8,128)S(1)}, bf16[4,2,192,256]{3,2,1,0:T(8,128)(2,1)S(1)}) custom-call(bf16[4,144,256]{2,1,0:T(8,128)(2,1)S(1)} %get-tuple-element.49.middle, f32[4,144,256]{2,1,0:T(8,128)S(1)} %get-tuple-element.50.change, f32[4,144,256]{2,1,0:T(8,128)S(1)} %get-tuple-element.43.base, ...), custom_call_target="tpu_custom_call" | custom-call | flops 2000000000 | bytes 5958656 | tf_op jit(solution)/shard_map/middle/pallas_call | solution.py:445
  30.4 0.7 %collective-permute-start.6 = (bf16[2,48,256]{2,1,0:T(8,128)(2,1)S(1)}, bf16[2,48,256]{2,1,0:T(8,128)(2,1)S(1)}, u32[]{:S(2)}, u32[]{:S(2)}) collective-permute-start(bf16[2,48,256]{2,1,0:T(8,128)(2,1)S(1)} %slice_bitcast_fusion), channel_id=1, source_target_pairs={{16,0},{17,1},{18,2},{19,3},{20,4},{21,5},{22,6},{23,7}} | collective-permute-start | bytes 147464 | tf_op jit(solution)/shard_map/ppermute | solution.py:461
  31.1 3.3 %collective-permute-start.5 = (bf16[2,48,256]{2,1,0:T(8,128)(2,1)S(1)}, bf16[2,48,256]{2,1,0:T(8,128)(2,1)S(1)}, u32[]{:S(2)}, u32[]{:S(2)}) collective-permute-start(bf16[2,48,256]{2,1,0:T(8,128)(2,1)S(1)} %slice_bitcast_fusion), channel_id=1, source_target_pairs={{8,0},{16,8},{9,1},{17,9},{10,2},{18,10},{11,3},{19,11},{12,4},{20... | collective-permute-start | bytes 147464 | tf_op jit(solution)/shard_map/ppermute | solution.py:461
  34.4 0.0 collective-permute-done.3.up
  34.4 0.0 collective-permute-done.4.down
  34.4 0.0 copy-start.3
  34.4 1.2 %backward_chain.1 = (f32[4,144,256]{2,1,0:T(8,128)S(1)}, f32[4,48,256]{2,1,0:T(8,128)S(1)}, bf16[48,256]{1,0:T(8,128)(2,1)S(1)}) custom-call(bf16[304,256]{1,0:T(8,128)(2,1)S(1)} %collective-permute-done.3.up, bf16[304,256]{1,0:T(8,128)(2,1)S(1)} %collective-permute-done.4.down, bf16[4,96,256]{2,1,0:T(8,128)(2,1)S(1)} %get-tuple-element.53.own, ...), custom_call_target="tpu_custom_call" | custom-call | flops 200000000 | bytes 5750784 | tf_op jit(solution)/shard_map/backward_chain/pallas_call | solution.py:445
  35.6 6.0 %all-gather.1 = bf16[192,256]{1,0:T(8,128)(2,1)S(1)} all-gather(bf16[48,256]{1,0:T(8,128)(2,1)S(1)} %get-tuple-element.55), channel_id=3, replica_groups=mesh['sweep'=4,'cross'=8] {'sweep'}, dimensions={0}, use_global_device_ids=true | all-gather | bytes 122880 | tf_op jit(solution)/shard_map/all_gather | solution.py:557
  41.7 0.0 collective-permute-done.6.next_near
  41.7 0.0 collective-permute-done.5.near
  41.7 0.0 copy-done.3
  41.7 2.8 %backward_finish.1 = bf16[4,8,32,135]{3,2,1,0:T(8,128)(2,1)} custom-call(bf16[4,48,256]{2,1,0:T(8,128)(2,1)S(1)} %bitcast.8, bf16[2,48,256]{2,1,0:T(8,128)(2,1)S(1)} %collective-permute-done.5.near, bf16[2,48,256]{2,1,0:T(8,128)(2,1)S(1)} %collective-permute-done.6.next_near, f32[4,144,256]{2,1,0:T(8,128)S(1)} %get-tuple-element.57.part, ...), custom_call_target="tpu_custom_call" | custom-call | flops 200000000 | bytes 2084832 | tf_op jit(solution)/shard_map/backward_finish/pallas_call | solution.py:445
  (1 shorter events, 0.0 us)
Async XLA Ops:
  0.0 1.0 %copy-start.4 = (bf16[4,8,32,135]{3,2,1,0:T(8,128)(2,1)S(1)}, bf16[4,8,32,135]{3,2,1,0:T(8,128)(2,1)}, u32[]{:S(2)}) copy-start(bf16[4,8,32,135]{3,2,1,0:T(8,128)(2,1)} %initial_there) | copy-start | bytes 829444
  1.4 15.5 %collective-permute-start.2 = (bf16[48,256]{1,0:T(8,128)(2,1)S(1)}, bf16[48,256]{1,0:T(8,128)(2,1)S(1)}, u32[]{:S(2)}, u32[]{:S(2)}) collective-permute-start(bf16[48,256]{1,0:T(8,128)(2,1)S(1)} %get-tuple-element.40), channel_id=1, source_target_pairs={{8,0},{16,8},{24,16},{9,1},{17,9},{25,17},{10,2},{18,10},{26,18},{... | collective-permute-start | bytes 73736 | tf_op jit(solution)/shard_map/ppermute | solution.py:489
  3.4 13.1 %collective-permute-start = (bf16[304,256]{1,0:T(8,128)(2,1)S(1)}, bf16[304,256]{1,0:T(8,128)(2,1)S(1)}, u32[]{:S(2)}, u32[]{:S(2)}) collective-permute-start(bf16[304,256]{1,0:T(8,128)(2,1)S(1)} %get-tuple-element.35), channel_id=1, source_target_pairs={{0,1},{1,2},{2,3},{3,4},{4,5},{5,6},{6,7},{7,0},{8,9},{9,10},{10,1... | collective-permute-start | bytes 466952 | tf_op jit(solution)/shard_map/ppermute | solution.py:484
  6.1 10.3 %collective-permute-start.1 = (bf16[304,256]{1,0:T(8,128)(2,1)S(1)}, bf16[304,256]{1,0:T(8,128)(2,1)S(1)}, u32[]{:S(2)}, u32[]{:S(2)}) collective-permute-start(bf16[304,256]{1,0:T(8,128)(2,1)S(1)} %get-tuple-element.36), channel_id=1, source_target_pairs={{0,7},{1,0},{2,1},{3,2},{4,3},{5,4},{6,5},{7,6},{8,15},{9,8},{10,9... | collective-permute-start | bytes 466952 | tf_op jit(solution)/shard_map/ppermute | solution.py:484
  9.2 7.3 %copy-start.1 = (bf16[4,96,112]{2,1,0:T(8,128)(2,1)S(1)}, bf16[4,96,112]{2,1,0:T(8,128)(2,1)}, u32[]{:S(2)}) copy-start(bf16[4,96,112]{2,1,0:T(8,128)(2,1)} %constant.14.clone.down_sel) | copy-start | bytes 258052
  9.2 7.3 %copy-start.2 = (bf16[4,96,112]{2,1,0:T(8,128)(2,1)S(1)}, bf16[4,96,112]{2,1,0:T(8,128)(2,1)}, u32[]{:S(2)}) copy-start(bf16[4,96,112]{2,1,0:T(8,128)(2,1)} %constant.13.clone.up_sel) | copy-start | bytes 258052
  16.9 7.1 %copy-start = (bf16[4,224,144]{2,1,0:T(8,128)(2,1)S(1)}, bf16[4,224,144]{2,1,0:T(8,128)(2,1)}, u32[]{:S(2)}) copy-start(bf16[4,224,144]{2,1,0:T(8,128)(2,1)} %constant.10.clone.send) | copy-start | bytes 774148
  17.8 11.8 %copy-start.5 = (bf16[96,144]{1,0:T(8,128)(2,1)S(1)}, bf16[96,144]{1,0:T(8,128)(2,1)}, u32[]{:S(2)}) copy-start(bf16[96,144]{1,0:T(8,128)(2,1)} %constant.11.clone.own_sel) | copy-start | bytes 82948
  25.4 9.0 %collective-permute-start.3 = (bf16[304,256]{1,0:T(8,128)(2,1)S(1)}, bf16[304,256]{1,0:T(8,128)(2,1)S(1)}, u32[]{:S(2)}, u32[]{:S(2)}) collective-permute-start(bf16[304,256]{1,0:T(8,128)(2,1)S(1)} %get-tuple-element.47), channel_id=1, source_target_pairs={{0,1},{1,2},{2,3},{3,4},{4,5},{5,6},{6,7},{7,0},{8,9},{9,10},{10,1... | collective-permute-start | bytes 466952 | tf_op jit(solution)/shard_map/ppermute | solution.py:484
  25.4 8.9 %collective-permute-start.4 = (bf16[304,256]{1,0:T(8,128)(2,1)S(1)}, bf16[304,256]{1,0:T(8,128)(2,1)S(1)}, u32[]{:S(2)}, u32[]{:S(2)}) collective-permute-start(bf16[304,256]{1,0:T(8,128)(2,1)S(1)} %get-tuple-element.48), channel_id=1, source_target_pairs={{0,7},{1,0},{2,1},{3,2},{4,3},{5,4},{6,5},{7,6},{8,15},{9,8},{10,9... | collective-permute-start | bytes 466952 | tf_op jit(solution)/shard_map/ppermute | solution.py:484
  30.4 11.3 %collective-permute-start.6 = (bf16[2,48,256]{2,1,0:T(8,128)(2,1)S(1)}, bf16[2,48,256]{2,1,0:T(8,128)(2,1)S(1)}, u32[]{:S(2)}, u32[]{:S(2)}) collective-permute-start(bf16[2,48,256]{2,1,0:T(8,128)(2,1)S(1)} %slice_bitcast_fusion), channel_id=1, source_target_pairs={{16,0},{17,1},{18,2},{19,3},{20,4},{21,5},{22,6},{23,7}} | collective-permute-start | bytes 147464 | tf_op jit(solution)/shard_map/ppermute | solution.py:461
  31.1 10.6 %collective-permute-start.5 = (bf16[2,48,256]{2,1,0:T(8,128)(2,1)S(1)}, bf16[2,48,256]{2,1,0:T(8,128)(2,1)S(1)}, u32[]{:S(2)}, u32[]{:S(2)}) collective-permute-start(bf16[2,48,256]{2,1,0:T(8,128)(2,1)S(1)} %slice_bitcast_fusion), channel_id=1, source_target_pairs={{8,0},{16,8},{9,1},{17,9},{10,2},{18,10},{11,3},{19,11},{12,4},{20... | collective-permute-start | bytes 147464 | tf_op jit(solution)/shard_map/ppermute | solution.py:461
  34.4 7.3 %copy-start.3 = (bf16[135,144]{1,0:T(8,128)(2,1)S(1)}, bf16[135,144]{1,0:T(8,128)(2,1)}, u32[]{:S(2)}) copy-start(bf16[135,144]{1,0:T(8,128)(2,1)} %constant.12.clone.back) | copy-start | bytes 116644

commit v12 on v11

--- a/solution.py
+++ b/solution.py
@@ -175,13 +175,15 @@
 
 
 def put_shared(out, ups, downs):
-    planes = len(out)
     height = out[0].shape[0] // 2
-    for target, start in ((ups, 0), (downs, height)):
-        for p in range(planes):
-            target[p * MAIN : (p + 1) * MAIN] = out[p][start : start + MAIN].astype(BF)
+    for pieces, start in ((ups, 0), (downs, height)):
         tails = [x[start + MAIN : start + height] for x in out]
-        target[planes * MAIN :] = sum(tails[1:], tails[0]).astype(BF)
+        parts = [x[start : start + MAIN] for x in out] + [sum(tails[1:], tails[0])]
+        whole = jnp.concatenate(parts, 0).astype(BF)
+        first = 0
+        for piece in pieces:
+            piece[...] = whole[first : first + piece.shape[0]]
+            first += piece.shape[0]
 
 
 def first_kernel(initial, up, down, above):
@@ -194,7 +196,7 @@
         out.append(mt(jnp.concatenate(tables, 0), x))
         if p == 0:
             above[...] = mt(picks(first_target(rows_of(FACE)), width), x).astype(BF)
-    put_shared(out, up, down)
+    put_shared(out, [up], [down])
 
 
 def turned(rows, raw, put):
@@ -295,6 +297,7 @@
     planes = up_sel.shape[0]
 
     def faces(received, select):
+        received = jnp.concatenate([x[...] for x in received], 0)
         tail = received[planes * MAIN :]
         wholes = [jnp.concatenate([received[p * MAIN : (p + 1) * MAIN], tail], 0) for p in range(planes)]
         return [mm(select[p], wholes[p]).astype(BF) for p in range(planes)]
@@ -305,11 +308,6 @@
         picked = mm(jnp.concatenate([x[FACE:] for x in side], 0), gathers[j, j]).astype(BF)
         sides.append([picked[p * FACE : (p + 1) * FACE] + own[p, j * FACE : (j + 1) * FACE] for p in range(planes)])
     return [jnp.concatenate([low[p][:FACE], high[p][:FACE], sides[0][p], sides[1][p]], 0) for p in range(planes)]
-
-
-def gather_kernel(up, down, own, gathers, up_sel, down_sel, operand):
-    for p, whole in enumerate(gathered(up, down, own, up_sel, down_sel, gathers)):
-        operand[p] = whole
 
 
 def known_part(known_c, operand, columns, rhs):
@@ -338,15 +336,18 @@
             message[(1 + h) * FACE : (2 + h) * FACE] = matrix[order[-1], h, PRODUCT]
 
 
-def forward_chain_kernel(operand, above, own, known, lower, base, *outs, rhs):
-    planes, _, size = operand.shape
+def forward_chain_kernel(up, down, above, own, gathers, up_sel, down_sel, known, lower, base, *outs, rhs):
+    wholes = gathered([up], [down], own, up_sel, down_sel, gathers)
+    planes, size = len(wholes), above.shape[1]
     pad = jnp.zeros((256 - 5 * FACE, size), BF)
     last_face = lambda p: jnp.concatenate([own[p, LAST] if p + 1 < planes else above[...], pad], 0)
-    chain_kernel(known, base, lower, operand, outs, range(planes), LAST, rhs, last_face)
-
-
-def backward_chain_kernel(up, down, own, gathers, up_sel, down_sel, known, upper, base, *outs, rhs):
-    wholes = gathered(up, down, own, up_sel, down_sel, gathers)
+    chain_kernel(known, base, lower, wholes, outs, range(planes), LAST, rhs, last_face)
+
+
+def backward_chain_kernel(
+    up, up_rest, down, down_rest, own, gathers, up_sel, down_sel, known, upper, base, *outs, rhs
+):
+    wholes = gathered([up, up_rest], [down, down_rest], own, up_sel, down_sel, gathers)
     last_face = lambda p: jnp.zeros((256 - 4 * FACE, up.shape[1]), BF)
     chain_kernel(known, base, upper, wholes, outs, range(len(wholes) - 1, -1, -1), FIRST, rhs, last_face)
 
@@ -368,7 +369,7 @@
 
 
 def forward_finish_kernel(
-    messages, part, traces, lower, send, middle, change, up, down, *, rhs
+    messages, part, traces, lower, send, middle, change, *pieces, rhs
 ):
     planes = part.shape[0]
     inside = lambda i: [messages[i, (1 + h) * FACE : (2 + h) * FACE] for h in range(2)]
@@ -383,7 +384,7 @@
         out.append(mm(send[p], whole))
         if p + 1 < planes:
             trace = traces[p] + chain_step(lower.at[p], entry, rhs, PRODUCT)
-    put_shared(out, up, down)
+    put_shared(out, pieces[:2], pieces[2:])
 
 
 def middle_kernel(middle, change, base, gathers, own_sel, known, own, out, upper):
@@ -518,27 +519,23 @@
     field = (planes, ROWS, size)
     trace = (planes, FACE, size)
     chain_outs = [(field, F32), (trace, F32)]
-    (operand,) = call(
-        gather_kernel,
-        [((planes, 4 * FACE, size), BF)],
-        (from_low, from_high, own, gathers, up_sel, down_sel),
-        "forward_gather",
-    )
     part, traces, message = call(
         functools.partial(forward_chain_kernel, rhs=rhs),
         chain_outs + [((3 * FACE, size), BF)],
-        (operand, from_above, own, known, lower, base),
+        (from_low, from_high, from_above, own, gathers, up_sel, down_sel, known, lower, base),
         "forward_chain",
     )
     messages = lax.all_gather(message, "sweep")
-    middle, change, up, down = call(
+    split = share[0] // 32 * 16
+    halves = [((rows, size), BF) for rows in (share[0] - split, split)]
+    middle, change, *pieces = call(
         functools.partial(forward_finish_kernel, rhs=rhs),
-        [(field, BF), (field, F32), (share, BF), (share, BF)],
+        [(field, BF), (field, F32)] + halves * 2,
         (messages, part, traces, lower, send_in),
         "forward_finish",
     )
-    from_low = ring(up, "cross", 1)
-    from_high = ring(down, "cross", -1)
+    from_low = [ring(x, "cross", 1) for x in pieces[:2]]
+    from_high = [ring(x, "cross", -1) for x in pieces[2:]]
     own, base, upper = call(
         middle_kernel,
         [((planes, 2 * FACE, size), BF), (field, F32), (lower.shape, BF)],
@@ -551,7 +548,7 @@
     part, traces, message = call(
         functools.partial(backward_chain_kernel, rhs=rhs),
         chain_outs + [((FACE, size), BF)],
-        (from_low, from_high, own, gathers, up_sel, down_sel, known, upper, base),
+        (*from_low, *from_high, own, gathers, up_sel, down_sel, known, upper, base),
         "backward_chain",
     )
     messages = lax.all_gather(message, "sweep")

time: 44.9 us -> 48.8 us (1.087)
  starting transfers between devices: 15.9 us -> 20.7 us
  blocking collectives: 12.2 us -> 11.4 us
    ppermute x4 -> x6, starting transfers between devices: 10.1 us -> 14.2 us  [ring(): return lax.ppermute(x, axis, [(i, (i + by) % n) for i in range(n)])]
    all_gather x2, blocking collectives: 12.2 us -> 11.4 us  [local(): messages = lax.all_gather(message, 'sweep')]
    ppermute x2, starting transfers between devices: 3.92 us -> 4.48 us  [products(): lax.ppermute(x, 'sweep', [(i, i + step) for i in inner if 0 <= i + step <...]
    pallas_call x8 -> x7, Pallas kernels: 15.1 us -> 15.1 us  [call(): pl.pallas_call(kernel, out_shape=shapes, in_specs=[pl.BlockSpec(memory_sp...]
  transfers between devices with their start and end apart: 7 -> 9, of which waited for: 0 -> 0; matrix products, arithmetic and copies ran while one was open for 0% -> 0% of each run, Pallas kernels for 22% -> 19%
where the time goes in v12:
time: 48.8 us; the launch traced here: 48.4 us
  starting transfers between devices  20.7 us (42%)
  Pallas kernels  15.1 us (31%)
  blocking collectives  11.4 us (23%)
  local copies, waits for them, and re-layouts  1.07 us (2%)
    pallas_call x7, Pallas kernels, call(): pl.pallas_call(kernel, out_shape=shapes, in_specs=[pl.BlockSpec(memory_sp...  15.1 us
    ppermute x6, starting transfers between devices, ring(): return lax.ppermute(x, axis, [(i, (i + by) % n) for i in range(n)])  14.2 us
    all_gather x2, blocking collectives, local(): messages = lax.all_gather(message, 'sweep')  11.4 us
    ppermute x2, starting transfers between devices, products(): lax.ppermute(x, 'sweep', [(i, i + step) for i in inner if 0 <= i + step <...  4.48 us
    ppermute x1, starting transfers between devices, shift(): lax.ppermute(x, axis, [(i, i + by) for i in range(n) if 0 <= i + by < n])  1.97 us
    unnamed x12, local copies, waits for them, and re-layouts  1.07 us
  transfers between devices with their start and end apart: 9, of which 0 were waited for; matrix products, arithmetic and copies ran while one was open for 0% of the time, Pallas kernels for 19%

profile of v12, /device:TPU:1, one launch (start us, length us, event | category | flops | bytes accessed | tf_op | source)
XLA Modules:
  0.0 48.4 jit_solution(13669693599191381992)
XLA Ops:
  0.0 0.0 copy-start.4
  0.0 1.0 %copy-done.4 = bf16[4,8,32,135]{3,2,1,0:T(8,128)(2,1)S(1)} copy-done((bf16[4,8,32,135]{3,2,1,0:T(8,128)(2,1)S(1)}, bf16[4,8,32,135]{3,2,1,0:T(8,128)(2,1)}, u32[]{:S(2)}) %copy-start.4) | copy-done | bytes 276504
  1.0 0.4 initial_traces.1
  1.4 2.0 %collective-permute-start.2 = (bf16[48,256]{1,0:T(8,128)(2,1)S(1)}, bf16[48,256]{1,0:T(8,128)(2,1)S(1)}, u32[]{:S(2)}, u32[]{:S(2)}) collective-permute-start(bf16[48,256]{1,0:T(8,128)(2,1)S(1)} %get-tuple-element.39), channel_id=1, source_target_pairs={{8,0},{16,8},{24,16},{9,1},{17,9},{25,17},{10,2},{18,10},{26,18},{... | collective-permute-start | bytes 73736 | tf_op jit(solution)/shard_map/ppermute | solution.py:490
  3.4 2.7 %collective-permute-start = (bf16[304,256]{1,0:T(8,128)(2,1)S(1)}, bf16[304,256]{1,0:T(8,128)(2,1)S(1)}, u32[]{:S(2)}, u32[]{:S(2)}) collective-permute-start(bf16[304,256]{1,0:T(8,128)(2,1)S(1)} %get-tuple-element.37), channel_id=1, source_target_pairs={{0,1},{1,2},{2,3},{3,4},{4,5},{5,6},{6,7},{7,0},{8,9},{9,10},{10,1... | collective-permute-start | bytes 466952 | tf_op jit(solution)/shard_map/ppermute | solution.py:485
  6.1 3.1 %collective-permute-start.1 = (bf16[304,256]{1,0:T(8,128)(2,1)S(1)}, bf16[304,256]{1,0:T(8,128)(2,1)S(1)}, u32[]{:S(2)}, u32[]{:S(2)}) collective-permute-start(bf16[304,256]{1,0:T(8,128)(2,1)S(1)} %get-tuple-element.38), channel_id=1, source_target_pairs={{0,7},{1,0},{2,1},{3,2},{4,3},{5,4},{6,5},{7,6},{8,15},{9,8},{10,9... | collective-permute-start | bytes 466952 | tf_op jit(solution)/shard_map/ppermute | solution.py:485
  9.2 0.0 copy-start.1
  9.2 0.0 copy-start.2
  9.2 7.2 %weights.1 = (bf16[4,8,144,256]{3,2,1,0:T(8,128)(2,1)S(1)}, bf16[4,2,192,256]{3,2,1,0:T(8,128)(2,1)S(1)}, f32[4,144,256]{2,1,0:T(8,128)S(1)}, bf16[4,144,256]{2,...) custom-call(bf16[4,135,8,135]{3,2,1,0:T(8,128)(2,1)} %bitcast.10, bf16[4,6,45,8,135]{4,3,2,1,0:T(8,128)(2,1)} %bitcast.9, ...), custom_call_target="tpu_custom_call" | custom-call | flops 10000000000 | bytes 8607040 | tf_op jit(solution)/shard_map/weights/pallas_call | solution.py:446
  16.5 0.0 collective-permute-done.2.above
  16.5 0.0 collective-permute-done.up
  16.5 0.0 collective-permute-done.1.down
  16.5 0.0 copy-done.1
  16.5 0.0 copy-done.2
  16.5 0.0 copy-start
  16.5 1.2 %forward_chain.1 = (f32[4,144,256]{2,1,0:T(8,128)S(1)}, f32[4,48,256]{2,1,0:T(8,128)S(1)}, bf16[144,256]{1,0:T(8,128)(2,1)S(1)}) custom-call(bf16[304,256]{1,0:T(8,128)(2,1)S(1)} %collective-permute-done.up, bf16[304,256]{1,0:T(8,128)(2,1)S(1)} %collective-permute-done.1.down, bf16[48,256]{1,0:T(8,128)(2,1)S(1)} %collective-permute-done.2.above, ...), custom_call_target="tpu_custom_call" | custom-call | flops 200000000 | bytes 5922816 | tf_op jit(solution)/shard_map/forward_chain/pallas_call | solution.py:446
  17.8 0.0 copy-start.5
  17.8 6.2 %all-gather = bf16[576,256]{1,0:T(8,128)(2,1)S(1)} all-gather(bf16[144,256]{1,0:T(8,128)(2,1)S(1)} %get-tuple-element.46), channel_id=2, replica_groups=mesh['sweep'=4,'cross'=8] {'sweep'}, dimensions={0}, use_global_device_ids=true | all-gather | bytes 368640 | tf_op jit(solution)/shard_map/all_gather | solution.py:528
  24.0 0.0 copy-done
  24.0 1.4 %forward_finish.1 = (bf16[4,144,256]{2,1,0:T(8,128)(2,1)S(1)}, f32[4,144,256]{2,1,0:T(8,128)S(1)}, bf16[160,256]{1,0:T(8,128)(2,1)S(1)}, bf16[144,256]{1,0:T(8,1...) custom-call(bf16[4,144,256]{2,1,0:T(8,128)(2,1)S(1)} %bitcast.7, ...), custom_call_target="tpu_custom_call" | custom-call | flops 200000000 | bytes 3321856 | tf_op jit(solution)/shard_map/forward_finish/pallas_call | solution.py:446
  25.3 0.1 collective-permute-start.4
  25.4 4.1 %collective-permute-start.6 = (bf16[144,256]{1,0:T(8,128)(2,1)S(1)}, bf16[144,256]{1,0:T(8,128)(2,1)S(1)}, u32[]{:S(2)}, u32[]{:S(2)}) collective-permute-start(bf16[144,256]{1,0:T(8,128)(2,1)S(1)} %get-tuple-element.52), channel_id=1, source_target_pairs={{0,7},{1,0},{2,1},{3,2},{4,3},{5,4},{6,5},{7,6},{8,15},{9,8},{10,9... | collective-permute-start | bytes 221192 | tf_op jit(solution)/shard_map/ppermute | solution.py:485
  29.6 0.0 collective-permute-start.3
  29.6 4.2 %collective-permute-start.5 = (bf16[160,256]{1,0:T(8,128)(2,1)S(1)}, bf16[160,256]{1,0:T(8,128)(2,1)S(1)}, u32[]{:S(2)}, u32[]{:S(2)}) collective-permute-start(bf16[160,256]{1,0:T(8,128)(2,1)S(1)} %get-tuple-element.51), channel_id=1, source_target_pairs={{0,7},{1,0},{2,1},{3,2},{4,3},{5,4},{6,5},{7,6},{8,15},{9,8},{10,9... | collective-permute-start | bytes 245768 | tf_op jit(solution)/shard_map/ppermute | solution.py:485
  33.7 0.0 copy-done.5
  33.7 0.8 %middle.1 = (bf16[4,96,256]{2,1,0:T(8,128)(2,1)S(1)}, f32[4,144,256]{2,1,0:T(8,128)S(1)}, bf16[4,2,192,256]{3,2,1,0:T(8,128)(2,1)S(1)}) custom-call(bf16[4,144,256]{2,1,0:T(8,128)(2,1)S(1)} %get-tuple-element.53.middle, f32[4,144,256]{2,1,0:T(8,128)S(1)} %get-tuple-element.54.change, f32[4,144,256]{2,1,0:T(8,128)S(1)} %get-tuple-element.45.base, ...), custom_call_target="tpu_custom_call" | custom-call | flops 2000000000 | bytes 5958656 | tf_op jit(solution)/shard_map/middle/pallas_call | solution.py:446
  34.5 0.7 %collective-permute-start.8 = (bf16[2,48,256]{2,1,0:T(8,128)(2,1)S(1)}, bf16[2,48,256]{2,1,0:T(8,128)(2,1)S(1)}, u32[]{:S(2)}, u32[]{:S(2)}) collective-permute-start(bf16[2,48,256]{2,1,0:T(8,128)(2,1)S(1)} %slice_bitcast_fusion), channel_id=1, source_target_pairs={{16,0},{17,1},{18,2},{19,3},{20,4},{21,5},{22,6},{23,7}} | collective-permute-start | bytes 147464 | tf_op jit(solution)/shard_map/ppermute | solution.py:462
  35.2 0.0 collective-permute-done.4.up_rest
  35.2 3.8 %collective-permute-start.7 = (bf16[2,48,256]{2,1,0:T(8,128)(2,1)S(1)}, bf16[2,48,256]{2,1,0:T(8,128)(2,1)S(1)}, u32[]{:S(2)}, u32[]{:S(2)}) collective-permute-start(bf16[2,48,256]{2,1,0:T(8,128)(2,1)S(1)} %slice_bitcast_fusion), channel_id=1, source_target_pairs={{8,0},{16,8},{9,1},{17,9},{10,2},{18,10},{11,3},{19,11},{12,4},{20... | collective-permute-start | bytes 147464 | tf_op jit(solution)/shard_map/ppermute | solution.py:462
  39.1 0.0 collective-permute-done.6.down_rest
  39.1 0.0 collective-permute-done.3.up
  39.1 0.0 collective-permute-done.5.down
  39.1 0.0 copy-start.3
  39.1 1.3 %backward_chain.1 = (f32[4,144,256]{2,1,0:T(8,128)S(1)}, f32[4,48,256]{2,1,0:T(8,128)S(1)}, bf16[48,256]{1,0:T(8,128)(2,1)S(1)}) custom-call(bf16[160,256]{1,0:T(8,128)(2,1)S(1)} %collective-permute-done.3.up, bf16[144,256]{1,0:T(8,128)(2,1)S(1)} %collective-permute-done.4.up_rest, bf16[160,256]{1,0:T(8,128)(2,1)S(1)} %collective-permute-done.5.down, ...), custom_call_target="tpu_custom_call" | custom-call | flops 200000000 | bytes 5750784 | tf_op jit(solution)/shard_map/backward_chain/pallas_call | solution.py:446
  40.4 5.2 %all-gather.1 = bf16[192,256]{1,0:T(8,128)(2,1)S(1)} all-gather(bf16[48,256]{1,0:T(8,128)(2,1)S(1)} %get-tuple-element.59), channel_id=3, replica_groups=mesh['sweep'=4,'cross'=8] {'sweep'}, dimensions={0}, use_global_device_ids=true | all-gather | bytes 122880 | tf_op jit(solution)/shard_map/all_gather | solution.py:554
  45.6 0.0 collective-permute-done.8.next_near
  45.6 0.0 collective-permute-done.7.near
  45.6 0.0 copy-done.3
  45.6 2.8 %backward_finish.1 = bf16[4,8,32,135]{3,2,1,0:T(8,128)(2,1)} custom-call(bf16[4,48,256]{2,1,0:T(8,128)(2,1)S(1)} %bitcast.8, bf16[2,48,256]{2,1,0:T(8,128)(2,1)S(1)} %collective-permute-done.7.near, bf16[2,48,256]{2,1,0:T(8,128)(2,1)S(1)} %collective-permute-done.8.next_near, f32[4,144,256]{2,1,0:T(8,128)S(1)} %get-tuple-element.61.part, ...), custom_call_target="tpu_custom_call" | custom-call | flops 200000000 | bytes 2084832 | tf_op jit(solution)/shard_map/backward_finish/pallas_call | solution.py:446
  (1 shorter events, 0.0 us)
Async XLA Ops:
  0.0 1.0 %copy-start.4 = (bf16[4,8,32,135]{3,2,1,0:T(8,128)(2,1)S(1)}, bf16[4,8,32,135]{3,2,1,0:T(8,128)(2,1)}, u32[]{:S(2)}) copy-start(bf16[4,8,32,135]{3,2,1,0:T(8,128)(2,1)} %initial_there) | copy-start | bytes 829444
  1.4 15.1 %collective-permute-start.2 = (bf16[48,256]{1,0:T(8,128)(2,1)S(1)}, bf16[48,256]{1,0:T(8,128)(2,1)S(1)}, u32[]{:S(2)}, u32[]{:S(2)}) collective-permute-start(bf16[48,256]{1,0:T(8,128)(2,1)S(1)} %get-tuple-element.39), channel_id=1, source_target_pairs={{8,0},{16,8},{24,16},{9,1},{17,9},{25,17},{10,2},{18,10},{26,18},{... | collective-permute-start | bytes 73736 | tf_op jit(solution)/shard_map/ppermute | solution.py:490
  3.4 13.1 %collective-permute-start = (bf16[304,256]{1,0:T(8,128)(2,1)S(1)}, bf16[304,256]{1,0:T(8,128)(2,1)S(1)}, u32[]{:S(2)}, u32[]{:S(2)}) collective-permute-start(bf16[304,256]{1,0:T(8,128)(2,1)S(1)} %get-tuple-element.37), channel_id=1, source_target_pairs={{0,1},{1,2},{2,3},{3,4},{4,5},{5,6},{6,7},{7,0},{8,9},{9,10},{10,1... | collective-permute-start | bytes 466952 | tf_op jit(solution)/shard_map/ppermute | solution.py:485
  6.1 10.4 %collective-permute-start.1 = (bf16[304,256]{1,0:T(8,128)(2,1)S(1)}, bf16[304,256]{1,0:T(8,128)(2,1)S(1)}, u32[]{:S(2)}, u32[]{:S(2)}) collective-permute-start(bf16[304,256]{1,0:T(8,128)(2,1)S(1)} %get-tuple-element.38), channel_id=1, source_target_pairs={{0,7},{1,0},{2,1},{3,2},{4,3},{5,4},{6,5},{7,6},{8,15},{9,8},{10,9... | collective-permute-start | bytes 466952 | tf_op jit(solution)/shard_map/ppermute | solution.py:485
  9.2 7.3 %copy-start.1 = (bf16[4,96,112]{2,1,0:T(8,128)(2,1)S(1)}, bf16[4,96,112]{2,1,0:T(8,128)(2,1)}, u32[]{:S(2)}) copy-start(bf16[4,96,112]{2,1,0:T(8,128)(2,1)} %constant.14.clone.down_sel) | copy-start | bytes 258052
  9.2 7.3 %copy-start.2 = (bf16[4,96,112]{2,1,0:T(8,128)(2,1)S(1)}, bf16[4,96,112]{2,1,0:T(8,128)(2,1)}, u32[]{:S(2)}) copy-start(bf16[4,96,112]{2,1,0:T(8,128)(2,1)} %constant.13.clone.up_sel) | copy-start | bytes 258052
  16.5 7.5 %copy-start = (bf16[4,224,144]{2,1,0:T(8,128)(2,1)S(1)}, bf16[4,224,144]{2,1,0:T(8,128)(2,1)}, u32[]{:S(2)}) copy-start(bf16[4,224,144]{2,1,0:T(8,128)(2,1)} %constant.10.clone.send) | copy-start | bytes 774148
  17.8 16.0 %copy-start.5 = (bf16[96,144]{1,0:T(8,128)(2,1)S(1)}, bf16[96,144]{1,0:T(8,128)(2,1)}, u32[]{:S(2)}) copy-start(bf16[96,144]{1,0:T(8,128)(2,1)} %constant.11.clone.own_sel) | copy-start | bytes 82948
  25.3 9.9 %collective-permute-start.4 = (bf16[144,256]{1,0:T(8,128)(2,1)S(1)}, bf16[144,256]{1,0:T(8,128)(2,1)S(1)}, u32[]{:S(2)}, u32[]{:S(2)}) collective-permute-start(bf16[144,256]{1,0:T(8,128)(2,1)S(1)} %get-tuple-element.50), channel_id=1, source_target_pairs={{0,1},{1,2},{2,3},{3,4},{4,5},{5,6},{6,7},{7,0},{8,9},{9,10},{10,1... | collective-permute-start | bytes 221192 | tf_op jit(solution)/shard_map/ppermute | solution.py:485
  25.4 13.7 %collective-permute-start.6 = (bf16[144,256]{1,0:T(8,128)(2,1)S(1)}, bf16[144,256]{1,0:T(8,128)(2,1)S(1)}, u32[]{:S(2)}, u32[]{:S(2)}) collective-permute-start(bf16[144,256]{1,0:T(8,128)(2,1)S(1)} %get-tuple-element.52), channel_id=1, source_target_pairs={{0,7},{1,0},{2,1},{3,2},{4,3},{5,4},{6,5},{7,6},{8,15},{9,8},{10,9... | collective-permute-start | bytes 221192 | tf_op jit(solution)/shard_map/ppermute | solution.py:485
  29.6 9.5 %collective-permute-start.3 = (bf16[160,256]{1,0:T(8,128)(2,1)S(1)}, bf16[160,256]{1,0:T(8,128)(2,1)S(1)}, u32[]{:S(2)}, u32[]{:S(2)}) collective-permute-start(bf16[160,256]{1,0:T(8,128)(2,1)S(1)} %get-tuple-element.49), channel_id=1, source_target_pairs={{0,1},{1,2},{2,3},{3,4},{4,5},{5,6},{6,7},{7,0},{8,9},{9,10},{10,1... | collective-permute-start | bytes 245768 | tf_op jit(solution)/shard_map/ppermute | solution.py:485
  29.6 9.5 %collective-permute-start.5 = (bf16[160,256]{1,0:T(8,128)(2,1)S(1)}, bf16[160,256]{1,0:T(8,128)(2,1)S(1)}, u32[]{:S(2)}, u32[]{:S(2)}) collective-permute-start(bf16[160,256]{1,0:T(8,128)(2,1)S(1)} %get-tuple-element.51), channel_id=1, source_target_pairs={{0,7},{1,0},{2,1},{3,2},{4,3},{5,4},{6,5},{7,6},{8,15},{9,8},{10,9... | collective-permute-start | bytes 245768 | tf_op jit(solution)/shard_map/ppermute | solution.py:485
  34.5 11.0 %collective-permute-start.8 = (bf16[2,48,256]{2,1,0:T(8,128)(2,1)S(1)}, bf16[2,48,256]{2,1,0:T(8,128)(2,1)S(1)}, u32[]{:S(2)}, u32[]{:S(2)}) collective-permute-start(bf16[2,48,256]{2,1,0:T(8,128)(2,1)S(1)} %slice_bitcast_fusion), channel_id=1, source_target_pairs={{16,0},{17,1},{18,2},{19,3},{20,4},{21,5},{22,6},{23,7}} | collective-permute-start | bytes 147464 | tf_op jit(solution)/shard_map/ppermute | solution.py:462
  35.2 10.4 %collective-permute-start.7 = (bf16[2,48,256]{2,1,0:T(8,128)(2,1)S(1)}, bf16[2,48,256]{2,1,0:T(8,128)(2,1)S(1)}, u32[]{:S(2)}, u32[]{:S(2)}) collective-permute-start(bf16[2,48,256]{2,1,0:T(8,128)(2,1)S(1)} %slice_bitcast_fusion), channel_id=1, source_target_pairs={{8,0},{16,8},{9,1},{17,9},{10,2},{18,10},{11,3},{19,11},{12,4},{20... | collective-permute-start | bytes 147464 | tf_op jit(solution)/shard_map/ppermute | solution.py:462
  39.1 6.5 %copy-start.3 = (bf16[135,144]{1,0:T(8,128)(2,1)S(1)}, bf16[135,144]{1,0:T(8,128)(2,1)}, u32[]{:S(2)}) copy-start(bf16[135,144]{1,0:T(8,128)(2,1)} %constant.12.clone.back) | copy-start | bytes 116644

commit v13 on v12

--- a/solution.py
+++ b/solution.py
@@ -174,19 +174,23 @@
     return out
 
 
-def put_shared(out, ups, downs):
+def even():
+    return lax.rem(lax.axis_index("cross"), 2) == 0
+
+
+def put_shared(out, near, far):
     height = out[0].shape[0] // 2
-    for pieces, start in ((ups, 0), (downs, height)):
+    messages = []
+    for start in (0, height):
         tails = [x[start + MAIN : start + height] for x in out]
         parts = [x[start : start + MAIN] for x in out] + [sum(tails[1:], tails[0])]
-        whole = jnp.concatenate(parts, 0).astype(BF)
-        first = 0
-        for piece in pieces:
-            piece[...] = whole[first : first + piece.shape[0]]
-            first += piece.shape[0]
-
-
-def first_kernel(initial, up, down, above):
+        messages.append(jnp.concatenate(parts, 0))
+    up, down = messages
+    near[...] = jnp.where(even(), up, down).astype(BF)
+    far[...] = jnp.where(even(), down, up).astype(BF)
+
+
+def first_kernel(initial, near, far, above):
     planes, columns, rhs, width = initial.shape
     row = rows_of(MAIN + tail_rows(planes))
     out = []
@@ -196,7 +200,7 @@
         out.append(mt(jnp.concatenate(tables, 0), x))
         if p == 0:
             above[...] = mt(picks(first_target(rows_of(FACE)), width), x).astype(BF)
-    put_shared(out, [up], [down])
+    put_shared(out, near, far)
 
 
 def turned(rows, raw, put):
@@ -293,16 +297,16 @@
             matrix[q, h, PRODUCT] = total.astype(BF)
 
 
-def gathered(received_up, received_down, own, up_sel, down_sel, gathers):
+def gathered(near, far, own, up_sel, down_sel, gathers):
     planes = up_sel.shape[0]
 
     def faces(received, select):
-        received = jnp.concatenate([x[...] for x in received], 0)
         tail = received[planes * MAIN :]
         wholes = [jnp.concatenate([received[p * MAIN : (p + 1) * MAIN], tail], 0) for p in range(planes)]
         return [mm(select[p], wholes[p]).astype(BF) for p in range(planes)]
 
-    low, high = faces(received_up, up_sel), faces(received_down, down_sel)
+    low = faces(jnp.where(even(), far[...], near[...]), up_sel)
+    high = faces(jnp.where(even(), near[...], far[...]), down_sel)
     sides = []
     for j, side in enumerate((low, high)):
         picked = mm(jnp.concatenate([x[FACE:] for x in side], 0), gathers[j, j]).astype(BF)
@@ -336,19 +340,17 @@
             message[(1 + h) * FACE : (2 + h) * FACE] = matrix[order[-1], h, PRODUCT]
 
 
-def forward_chain_kernel(up, down, above, own, gathers, up_sel, down_sel, known, lower, base, *outs, rhs):
-    wholes = gathered([up], [down], own, up_sel, down_sel, gathers)
+def forward_chain_kernel(near, far, above, own, gathers, up_sel, down_sel, known, lower, base, *outs, rhs):
+    wholes = gathered(near, far, own, up_sel, down_sel, gathers)
     planes, size = len(wholes), above.shape[1]
     pad = jnp.zeros((256 - 5 * FACE, size), BF)
     last_face = lambda p: jnp.concatenate([own[p, LAST] if p + 1 < planes else above[...], pad], 0)
     chain_kernel(known, base, lower, wholes, outs, range(planes), LAST, rhs, last_face)
 
 
-def backward_chain_kernel(
-    up, up_rest, down, down_rest, own, gathers, up_sel, down_sel, known, upper, base, *outs, rhs
-):
-    wholes = gathered([up, up_rest], [down, down_rest], own, up_sel, down_sel, gathers)
-    last_face = lambda p: jnp.zeros((256 - 4 * FACE, up.shape[1]), BF)
+def backward_chain_kernel(near, far, own, gathers, up_sel, down_sel, known, upper, base, *outs, rhs):
+    wholes = gathered(near, far, own, up_sel, down_sel, gathers)
+    last_face = lambda p: jnp.zeros((256 - 4 * FACE, near.shape[1]), BF)
     chain_kernel(known, base, upper, wholes, outs, range(len(wholes) - 1, -1, -1), FIRST, rhs, last_face)
 
 
@@ -369,7 +371,7 @@
 
 
 def forward_finish_kernel(
-    messages, part, traces, lower, send, middle, change, *pieces, rhs
+    messages, part, traces, lower, send, middle, change, near, far, *, rhs
 ):
     planes = part.shape[0]
     inside = lambda i: [messages[i, (1 + h) * FACE : (2 + h) * FACE] for h in range(2)]
@@ -384,7 +386,7 @@
         out.append(mm(send[p], whole))
         if p + 1 < planes:
             trace = traces[p] + chain_step(lower.at[p], entry, rhs, PRODUCT)
-    put_shared(out, pieces[:2], pieces[2:])
+    put_shared(out, near, far)
 
 
 def middle_kernel(middle, change, base, gathers, own_sel, known, own, out, upper):
@@ -480,9 +482,10 @@
     return call(weight_kernel, outs, operands, "weights", 1e10, (0, 1, 2, 3, 4), scratch)
 
 
-def ring(x, axis, by):
+def swapped(x, axis, first):
     n = lax.axis_size(axis)
-    return lax.ppermute(x, axis, [(i, (i + by) % n) for i in range(n)])
+    pairs = [(i, (i + 1) % n) for i in range(first, n, 2)]
+    return lax.ppermute(x, axis, [pair for i, j in pairs for pair in ((i, j), (j, i))])
 
 
 def shift(x, axis, by):
@@ -502,15 +505,14 @@
     beside = neighbours.T
 
     share = (planes * MAIN + tail_rows(planes), size)
-    up, down, above = call(
+    near, far, above = call(
         first_kernel,
         [(share, BF), (share, BF), ((FACE, size), BF)],
         (initial,),
         "initial_traces",
     )
-    up, down, above, initial = lax.optimization_barrier((up, down, above, initial))
-    from_low = ring(up, "cross", 1)
-    from_high = ring(down, "cross", -1)
+    near, far, above, initial = lax.optimization_barrier((near, far, above, initial))
+    near, far = swapped(near, "cross", 0), swapped(far, "cross", 1)
     from_above = shift(above, "sweep", -1)
     known, lower, base, own, gathers = weights(
         inverse_blocks.transpose(0, 2, 1, 3), couplings.transpose(0, 2, 3, 1, 4), right_sides, initial, beside
@@ -522,20 +524,17 @@
     part, traces, message = call(
         functools.partial(forward_chain_kernel, rhs=rhs),
         chain_outs + [((3 * FACE, size), BF)],
-        (from_low, from_high, from_above, own, gathers, up_sel, down_sel, known, lower, base),
+        (near, far, from_above, own, gathers, up_sel, down_sel, known, lower, base),
         "forward_chain",
     )
     messages = lax.all_gather(message, "sweep")
-    split = share[0] // 32 * 16
-    halves = [((rows, size), BF) for rows in (share[0] - split, split)]
-    middle, change, *pieces = call(
+    middle, change, near, far = call(
         functools.partial(forward_finish_kernel, rhs=rhs),
-        [(field, BF), (field, F32)] + halves * 2,
+        [(field, BF), (field, F32), (share, BF), (share, BF)],
         (messages, part, traces, lower, send_in),
         "forward_finish",
     )
-    from_low = [ring(x, "cross", 1) for x in pieces[:2]]
-    from_high = [ring(x, "cross", -1) for x in pieces[2:]]
+    near, far = swapped(near, "cross", 0), swapped(far, "cross", 1)
     own, base, upper = call(
         middle_kernel,
         [((planes, 2 * FACE, size), BF), (field, F32), (lower.shape, BF)],
@@ -548,7 +547,7 @@
     part, traces, message = call(
         functools.partial(backward_chain_kernel, rhs=rhs),
         chain_outs + [((FACE, size), BF)],
-        (*from_low, *from_high, own, gathers, up_sel, down_sel, known, upper, base),
+        (near, far, own, gathers, up_sel, down_sel, known, upper, base),
         "backward_chain",
     )
     messages = lax.all_gather(message, "sweep")

time: 48.8 us -> 45.1 us (0.924)
  starting transfers between devices: 20.7 us -> 13.9 us
  blocking collectives: 11.4 us -> 13 us
  waiting for transfers between devices: 0.02 us -> 1.52 us
    ppermute x6 -> x4, starting transfers between devices: 14.2 us -> 8.03 us  [swapped(): lax.ppermute(x, axis, [pair for i, j in pairs for pair in ((i, j), (j, i))])]
    all_gather x2, blocking collectives: 11.4 us -> 13 us  [local(): messages = lax.all_gather(message, 'sweep')]
    ppermute x6 -> x4, waiting for transfers between devices: 0.02 us -> 1.51 us  [swapped(): lax.ppermute(x, axis, [pair for i, j in pairs for pair in ((i, j), (j, i))])]
    ppermute x2, starting transfers between devices: 4.48 us -> 3.93 us  [products(): lax.ppermute(x, 'sweep', [(i, i + step) for i in inner if 0 <= i + step <...]
  transfers between devices with their start and end apart: 9 -> 7, of which waited for: 0 -> 1; matrix products, arithmetic and copies ran while one was open for 0% -> 0% of each run, Pallas kernels for 19% -> 21%
where the time goes in v13:
time: 45.1 us; the launch traced here: 44.8 us
  Pallas kernels  15.1 us (33%)
  starting transfers between devices  13.9 us (31%)
  blocking collectives  13 us (29%)
  waiting for transfers between devices  1.52 us (3%)
  local copies, waits for them, and re-layouts  1.07 us (2%)
    pallas_call x7, Pallas kernels, call(): pl.pallas_call(kernel, out_shape=shapes, in_specs=[pl.BlockSpec(memory_sp...  15.1 us
    all_gather x2, blocking collectives, local(): messages = lax.all_gather(message, 'sweep')  13 us
    ppermute x4, starting transfers between devices, swapped(): lax.ppermute(x, axis, [pair for i, j in pairs for pair in ((i, j), (j, i))])  8.03 us
    ppermute x2, starting transfers between devices, products(): lax.ppermute(x, 'sweep', [(i, i + step) for i in inner if 0 <= i + step <...  3.93 us
    ppermute x1, starting transfers between devices, shift(): lax.ppermute(x, axis, [(i, i + by) for i in range(n) if 0 <= i + by < n])  1.97 us
    ppermute x4, waiting for transfers between devices, swapped(): lax.ppermute(x, axis, [pair for i, j in pairs for pair in ((i, j), (j, i))])  1.51 us
    unnamed x12, local copies, waits for them, and re-layouts  1.07 us
  transfers between devices with their start and end apart: 7, of which 1 were waited for; matrix products, arithmetic and copies ran while one was open for 0% of the time, Pallas kernels for 21%

profile of v13, /device:TPU:1, one launch (start us, length us, event | category | flops | bytes accessed | tf_op | source)
XLA Modules:
  0.0 44.8 jit_solution(12074914205371369425)
XLA Ops:
  0.0 0.0 copy-start.4
  0.0 1.0 %copy-done.4 = bf16[4,8,32,135]{3,2,1,0:T(8,128)(2,1)S(1)} copy-done((bf16[4,8,32,135]{3,2,1,0:T(8,128)(2,1)S(1)}, bf16[4,8,32,135]{3,2,1,0:T(8,128)(2,1)}, u32[]{:S(2)}) %copy-start.4) | copy-done | bytes 276504
  1.0 0.4 initial_traces.1
  1.4 2.0 %collective-permute-start.2 = (bf16[48,256]{1,0:T(8,128)(2,1)S(1)}, bf16[48,256]{1,0:T(8,128)(2,1)S(1)}, u32[]{:S(2)}, u32[]{:S(2)}) collective-permute-start(bf16[48,256]{1,0:T(8,128)(2,1)S(1)} %get-tuple-element.37), channel_id=1, source_target_pairs={{8,0},{16,8},{24,16},{9,1},{17,9},{25,17},{10,2},{18,10},{26,18},{... | collective-permute-start | bytes 73736 | tf_op jit(solution)/shard_map/ppermute | solution.py:493
  3.4 2.8 %collective-permute-start = (bf16[304,256]{1,0:T(8,128)(2,1)S(1)}, bf16[304,256]{1,0:T(8,128)(2,1)S(1)}, u32[]{:S(2)}, u32[]{:S(2)}) collective-permute-start(bf16[304,256]{1,0:T(8,128)(2,1)S(1)} %get-tuple-element.35), channel_id=1, source_target_pairs={{0,1},{1,0},{2,3},{3,2},{4,5},{5,4},{6,7},{7,6},{8,9},{9,8},{10,11... | collective-permute-start | bytes 466952 | tf_op jit(solution)/shard_map/ppermute | solution.py:488
  6.1 3.3 %collective-permute-start.1 = (bf16[304,256]{1,0:T(8,128)(2,1)S(1)}, bf16[304,256]{1,0:T(8,128)(2,1)S(1)}, u32[]{:S(2)}, u32[]{:S(2)}) collective-permute-start(bf16[304,256]{1,0:T(8,128)(2,1)S(1)} %get-tuple-element.36), channel_id=1, source_target_pairs={{1,2},{2,1},{3,4},{4,3},{5,6},{6,5},{7,0},{0,7},{9,10},{10,9},{11,... | collective-permute-start | bytes 466952 | tf_op jit(solution)/shard_map/ppermute | solution.py:488
  9.4 0.0 copy-start.1
  9.4 0.0 copy-start.2
  9.4 7.2 %weights.1 = (bf16[4,8,144,256]{3,2,1,0:T(8,128)(2,1)S(1)}, bf16[4,2,192,256]{3,2,1,0:T(8,128)(2,1)S(1)}, f32[4,144,256]{2,1,0:T(8,128)S(1)}, bf16[4,144,256]{2,...) custom-call(bf16[4,135,8,135]{3,2,1,0:T(8,128)(2,1)} %bitcast.10, bf16[4,6,45,8,135]{4,3,2,1,0:T(8,128)(2,1)} %bitcast.9, ...), custom_call_target="tpu_custom_call" | custom-call | flops 10000000000 | bytes 8607040 | tf_op jit(solution)/shard_map/weights/pallas_call | solution.py:448
  16.6 0.0 collective-permute-done.2.above
  16.7 0.0 collective-permute-done.near
  16.7 0.0 collective-permute-done.1.far
  16.7 0.0 copy-done.1
  16.7 0.0 copy-done.2
  16.7 0.0 copy-start
  16.7 1.3 %forward_chain.1 = (f32[4,144,256]{2,1,0:T(8,128)S(1)}, f32[4,48,256]{2,1,0:T(8,128)S(1)}, bf16[144,256]{1,0:T(8,128)(2,1)S(1)}) custom-call(bf16[304,256]{1,0:T(8,128)(2,1)S(1)} %collective-permute-done.near, bf16[304,256]{1,0:T(8,128)(2,1)S(1)} %collective-permute-done.1.far, bf16[48,256]{1,0:T(8,128)(2,1)S(1)} %collective-permute-done.2.above, ...), custom_call_target="tpu_custom_call" | custom-call | flops 200000000 | bytes 5922816 | tf_op jit(solution)/shard_map/forward_chain/pallas_call | solution.py:448
  18.0 0.0 copy-start.5
  18.0 6.3 %all-gather = bf16[576,256]{1,0:T(8,128)(2,1)S(1)} all-gather(bf16[144,256]{1,0:T(8,128)(2,1)S(1)} %get-tuple-element.44), channel_id=2, replica_groups=mesh['sweep'=4,'cross'=8] {'sweep'}, dimensions={0}, use_global_device_ids=true | all-gather | bytes 368640 | tf_op jit(solution)/shard_map/all_gather | solution.py:530
  24.3 0.0 copy-done
  24.3 1.4 %forward_finish.1 = (bf16[4,144,256]{2,1,0:T(8,128)(2,1)S(1)}, f32[4,144,256]{2,1,0:T(8,128)S(1)}, bf16[304,256]{1,0:T(8,128)(2,1)S(1)}, bf16[304,256]{1,0:T(8,128)(2,1)S(1)}) custom-call(bf16[4,144,256]{2,1,0:T(8,128)(2,1)S(1)} %bitcast.7, f32[4,144,256]{2,1,0:T(8,128)S(1)} %get-tuple-element.45.part, f32[4,48,256]{2,1,0:T(8,128)S(1)} %get-tuple-element.46.traces, ...), custom_call_target="tpu_custom_call" | custom-call | flops 200000000 | bytes 3321856 | tf_op jit(solution)/shard_map/forward_finish/pallas_call | solution.py:448
  25.6 0.1 collective-permute-start.3
  25.7 1.9 %collective-permute-start.4 = (bf16[304,256]{1,0:T(8,128)(2,1)S(1)}, bf16[304,256]{1,0:T(8,128)(2,1)S(1)}, u32[]{:S(2)}, u32[]{:S(2)}) collective-permute-start(bf16[304,256]{1,0:T(8,128)(2,1)S(1)} %get-tuple-element.48), channel_id=1, source_target_pairs={{1,2},{2,1},{3,4},{4,3},{5,6},{6,5},{7,0},{0,7},{9,10},{10,9},{11,... | collective-permute-start | bytes 466952 | tf_op jit(solution)/shard_map/ppermute | solution.py:488
  27.7 0.0 copy-done.5
  27.7 0.8 %middle.1 = (bf16[4,96,256]{2,1,0:T(8,128)(2,1)S(1)}, f32[4,144,256]{2,1,0:T(8,128)S(1)}, bf16[4,2,192,256]{3,2,1,0:T(8,128)(2,1)S(1)}) custom-call(bf16[4,144,256]{2,1,0:T(8,128)(2,1)S(1)} %get-tuple-element.49.middle, f32[4,144,256]{2,1,0:T(8,128)S(1)} %get-tuple-element.50.change, f32[4,144,256]{2,1,0:T(8,128)S(1)} %get-tuple-element.43.base, ...), custom_call_target="tpu_custom_call" | custom-call | flops 2000000000 | bytes 5958656 | tf_op jit(solution)/shard_map/middle/pallas_call | solution.py:448
  28.5 0.7 %collective-permute-start.6 = (bf16[2,48,256]{2,1,0:T(8,128)(2,1)S(1)}, bf16[2,48,256]{2,1,0:T(8,128)(2,1)S(1)}, u32[]{:S(2)}, u32[]{:S(2)}) collective-permute-start(bf16[2,48,256]{2,1,0:T(8,128)(2,1)S(1)} %slice_bitcast_fusion), channel_id=1, source_target_pairs={{16,0},{17,1},{18,2},{19,3},{20,4},{21,5},{22,6},{23,7}} | collective-permute-start | bytes 147464 | tf_op jit(solution)/shard_map/ppermute | solution.py:464
  29.2 3.3 %collective-permute-start.5 = (bf16[2,48,256]{2,1,0:T(8,128)(2,1)S(1)}, bf16[2,48,256]{2,1,0:T(8,128)(2,1)S(1)}, u32[]{:S(2)}, u32[]{:S(2)}) collective-permute-start(bf16[2,48,256]{2,1,0:T(8,128)(2,1)S(1)} %slice_bitcast_fusion), channel_id=1, source_target_pairs={{8,0},{16,8},{9,1},{17,9},{10,2},{18,10},{11,3},{19,11},{12,4},{20... | collective-permute-start | bytes 147464 | tf_op jit(solution)/shard_map/ppermute | solution.py:464
  32.4 0.0 collective-permute-done.3.near
  32.5 1.5 %collective-permute-done.4.far = bf16[304,256]{1,0:T(8,128)(2,1)S(1)} collective-permute-done((bf16[304,256]{1,0:T(8,128)(2,1)S(1)}, bf16[304,256]{1,0:T(8,128)(2,1)S(1)}, u32[]{:S(2)}, u32[]{:S(2)}) %collective-permute-start.4) | collective-permute-done | bytes 155680 | tf_op jit(solution)/shard_map/ppermute | solution.py:488
  33.9 0.0 copy-start.3
  33.9 1.3 %backward_chain.1 = (f32[4,144,256]{2,1,0:T(8,128)S(1)}, f32[4,48,256]{2,1,0:T(8,128)S(1)}, bf16[48,256]{1,0:T(8,128)(2,1)S(1)}) custom-call(bf16[304,256]{1,0:T(8,128)(2,1)S(1)} %collective-permute-done.3.near, bf16[304,256]{1,0:T(8,128)(2,1)S(1)} %collective-permute-done.4.far, bf16[4,96,256]{2,1,0:T(8,128)(2,1)S(1)} %get-tuple-element.53.own, ...), custom_call_target="tpu_custom_call" | custom-call | flops 200000000 | bytes 5750784 | tf_op jit(solution)/shard_map/backward_chain/pallas_call | solution.py:448
  35.2 6.7 %all-gather.1 = bf16[192,256]{1,0:T(8,128)(2,1)S(1)} all-gather(bf16[48,256]{1,0:T(8,128)(2,1)S(1)} %get-tuple-element.55), channel_id=3, replica_groups=mesh['sweep'=4,'cross'=8] {'sweep'}, dimensions={0}, use_global_device_ids=true | all-gather | bytes 122880 | tf_op jit(solution)/shard_map/all_gather | solution.py:553
  41.9 0.0 collective-permute-done.6.next_near
  41.9 0.0 collective-permute-done.5.near
  41.9 0.0 copy-done.3
  41.9 2.8 %backward_finish.1 = bf16[4,8,32,135]{3,2,1,0:T(8,128)(2,1)} custom-call(bf16[4,48,256]{2,1,0:T(8,128)(2,1)S(1)} %bitcast.8, bf16[2,48,256]{2,1,0:T(8,128)(2,1)S(1)} %collective-permute-done.5.near, bf16[2,48,256]{2,1,0:T(8,128)(2,1)S(1)} %collective-permute-done.6.next_near, f32[4,144,256]{2,1,0:T(8,128)S(1)} %get-tuple-element.57.part, ...), custom_call_target="tpu_custom_call" | custom-call | flops 200000000 | bytes 2084832 | tf_op jit(solution)/shard_map/backward_finish/pallas_call | solution.py:448
  (1 shorter events, 0.0 us)
Async XLA Ops:
  0.0 1.0 %copy-start.4 = (bf16[4,8,32,135]{3,2,1,0:T(8,128)(2,1)S(1)}, bf16[4,8,32,135]{3,2,1,0:T(8,128)(2,1)}, u32[]{:S(2)}) copy-start(bf16[4,8,32,135]{3,2,1,0:T(8,128)(2,1)} %initial_there) | copy-start | bytes 829444
  1.4 15.2 %collective-permute-start.2 = (bf16[48,256]{1,0:T(8,128)(2,1)S(1)}, bf16[48,256]{1,0:T(8,128)(2,1)S(1)}, u32[]{:S(2)}, u32[]{:S(2)}) collective-permute-start(bf16[48,256]{1,0:T(8,128)(2,1)S(1)} %get-tuple-element.37), channel_id=1, source_target_pairs={{8,0},{16,8},{24,16},{9,1},{17,9},{25,17},{10,2},{18,10},{26,18},{... | collective-permute-start | bytes 73736 | tf_op jit(solution)/shard_map/ppermute | solution.py:493
  3.4 13.3 %collective-permute-start = (bf16[304,256]{1,0:T(8,128)(2,1)S(1)}, bf16[304,256]{1,0:T(8,128)(2,1)S(1)}, u32[]{:S(2)}, u32[]{:S(2)}) collective-permute-start(bf16[304,256]{1,0:T(8,128)(2,1)S(1)} %get-tuple-element.35), channel_id=1, source_target_pairs={{0,1},{1,0},{2,3},{3,2},{4,5},{5,4},{6,7},{7,6},{8,9},{9,8},{10,11... | collective-permute-start | bytes 466952 | tf_op jit(solution)/shard_map/ppermute | solution.py:488
  6.1 10.5 %collective-permute-start.1 = (bf16[304,256]{1,0:T(8,128)(2,1)S(1)}, bf16[304,256]{1,0:T(8,128)(2,1)S(1)}, u32[]{:S(2)}, u32[]{:S(2)}) collective-permute-start(bf16[304,256]{1,0:T(8,128)(2,1)S(1)} %get-tuple-element.36), channel_id=1, source_target_pairs={{1,2},{2,1},{3,4},{4,3},{5,6},{6,5},{7,0},{0,7},{9,10},{10,9},{11,... | collective-permute-start | bytes 466952 | tf_op jit(solution)/shard_map/ppermute | solution.py:488
  9.4 7.3 %copy-start.1 = (bf16[4,96,112]{2,1,0:T(8,128)(2,1)S(1)}, bf16[4,96,112]{2,1,0:T(8,128)(2,1)}, u32[]{:S(2)}) copy-start(bf16[4,96,112]{2,1,0:T(8,128)(2,1)} %constant.14.clone.down_sel) | copy-start | bytes 258052
  9.4 7.3 %copy-start.2 = (bf16[4,96,112]{2,1,0:T(8,128)(2,1)S(1)}, bf16[4,96,112]{2,1,0:T(8,128)(2,1)}, u32[]{:S(2)}) copy-start(bf16[4,96,112]{2,1,0:T(8,128)(2,1)} %constant.13.clone.up_sel) | copy-start | bytes 258052
  16.7 7.6 %copy-start = (bf16[4,224,144]{2,1,0:T(8,128)(2,1)S(1)}, bf16[4,224,144]{2,1,0:T(8,128)(2,1)}, u32[]{:S(2)}) copy-start(bf16[4,224,144]{2,1,0:T(8,128)(2,1)} %constant.10.clone.send) | copy-start | bytes 774148
  18.0 9.7 %copy-start.5 = (bf16[96,144]{1,0:T(8,128)(2,1)S(1)}, bf16[96,144]{1,0:T(8,128)(2,1)}, u32[]{:S(2)}) copy-start(bf16[96,144]{1,0:T(8,128)(2,1)} %constant.11.clone.own_sel) | copy-start | bytes 82948
  25.6 6.8 %collective-permute-start.3 = (bf16[304,256]{1,0:T(8,128)(2,1)S(1)}, bf16[304,256]{1,0:T(8,128)(2,1)S(1)}, u32[]{:S(2)}, u32[]{:S(2)}) collective-permute-start(bf16[304,256]{1,0:T(8,128)(2,1)S(1)} %get-tuple-element.47), channel_id=1, source_target_pairs={{0,1},{1,0},{2,3},{3,2},{4,5},{5,4},{6,7},{7,6},{8,9},{9,8},{10,11... | collective-permute-start | bytes 466952 | tf_op jit(solution)/shard_map/ppermute | solution.py:488
  25.7 8.2 %collective-permute-start.4 = (bf16[304,256]{1,0:T(8,128)(2,1)S(1)}, bf16[304,256]{1,0:T(8,128)(2,1)S(1)}, u32[]{:S(2)}, u32[]{:S(2)}) collective-permute-start(bf16[304,256]{1,0:T(8,128)(2,1)S(1)} %get-tuple-element.48), channel_id=1, source_target_pairs={{1,2},{2,1},{3,4},{4,3},{5,6},{6,5},{7,0},{0,7},{9,10},{10,9},{11,... | collective-permute-start | bytes 466952 | tf_op jit(solution)/shard_map/ppermute | solution.py:488
  28.5 13.4 %collective-permute-start.6 = (bf16[2,48,256]{2,1,0:T(8,128)(2,1)S(1)}, bf16[2,48,256]{2,1,0:T(8,128)(2,1)S(1)}, u32[]{:S(2)}, u32[]{:S(2)}) collective-permute-start(bf16[2,48,256]{2,1,0:T(8,128)(2,1)S(1)} %slice_bitcast_fusion), channel_id=1, source_target_pairs={{16,0},{17,1},{18,2},{19,3},{20,4},{21,5},{22,6},{23,7}} | collective-permute-start | bytes 147464 | tf_op jit(solution)/shard_map/ppermute | solution.py:464
  29.2 12.8 %collective-permute-start.5 = (bf16[2,48,256]{2,1,0:T(8,128)(2,1)S(1)}, bf16[2,48,256]{2,1,0:T(8,128)(2,1)S(1)}, u32[]{:S(2)}, u32[]{:S(2)}) collective-permute-start(bf16[2,48,256]{2,1,0:T(8,128)(2,1)S(1)} %slice_bitcast_fusion), channel_id=1, source_target_pairs={{8,0},{16,8},{9,1},{17,9},{10,2},{18,10},{11,3},{19,11},{12,4},{20... | collective-permute-start | bytes 147464 | tf_op jit(solution)/shard_map/ppermute | solution.py:464
  33.9 8.0 %copy-start.3 = (bf16[135,144]{1,0:T(8,128)(2,1)S(1)}, bf16[135,144]{1,0:T(8,128)(2,1)}, u32[]{:S(2)}) copy-start(bf16[135,144]{1,0:T(8,128)(2,1)} %constant.12.clone.back) | copy-start | bytes 116644

commit v14 on v13

--- a/solution.py
+++ b/solution.py
@@ -206,7 +206,8 @@
 def turned(rows, raw, put):
     count, columns, width = rows.shape
     raw[0, : count * columns] = rows[:, :, :128].astype(F32).reshape(count * columns, 128)
-    raw[1, : count * columns, : width - 128] = rows[:, :, 128:].astype(F32).reshape(count * columns, width - 128)
+    rest = rows[:, :, 128:].astype(F32).reshape(count * columns, width - 128)
+    raw[1, : count * columns] = jnp.concatenate([rest, jnp.zeros((count * columns, 256 - width), F32)], 1)
     for c in range(columns):
         put(c, jnp.concatenate([raw[i, pl.ds(c, FACE, stride=columns), :] for i in range(2)], 1))
 
@@ -231,8 +232,9 @@
         copies.append([pltpu.make_async_copy(x.at[p], y.at[p], done.at[i, p]) for i, (x, y) in enumerate(pairs)])
         for copy in copies[p]:
             copy.start()
-    faces[...] = jnp.zeros(faces.shape, BF)
-    raw[...] = jnp.zeros(raw.shape, F32)
+    for start, stop in ((5 * FACE, 256), (256 + FACE, 256 + 2 * SLOT)):
+        faces[:, :, start:stop] = jnp.zeros((2, columns, stop - start, 256), BF)
+    raw[:, :, :, NT * columns :] = jnp.zeros((2, 9, 2, (FACE - NT) * columns, 128), F32)
     for copy in early:
         copy.wait()
     source = sources(neighbours, columns, rhs)

time: 45.1 us -> 45.1 us (level)
  no operation moved by 1% of the time
where the time goes in v14:
time: 45.1 us; the launch traced here: 44.8 us
  Pallas kernels  15.1 us (33%)
  starting transfers between devices  13.9 us (31%)
  blocking collectives  13 us (29%)
  waiting for transfers between devices  1.51 us (3%)
  local copies, waits for them, and re-layouts  1.07 us (2%)
    pallas_call x7, Pallas kernels, call(): pl.pallas_call(kernel, out_shape=shapes, in_specs=[pl.BlockSpec(memory_sp...  15.1 us
    all_gather x2, blocking collectives, local(): messages = lax.all_gather(message, 'sweep')  13 us
    ppermute x4, starting transfers between devices, swapped(): lax.ppermute(x, axis, [pair for i, j in pairs for pair in ((i, j), (j, i))])  8.04 us
    ppermute x2, starting transfers between devices, products(): lax.ppermute(x, 'sweep', [(i, i + step) for i in inner if 0 <= i + step <...  3.93 us
    ppermute x1, starting transfers between devices, shift(): lax.ppermute(x, axis, [(i, i + by) for i in range(n) if 0 <= i + by < n])  1.97 us
    ppermute x4, waiting for transfers between devices, swapped(): lax.ppermute(x, axis, [pair for i, j in pairs for pair in ((i, j), (j, i))])  1.5 us
    unnamed x12, local copies, waits for them, and re-layouts  1.07 us
  transfers between devices with their start and end apart: 7, of which 1 were waited for; matrix products, arithmetic and copies ran while one was open for 0% of the time, Pallas kernels for 21%

profile of v14, /device:TPU:1, one launch (start us, length us, event | category | flops | bytes accessed | tf_op | source)
XLA Modules:
  0.0 44.8 jit_solution(13184347247159049432)
XLA Ops:
  0.0 0.0 copy-start.4
  0.0 1.0 %copy-done.4 = bf16[4,8,32,135]{3,2,1,0:T(8,128)(2,1)S(1)} copy-done((bf16[4,8,32,135]{3,2,1,0:T(8,128)(2,1)S(1)}, bf16[4,8,32,135]{3,2,1,0:T(8,128)(2,1)}, u32[]{:S(2)}) %copy-start.4) | copy-done | bytes 276504
  1.0 0.4 initial_traces.1
  1.4 2.0 %collective-permute-start.2 = (bf16[48,256]{1,0:T(8,128)(2,1)S(1)}, bf16[48,256]{1,0:T(8,128)(2,1)S(1)}, u32[]{:S(2)}, u32[]{:S(2)}) collective-permute-start(bf16[48,256]{1,0:T(8,128)(2,1)S(1)} %get-tuple-element.37), channel_id=1, source_target_pairs={{8,0},{16,8},{24,16},{9,1},{17,9},{25,17},{10,2},{18,10},{26,18},{... | collective-permute-start | bytes 73736 | tf_op jit(solution)/shard_map/ppermute | solution.py:495
  3.4 2.8 %collective-permute-start = (bf16[304,256]{1,0:T(8,128)(2,1)S(1)}, bf16[304,256]{1,0:T(8,128)(2,1)S(1)}, u32[]{:S(2)}, u32[]{:S(2)}) collective-permute-start(bf16[304,256]{1,0:T(8,128)(2,1)S(1)} %get-tuple-element.35), channel_id=1, source_target_pairs={{0,1},{1,0},{2,3},{3,2},{4,5},{5,4},{6,7},{7,6},{8,9},{9,8},{10,11... | collective-permute-start | bytes 466952 | tf_op jit(solution)/shard_map/ppermute | solution.py:490
  6.1 3.3 %collective-permute-start.1 = (bf16[304,256]{1,0:T(8,128)(2,1)S(1)}, bf16[304,256]{1,0:T(8,128)(2,1)S(1)}, u32[]{:S(2)}, u32[]{:S(2)}) collective-permute-start(bf16[304,256]{1,0:T(8,128)(2,1)S(1)} %get-tuple-element.36), channel_id=1, source_target_pairs={{1,2},{2,1},{3,4},{4,3},{5,6},{6,5},{7,0},{0,7},{9,10},{10,9},{11,... | collective-permute-start | bytes 466952 | tf_op jit(solution)/shard_map/ppermute | solution.py:490
  9.4 0.0 copy-start.1
  9.4 0.0 copy-start.2
  9.4 7.2 %weights.1 = (bf16[4,8,144,256]{3,2,1,0:T(8,128)(2,1)S(1)}, bf16[4,2,192,256]{3,2,1,0:T(8,128)(2,1)S(1)}, f32[4,144,256]{2,1,0:T(8,128)S(1)}, bf16[4,144,256]{2,...) custom-call(bf16[4,135,8,135]{3,2,1,0:T(8,128)(2,1)} %bitcast.10, bf16[4,6,45,8,135]{4,3,2,1,0:T(8,128)(2,1)} %bitcast.9, ...), custom_call_target="tpu_custom_call" | custom-call | flops 10000000000 | bytes 8607040 | tf_op jit(solution)/shard_map/weights/pallas_call | solution.py:450
  16.6 0.0 collective-permute-done.2.above
  16.6 0.0 collective-permute-done.near
  16.6 0.0 collective-permute-done.1.far
  16.6 0.0 copy-done.1
  16.6 0.0 copy-done.2
  16.7 0.0 copy-start
  16.7 1.2 %forward_chain.1 = (f32[4,144,256]{2,1,0:T(8,128)S(1)}, f32[4,48,256]{2,1,0:T(8,128)S(1)}, bf16[144,256]{1,0:T(8,128)(2,1)S(1)}) custom-call(bf16[304,256]{1,0:T(8,128)(2,1)S(1)} %collective-permute-done.near, bf16[304,256]{1,0:T(8,128)(2,1)S(1)} %collective-permute-done.1.far, bf16[48,256]{1,0:T(8,128)(2,1)S(1)} %collective-permute-done.2.above, ...), custom_call_target="tpu_custom_call" | custom-call | flops 200000000 | bytes 5922816 | tf_op jit(solution)/shard_map/forward_chain/pallas_call | solution.py:450
  17.9 0.0 copy-start.5
  17.9 6.3 %all-gather = bf16[576,256]{1,0:T(8,128)(2,1)S(1)} all-gather(bf16[144,256]{1,0:T(8,128)(2,1)S(1)} %get-tuple-element.44), channel_id=2, replica_groups=mesh['sweep'=4,'cross'=8] {'sweep'}, dimensions={0}, use_global_device_ids=true | all-gather | bytes 368640 | tf_op jit(solution)/shard_map/all_gather | solution.py:532
  24.3 0.0 copy-done
  24.3 1.4 %forward_finish.1 = (bf16[4,144,256]{2,1,0:T(8,128)(2,1)S(1)}, f32[4,144,256]{2,1,0:T(8,128)S(1)}, bf16[304,256]{1,0:T(8,128)(2,1)S(1)}, bf16[304,256]{1,0:T(8,128)(2,1)S(1)}) custom-call(bf16[4,144,256]{2,1,0:T(8,128)(2,1)S(1)} %bitcast.7, f32[4,144,256]{2,1,0:T(8,128)S(1)} %get-tuple-element.45.part, f32[4,48,256]{2,1,0:T(8,128)S(1)} %get-tuple-element.46.traces, ...), custom_call_target="tpu_custom_call" | custom-call | flops 200000000 | bytes 3321856 | tf_op jit(solution)/shard_map/forward_finish/pallas_call | solution.py:450
  25.6 0.1 collective-permute-start.3
  25.7 2.0 %collective-permute-start.4 = (bf16[304,256]{1,0:T(8,128)(2,1)S(1)}, bf16[304,256]{1,0:T(8,128)(2,1)S(1)}, u32[]{:S(2)}, u32[]{:S(2)}) collective-permute-start(bf16[304,256]{1,0:T(8,128)(2,1)S(1)} %get-tuple-element.48), channel_id=1, source_target_pairs={{1,2},{2,1},{3,4},{4,3},{5,6},{6,5},{7,0},{0,7},{9,10},{10,9},{11,... | collective-permute-start | bytes 466952 | tf_op jit(solution)/shard_map/ppermute | solution.py:490
  27.7 0.0 copy-done.5
  27.7 0.8 %middle.1 = (bf16[4,96,256]{2,1,0:T(8,128)(2,1)S(1)}, f32[4,144,256]{2,1,0:T(8,128)S(1)}, bf16[4,2,192,256]{3,2,1,0:T(8,128)(2,1)S(1)}) custom-call(bf16[4,144,256]{2,1,0:T(8,128)(2,1)S(1)} %get-tuple-element.49.middle, f32[4,144,256]{2,1,0:T(8,128)S(1)} %get-tuple-element.50.change, f32[4,144,256]{2,1,0:T(8,128)S(1)} %get-tuple-element.43.base, ...), custom_call_target="tpu_custom_call" | custom-call | flops 2000000000 | bytes 5958656 | tf_op jit(solution)/shard_map/middle/pallas_call | solution.py:450
  28.5 0.7 %collective-permute-start.6 = (bf16[2,48,256]{2,1,0:T(8,128)(2,1)S(1)}, bf16[2,48,256]{2,1,0:T(8,128)(2,1)S(1)}, u32[]{:S(2)}, u32[]{:S(2)}) collective-permute-start(bf16[2,48,256]{2,1,0:T(8,128)(2,1)S(1)} %slice_bitcast_fusion), channel_id=1, source_target_pairs={{16,0},{17,1},{18,2},{19,3},{20,4},{21,5},{22,6},{23,7}} | collective-permute-start | bytes 147464 | tf_op jit(solution)/shard_map/ppermute | solution.py:466
  29.2 3.3 %collective-permute-start.5 = (bf16[2,48,256]{2,1,0:T(8,128)(2,1)S(1)}, bf16[2,48,256]{2,1,0:T(8,128)(2,1)S(1)}, u32[]{:S(2)}, u32[]{:S(2)}) collective-permute-start(bf16[2,48,256]{2,1,0:T(8,128)(2,1)S(1)} %slice_bitcast_fusion), channel_id=1, source_target_pairs={{8,0},{16,8},{9,1},{17,9},{10,2},{18,10},{11,3},{19,11},{12,4},{20... | collective-permute-start | bytes 147464 | tf_op jit(solution)/shard_map/ppermute | solution.py:466
  32.4 0.0 collective-permute-done.3.near
  32.5 1.5 %collective-permute-done.4.far = bf16[304,256]{1,0:T(8,128)(2,1)S(1)} collective-permute-done((bf16[304,256]{1,0:T(8,128)(2,1)S(1)}, bf16[304,256]{1,0:T(8,128)(2,1)S(1)}, u32[]{:S(2)}, u32[]{:S(2)}) %collective-permute-start.4) | collective-permute-done | bytes 155680 | tf_op jit(solution)/shard_map/ppermute | solution.py:490
  33.9 0.0 copy-start.3
  33.9 1.3 %backward_chain.1 = (f32[4,144,256]{2,1,0:T(8,128)S(1)}, f32[4,48,256]{2,1,0:T(8,128)S(1)}, bf16[48,256]{1,0:T(8,128)(2,1)S(1)}) custom-call(bf16[304,256]{1,0:T(8,128)(2,1)S(1)} %collective-permute-done.3.near, bf16[304,256]{1,0:T(8,128)(2,1)S(1)} %collective-permute-done.4.far, bf16[4,96,256]{2,1,0:T(8,128)(2,1)S(1)} %get-tuple-element.53.own, ...), custom_call_target="tpu_custom_call" | custom-call | flops 200000000 | bytes 5750784 | tf_op jit(solution)/shard_map/backward_chain/pallas_call | solution.py:450
  35.2 6.7 %all-gather.1 = bf16[192,256]{1,0:T(8,128)(2,1)S(1)} all-gather(bf16[48,256]{1,0:T(8,128)(2,1)S(1)} %get-tuple-element.55), channel_id=3, replica_groups=mesh['sweep'=4,'cross'=8] {'sweep'}, dimensions={0}, use_global_device_ids=true | all-gather | bytes 122880 | tf_op jit(solution)/shard_map/all_gather | solution.py:555
  41.9 0.0 collective-permute-done.6.next_near
  41.9 0.0 collective-permute-done.5.near
  41.9 0.0 copy-done.3
  41.9 2.8 %backward_finish.1 = bf16[4,8,32,135]{3,2,1,0:T(8,128)(2,1)} custom-call(bf16[4,48,256]{2,1,0:T(8,128)(2,1)S(1)} %bitcast.8, bf16[2,48,256]{2,1,0:T(8,128)(2,1)S(1)} %collective-permute-done.5.near, bf16[2,48,256]{2,1,0:T(8,128)(2,1)S(1)} %collective-permute-done.6.next_near, f32[4,144,256]{2,1,0:T(8,128)S(1)} %get-tuple-element.57.part, ...), custom_call_target="tpu_custom_call" | custom-call | flops 200000000 | bytes 2084832 | tf_op jit(solution)/shard_map/backward_finish/pallas_call | solution.py:450
  (1 shorter events, 0.0 us)
Async XLA Ops:
  0.0 1.0 %copy-start.4 = (bf16[4,8,32,135]{3,2,1,0:T(8,128)(2,1)S(1)}, bf16[4,8,32,135]{3,2,1,0:T(8,128)(2,1)}, u32[]{:S(2)}) copy-start(bf16[4,8,32,135]{3,2,1,0:T(8,128)(2,1)} %initial_there) | copy-start | bytes 829444
  1.4 15.2 %collective-permute-start.2 = (bf16[48,256]{1,0:T(8,128)(2,1)S(1)}, bf16[48,256]{1,0:T(8,128)(2,1)S(1)}, u32[]{:S(2)}, u32[]{:S(2)}) collective-permute-start(bf16[48,256]{1,0:T(8,128)(2,1)S(1)} %get-tuple-element.37), channel_id=1, source_target_pairs={{8,0},{16,8},{24,16},{9,1},{17,9},{25,17},{10,2},{18,10},{26,18},{... | collective-permute-start | bytes 73736 | tf_op jit(solution)/shard_map/ppermute | solution.py:495
  3.4 13.2 %collective-permute-start = (bf16[304,256]{1,0:T(8,128)(2,1)S(1)}, bf16[304,256]{1,0:T(8,128)(2,1)S(1)}, u32[]{:S(2)}, u32[]{:S(2)}) collective-permute-start(bf16[304,256]{1,0:T(8,128)(2,1)S(1)} %get-tuple-element.35), channel_id=1, source_target_pairs={{0,1},{1,0},{2,3},{3,2},{4,5},{5,4},{6,7},{7,6},{8,9},{9,8},{10,11... | collective-permute-start | bytes 466952 | tf_op jit(solution)/shard_map/ppermute | solution.py:490
  6.1 10.5 %collective-permute-start.1 = (bf16[304,256]{1,0:T(8,128)(2,1)S(1)}, bf16[304,256]{1,0:T(8,128)(2,1)S(1)}, u32[]{:S(2)}, u32[]{:S(2)}) collective-permute-start(bf16[304,256]{1,0:T(8,128)(2,1)S(1)} %get-tuple-element.36), channel_id=1, source_target_pairs={{1,2},{2,1},{3,4},{4,3},{5,6},{6,5},{7,0},{0,7},{9,10},{10,9},{11,... | collective-permute-start | bytes 466952 | tf_op jit(solution)/shard_map/ppermute | solution.py:490
  9.4 7.2 %copy-start.1 = (bf16[4,96,112]{2,1,0:T(8,128)(2,1)S(1)}, bf16[4,96,112]{2,1,0:T(8,128)(2,1)}, u32[]{:S(2)}) copy-start(bf16[4,96,112]{2,1,0:T(8,128)(2,1)} %constant.14.clone.down_sel) | copy-start | bytes 258052
  9.4 7.2 %copy-start.2 = (bf16[4,96,112]{2,1,0:T(8,128)(2,1)S(1)}, bf16[4,96,112]{2,1,0:T(8,128)(2,1)}, u32[]{:S(2)}) copy-start(bf16[4,96,112]{2,1,0:T(8,128)(2,1)} %constant.13.clone.up_sel) | copy-start | bytes 258052
  16.7 7.6 %copy-start = (bf16[4,224,144]{2,1,0:T(8,128)(2,1)S(1)}, bf16[4,224,144]{2,1,0:T(8,128)(2,1)}, u32[]{:S(2)}) copy-start(bf16[4,224,144]{2,1,0:T(8,128)(2,1)} %constant.10.clone.send) | copy-start | bytes 774148
  17.9 9.7 %copy-start.5 = (bf16[96,144]{1,0:T(8,128)(2,1)S(1)}, bf16[96,144]{1,0:T(8,128)(2,1)}, u32[]{:S(2)}) copy-start(bf16[96,144]{1,0:T(8,128)(2,1)} %constant.11.clone.own_sel) | copy-start | bytes 82948
  25.6 6.8 %collective-permute-start.3 = (bf16[304,256]{1,0:T(8,128)(2,1)S(1)}, bf16[304,256]{1,0:T(8,128)(2,1)S(1)}, u32[]{:S(2)}, u32[]{:S(2)}) collective-permute-start(bf16[304,256]{1,0:T(8,128)(2,1)S(1)} %get-tuple-element.47), channel_id=1, source_target_pairs={{0,1},{1,0},{2,3},{3,2},{4,5},{5,4},{6,7},{7,6},{8,9},{9,8},{10,11... | collective-permute-start | bytes 466952 | tf_op jit(solution)/shard_map/ppermute | solution.py:490
  25.7 8.2 %collective-permute-start.4 = (bf16[304,256]{1,0:T(8,128)(2,1)S(1)}, bf16[304,256]{1,0:T(8,128)(2,1)S(1)}, u32[]{:S(2)}, u32[]{:S(2)}) collective-permute-start(bf16[304,256]{1,0:T(8,128)(2,1)S(1)} %get-tuple-element.48), channel_id=1, source_target_pairs={{1,2},{2,1},{3,4},{4,3},{5,6},{6,5},{7,0},{0,7},{9,10},{10,9},{11,... | collective-permute-start | bytes 466952 | tf_op jit(solution)/shard_map/ppermute | solution.py:490
  28.5 13.4 %collective-permute-start.6 = (bf16[2,48,256]{2,1,0:T(8,128)(2,1)S(1)}, bf16[2,48,256]{2,1,0:T(8,128)(2,1)S(1)}, u32[]{:S(2)}, u32[]{:S(2)}) collective-permute-start(bf16[2,48,256]{2,1,0:T(8,128)(2,1)S(1)} %slice_bitcast_fusion), channel_id=1, source_target_pairs={{16,0},{17,1},{18,2},{19,3},{20,4},{21,5},{22,6},{23,7}} | collective-permute-start | bytes 147464 | tf_op jit(solution)/shard_map/ppermute | solution.py:466
  29.2 12.8 %collective-permute-start.5 = (bf16[2,48,256]{2,1,0:T(8,128)(2,1)S(1)}, bf16[2,48,256]{2,1,0:T(8,128)(2,1)S(1)}, u32[]{:S(2)}, u32[]{:S(2)}) collective-permute-start(bf16[2,48,256]{2,1,0:T(8,128)(2,1)S(1)} %slice_bitcast_fusion), channel_id=1, source_target_pairs={{8,0},{16,8},{9,1},{17,9},{10,2},{18,10},{11,3},{19,11},{12,4},{20... | collective-permute-start | bytes 147464 | tf_op jit(solution)/shard_map/ppermute | solution.py:466
  33.9 8.0 %copy-start.3 = (bf16[135,144]{1,0:T(8,128)(2,1)S(1)}, bf16[135,144]{1,0:T(8,128)(2,1)}, u32[]{:S(2)}) copy-start(bf16[135,144]{1,0:T(8,128)(2,1)} %constant.12.clone.back) | copy-start | bytes 116644

commit v15 on v14

--- a/solution.py
+++ b/solution.py
@@ -224,19 +224,19 @@
         pltpu.make_async_copy(neighbours_there, neighbours, done.at[3, 0]),
         pltpu.make_async_copy(initial_there, initial, done.at[3, 1]),
     ]
-    for copy in early:
-        copy.start()
     copies = []
     for p in range(planes):
         pairs = ((inverse, inverse_in), (couplings, couplings_in), (right, right_in))
         copies.append([pltpu.make_async_copy(x.at[p], y.at[p], done.at[i, p]) for i, (x, y) in enumerate(pairs)])
-        for copy in copies[p]:
-            copy.start()
+    for copy in copies[0] + early:
+        copy.start()
     for start, stop in ((5 * FACE, 256), (256 + FACE, 256 + 2 * SLOT)):
         faces[:, :, start:stop] = jnp.zeros((2, columns, stop - start, 256), BF)
     raw[:, :, :, NT * columns :] = jnp.zeros((2, 9, 2, (FACE - NT) * columns, 128), F32)
     for copy in early:
         copy.wait()
+    for copy in sum(copies[1:2], []):
+        copy.start()
     source = sources(neighbours, columns, rhs)
     for i, start in enumerate((0, size)):
         for j in range(2):
@@ -257,6 +257,8 @@
         slot = p % 2
         for copy in copies[p]:
             copy.wait()
+        for copy in sum(copies[p + 2 : p + 3], []):
+            copy.start()
         faces[slot, :, 256 + SLOT : 256 + SLOT + rhs, :width] = right_in[p]
         for a in range(3):
             rows = [inverse_in[p, v * 27 + a * 9 : v * 27 + a * 9 + 9] for v in range(5)]
@@ -420,17 +422,13 @@
     here = lax.axis_index("sweep")
     beside = lambda i: [jnp.where(here + 1 == i, near[h], next_near[h]) for h in range(2)]
     entry = incoming(messages, beside, False, rhs)
-    size = entry.shape[1]
-    row = lax.broadcasted_iota(jnp.int32, (size, size), 0)
-    column = lax.broadcasted_iota(jnp.int32, (size, size), 1)
-    unit = jnp.where(row == column, 1.0, 0.0).astype(BF)
     columns, _, width = result.shape[1:]
     copies = []
     trace = entry
     for p in range(planes - 1, -1, -1):
         whole = part[p] + chain_step(upper.at[p], trace, rhs, FULL)
-        flat = mm(back[...], whole.astype(BF)).astype(BF)
-        results[p] = mt(unit, flat).astype(BF).reshape(columns, rhs, width)
+        flat = lax.dot_general(whole.astype(BF), back[...], (((0,), (0,)), ((), ())), preferred_element_type=F32)
+        results[p] = flat.astype(BF).reshape(columns, rhs, width)
         copies.append(pltpu.make_async_copy(results.at[p], result.at[p], sem.at[p]))
         copies[-1].start()
         if p:
@@ -501,7 +499,7 @@
     const = lambda x: jnp.asarray(x, BF)
     send_in = const(send_table(ROWS, inner, planes))
     own_in = const(own_table(ROWS, inner))
-    back = const(table(width, ROWS, [(natural(*n), n) for n in NODES], inner))
+    back = const(table(ROWS, width, [(inner(*n), n) for n in NODES], natural))
     up_sel = const(receive_table(2, planes))
     down_sel = const(receive_table(0, planes))
     beside = neighbours.T

time: 45.1 us -> 45.1 us (level)
  waiting for transfers between devices: 1.51 us -> 2.05 us
  starting transfers between devices: 13.9 us -> 13.4 us
    ppermute x4, waiting for transfers between devices: 1.5 us -> 2.04 us  [swapped(): lax.ppermute(x, axis, [pair for i, j in pairs for pair in ((i, j), (j, i))])]
    ppermute x4, starting transfers between devices: 8.04 us -> 7.5 us  [swapped(): lax.ppermute(x, axis, [pair for i, j in pairs for pair in ((i, j), (j, i))])]
  transfers between devices with their start and end apart: 7 -> 7, of which waited for: 1 -> 2; matrix products, arithmetic and copies ran while one was open for 0% -> 0% of each run, Pallas kernels for 21% -> 22%
where the time goes in v15:
time: 45.1 us; the launch traced here: 44.7 us
  Pallas kernels  15 us (33%)
  starting transfers between devices  13.4 us (30%)
  blocking collectives  13 us (29%)
  waiting for transfers between devices  2.05 us (5%)
  local copies, waits for them, and re-layouts  1.07 us (2%)
    pallas_call x7, Pallas kernels, call(): pl.pallas_call(kernel, out_shape=shapes, in_specs=[pl.BlockSpec(memory_sp...  15 us
    all_gather x2, blocking collectives, local(): messages = lax.all_gather(message, 'sweep')  13 us
    ppermute x4, starting transfers between devices, swapped(): lax.ppermute(x, axis, [pair for i, j in pairs for pair in ((i, j), (j, i))])  7.5 us
    ppermute x2, starting transfers between devices, products(): lax.ppermute(x, 'sweep', [(i, i + step) for i in inner if 0 <= i + step <...  3.93 us
    ppermute x4, waiting for transfers between devices, swapped(): lax.ppermute(x, axis, [pair for i, j in pairs for pair in ((i, j), (j, i))])  2.04 us
    ppermute x1, starting transfers between devices, shift(): lax.ppermute(x, axis, [(i, i + by) for i in range(n) if 0 <= i + by < n])  1.97 us
    unnamed x12, local copies, waits for them, and re-layouts  1.07 us
  transfers between devices with their start and end apart: 7, of which 2 were waited for; matrix products, arithmetic and copies ran while one was open for 0% of the time, Pallas kernels for 22%

profile of v15, /device:TPU:1, one launch (start us, length us, event | category | flops | bytes accessed | tf_op | source)
XLA Modules:
  0.0 44.7 jit_solution(15807546545362717219)
XLA Ops:
  0.0 0.0 copy-start.4
  0.0 1.0 %copy-done.4 = bf16[4,8,32,135]{3,2,1,0:T(8,128)(2,1)S(1)} copy-done((bf16[4,8,32,135]{3,2,1,0:T(8,128)(2,1)S(1)}, bf16[4,8,32,135]{3,2,1,0:T(8,128)(2,1)}, u32[]{:S(2)}) %copy-start.4) | copy-done | bytes 276504
  1.0 0.4 initial_traces.1
  1.4 2.0 %collective-permute-start.2 = (bf16[48,256]{1,0:T(8,128)(2,1)S(1)}, bf16[48,256]{1,0:T(8,128)(2,1)S(1)}, u32[]{:S(2)}, u32[]{:S(2)}) collective-permute-start(bf16[48,256]{1,0:T(8,128)(2,1)S(1)} %get-tuple-element.37), channel_id=1, source_target_pairs={{8,0},{16,8},{24,16},{9,1},{17,9},{25,17},{10,2},{18,10},{26,18},{... | collective-permute-start | bytes 73736 | tf_op jit(solution)/shard_map/ppermute | solution.py:493
  3.4 2.8 %collective-permute-start = (bf16[304,256]{1,0:T(8,128)(2,1)S(1)}, bf16[304,256]{1,0:T(8,128)(2,1)S(1)}, u32[]{:S(2)}, u32[]{:S(2)}) collective-permute-start(bf16[304,256]{1,0:T(8,128)(2,1)S(1)} %get-tuple-element.35), channel_id=1, source_target_pairs={{0,1},{1,0},{2,3},{3,2},{4,5},{5,4},{6,7},{7,6},{8,9},{9,8},{10,11... | collective-permute-start | bytes 466952 | tf_op jit(solution)/shard_map/ppermute | solution.py:488
  6.1 3.3 %collective-permute-start.1 = (bf16[304,256]{1,0:T(8,128)(2,1)S(1)}, bf16[304,256]{1,0:T(8,128)(2,1)S(1)}, u32[]{:S(2)}, u32[]{:S(2)}) collective-permute-start(bf16[304,256]{1,0:T(8,128)(2,1)S(1)} %get-tuple-element.36), channel_id=1, source_target_pairs={{1,2},{2,1},{3,4},{4,3},{5,6},{6,5},{7,0},{0,7},{9,10},{10,9},{11,... | collective-permute-start | bytes 466952 | tf_op jit(solution)/shard_map/ppermute | solution.py:488
  9.4 0.0 copy-start.1
  9.4 0.0 copy-start.2
  9.4 7.7 %weights.1 = (bf16[4,8,144,256]{3,2,1,0:T(8,128)(2,1)S(1)}, bf16[4,2,192,256]{3,2,1,0:T(8,128)(2,1)S(1)}, f32[4,144,256]{2,1,0:T(8,128)S(1)}, bf16[4,144,256]{2,...) custom-call(bf16[4,135,8,135]{3,2,1,0:T(8,128)(2,1)} %bitcast.10, bf16[4,6,45,8,135]{4,3,2,1,0:T(8,128)(2,1)} %bitcast.9, ...), custom_call_target="tpu_custom_call" | custom-call | flops 10000000000 | bytes 8607040 | tf_op jit(solution)/shard_map/weights/pallas_call | solution.py:448
  17.1 0.0 collective-permute-done.2.above
  17.2 0.0 collective-permute-done.near
  17.2 0.0 collective-permute-done.1.far
  17.2 0.0 copy-done.1
  17.2 0.0 copy-done.2
  17.2 0.0 copy-start
  17.2 1.2 %forward_chain.1 = (f32[4,144,256]{2,1,0:T(8,128)S(1)}, f32[4,48,256]{2,1,0:T(8,128)S(1)}, bf16[144,256]{1,0:T(8,128)(2,1)S(1)}) custom-call(bf16[304,256]{1,0:T(8,128)(2,1)S(1)} %collective-permute-done.near, bf16[304,256]{1,0:T(8,128)(2,1)S(1)} %collective-permute-done.1.far, bf16[48,256]{1,0:T(8,128)(2,1)S(1)} %collective-permute-done.2.above, ...), custom_call_target="tpu_custom_call" | custom-call | flops 200000000 | bytes 5922816 | tf_op jit(solution)/shard_map/forward_chain/pallas_call | solution.py:448
  18.5 0.0 copy-start.5
  18.5 6.3 %all-gather = bf16[576,256]{1,0:T(8,128)(2,1)S(1)} all-gather(bf16[144,256]{1,0:T(8,128)(2,1)S(1)} %get-tuple-element.44), channel_id=2, replica_groups=mesh['sweep'=4,'cross'=8] {'sweep'}, dimensions={0}, use_global_device_ids=true | all-gather | bytes 368640 | tf_op jit(solution)/shard_map/all_gather | solution.py:530
  24.8 0.0 copy-done
  24.8 1.4 %forward_finish.1 = (bf16[4,144,256]{2,1,0:T(8,128)(2,1)S(1)}, f32[4,144,256]{2,1,0:T(8,128)S(1)}, bf16[304,256]{1,0:T(8,128)(2,1)S(1)}, bf16[304,256]{1,0:T(8,128)(2,1)S(1)}) custom-call(bf16[4,144,256]{2,1,0:T(8,128)(2,1)S(1)} %bitcast.7, f32[4,144,256]{2,1,0:T(8,128)S(1)} %get-tuple-element.45.part, f32[4,48,256]{2,1,0:T(8,128)S(1)} %get-tuple-element.46.traces, ...), custom_call_target="tpu_custom_call" | custom-call | flops 200000000 | bytes 3321856 | tf_op jit(solution)/shard_map/forward_finish/pallas_call | solution.py:448
  26.2 0.1 collective-permute-start.3
  26.2 1.4 %collective-permute-start.4 = (bf16[304,256]{1,0:T(8,128)(2,1)S(1)}, bf16[304,256]{1,0:T(8,128)(2,1)S(1)}, u32[]{:S(2)}, u32[]{:S(2)}) collective-permute-start(bf16[304,256]{1,0:T(8,128)(2,1)S(1)} %get-tuple-element.48), channel_id=1, source_target_pairs={{1,2},{2,1},{3,4},{4,3},{5,6},{6,5},{7,0},{0,7},{9,10},{10,9},{11,... | collective-permute-start | bytes 466952 | tf_op jit(solution)/shard_map/ppermute | solution.py:488
  27.7 0.0 copy-done.5
  27.7 0.8 %middle.1 = (bf16[4,96,256]{2,1,0:T(8,128)(2,1)S(1)}, f32[4,144,256]{2,1,0:T(8,128)S(1)}, bf16[4,2,192,256]{3,2,1,0:T(8,128)(2,1)S(1)}) custom-call(bf16[4,144,256]{2,1,0:T(8,128)(2,1)S(1)} %get-tuple-element.49.middle, f32[4,144,256]{2,1,0:T(8,128)S(1)} %get-tuple-element.50.change, f32[4,144,256]{2,1,0:T(8,128)S(1)} %get-tuple-element.43.base, ...), custom_call_target="tpu_custom_call" | custom-call | flops 2000000000 | bytes 5958656 | tf_op jit(solution)/shard_map/middle/pallas_call | solution.py:448
  28.5 0.7 %collective-permute-start.6 = (bf16[2,48,256]{2,1,0:T(8,128)(2,1)S(1)}, bf16[2,48,256]{2,1,0:T(8,128)(2,1)S(1)}, u32[]{:S(2)}, u32[]{:S(2)}) collective-permute-start(bf16[2,48,256]{2,1,0:T(8,128)(2,1)S(1)} %slice_bitcast_fusion), channel_id=1, source_target_pairs={{16,0},{17,1},{18,2},{19,3},{20,4},{21,5},{22,6},{23,7}} | collective-permute-start | bytes 147464 | tf_op jit(solution)/shard_map/ppermute | solution.py:464
  29.2 3.3 %collective-permute-start.5 = (bf16[2,48,256]{2,1,0:T(8,128)(2,1)S(1)}, bf16[2,48,256]{2,1,0:T(8,128)(2,1)S(1)}, u32[]{:S(2)}, u32[]{:S(2)}) collective-permute-start(bf16[2,48,256]{2,1,0:T(8,128)(2,1)S(1)} %slice_bitcast_fusion), channel_id=1, source_target_pairs={{8,0},{16,8},{9,1},{17,9},{10,2},{18,10},{11,3},{19,11},{12,4},{20... | collective-permute-start | bytes 147464 | tf_op jit(solution)/shard_map/ppermute | solution.py:464
  32.4 0.6 %collective-permute-done.3.near = bf16[304,256]{1,0:T(8,128)(2,1)S(1)} collective-permute-done((bf16[304,256]{1,0:T(8,128)(2,1)S(1)}, bf16[304,256]{1,0:T(8,128)(2,1)S(1)}, u32[]{:S(2)}, u32[]{:S(2)}) %collective-permute-start.3) | collective-permute-done | bytes 155680 | tf_op jit(solution)/shard_map/ppermute | solution.py:488
  33.0 1.5 %collective-permute-done.4.far = bf16[304,256]{1,0:T(8,128)(2,1)S(1)} collective-permute-done((bf16[304,256]{1,0:T(8,128)(2,1)S(1)}, bf16[304,256]{1,0:T(8,128)(2,1)S(1)}, u32[]{:S(2)}, u32[]{:S(2)}) %collective-permute-start.4) | collective-permute-done | bytes 155680 | tf_op jit(solution)/shard_map/ppermute | solution.py:488
  34.5 0.0 copy-start.3
  34.5 1.3 %backward_chain.1 = (f32[4,144,256]{2,1,0:T(8,128)S(1)}, f32[4,48,256]{2,1,0:T(8,128)S(1)}, bf16[48,256]{1,0:T(8,128)(2,1)S(1)}) custom-call(bf16[304,256]{1,0:T(8,128)(2,1)S(1)} %collective-permute-done.3.near, bf16[304,256]{1,0:T(8,128)(2,1)S(1)} %collective-permute-done.4.far, bf16[4,96,256]{2,1,0:T(8,128)(2,1)S(1)} %get-tuple-element.53.own, ...), custom_call_target="tpu_custom_call" | custom-call | flops 200000000 | bytes 5750784 | tf_op jit(solution)/shard_map/backward_chain/pallas_call | solution.py:448
  35.8 6.7 %all-gather.1 = bf16[192,256]{1,0:T(8,128)(2,1)S(1)} all-gather(bf16[48,256]{1,0:T(8,128)(2,1)S(1)} %get-tuple-element.55), channel_id=3, replica_groups=mesh['sweep'=4,'cross'=8] {'sweep'}, dimensions={0}, use_global_device_ids=true | all-gather | bytes 122880 | tf_op jit(solution)/shard_map/all_gather | solution.py:553
  42.5 0.0 collective-permute-done.6.next_near
  42.5 0.0 collective-permute-done.5.near
  42.5 0.0 copy-done.3
  42.5 2.2 %backward_finish.1 = bf16[4,8,32,135]{3,2,1,0:T(8,128)(2,1)} custom-call(bf16[4,48,256]{2,1,0:T(8,128)(2,1)S(1)} %bitcast.8, bf16[2,48,256]{2,1,0:T(8,128)(2,1)S(1)} %collective-permute-done.5.near, bf16[2,48,256]{2,1,0:T(8,128)(2,1)S(1)} %collective-permute-done.6.next_near, f32[4,144,256]{2,1,0:T(8,128)S(1)} %get-tuple-element.57.part, ...), custom_call_target="tpu_custom_call" | custom-call | flops 200000000 | bytes 2084832 | tf_op jit(solution)/shard_map/backward_finish/pallas_call | solution.py:448
  (1 shorter events, 0.0 us)
Async XLA Ops:
  0.0 1.0 %copy-start.4 = (bf16[4,8,32,135]{3,2,1,0:T(8,128)(2,1)S(1)}, bf16[4,8,32,135]{3,2,1,0:T(8,128)(2,1)}, u32[]{:S(2)}) copy-start(bf16[4,8,32,135]{3,2,1,0:T(8,128)(2,1)} %initial_there) | copy-start | bytes 829444
  1.4 15.7 %collective-permute-start.2 = (bf16[48,256]{1,0:T(8,128)(2,1)S(1)}, bf16[48,256]{1,0:T(8,128)(2,1)S(1)}, u32[]{:S(2)}, u32[]{:S(2)}) collective-permute-start(bf16[48,256]{1,0:T(8,128)(2,1)S(1)} %get-tuple-element.37), channel_id=1, source_target_pairs={{8,0},{16,8},{24,16},{9,1},{17,9},{25,17},{10,2},{18,10},{26,18},{... | collective-permute-start | bytes 73736 | tf_op jit(solution)/shard_map/ppermute | solution.py:493
  3.4 13.8 %collective-permute-start = (bf16[304,256]{1,0:T(8,128)(2,1)S(1)}, bf16[304,256]{1,0:T(8,128)(2,1)S(1)}, u32[]{:S(2)}, u32[]{:S(2)}) collective-permute-start(bf16[304,256]{1,0:T(8,128)(2,1)S(1)} %get-tuple-element.35), channel_id=1, source_target_pairs={{0,1},{1,0},{2,3},{3,2},{4,5},{5,4},{6,7},{7,6},{8,9},{9,8},{10,11... | collective-permute-start | bytes 466952 | tf_op jit(solution)/shard_map/ppermute | solution.py:488
  6.1 11.0 %collective-permute-start.1 = (bf16[304,256]{1,0:T(8,128)(2,1)S(1)}, bf16[304,256]{1,0:T(8,128)(2,1)S(1)}, u32[]{:S(2)}, u32[]{:S(2)}) collective-permute-start(bf16[304,256]{1,0:T(8,128)(2,1)S(1)} %get-tuple-element.36), channel_id=1, source_target_pairs={{1,2},{2,1},{3,4},{4,3},{5,6},{6,5},{7,0},{0,7},{9,10},{10,9},{11,... | collective-permute-start | bytes 466952 | tf_op jit(solution)/shard_map/ppermute | solution.py:488
  9.4 7.8 %copy-start.1 = (bf16[4,96,112]{2,1,0:T(8,128)(2,1)S(1)}, bf16[4,96,112]{2,1,0:T(8,128)(2,1)}, u32[]{:S(2)}) copy-start(bf16[4,96,112]{2,1,0:T(8,128)(2,1)} %constant.14.clone.down_sel) | copy-start | bytes 258052
  9.4 7.8 %copy-start.2 = (bf16[4,96,112]{2,1,0:T(8,128)(2,1)S(1)}, bf16[4,96,112]{2,1,0:T(8,128)(2,1)}, u32[]{:S(2)}) copy-start(bf16[4,96,112]{2,1,0:T(8,128)(2,1)} %constant.13.clone.up_sel) | copy-start | bytes 258052
  17.2 7.6 %copy-start = (bf16[4,224,144]{2,1,0:T(8,128)(2,1)S(1)}, bf16[4,224,144]{2,1,0:T(8,128)(2,1)}, u32[]{:S(2)}) copy-start(bf16[4,224,144]{2,1,0:T(8,128)(2,1)} %constant.10.clone.send) | copy-start | bytes 774148
  18.5 9.2 %copy-start.5 = (bf16[96,144]{1,0:T(8,128)(2,1)S(1)}, bf16[96,144]{1,0:T(8,128)(2,1)}, u32[]{:S(2)}) copy-start(bf16[96,144]{1,0:T(8,128)(2,1)} %constant.11.clone.own_sel) | copy-start | bytes 82948
  26.2 6.8 %collective-permute-start.3 = (bf16[304,256]{1,0:T(8,128)(2,1)S(1)}, bf16[304,256]{1,0:T(8,128)(2,1)S(1)}, u32[]{:S(2)}, u32[]{:S(2)}) collective-permute-start(bf16[304,256]{1,0:T(8,128)(2,1)S(1)} %get-tuple-element.47), channel_id=1, source_target_pairs={{0,1},{1,0},{2,3},{3,2},{4,5},{5,4},{6,7},{7,6},{8,9},{9,8},{10,11... | collective-permute-start | bytes 466952 | tf_op jit(solution)/shard_map/ppermute | solution.py:488
  26.2 8.2 %collective-permute-start.4 = (bf16[304,256]{1,0:T(8,128)(2,1)S(1)}, bf16[304,256]{1,0:T(8,128)(2,1)S(1)}, u32[]{:S(2)}, u32[]{:S(2)}) collective-permute-start(bf16[304,256]{1,0:T(8,128)(2,1)S(1)} %get-tuple-element.48), channel_id=1, source_target_pairs={{1,2},{2,1},{3,4},{4,3},{5,6},{6,5},{7,0},{0,7},{9,10},{10,9},{11,... | collective-permute-start | bytes 466952 | tf_op jit(solution)/shard_map/ppermute | solution.py:488
  28.5 14.0 %collective-permute-start.6 = (bf16[2,48,256]{2,1,0:T(8,128)(2,1)S(1)}, bf16[2,48,256]{2,1,0:T(8,128)(2,1)S(1)}, u32[]{:S(2)}, u32[]{:S(2)}) collective-permute-start(bf16[2,48,256]{2,1,0:T(8,128)(2,1)S(1)} %slice_bitcast_fusion), channel_id=1, source_target_pairs={{16,0},{17,1},{18,2},{19,3},{20,4},{21,5},{22,6},{23,7}} | collective-permute-start | bytes 147464 | tf_op jit(solution)/shard_map/ppermute | solution.py:464
  29.2 13.3 %collective-permute-start.5 = (bf16[2,48,256]{2,1,0:T(8,128)(2,1)S(1)}, bf16[2,48,256]{2,1,0:T(8,128)(2,1)S(1)}, u32[]{:S(2)}, u32[]{:S(2)}) collective-permute-start(bf16[2,48,256]{2,1,0:T(8,128)(2,1)S(1)} %slice_bitcast_fusion), channel_id=1, source_target_pairs={{8,0},{16,8},{9,1},{17,9},{10,2},{18,10},{11,3},{19,11},{12,4},{20... | collective-permute-start | bytes 147464 | tf_op jit(solution)/shard_map/ppermute | solution.py:464
  34.5 8.0 %copy-start.3 = (bf16[144,135]{1,0:T(8,128)(2,1)S(1)}, bf16[144,135]{1,0:T(8,128)(2,1)}, u32[]{:S(2)}) copy-start(bf16[144,135]{1,0:T(8,128)(2,1)} %constant.12.clone.back) | copy-start | bytes 116644

commit v16 on v15

--- a/solution.py
+++ b/solution.py
@@ -228,15 +228,13 @@
     for p in range(planes):
         pairs = ((inverse, inverse_in), (couplings, couplings_in), (right, right_in))
         copies.append([pltpu.make_async_copy(x.at[p], y.at[p], done.at[i, p]) for i, (x, y) in enumerate(pairs)])
-    for copy in copies[0] + early:
+    for copy in early + sum(copies, []):
         copy.start()
     for start, stop in ((5 * FACE, 256), (256 + FACE, 256 + 2 * SLOT)):
         faces[:, :, start:stop] = jnp.zeros((2, columns, stop - start, 256), BF)
     raw[:, :, :, NT * columns :] = jnp.zeros((2, 9, 2, (FACE - NT) * columns, 128), F32)
     for copy in early:
         copy.wait()
-    for copy in sum(copies[1:2], []):
-        copy.start()
     source = sources(neighbours, columns, rhs)
     for i, start in enumerate((0, size)):
         for j in range(2):
@@ -253,12 +251,10 @@
         own[p, LAST] = mt(first_table, fields[min(p + 1, planes - 1)]).astype(BF)
     lane = lax.broadcasted_iota(jnp.int32, (ROWS, 2 * SLOT), 1)
 
-    for p in range(planes):
+    def prepare(p):
         slot = p % 2
         for copy in copies[p]:
             copy.wait()
-        for copy in sum(copies[p + 2 : p + 3], []):
-            copy.start()
         faces[slot, :, 256 + SLOT : 256 + SLOT + rhs, :width] = right_in[p]
         for a in range(3):
             rows = [inverse_in[p, v * 27 + a * 9 : v * 27 + a * 9 + 9] for v in range(5)]
@@ -273,6 +269,12 @@
                 faces[slot, c, place : place + FACE] = value.astype(BF)
 
             turned(couplings_in[p, f], raw.at[slot, 3 + f], put)
+
+    prepare(0)
+    for p in range(planes):
+        slot = p % 2
+        if p + 1 < planes:
+            prepare(p + 1)
         bases, lowers = [], []
         before = None
         for c in range(columns):

time: 45.1 us -> 45.3 us (level)
  no operation moved by 1% of the time
where the time goes in v16:
time: 45.3 us; the launch traced here: 44.9 us
  Pallas kernels  15.2 us (34%)
  starting transfers between devices  13.3 us (29%)
  blocking collectives  13 us (29%)
  waiting for transfers between devices  2.16 us (5%)
  local copies, waits for them, and re-layouts  1.07 us (2%)
    pallas_call x7, Pallas kernels, call(): pl.pallas_call(kernel, out_shape=shapes, in_specs=[pl.BlockSpec(memory_sp...  15.2 us
    all_gather x2, blocking collectives, local(): messages = lax.all_gather(message, 'sweep')  13 us
    ppermute x4, starting transfers between devices, swapped(): lax.ppermute(x, axis, [pair for i, j in pairs for pair in ((i, j), (j, i))])  7.39 us
    ppermute x2, starting transfers between devices, products(): lax.ppermute(x, 'sweep', [(i, i + step) for i in inner if 0 <= i + step <...  3.92 us
    ppermute x4, waiting for transfers between devices, swapped(): lax.ppermute(x, axis, [pair for i, j in pairs for pair in ((i, j), (j, i))])  2.16 us
    ppermute x1, starting transfers between devices, shift(): lax.ppermute(x, axis, [(i, i + by) for i in range(n) if 0 <= i + by < n])  1.97 us
    unnamed x12, local copies, waits for them, and re-layouts  1.07 us
  transfers between devices with their start and end apart: 7, of which 2 were waited for; matrix products, arithmetic and copies ran while one was open for 0% of the time, Pallas kernels for 22%

profile of v16, /device:TPU:1, one launch (start us, length us, event | category | flops | bytes accessed | tf_op | source)
XLA Modules:
  0.0 44.9 jit_solution(568345217986590347)
XLA Ops:
  0.0 0.0 copy-start.4
  0.0 1.0 %copy-done.4 = bf16[4,8,32,135]{3,2,1,0:T(8,128)(2,1)S(1)} copy-done((bf16[4,8,32,135]{3,2,1,0:T(8,128)(2,1)S(1)}, bf16[4,8,32,135]{3,2,1,0:T(8,128)(2,1)}, u32[]{:S(2)}) %copy-start.4) | copy-done | bytes 276504
  1.0 0.4 initial_traces.1
  1.4 2.0 %collective-permute-start.2 = (bf16[48,256]{1,0:T(8,128)(2,1)S(1)}, bf16[48,256]{1,0:T(8,128)(2,1)S(1)}, u32[]{:S(2)}, u32[]{:S(2)}) collective-permute-start(bf16[48,256]{1,0:T(8,128)(2,1)S(1)} %get-tuple-element.37), channel_id=1, source_target_pairs={{8,0},{16,8},{24,16},{9,1},{17,9},{25,17},{10,2},{18,10},{26,18},{... | collective-permute-start | bytes 73736 | tf_op jit(solution)/shard_map/ppermute | solution.py:495
  3.4 2.8 %collective-permute-start = (bf16[304,256]{1,0:T(8,128)(2,1)S(1)}, bf16[304,256]{1,0:T(8,128)(2,1)S(1)}, u32[]{:S(2)}, u32[]{:S(2)}) collective-permute-start(bf16[304,256]{1,0:T(8,128)(2,1)S(1)} %get-tuple-element.35), channel_id=1, source_target_pairs={{0,1},{1,0},{2,3},{3,2},{4,5},{5,4},{6,7},{7,6},{8,9},{9,8},{10,11... | collective-permute-start | bytes 466952 | tf_op jit(solution)/shard_map/ppermute | solution.py:490
  6.1 3.3 %collective-permute-start.1 = (bf16[304,256]{1,0:T(8,128)(2,1)S(1)}, bf16[304,256]{1,0:T(8,128)(2,1)S(1)}, u32[]{:S(2)}, u32[]{:S(2)}) collective-permute-start(bf16[304,256]{1,0:T(8,128)(2,1)S(1)} %get-tuple-element.36), channel_id=1, source_target_pairs={{1,2},{2,1},{3,4},{4,3},{5,6},{6,5},{7,0},{0,7},{9,10},{10,9},{11,... | collective-permute-start | bytes 466952 | tf_op jit(solution)/shard_map/ppermute | solution.py:490
  9.4 0.0 copy-start.1
  9.4 0.0 copy-start.2
  9.4 7.9 %weights.1 = (bf16[4,8,144,256]{3,2,1,0:T(8,128)(2,1)S(1)}, bf16[4,2,192,256]{3,2,1,0:T(8,128)(2,1)S(1)}, f32[4,144,256]{2,1,0:T(8,128)S(1)}, bf16[4,144,256]{2,...) custom-call(bf16[4,135,8,135]{3,2,1,0:T(8,128)(2,1)} %bitcast.10, bf16[4,6,45,8,135]{4,3,2,1,0:T(8,128)(2,1)} %bitcast.9, ...), custom_call_target="tpu_custom_call" | custom-call | flops 10000000000 | bytes 8607040 | tf_op jit(solution)/shard_map/weights/pallas_call | solution.py:450
  17.3 0.0 collective-permute-done.2.above
  17.3 0.0 collective-permute-done.near
  17.3 0.0 collective-permute-done.1.far
  17.3 0.0 copy-done.1
  17.4 0.0 copy-done.2
  17.4 0.0 copy-start
  17.4 1.3 %forward_chain.1 = (f32[4,144,256]{2,1,0:T(8,128)S(1)}, f32[4,48,256]{2,1,0:T(8,128)S(1)}, bf16[144,256]{1,0:T(8,128)(2,1)S(1)}) custom-call(bf16[304,256]{1,0:T(8,128)(2,1)S(1)} %collective-permute-done.near, bf16[304,256]{1,0:T(8,128)(2,1)S(1)} %collective-permute-done.1.far, bf16[48,256]{1,0:T(8,128)(2,1)S(1)} %collective-permute-done.2.above, ...), custom_call_target="tpu_custom_call" | custom-call | flops 200000000 | bytes 5922816 | tf_op jit(solution)/shard_map/forward_chain/pallas_call | solution.py:450
  18.7 0.0 copy-start.5
  18.7 6.3 %all-gather = bf16[576,256]{1,0:T(8,128)(2,1)S(1)} all-gather(bf16[144,256]{1,0:T(8,128)(2,1)S(1)} %get-tuple-element.44), channel_id=2, replica_groups=mesh['sweep'=4,'cross'=8] {'sweep'}, dimensions={0}, use_global_device_ids=true | all-gather | bytes 368640 | tf_op jit(solution)/shard_map/all_gather | solution.py:532
  25.0 0.0 copy-done
  25.0 1.4 %forward_finish.1 = (bf16[4,144,256]{2,1,0:T(8,128)(2,1)S(1)}, f32[4,144,256]{2,1,0:T(8,128)S(1)}, bf16[304,256]{1,0:T(8,128)(2,1)S(1)}, bf16[304,256]{1,0:T(8,128)(2,1)S(1)}) custom-call(bf16[4,144,256]{2,1,0:T(8,128)(2,1)S(1)} %bitcast.7, f32[4,144,256]{2,1,0:T(8,128)S(1)} %get-tuple-element.45.part, f32[4,48,256]{2,1,0:T(8,128)S(1)} %get-tuple-element.46.traces, ...), custom_call_target="tpu_custom_call" | custom-call | flops 200000000 | bytes 3321856 | tf_op jit(solution)/shard_map/forward_finish/pallas_call | solution.py:450
  26.4 0.1 collective-permute-start.3
  26.5 1.3 %collective-permute-start.4 = (bf16[304,256]{1,0:T(8,128)(2,1)S(1)}, bf16[304,256]{1,0:T(8,128)(2,1)S(1)}, u32[]{:S(2)}, u32[]{:S(2)}) collective-permute-start(bf16[304,256]{1,0:T(8,128)(2,1)S(1)} %get-tuple-element.48), channel_id=1, source_target_pairs={{1,2},{2,1},{3,4},{4,3},{5,6},{6,5},{7,0},{0,7},{9,10},{10,9},{11,... | collective-permute-start | bytes 466952 | tf_op jit(solution)/shard_map/ppermute | solution.py:490
  27.8 0.0 copy-done.5
  27.8 0.8 %middle.1 = (bf16[4,96,256]{2,1,0:T(8,128)(2,1)S(1)}, f32[4,144,256]{2,1,0:T(8,128)S(1)}, bf16[4,2,192,256]{3,2,1,0:T(8,128)(2,1)S(1)}) custom-call(bf16[4,144,256]{2,1,0:T(8,128)(2,1)S(1)} %get-tuple-element.49.middle, f32[4,144,256]{2,1,0:T(8,128)S(1)} %get-tuple-element.50.change, f32[4,144,256]{2,1,0:T(8,128)S(1)} %get-tuple-element.43.base, ...), custom_call_target="tpu_custom_call" | custom-call | flops 2000000000 | bytes 5958656 | tf_op jit(solution)/shard_map/middle/pallas_call | solution.py:450
  28.6 0.7 %collective-permute-start.6 = (bf16[2,48,256]{2,1,0:T(8,128)(2,1)S(1)}, bf16[2,48,256]{2,1,0:T(8,128)(2,1)S(1)}, u32[]{:S(2)}, u32[]{:S(2)}) collective-permute-start(bf16[2,48,256]{2,1,0:T(8,128)(2,1)S(1)} %slice_bitcast_fusion), channel_id=1, source_target_pairs={{16,0},{17,1},{18,2},{19,3},{20,4},{21,5},{22,6},{23,7}} | collective-permute-start | bytes 147464 | tf_op jit(solution)/shard_map/ppermute | solution.py:466
  29.3 3.3 %collective-permute-start.5 = (bf16[2,48,256]{2,1,0:T(8,128)(2,1)S(1)}, bf16[2,48,256]{2,1,0:T(8,128)(2,1)S(1)}, u32[]{:S(2)}, u32[]{:S(2)}) collective-permute-start(bf16[2,48,256]{2,1,0:T(8,128)(2,1)S(1)} %slice_bitcast_fusion), channel_id=1, source_target_pairs={{8,0},{16,8},{9,1},{17,9},{10,2},{18,10},{11,3},{19,11},{12,4},{20... | collective-permute-start | bytes 147464 | tf_op jit(solution)/shard_map/ppermute | solution.py:466
  32.5 0.6 %collective-permute-done.3.near = bf16[304,256]{1,0:T(8,128)(2,1)S(1)} collective-permute-done((bf16[304,256]{1,0:T(8,128)(2,1)S(1)}, bf16[304,256]{1,0:T(8,128)(2,1)S(1)}, u32[]{:S(2)}, u32[]{:S(2)}) %collective-permute-start.3) | collective-permute-done | bytes 155680 | tf_op jit(solution)/shard_map/ppermute | solution.py:490
  33.1 1.5 %collective-permute-done.4.far = bf16[304,256]{1,0:T(8,128)(2,1)S(1)} collective-permute-done((bf16[304,256]{1,0:T(8,128)(2,1)S(1)}, bf16[304,256]{1,0:T(8,128)(2,1)S(1)}, u32[]{:S(2)}, u32[]{:S(2)}) %collective-permute-start.4) | collective-permute-done | bytes 155680 | tf_op jit(solution)/shard_map/ppermute | solution.py:490
  34.7 0.0 copy-start.3
  34.7 1.3 %backward_chain.1 = (f32[4,144,256]{2,1,0:T(8,128)S(1)}, f32[4,48,256]{2,1,0:T(8,128)S(1)}, bf16[48,256]{1,0:T(8,128)(2,1)S(1)}) custom-call(bf16[304,256]{1,0:T(8,128)(2,1)S(1)} %collective-permute-done.3.near, bf16[304,256]{1,0:T(8,128)(2,1)S(1)} %collective-permute-done.4.far, bf16[4,96,256]{2,1,0:T(8,128)(2,1)S(1)} %get-tuple-element.53.own, ...), custom_call_target="tpu_custom_call" | custom-call | flops 200000000 | bytes 5750784 | tf_op jit(solution)/shard_map/backward_chain/pallas_call | solution.py:450
  36.0 6.7 %all-gather.1 = bf16[192,256]{1,0:T(8,128)(2,1)S(1)} all-gather(bf16[48,256]{1,0:T(8,128)(2,1)S(1)} %get-tuple-element.55), channel_id=3, replica_groups=mesh['sweep'=4,'cross'=8] {'sweep'}, dimensions={0}, use_global_device_ids=true | all-gather | bytes 122880 | tf_op jit(solution)/shard_map/all_gather | solution.py:555
  42.7 0.0 collective-permute-done.6.next_near
  42.7 0.0 collective-permute-done.5.near
  42.7 0.0 copy-done.3
  42.7 2.2 %backward_finish.1 = bf16[4,8,32,135]{3,2,1,0:T(8,128)(2,1)} custom-call(bf16[4,48,256]{2,1,0:T(8,128)(2,1)S(1)} %bitcast.8, bf16[2,48,256]{2,1,0:T(8,128)(2,1)S(1)} %collective-permute-done.5.near, bf16[2,48,256]{2,1,0:T(8,128)(2,1)S(1)} %collective-permute-done.6.next_near, f32[4,144,256]{2,1,0:T(8,128)S(1)} %get-tuple-element.57.part, ...), custom_call_target="tpu_custom_call" | custom-call | flops 200000000 | bytes 2084832 | tf_op jit(solution)/shard_map/backward_finish/pallas_call | solution.py:450
  (1 shorter events, 0.0 us)
Async XLA Ops:
  0.0 1.0 %copy-start.4 = (bf16[4,8,32,135]{3,2,1,0:T(8,128)(2,1)S(1)}, bf16[4,8,32,135]{3,2,1,0:T(8,128)(2,1)}, u32[]{:S(2)}) copy-start(bf16[4,8,32,135]{3,2,1,0:T(8,128)(2,1)} %initial_there) | copy-start | bytes 829444
  1.4 15.9 %collective-permute-start.2 = (bf16[48,256]{1,0:T(8,128)(2,1)S(1)}, bf16[48,256]{1,0:T(8,128)(2,1)S(1)}, u32[]{:S(2)}, u32[]{:S(2)}) collective-permute-start(bf16[48,256]{1,0:T(8,128)(2,1)S(1)} %get-tuple-element.37), channel_id=1, source_target_pairs={{8,0},{16,8},{24,16},{9,1},{17,9},{25,17},{10,2},{18,10},{26,18},{... | collective-permute-start | bytes 73736 | tf_op jit(solution)/shard_map/ppermute | solution.py:495
  3.4 13.9 %collective-permute-start = (bf16[304,256]{1,0:T(8,128)(2,1)S(1)}, bf16[304,256]{1,0:T(8,128)(2,1)S(1)}, u32[]{:S(2)}, u32[]{:S(2)}) collective-permute-start(bf16[304,256]{1,0:T(8,128)(2,1)S(1)} %get-tuple-element.35), channel_id=1, source_target_pairs={{0,1},{1,0},{2,3},{3,2},{4,5},{5,4},{6,7},{7,6},{8,9},{9,8},{10,11... | collective-permute-start | bytes 466952 | tf_op jit(solution)/shard_map/ppermute | solution.py:490
  6.1 11.2 %collective-permute-start.1 = (bf16[304,256]{1,0:T(8,128)(2,1)S(1)}, bf16[304,256]{1,0:T(8,128)(2,1)S(1)}, u32[]{:S(2)}, u32[]{:S(2)}) collective-permute-start(bf16[304,256]{1,0:T(8,128)(2,1)S(1)} %get-tuple-element.36), channel_id=1, source_target_pairs={{1,2},{2,1},{3,4},{4,3},{5,6},{6,5},{7,0},{0,7},{9,10},{10,9},{11,... | collective-permute-start | bytes 466952 | tf_op jit(solution)/shard_map/ppermute | solution.py:490
  9.4 7.9 %copy-start.1 = (bf16[4,96,112]{2,1,0:T(8,128)(2,1)S(1)}, bf16[4,96,112]{2,1,0:T(8,128)(2,1)}, u32[]{:S(2)}) copy-start(bf16[4,96,112]{2,1,0:T(8,128)(2,1)} %constant.14.clone.down_sel) | copy-start | bytes 258052
  9.4 7.9 %copy-start.2 = (bf16[4,96,112]{2,1,0:T(8,128)(2,1)S(1)}, bf16[4,96,112]{2,1,0:T(8,128)(2,1)}, u32[]{:S(2)}) copy-start(bf16[4,96,112]{2,1,0:T(8,128)(2,1)} %constant.13.clone.up_sel) | copy-start | bytes 258052
  17.4 7.6 %copy-start = (bf16[4,224,144]{2,1,0:T(8,128)(2,1)S(1)}, bf16[4,224,144]{2,1,0:T(8,128)(2,1)}, u32[]{:S(2)}) copy-start(bf16[4,224,144]{2,1,0:T(8,128)(2,1)} %constant.10.clone.send) | copy-start | bytes 774148
  18.7 9.1 %copy-start.5 = (bf16[96,144]{1,0:T(8,128)(2,1)S(1)}, bf16[96,144]{1,0:T(8,128)(2,1)}, u32[]{:S(2)}) copy-start(bf16[96,144]{1,0:T(8,128)(2,1)} %constant.11.clone.own_sel) | copy-start | bytes 82948
  26.4 6.8 %collective-permute-start.3 = (bf16[304,256]{1,0:T(8,128)(2,1)S(1)}, bf16[304,256]{1,0:T(8,128)(2,1)S(1)}, u32[]{:S(2)}, u32[]{:S(2)}) collective-permute-start(bf16[304,256]{1,0:T(8,128)(2,1)S(1)} %get-tuple-element.47), channel_id=1, source_target_pairs={{0,1},{1,0},{2,3},{3,2},{4,5},{5,4},{6,7},{7,6},{8,9},{9,8},{10,11... | collective-permute-start | bytes 466952 | tf_op jit(solution)/shard_map/ppermute | solution.py:490
  26.5 8.2 %collective-permute-start.4 = (bf16[304,256]{1,0:T(8,128)(2,1)S(1)}, bf16[304,256]{1,0:T(8,128)(2,1)S(1)}, u32[]{:S(2)}, u32[]{:S(2)}) collective-permute-start(bf16[304,256]{1,0:T(8,128)(2,1)S(1)} %get-tuple-element.48), channel_id=1, source_target_pairs={{1,2},{2,1},{3,4},{4,3},{5,6},{6,5},{7,0},{0,7},{9,10},{10,9},{11,... | collective-permute-start | bytes 466952 | tf_op jit(solution)/shard_map/ppermute | solution.py:490
  28.6 14.1 %collective-permute-start.6 = (bf16[2,48,256]{2,1,0:T(8,128)(2,1)S(1)}, bf16[2,48,256]{2,1,0:T(8,128)(2,1)S(1)}, u32[]{:S(2)}, u32[]{:S(2)}) collective-permute-start(bf16[2,48,256]{2,1,0:T(8,128)(2,1)S(1)} %slice_bitcast_fusion), channel_id=1, source_target_pairs={{16,0},{17,1},{18,2},{19,3},{20,4},{21,5},{22,6},{23,7}} | collective-permute-start | bytes 147464 | tf_op jit(solution)/shard_map/ppermute | solution.py:466
  29.3 13.4 %collective-permute-start.5 = (bf16[2,48,256]{2,1,0:T(8,128)(2,1)S(1)}, bf16[2,48,256]{2,1,0:T(8,128)(2,1)S(1)}, u32[]{:S(2)}, u32[]{:S(2)}) collective-permute-start(bf16[2,48,256]{2,1,0:T(8,128)(2,1)S(1)} %slice_bitcast_fusion), channel_id=1, source_target_pairs={{8,0},{16,8},{9,1},{17,9},{10,2},{18,10},{11,3},{19,11},{12,4},{20... | collective-permute-start | bytes 147464 | tf_op jit(solution)/shard_map/ppermute | solution.py:466
  34.7 8.0 %copy-start.3 = (bf16[144,135]{1,0:T(8,128)(2,1)S(1)}, bf16[144,135]{1,0:T(8,128)(2,1)}, u32[]{:S(2)}) copy-start(bf16[144,135]{1,0:T(8,128)(2,1)} %constant.12.clone.back) | copy-start | bytes 116644

commit v17 on v16

--- a/solution.py
+++ b/solution.py
@@ -221,14 +221,20 @@
     size = columns * rhs
     half = columns // 2
     early = [
-        pltpu.make_async_copy(neighbours_there, neighbours, done.at[3, 0]),
-        pltpu.make_async_copy(initial_there, initial, done.at[3, 1]),
+        pltpu.make_async_copy(neighbours_there, neighbours, done.at[6, 0]),
+        pltpu.make_async_copy(initial_there, initial, done.at[6, 1]),
     ]
     copies = []
     for p in range(planes):
-        pairs = ((inverse, inverse_in), (couplings, couplings_in), (right, right_in))
-        copies.append([pltpu.make_async_copy(x.at[p], y.at[p], done.at[i, p]) for i, (x, y) in enumerate(pairs)])
-    for copy in early + sum(copies, []):
+        blocks = [(inverse, inverse_in, 0, 64), (inverse, inverse_in, 64, width - 64)]
+        blocks += [(couplings, couplings_in, f, 2) for f in range(0, 6, 2)] + [(right, right_in, 0, columns)]
+        copies.append(
+            [
+                pltpu.make_async_copy(x.at[p, pl.ds(start, count)], y.at[p, pl.ds(start, count)], done.at[i, p])
+                for i, (x, y, start, count) in enumerate(blocks)
+            ]
+        )
+    for copy in copies[0] + early + sum(copies[1:], []):
         copy.start()
     for start, stop in ((5 * FACE, 256), (256 + FACE, 256 + 2 * SLOT)):
         faces[:, :, start:stop] = jnp.zeros((2, columns, stop - start, 256), BF)
@@ -270,11 +276,9 @@
 
             turned(couplings_in[p, f], raw.at[slot, 3 + f], put)
 
-    prepare(0)
     for p in range(planes):
         slot = p % 2
-        if p + 1 < planes:
-            prepare(p + 1)
+        prepare(p)
         bases, lowers = [], []
         before = None
         for c in range(columns):
@@ -479,7 +483,7 @@
         pltpu.VMEM((2, columns, ROWS, 256), BF),
         pltpu.VMEM((2, columns, 256 + 2 * SLOT, 256), BF),
         pltpu.VMEM((2, 9, 2, FACE * columns, 128), F32),
-        pltpu.SemaphoreType.DMA((4, planes)),
+        pltpu.SemaphoreType.DMA((7, planes)),
     ]
     return call(weight_kernel, outs, operands, "weights", 1e10, (0, 1, 2, 3, 4), scratch)
 

time: 45.3 us -> 45.2 us (level)
  no operation moved by 1% of the time
where the time goes in v17:
time: 45.2 us; the launch traced here: 44.8 us
  Pallas kernels  15.1 us (33%)
  starting transfers between devices  13.3 us (29%)
  blocking collectives  13 us (29%)
  waiting for transfers between devices  2.12 us (5%)
  local copies, waits for them, and re-layouts  1.07 us (2%)
    pallas_call x7, Pallas kernels, call(): pl.pallas_call(kernel, out_shape=shapes, in_specs=[pl.BlockSpec(memory_sp...  15.1 us
    all_gather x2, blocking collectives, local(): messages = lax.all_gather(message, 'sweep')  13 us
    ppermute x4, starting transfers between devices, swapped(): lax.ppermute(x, axis, [pair for i, j in pairs for pair in ((i, j), (j, i))])  7.43 us
    ppermute x2, starting transfers between devices, products(): lax.ppermute(x, 'sweep', [(i, i + step) for i in inner if 0 <= i + step <...  3.93 us
    ppermute x4, waiting for transfers between devices, swapped(): lax.ppermute(x, axis, [pair for i, j in pairs for pair in ((i, j), (j, i))])  2.11 us
    ppermute x1, starting transfers between devices, shift(): lax.ppermute(x, axis, [(i, i + by) for i in range(n) if 0 <= i + by < n])  1.97 us
    unnamed x12, local copies, waits for them, and re-layouts  1.07 us
  transfers between devices with their start and end apart: 7, of which 2 were waited for; matrix products, arithmetic and copies ran while one was open for 0% of the time, Pallas kernels for 22%

profile of v17, /device:TPU:1, one launch (start us, length us, event | category | flops | bytes accessed | tf_op | source)
XLA Modules:
  0.0 44.8 jit_solution(17253300118068612099)
XLA Ops:
  0.0 0.0 copy-start.4
  0.0 1.0 %copy-done.4 = bf16[4,8,32,135]{3,2,1,0:T(8,128)(2,1)S(1)} copy-done((bf16[4,8,32,135]{3,2,1,0:T(8,128)(2,1)S(1)}, bf16[4,8,32,135]{3,2,1,0:T(8,128)(2,1)}, u32[]{:S(2)}) %copy-start.4) | copy-done | bytes 276504
  1.0 0.4 initial_traces.1
  1.4 2.0 %collective-permute-start.2 = (bf16[48,256]{1,0:T(8,128)(2,1)S(1)}, bf16[48,256]{1,0:T(8,128)(2,1)S(1)}, u32[]{:S(2)}, u32[]{:S(2)}) collective-permute-start(bf16[48,256]{1,0:T(8,128)(2,1)S(1)} %get-tuple-element.37), channel_id=1, source_target_pairs={{8,0},{16,8},{24,16},{9,1},{17,9},{25,17},{10,2},{18,10},{26,18},{... | collective-permute-start | bytes 73736 | tf_op jit(solution)/shard_map/ppermute | solution.py:499
  3.4 2.8 %collective-permute-start = (bf16[304,256]{1,0:T(8,128)(2,1)S(1)}, bf16[304,256]{1,0:T(8,128)(2,1)S(1)}, u32[]{:S(2)}, u32[]{:S(2)}) collective-permute-start(bf16[304,256]{1,0:T(8,128)(2,1)S(1)} %get-tuple-element.35), channel_id=1, source_target_pairs={{0,1},{1,0},{2,3},{3,2},{4,5},{5,4},{6,7},{7,6},{8,9},{9,8},{10,11... | collective-permute-start | bytes 466952 | tf_op jit(solution)/shard_map/ppermute | solution.py:494
  6.1 3.3 %collective-permute-start.1 = (bf16[304,256]{1,0:T(8,128)(2,1)S(1)}, bf16[304,256]{1,0:T(8,128)(2,1)S(1)}, u32[]{:S(2)}, u32[]{:S(2)}) collective-permute-start(bf16[304,256]{1,0:T(8,128)(2,1)S(1)} %get-tuple-element.36), channel_id=1, source_target_pairs={{1,2},{2,1},{3,4},{4,3},{5,6},{6,5},{7,0},{0,7},{9,10},{10,9},{11,... | collective-permute-start | bytes 466952 | tf_op jit(solution)/shard_map/ppermute | solution.py:494
  9.4 0.0 copy-start.1
  9.4 0.0 copy-start.2
  9.4 7.8 %weights.1 = (bf16[4,8,144,256]{3,2,1,0:T(8,128)(2,1)S(1)}, bf16[4,2,192,256]{3,2,1,0:T(8,128)(2,1)S(1)}, f32[4,144,256]{2,1,0:T(8,128)S(1)}, bf16[4,144,256]{2,...) custom-call(bf16[4,135,8,135]{3,2,1,0:T(8,128)(2,1)} %bitcast.10, bf16[4,6,45,8,135]{4,3,2,1,0:T(8,128)(2,1)} %bitcast.9, ...), custom_call_target="tpu_custom_call" | custom-call | flops 10000000000 | bytes 8607040 | tf_op jit(solution)/shard_map/weights/pallas_call | solution.py:454
  17.3 0.0 collective-permute-done.2.above
  17.3 0.0 collective-permute-done.near
  17.3 0.0 collective-permute-done.1.far
  17.3 0.0 copy-done.1
  17.3 0.0 copy-done.2
  17.3 0.0 copy-start
  17.3 1.2 %forward_chain.1 = (f32[4,144,256]{2,1,0:T(8,128)S(1)}, f32[4,48,256]{2,1,0:T(8,128)S(1)}, bf16[144,256]{1,0:T(8,128)(2,1)S(1)}) custom-call(bf16[304,256]{1,0:T(8,128)(2,1)S(1)} %collective-permute-done.near, bf16[304,256]{1,0:T(8,128)(2,1)S(1)} %collective-permute-done.1.far, bf16[48,256]{1,0:T(8,128)(2,1)S(1)} %collective-permute-done.2.above, ...), custom_call_target="tpu_custom_call" | custom-call | flops 200000000 | bytes 5922816 | tf_op jit(solution)/shard_map/forward_chain/pallas_call | solution.py:454
  18.6 0.0 copy-start.5
  18.6 6.3 %all-gather = bf16[576,256]{1,0:T(8,128)(2,1)S(1)} all-gather(bf16[144,256]{1,0:T(8,128)(2,1)S(1)} %get-tuple-element.44), channel_id=2, replica_groups=mesh['sweep'=4,'cross'=8] {'sweep'}, dimensions={0}, use_global_device_ids=true | all-gather | bytes 368640 | tf_op jit(solution)/shard_map/all_gather | solution.py:536
  24.9 0.0 copy-done
  24.9 1.4 %forward_finish.1 = (bf16[4,144,256]{2,1,0:T(8,128)(2,1)S(1)}, f32[4,144,256]{2,1,0:T(8,128)S(1)}, bf16[304,256]{1,0:T(8,128)(2,1)S(1)}, bf16[304,256]{1,0:T(8,128)(2,1)S(1)}) custom-call(bf16[4,144,256]{2,1,0:T(8,128)(2,1)S(1)} %bitcast.7, f32[4,144,256]{2,1,0:T(8,128)S(1)} %get-tuple-element.45.part, f32[4,48,256]{2,1,0:T(8,128)S(1)} %get-tuple-element.46.traces, ...), custom_call_target="tpu_custom_call" | custom-call | flops 200000000 | bytes 3321856 | tf_op jit(solution)/shard_map/forward_finish/pallas_call | solution.py:454
  26.3 0.1 collective-permute-start.3
  26.4 1.3 %collective-permute-start.4 = (bf16[304,256]{1,0:T(8,128)(2,1)S(1)}, bf16[304,256]{1,0:T(8,128)(2,1)S(1)}, u32[]{:S(2)}, u32[]{:S(2)}) collective-permute-start(bf16[304,256]{1,0:T(8,128)(2,1)S(1)} %get-tuple-element.48), channel_id=1, source_target_pairs={{1,2},{2,1},{3,4},{4,3},{5,6},{6,5},{7,0},{0,7},{9,10},{10,9},{11,... | collective-permute-start | bytes 466952 | tf_op jit(solution)/shard_map/ppermute | solution.py:494
  27.7 0.0 copy-done.5
  27.7 0.8 %middle.1 = (bf16[4,96,256]{2,1,0:T(8,128)(2,1)S(1)}, f32[4,144,256]{2,1,0:T(8,128)S(1)}, bf16[4,2,192,256]{3,2,1,0:T(8,128)(2,1)S(1)}) custom-call(bf16[4,144,256]{2,1,0:T(8,128)(2,1)S(1)} %get-tuple-element.49.middle, f32[4,144,256]{2,1,0:T(8,128)S(1)} %get-tuple-element.50.change, f32[4,144,256]{2,1,0:T(8,128)S(1)} %get-tuple-element.43.base, ...), custom_call_target="tpu_custom_call" | custom-call | flops 2000000000 | bytes 5958656 | tf_op jit(solution)/shard_map/middle/pallas_call | solution.py:454
  28.5 0.7 %collective-permute-start.6 = (bf16[2,48,256]{2,1,0:T(8,128)(2,1)S(1)}, bf16[2,48,256]{2,1,0:T(8,128)(2,1)S(1)}, u32[]{:S(2)}, u32[]{:S(2)}) collective-permute-start(bf16[2,48,256]{2,1,0:T(8,128)(2,1)S(1)} %slice_bitcast_fusion), channel_id=1, source_target_pairs={{16,0},{17,1},{18,2},{19,3},{20,4},{21,5},{22,6},{23,7}} | collective-permute-start | bytes 147464 | tf_op jit(solution)/shard_map/ppermute | solution.py:470
  29.2 3.3 %collective-permute-start.5 = (bf16[2,48,256]{2,1,0:T(8,128)(2,1)S(1)}, bf16[2,48,256]{2,1,0:T(8,128)(2,1)S(1)}, u32[]{:S(2)}, u32[]{:S(2)}) collective-permute-start(bf16[2,48,256]{2,1,0:T(8,128)(2,1)S(1)} %slice_bitcast_fusion), channel_id=1, source_target_pairs={{8,0},{16,8},{9,1},{17,9},{10,2},{18,10},{11,3},{19,11},{12,4},{20... | collective-permute-start | bytes 147464 | tf_op jit(solution)/shard_map/ppermute | solution.py:470
  32.5 0.6 %collective-permute-done.3.near = bf16[304,256]{1,0:T(8,128)(2,1)S(1)} collective-permute-done((bf16[304,256]{1,0:T(8,128)(2,1)S(1)}, bf16[304,256]{1,0:T(8,128)(2,1)S(1)}, u32[]{:S(2)}, u32[]{:S(2)}) %collective-permute-start.3) | collective-permute-done | bytes 155680 | tf_op jit(solution)/shard_map/ppermute | solution.py:494
  33.1 1.5 %collective-permute-done.4.far = bf16[304,256]{1,0:T(8,128)(2,1)S(1)} collective-permute-done((bf16[304,256]{1,0:T(8,128)(2,1)S(1)}, bf16[304,256]{1,0:T(8,128)(2,1)S(1)}, u32[]{:S(2)}, u32[]{:S(2)}) %collective-permute-start.4) | collective-permute-done | bytes 155680 | tf_op jit(solution)/shard_map/ppermute | solution.py:494
  34.6 0.0 copy-start.3
  34.6 1.3 %backward_chain.1 = (f32[4,144,256]{2,1,0:T(8,128)S(1)}, f32[4,48,256]{2,1,0:T(8,128)S(1)}, bf16[48,256]{1,0:T(8,128)(2,1)S(1)}) custom-call(bf16[304,256]{1,0:T(8,128)(2,1)S(1)} %collective-permute-done.3.near, bf16[304,256]{1,0:T(8,128)(2,1)S(1)} %collective-permute-done.4.far, bf16[4,96,256]{2,1,0:T(8,128)(2,1)S(1)} %get-tuple-element.53.own, ...), custom_call_target="tpu_custom_call" | custom-call | flops 200000000 | bytes 5750784 | tf_op jit(solution)/shard_map/backward_chain/pallas_call | solution.py:454
  35.9 6.7 %all-gather.1 = bf16[192,256]{1,0:T(8,128)(2,1)S(1)} all-gather(bf16[48,256]{1,0:T(8,128)(2,1)S(1)} %get-tuple-element.55), channel_id=3, replica_groups=mesh['sweep'=4,'cross'=8] {'sweep'}, dimensions={0}, use_global_device_ids=true | all-gather | bytes 122880 | tf_op jit(solution)/shard_map/all_gather | solution.py:559
  42.6 0.0 collective-permute-done.6.next_near
  42.6 0.0 collective-permute-done.5.near
  42.6 0.0 copy-done.3
  42.6 2.2 %backward_finish.1 = bf16[4,8,32,135]{3,2,1,0:T(8,128)(2,1)} custom-call(bf16[4,48,256]{2,1,0:T(8,128)(2,1)S(1)} %bitcast.8, bf16[2,48,256]{2,1,0:T(8,128)(2,1)S(1)} %collective-permute-done.5.near, bf16[2,48,256]{2,1,0:T(8,128)(2,1)S(1)} %collective-permute-done.6.next_near, f32[4,144,256]{2,1,0:T(8,128)S(1)} %get-tuple-element.57.part, ...), custom_call_target="tpu_custom_call" | custom-call | flops 200000000 | bytes 2084832 | tf_op jit(solution)/shard_map/backward_finish/pallas_call | solution.py:454
  (1 shorter events, 0.0 us)
Async XLA Ops:
  0.0 1.0 %copy-start.4 = (bf16[4,8,32,135]{3,2,1,0:T(8,128)(2,1)S(1)}, bf16[4,8,32,135]{3,2,1,0:T(8,128)(2,1)}, u32[]{:S(2)}) copy-start(bf16[4,8,32,135]{3,2,1,0:T(8,128)(2,1)} %initial_there) | copy-start | bytes 829444
  1.4 15.8 %collective-permute-start.2 = (bf16[48,256]{1,0:T(8,128)(2,1)S(1)}, bf16[48,256]{1,0:T(8,128)(2,1)S(1)}, u32[]{:S(2)}, u32[]{:S(2)}) collective-permute-start(bf16[48,256]{1,0:T(8,128)(2,1)S(1)} %get-tuple-element.37), channel_id=1, source_target_pairs={{8,0},{16,8},{24,16},{9,1},{17,9},{25,17},{10,2},{18,10},{26,18},{... | collective-permute-start | bytes 73736 | tf_op jit(solution)/shard_map/ppermute | solution.py:499
  3.4 13.9 %collective-permute-start = (bf16[304,256]{1,0:T(8,128)(2,1)S(1)}, bf16[304,256]{1,0:T(8,128)(2,1)S(1)}, u32[]{:S(2)}, u32[]{:S(2)}) collective-permute-start(bf16[304,256]{1,0:T(8,128)(2,1)S(1)} %get-tuple-element.35), channel_id=1, source_target_pairs={{0,1},{1,0},{2,3},{3,2},{4,5},{5,4},{6,7},{7,6},{8,9},{9,8},{10,11... | collective-permute-start | bytes 466952 | tf_op jit(solution)/shard_map/ppermute | solution.py:494
  6.1 11.1 %collective-permute-start.1 = (bf16[304,256]{1,0:T(8,128)(2,1)S(1)}, bf16[304,256]{1,0:T(8,128)(2,1)S(1)}, u32[]{:S(2)}, u32[]{:S(2)}) collective-permute-start(bf16[304,256]{1,0:T(8,128)(2,1)S(1)} %get-tuple-element.36), channel_id=1, source_target_pairs={{1,2},{2,1},{3,4},{4,3},{5,6},{6,5},{7,0},{0,7},{9,10},{10,9},{11,... | collective-permute-start | bytes 466952 | tf_op jit(solution)/shard_map/ppermute | solution.py:494
  9.4 7.9 %copy-start.1 = (bf16[4,96,112]{2,1,0:T(8,128)(2,1)S(1)}, bf16[4,96,112]{2,1,0:T(8,128)(2,1)}, u32[]{:S(2)}) copy-start(bf16[4,96,112]{2,1,0:T(8,128)(2,1)} %constant.14.clone.down_sel) | copy-start | bytes 258052
  9.4 7.9 %copy-start.2 = (bf16[4,96,112]{2,1,0:T(8,128)(2,1)S(1)}, bf16[4,96,112]{2,1,0:T(8,128)(2,1)}, u32[]{:S(2)}) copy-start(bf16[4,96,112]{2,1,0:T(8,128)(2,1)} %constant.13.clone.up_sel) | copy-start | bytes 258052
  17.3 7.6 %copy-start = (bf16[4,224,144]{2,1,0:T(8,128)(2,1)S(1)}, bf16[4,224,144]{2,1,0:T(8,128)(2,1)}, u32[]{:S(2)}) copy-start(bf16[4,224,144]{2,1,0:T(8,128)(2,1)} %constant.10.clone.send) | copy-start | bytes 774148
  18.6 9.1 %copy-start.5 = (bf16[96,144]{1,0:T(8,128)(2,1)S(1)}, bf16[96,144]{1,0:T(8,128)(2,1)}, u32[]{:S(2)}) copy-start(bf16[96,144]{1,0:T(8,128)(2,1)} %constant.11.clone.own_sel) | copy-start | bytes 82948
  26.3 6.8 %collective-permute-start.3 = (bf16[304,256]{1,0:T(8,128)(2,1)S(1)}, bf16[304,256]{1,0:T(8,128)(2,1)S(1)}, u32[]{:S(2)}, u32[]{:S(2)}) collective-permute-start(bf16[304,256]{1,0:T(8,128)(2,1)S(1)} %get-tuple-element.47), channel_id=1, source_target_pairs={{0,1},{1,0},{2,3},{3,2},{4,5},{5,4},{6,7},{7,6},{8,9},{9,8},{10,11... | collective-permute-start | bytes 466952 | tf_op jit(solution)/shard_map/ppermute | solution.py:494
  26.4 8.2 %collective-permute-start.4 = (bf16[304,256]{1,0:T(8,128)(2,1)S(1)}, bf16[304,256]{1,0:T(8,128)(2,1)S(1)}, u32[]{:S(2)}, u32[]{:S(2)}) collective-permute-start(bf16[304,256]{1,0:T(8,128)(2,1)S(1)} %get-tuple-element.48), channel_id=1, source_target_pairs={{1,2},{2,1},{3,4},{4,3},{5,6},{6,5},{7,0},{0,7},{9,10},{10,9},{11,... | collective-permute-start | bytes 466952 | tf_op jit(solution)/shard_map/ppermute | solution.py:494
  28.5 14.0 %collective-permute-start.6 = (bf16[2,48,256]{2,1,0:T(8,128)(2,1)S(1)}, bf16[2,48,256]{2,1,0:T(8,128)(2,1)S(1)}, u32[]{:S(2)}, u32[]{:S(2)}) collective-permute-start(bf16[2,48,256]{2,1,0:T(8,128)(2,1)S(1)} %slice_bitcast_fusion), channel_id=1, source_target_pairs={{16,0},{17,1},{18,2},{19,3},{20,4},{21,5},{22,6},{23,7}} | collective-permute-start | bytes 147464 | tf_op jit(solution)/shard_map/ppermute | solution.py:470
  29.2 13.4 %collective-permute-start.5 = (bf16[2,48,256]{2,1,0:T(8,128)(2,1)S(1)}, bf16[2,48,256]{2,1,0:T(8,128)(2,1)S(1)}, u32[]{:S(2)}, u32[]{:S(2)}) collective-permute-start(bf16[2,48,256]{2,1,0:T(8,128)(2,1)S(1)} %slice_bitcast_fusion), channel_id=1, source_target_pairs={{8,0},{16,8},{9,1},{17,9},{10,2},{18,10},{11,3},{19,11},{12,4},{20... | collective-permute-start | bytes 147464 | tf_op jit(solution)/shard_map/ppermute | solution.py:470
  34.6 8.0 %copy-start.3 = (bf16[144,135]{1,0:T(8,128)(2,1)S(1)}, bf16[144,135]{1,0:T(8,128)(2,1)}, u32[]{:S(2)}) copy-start(bf16[144,135]{1,0:T(8,128)(2,1)} %constant.12.clone.back) | copy-start | bytes 116644

commit v18 on v16

--- a/solution.py
+++ b/solution.py
@@ -213,42 +213,39 @@
 
 
 def weight_kernel(
-    inverse, couplings, right, initial_there, neighbours_there,
+    inverse, couplings, right, initial, neighbours_there,
     known, lower, base, own, gathers,
-    inverse_in, couplings_in, right_in, initial, neighbours, solves, faces, raw, done,
+    inverse_in, couplings_in, right_in, neighbours, solves, faces, raw, done,
 ):
     planes, columns, rhs, width = initial.shape
     size = columns * rhs
     half = columns // 2
-    early = [
-        pltpu.make_async_copy(neighbours_there, neighbours, done.at[3, 0]),
-        pltpu.make_async_copy(initial_there, initial, done.at[3, 1]),
-    ]
+    early = pltpu.make_async_copy(neighbours_there, neighbours, done.at[3, 0])
+    early.start()
     copies = []
     for p in range(planes):
         pairs = ((inverse, inverse_in), (couplings, couplings_in), (right, right_in))
         copies.append([pltpu.make_async_copy(x.at[p], y.at[p], done.at[i, p]) for i, (x, y) in enumerate(pairs)])
-    for copy in early + sum(copies, []):
-        copy.start()
+        for copy in copies[p]:
+            copy.start()
     for start, stop in ((5 * FACE, 256), (256 + FACE, 256 + 2 * SLOT)):
         faces[:, :, start:stop] = jnp.zeros((2, columns, stop - start, 256), BF)
     raw[:, :, :, NT * columns :] = jnp.zeros((2, 9, 2, (FACE - NT) * columns, 128), F32)
-    for copy in early:
-        copy.wait()
+    own_table = [picks(c_target(rows_of(FACE), which), width) for which in (2, 0)]
+    first_table = picks(first_target(rows_of(FACE)), width)
+    fields = [initial[p].reshape(size, width) for p in range(planes)]
+    sides = [jnp.concatenate([mt(own_table[j], x).astype(BF) for x in fields], 0) for j in range(2)]
+    for p in range(planes):
+        own[p, LAST] = mt(first_table, fields[min(p + 1, planes - 1)]).astype(BF)
+    early.wait()
     source = sources(neighbours, columns, rhs)
     for i, start in enumerate((0, size)):
         for j in range(2):
             gathers[i, j] = one_hot(source[j], start, size)
-    own_table = [picks(c_target(rows_of(FACE), which), width) for which in (2, 0)]
-    first_table = picks(first_target(rows_of(FACE)), width)
-    fields = [initial[p].reshape(size, width) for p in range(planes)]
     for j in range(2):
-        mine = jnp.concatenate([mt(own_table[j], x).astype(BF) for x in fields], 0)
-        mine = mm(mine, gathers[1 - j, j]).astype(BF)
+        mine = mm(sides[j], gathers[1 - j, j]).astype(BF)
         for p in range(planes):
             own[p, j * FACE : (j + 1) * FACE] = mine[p * FACE : (p + 1) * FACE]
-    for p in range(planes):
-        own[p, LAST] = mt(first_table, fields[min(p + 1, planes - 1)]).astype(BF)
     lane = lax.broadcasted_iota(jnp.int32, (ROWS, 2 * SLOT), 1)
 
     def prepare(p):
@@ -270,11 +267,9 @@
 
             turned(couplings_in[p, f], raw.at[slot, 3 + f], put)
 
-    prepare(0)
     for p in range(planes):
         slot = p % 2
-        if p + 1 < planes:
-            prepare(p + 1)
+        prepare(p)
         bases, lowers = [], []
         before = None
         for c in range(columns):
@@ -474,14 +469,14 @@
     field = (planes, ROWS, size)
     outs = [((planes, columns, ROWS, 256), BF), (pack, BF), (field, F32), (field, BF), ((2, 2, size, size), BF)]
     operands = (inverse, couplings, right, initial, neighbours)
-    scratch = [pltpu.VMEM(x.shape, BF) for x in operands[:4]] + [
+    scratch = [pltpu.VMEM(x.shape, BF) for x in operands[:3]] + [
         pltpu.SMEM(neighbours.shape, jnp.int32),
         pltpu.VMEM((2, columns, ROWS, 256), BF),
         pltpu.VMEM((2, columns, 256 + 2 * SLOT, 256), BF),
         pltpu.VMEM((2, 9, 2, FACE * columns, 128), F32),
         pltpu.SemaphoreType.DMA((4, planes)),
     ]
-    return call(weight_kernel, outs, operands, "weights", 1e10, (0, 1, 2, 3, 4), scratch)
+    return call(weight_kernel, outs, operands, "weights", 1e10, (0, 1, 2, 4), scratch)
 
 
 def swapped(x, axis, first):

time: 45.3 us -> 44.3 us (0.978)
  Pallas kernels: 15.2 us -> 14.2 us
  waiting for transfers between devices: 2.16 us -> 1.2 us
  starting transfers between devices: 13.3 us -> 14.2 us
    pallas_call x7, Pallas kernels: 15.2 us -> 14.2 us  [call(): pl.pallas_call(kernel, out_shape=shapes, in_specs=[pl.BlockSpec(memory_sp...]
    ppermute x4, waiting for transfers between devices: 2.16 us -> 1.19 us  [swapped(): lax.ppermute(x, axis, [pair for i, j in pairs for pair in ((i, j), (j, i))])]
    ppermute x4, starting transfers between devices: 7.39 us -> 8.34 us  [swapped(): lax.ppermute(x, axis, [pair for i, j in pairs for pair in ((i, j), (j, i))])]
  transfers between devices with their start and end apart: 7 -> 7, of which waited for: 2 -> 1; matrix products, arithmetic and copies ran while one was open for 0% -> 0% of each run, Pallas kernels for 22% -> 20%
where the time goes in v18:
time: 44.3 us; the launch traced here: 43.9 us
  Pallas kernels  14.2 us (32%)
  starting transfers between devices  14.2 us (32%)
  blocking collectives  13 us (29%)
  waiting for transfers between devices  1.2 us (3%)
  local copies, waits for them, and re-layouts  1.07 us (2%)
    pallas_call x7, Pallas kernels, call(): pl.pallas_call(kernel, out_shape=shapes, in_specs=[pl.BlockSpec(memory_sp...  14.2 us
    all_gather x2, blocking collectives, local(): messages = lax.all_gather(message, 'sweep')  13 us
    ppermute x4, starting transfers between devices, swapped(): lax.ppermute(x, axis, [pair for i, j in pairs for pair in ((i, j), (j, i))])  8.34 us
    ppermute x2, starting transfers between devices, products(): lax.ppermute(x, 'sweep', [(i, i + step) for i in inner if 0 <= i + step <...  3.93 us
    ppermute x1, starting transfers between devices, shift(): lax.ppermute(x, axis, [(i, i + by) for i in range(n) if 0 <= i + by < n])  1.97 us
    ppermute x4, waiting for transfers between devices, swapped(): lax.ppermute(x, axis, [pair for i, j in pairs for pair in ((i, j), (j, i))])  1.19 us
    unnamed x12, local copies, waits for them, and re-layouts  1.07 us
  transfers between devices with their start and end apart: 7, of which 1 were waited for; matrix products, arithmetic and copies ran while one was open for 0% of the time, Pallas kernels for 20%

profile of v18, /device:TPU:1, one launch (start us, length us, event | category | flops | bytes accessed | tf_op | source)
XLA Modules:
  0.0 43.9 jit_solution(6069386995241274883)
XLA Ops:
  0.0 0.0 copy-start.4
  0.0 1.0 %copy-done.4 = bf16[4,8,32,135]{3,2,1,0:T(8,128)(2,1)S(1)} copy-done((bf16[4,8,32,135]{3,2,1,0:T(8,128)(2,1)S(1)}, bf16[4,8,32,135]{3,2,1,0:T(8,128)(2,1)}, u32[]{:S(2)}) %copy-start.4) | copy-done | bytes 276504
  1.0 0.4 initial_traces.1
  1.4 2.0 %collective-permute-start.2 = (bf16[48,256]{1,0:T(8,128)(2,1)S(1)}, bf16[48,256]{1,0:T(8,128)(2,1)S(1)}, u32[]{:S(2)}, u32[]{:S(2)}) collective-permute-start(bf16[48,256]{1,0:T(8,128)(2,1)S(1)} %get-tuple-element.37), channel_id=1, source_target_pairs={{8,0},{16,8},{24,16},{9,1},{17,9},{25,17},{10,2},{18,10},{26,18},{... | collective-permute-start | bytes 73736 | tf_op jit(solution)/shard_map/ppermute | solution.py:490
  3.4 2.8 %collective-permute-start = (bf16[304,256]{1,0:T(8,128)(2,1)S(1)}, bf16[304,256]{1,0:T(8,128)(2,1)S(1)}, u32[]{:S(2)}, u32[]{:S(2)}) collective-permute-start(bf16[304,256]{1,0:T(8,128)(2,1)S(1)} %get-tuple-element.35), channel_id=1, source_target_pairs={{0,1},{1,0},{2,3},{3,2},{4,5},{5,4},{6,7},{7,6},{8,9},{9,8},{10,11... | collective-permute-start | bytes 466952 | tf_op jit(solution)/shard_map/ppermute | solution.py:485
  6.1 3.3 %collective-permute-start.1 = (bf16[304,256]{1,0:T(8,128)(2,1)S(1)}, bf16[304,256]{1,0:T(8,128)(2,1)S(1)}, u32[]{:S(2)}, u32[]{:S(2)}) collective-permute-start(bf16[304,256]{1,0:T(8,128)(2,1)S(1)} %get-tuple-element.36), channel_id=1, source_target_pairs={{1,2},{2,1},{3,4},{4,3},{5,6},{6,5},{7,0},{0,7},{9,10},{10,9},{11,... | collective-permute-start | bytes 466952 | tf_op jit(solution)/shard_map/ppermute | solution.py:485
  9.4 0.0 copy-start.1
  9.4 0.0 copy-start.2
  9.4 6.9 %weights.1 = (bf16[4,8,144,256]{3,2,1,0:T(8,128)(2,1)S(1)}, bf16[4,2,192,256]{3,2,1,0:T(8,128)(2,1)S(1)}, f32[4,144,256]{2,1,0:T(8,128)S(1)}, bf16[4,144,256]{2,...) custom-call(bf16[4,135,8,135]{3,2,1,0:T(8,128)(2,1)} %bitcast.10, bf16[4,6,45,8,135]{4,3,2,1,0:T(8,128)(2,1)} %bitcast.9, ...), custom_call_target="tpu_custom_call" | custom-call | flops 10000000000 | bytes 8607040 | tf_op jit(solution)/shard_map/weights/pallas_call | solution.py:445
  16.3 0.0 collective-permute-done.2.above
  16.3 0.0 collective-permute-done.near
  16.3 0.0 collective-permute-done.1.far
  16.3 0.0 copy-done.1
  16.3 0.0 copy-done.2
  16.4 0.0 copy-start
  16.4 1.2 %forward_chain.1 = (f32[4,144,256]{2,1,0:T(8,128)S(1)}, f32[4,48,256]{2,1,0:T(8,128)S(1)}, bf16[144,256]{1,0:T(8,128)(2,1)S(1)}) custom-call(bf16[304,256]{1,0:T(8,128)(2,1)S(1)} %collective-permute-done.near, bf16[304,256]{1,0:T(8,128)(2,1)S(1)} %collective-permute-done.1.far, bf16[48,256]{1,0:T(8,128)(2,1)S(1)} %collective-permute-done.2.above, ...), custom_call_target="tpu_custom_call" | custom-call | flops 200000000 | bytes 5922816 | tf_op jit(solution)/shard_map/forward_chain/pallas_call | solution.py:445
  17.6 0.0 copy-start.5
  17.6 6.3 %all-gather = bf16[576,256]{1,0:T(8,128)(2,1)S(1)} all-gather(bf16[144,256]{1,0:T(8,128)(2,1)S(1)} %get-tuple-element.44), channel_id=2, replica_groups=mesh['sweep'=4,'cross'=8] {'sweep'}, dimensions={0}, use_global_device_ids=true | all-gather | bytes 368640 | tf_op jit(solution)/shard_map/all_gather | solution.py:527
  24.0 0.0 copy-done
  24.0 1.4 %forward_finish.1 = (bf16[4,144,256]{2,1,0:T(8,128)(2,1)S(1)}, f32[4,144,256]{2,1,0:T(8,128)S(1)}, bf16[304,256]{1,0:T(8,128)(2,1)S(1)}, bf16[304,256]{1,0:T(8,128)(2,1)S(1)}) custom-call(bf16[4,144,256]{2,1,0:T(8,128)(2,1)S(1)} %bitcast.7, f32[4,144,256]{2,1,0:T(8,128)S(1)} %get-tuple-element.45.part, f32[4,48,256]{2,1,0:T(8,128)S(1)} %get-tuple-element.46.traces, ...), custom_call_target="tpu_custom_call" | custom-call | flops 200000000 | bytes 3321856 | tf_op jit(solution)/shard_map/forward_finish/pallas_call | solution.py:445
  25.3 0.1 collective-permute-start.3
  25.4 2.3 %collective-permute-start.4 = (bf16[304,256]{1,0:T(8,128)(2,1)S(1)}, bf16[304,256]{1,0:T(8,128)(2,1)S(1)}, u32[]{:S(2)}, u32[]{:S(2)}) collective-permute-start(bf16[304,256]{1,0:T(8,128)(2,1)S(1)} %get-tuple-element.48), channel_id=1, source_target_pairs={{1,2},{2,1},{3,4},{4,3},{5,6},{6,5},{7,0},{0,7},{9,10},{10,9},{11,... | collective-permute-start | bytes 466952 | tf_op jit(solution)/shard_map/ppermute | solution.py:485
  27.7 0.0 copy-done.5
  27.7 0.8 %middle.1 = (bf16[4,96,256]{2,1,0:T(8,128)(2,1)S(1)}, f32[4,144,256]{2,1,0:T(8,128)S(1)}, bf16[4,2,192,256]{3,2,1,0:T(8,128)(2,1)S(1)}) custom-call(bf16[4,144,256]{2,1,0:T(8,128)(2,1)S(1)} %get-tuple-element.49.middle, f32[4,144,256]{2,1,0:T(8,128)S(1)} %get-tuple-element.50.change, f32[4,144,256]{2,1,0:T(8,128)S(1)} %get-tuple-element.43.base, ...), custom_call_target="tpu_custom_call" | custom-call | flops 2000000000 | bytes 5958656 | tf_op jit(solution)/shard_map/middle/pallas_call | solution.py:445
  28.5 0.7 %collective-permute-start.6 = (bf16[2,48,256]{2,1,0:T(8,128)(2,1)S(1)}, bf16[2,48,256]{2,1,0:T(8,128)(2,1)S(1)}, u32[]{:S(2)}, u32[]{:S(2)}) collective-permute-start(bf16[2,48,256]{2,1,0:T(8,128)(2,1)S(1)} %slice_bitcast_fusion), channel_id=1, source_target_pairs={{16,0},{17,1},{18,2},{19,3},{20,4},{21,5},{22,6},{23,7}} | collective-permute-start | bytes 147464 | tf_op jit(solution)/shard_map/ppermute | solution.py:461
  29.2 3.3 %collective-permute-start.5 = (bf16[2,48,256]{2,1,0:T(8,128)(2,1)S(1)}, bf16[2,48,256]{2,1,0:T(8,128)(2,1)S(1)}, u32[]{:S(2)}, u32[]{:S(2)}) collective-permute-start(bf16[2,48,256]{2,1,0:T(8,128)(2,1)S(1)} %slice_bitcast_fusion), channel_id=1, source_target_pairs={{8,0},{16,8},{9,1},{17,9},{10,2},{18,10},{11,3},{19,11},{12,4},{20... | collective-permute-start | bytes 147464 | tf_op jit(solution)/shard_map/ppermute | solution.py:461
  32.4 0.0 collective-permute-done.3.near
  32.4 1.2 %collective-permute-done.4.far = bf16[304,256]{1,0:T(8,128)(2,1)S(1)} collective-permute-done((bf16[304,256]{1,0:T(8,128)(2,1)S(1)}, bf16[304,256]{1,0:T(8,128)(2,1)S(1)}, u32[]{:S(2)}, u32[]{:S(2)}) %collective-permute-start.4) | collective-permute-done | bytes 155680 | tf_op jit(solution)/shard_map/ppermute | solution.py:485
  33.6 0.0 copy-start.3
  33.6 1.3 %backward_chain.1 = (f32[4,144,256]{2,1,0:T(8,128)S(1)}, f32[4,48,256]{2,1,0:T(8,128)S(1)}, bf16[48,256]{1,0:T(8,128)(2,1)S(1)}) custom-call(bf16[304,256]{1,0:T(8,128)(2,1)S(1)} %collective-permute-done.3.near, bf16[304,256]{1,0:T(8,128)(2,1)S(1)} %collective-permute-done.4.far, bf16[4,96,256]{2,1,0:T(8,128)(2,1)S(1)} %get-tuple-element.53.own, ...), custom_call_target="tpu_custom_call" | custom-call | flops 200000000 | bytes 5750784 | tf_op jit(solution)/shard_map/backward_chain/pallas_call | solution.py:445
  34.9 6.7 %all-gather.1 = bf16[192,256]{1,0:T(8,128)(2,1)S(1)} all-gather(bf16[48,256]{1,0:T(8,128)(2,1)S(1)} %get-tuple-element.55), channel_id=3, replica_groups=mesh['sweep'=4,'cross'=8] {'sweep'}, dimensions={0}, use_global_device_ids=true | all-gather | bytes 122880 | tf_op jit(solution)/shard_map/all_gather | solution.py:550
  41.6 0.0 collective-permute-done.6.next_near
  41.6 0.0 collective-permute-done.5.near
  41.6 0.0 copy-done.3
  41.6 2.2 %backward_finish.1 = bf16[4,8,32,135]{3,2,1,0:T(8,128)(2,1)} custom-call(bf16[4,48,256]{2,1,0:T(8,128)(2,1)S(1)} %bitcast.8, bf16[2,48,256]{2,1,0:T(8,128)(2,1)S(1)} %collective-permute-done.5.near, bf16[2,48,256]{2,1,0:T(8,128)(2,1)S(1)} %collective-permute-done.6.next_near, f32[4,144,256]{2,1,0:T(8,128)S(1)} %get-tuple-element.57.part, ...), custom_call_target="tpu_custom_call" | custom-call | flops 200000000 | bytes 2084832 | tf_op jit(solution)/shard_map/backward_finish/pallas_call | solution.py:445
  (1 shorter events, 0.0 us)
Async XLA Ops:
  0.0 1.0 %copy-start.4 = (bf16[4,8,32,135]{3,2,1,0:T(8,128)(2,1)S(1)}, bf16[4,8,32,135]{3,2,1,0:T(8,128)(2,1)}, u32[]{:S(2)}) copy-start(bf16[4,8,32,135]{3,2,1,0:T(8,128)(2,1)} %initial.2) | copy-start | bytes 829444
  1.4 14.9 %collective-permute-start.2 = (bf16[48,256]{1,0:T(8,128)(2,1)S(1)}, bf16[48,256]{1,0:T(8,128)(2,1)S(1)}, u32[]{:S(2)}, u32[]{:S(2)}) collective-permute-start(bf16[48,256]{1,0:T(8,128)(2,1)S(1)} %get-tuple-element.37), channel_id=1, source_target_pairs={{8,0},{16,8},{24,16},{9,1},{17,9},{25,17},{10,2},{18,10},{26,18},{... | collective-permute-start | bytes 73736 | tf_op jit(solution)/shard_map/ppermute | solution.py:490
  3.4 12.9 %collective-permute-start = (bf16[304,256]{1,0:T(8,128)(2,1)S(1)}, bf16[304,256]{1,0:T(8,128)(2,1)S(1)}, u32[]{:S(2)}, u32[]{:S(2)}) collective-permute-start(bf16[304,256]{1,0:T(8,128)(2,1)S(1)} %get-tuple-element.35), channel_id=1, source_target_pairs={{0,1},{1,0},{2,3},{3,2},{4,5},{5,4},{6,7},{7,6},{8,9},{9,8},{10,11... | collective-permute-start | bytes 466952 | tf_op jit(solution)/shard_map/ppermute | solution.py:485
  6.1 10.2 %collective-permute-start.1 = (bf16[304,256]{1,0:T(8,128)(2,1)S(1)}, bf16[304,256]{1,0:T(8,128)(2,1)S(1)}, u32[]{:S(2)}, u32[]{:S(2)}) collective-permute-start(bf16[304,256]{1,0:T(8,128)(2,1)S(1)} %get-tuple-element.36), channel_id=1, source_target_pairs={{1,2},{2,1},{3,4},{4,3},{5,6},{6,5},{7,0},{0,7},{9,10},{10,9},{11,... | collective-permute-start | bytes 466952 | tf_op jit(solution)/shard_map/ppermute | solution.py:485
  9.4 6.9 %copy-start.1 = (bf16[4,96,112]{2,1,0:T(8,128)(2,1)S(1)}, bf16[4,96,112]{2,1,0:T(8,128)(2,1)}, u32[]{:S(2)}) copy-start(bf16[4,96,112]{2,1,0:T(8,128)(2,1)} %constant.14.clone.down_sel) | copy-start | bytes 258052
  9.4 6.9 %copy-start.2 = (bf16[4,96,112]{2,1,0:T(8,128)(2,1)S(1)}, bf16[4,96,112]{2,1,0:T(8,128)(2,1)}, u32[]{:S(2)}) copy-start(bf16[4,96,112]{2,1,0:T(8,128)(2,1)} %constant.13.clone.up_sel) | copy-start | bytes 258052
  16.4 7.6 %copy-start = (bf16[4,224,144]{2,1,0:T(8,128)(2,1)S(1)}, bf16[4,224,144]{2,1,0:T(8,128)(2,1)}, u32[]{:S(2)}) copy-start(bf16[4,224,144]{2,1,0:T(8,128)(2,1)} %constant.10.clone.send) | copy-start | bytes 774148
  17.6 10.0 %copy-start.5 = (bf16[96,144]{1,0:T(8,128)(2,1)S(1)}, bf16[96,144]{1,0:T(8,128)(2,1)}, u32[]{:S(2)}) copy-start(bf16[96,144]{1,0:T(8,128)(2,1)} %constant.11.clone.own_sel) | copy-start | bytes 82948
  25.3 7.1 %collective-permute-start.3 = (bf16[304,256]{1,0:T(8,128)(2,1)S(1)}, bf16[304,256]{1,0:T(8,128)(2,1)S(1)}, u32[]{:S(2)}, u32[]{:S(2)}) collective-permute-start(bf16[304,256]{1,0:T(8,128)(2,1)S(1)} %get-tuple-element.47), channel_id=1, source_target_pairs={{0,1},{1,0},{2,3},{3,2},{4,5},{5,4},{6,7},{7,6},{8,9},{9,8},{10,11... | collective-permute-start | bytes 466952 | tf_op jit(solution)/shard_map/ppermute | solution.py:485
  25.4 8.2 %collective-permute-start.4 = (bf16[304,256]{1,0:T(8,128)(2,1)S(1)}, bf16[304,256]{1,0:T(8,128)(2,1)S(1)}, u32[]{:S(2)}, u32[]{:S(2)}) collective-permute-start(bf16[304,256]{1,0:T(8,128)(2,1)S(1)} %get-tuple-element.48), channel_id=1, source_target_pairs={{1,2},{2,1},{3,4},{4,3},{5,6},{6,5},{7,0},{0,7},{9,10},{10,9},{11,... | collective-permute-start | bytes 466952 | tf_op jit(solution)/shard_map/ppermute | solution.py:485
  28.5 13.1 %collective-permute-start.6 = (bf16[2,48,256]{2,1,0:T(8,128)(2,1)S(1)}, bf16[2,48,256]{2,1,0:T(8,128)(2,1)S(1)}, u32[]{:S(2)}, u32[]{:S(2)}) collective-permute-start(bf16[2,48,256]{2,1,0:T(8,128)(2,1)S(1)} %slice_bitcast_fusion), channel_id=1, source_target_pairs={{16,0},{17,1},{18,2},{19,3},{20,4},{21,5},{22,6},{23,7}} | collective-permute-start | bytes 147464 | tf_op jit(solution)/shard_map/ppermute | solution.py:461
  29.2 12.5 %collective-permute-start.5 = (bf16[2,48,256]{2,1,0:T(8,128)(2,1)S(1)}, bf16[2,48,256]{2,1,0:T(8,128)(2,1)S(1)}, u32[]{:S(2)}, u32[]{:S(2)}) collective-permute-start(bf16[2,48,256]{2,1,0:T(8,128)(2,1)S(1)} %slice_bitcast_fusion), channel_id=1, source_target_pairs={{8,0},{16,8},{9,1},{17,9},{10,2},{18,10},{11,3},{19,11},{12,4},{20... | collective-permute-start | bytes 147464 | tf_op jit(solution)/shard_map/ppermute | solution.py:461
  33.6 8.0 %copy-start.3 = (bf16[144,135]{1,0:T(8,128)(2,1)S(1)}, bf16[144,135]{1,0:T(8,128)(2,1)}, u32[]{:S(2)}) copy-start(bf16[144,135]{1,0:T(8,128)(2,1)} %constant.12.clone.back) | copy-start | bytes 116644

commit v19 on v18

--- a/solution.py
+++ b/solution.py
@@ -426,8 +426,10 @@
         whole = part[p] + chain_step(upper.at[p], trace, rhs, FULL)
         flat = lax.dot_general(whole.astype(BF), back[...], (((0,), (0,)), ((), ())), preferred_element_type=F32)
         results[p] = flat.astype(BF).reshape(columns, rhs, width)
-        copies.append(pltpu.make_async_copy(results.at[p], result.at[p], sem.at[p]))
-        copies[-1].start()
+        if p % 2 == 0:
+            pair = pl.ds(p, min(2, planes - p))
+            copies.append(pltpu.make_async_copy(results.at[pair], result.at[pair], sem.at[p]))
+            copies[-1].start()
         if p:
             trace = traces[p] + chain_step(upper.at[p], entry, rhs, PRODUCT)
     for copy in copies:

time: 44.3 us -> 44.3 us (level)
  no operation moved by 1% of the time
where the time goes in v19:
time: 44.3 us; the launch traced here: 43.9 us
  Pallas kernels  14.2 us (32%)
  starting transfers between devices  14.2 us (32%)
  blocking collectives  13 us (29%)
  waiting for transfers between devices  1.2 us (3%)
  local copies, waits for them, and re-layouts  1.07 us (2%)
    pallas_call x7, Pallas kernels, call(): pl.pallas_call(kernel, out_shape=shapes, in_specs=[pl.BlockSpec(memory_sp...  14.2 us
    all_gather x2, blocking collectives, local(): messages = lax.all_gather(message, 'sweep')  13 us
    ppermute x4, starting transfers between devices, swapped(): lax.ppermute(x, axis, [pair for i, j in pairs for pair in ((i, j), (j, i))])  8.34 us
    ppermute x2, starting transfers between devices, products(): lax.ppermute(x, 'sweep', [(i, i + step) for i in inner if 0 <= i + step <...  3.93 us
    ppermute x1, starting transfers between devices, shift(): lax.ppermute(x, axis, [(i, i + by) for i in range(n) if 0 <= i + by < n])  1.97 us
    ppermute x4, waiting for transfers between devices, swapped(): lax.ppermute(x, axis, [pair for i, j in pairs for pair in ((i, j), (j, i))])  1.19 us
    unnamed x12, local copies, waits for them, and re-layouts  1.07 us
  transfers between devices with their start and end apart: 7, of which 1 were waited for; matrix products, arithmetic and copies ran while one was open for 0% of the time, Pallas kernels for 20%

profile of v19, /device:TPU:1, one launch (start us, length us, event | category | flops | bytes accessed | tf_op | source)
XLA Modules:
  0.0 43.9 jit_solution(7281734128055408394)
XLA Ops:
  0.0 0.0 copy-start.4
  0.0 1.0 %copy-done.4 = bf16[4,8,32,135]{3,2,1,0:T(8,128)(2,1)S(1)} copy-done((bf16[4,8,32,135]{3,2,1,0:T(8,128)(2,1)S(1)}, bf16[4,8,32,135]{3,2,1,0:T(8,128)(2,1)}, u32[]{:S(2)}) %copy-start.4) | copy-done | bytes 276504
  1.0 0.4 initial_traces.1
  1.4 2.0 %collective-permute-start.2 = (bf16[48,256]{1,0:T(8,128)(2,1)S(1)}, bf16[48,256]{1,0:T(8,128)(2,1)S(1)}, u32[]{:S(2)}, u32[]{:S(2)}) collective-permute-start(bf16[48,256]{1,0:T(8,128)(2,1)S(1)} %get-tuple-element.37), channel_id=1, source_target_pairs={{8,0},{16,8},{24,16},{9,1},{17,9},{25,17},{10,2},{18,10},{26,18},{... | collective-permute-start | bytes 73736 | tf_op jit(solution)/shard_map/ppermute | solution.py:492
  3.4 2.8 %collective-permute-start = (bf16[304,256]{1,0:T(8,128)(2,1)S(1)}, bf16[304,256]{1,0:T(8,128)(2,1)S(1)}, u32[]{:S(2)}, u32[]{:S(2)}) collective-permute-start(bf16[304,256]{1,0:T(8,128)(2,1)S(1)} %get-tuple-element.35), channel_id=1, source_target_pairs={{0,1},{1,0},{2,3},{3,2},{4,5},{5,4},{6,7},{7,6},{8,9},{9,8},{10,11... | collective-permute-start | bytes 466952 | tf_op jit(solution)/shard_map/ppermute | solution.py:487
  6.1 3.3 %collective-permute-start.1 = (bf16[304,256]{1,0:T(8,128)(2,1)S(1)}, bf16[304,256]{1,0:T(8,128)(2,1)S(1)}, u32[]{:S(2)}, u32[]{:S(2)}) collective-permute-start(bf16[304,256]{1,0:T(8,128)(2,1)S(1)} %get-tuple-element.36), channel_id=1, source_target_pairs={{1,2},{2,1},{3,4},{4,3},{5,6},{6,5},{7,0},{0,7},{9,10},{10,9},{11,... | collective-permute-start | bytes 466952 | tf_op jit(solution)/shard_map/ppermute | solution.py:487
  9.4 0.0 copy-start.1
  9.4 0.0 copy-start.2
  9.4 6.9 %weights.1 = (bf16[4,8,144,256]{3,2,1,0:T(8,128)(2,1)S(1)}, bf16[4,2,192,256]{3,2,1,0:T(8,128)(2,1)S(1)}, f32[4,144,256]{2,1,0:T(8,128)S(1)}, bf16[4,144,256]{2,...) custom-call(bf16[4,135,8,135]{3,2,1,0:T(8,128)(2,1)} %bitcast.10, bf16[4,6,45,8,135]{4,3,2,1,0:T(8,128)(2,1)} %bitcast.9, ...), custom_call_target="tpu_custom_call" | custom-call | flops 10000000000 | bytes 8607040 | tf_op jit(solution)/shard_map/weights/pallas_call | solution.py:447
  16.3 0.0 collective-permute-done.2.above
  16.3 0.0 collective-permute-done.near
  16.3 0.0 collective-permute-done.1.far
  16.3 0.0 copy-done.1
  16.3 0.0 copy-done.2
  16.4 0.0 copy-start
  16.4 1.2 %forward_chain.1 = (f32[4,144,256]{2,1,0:T(8,128)S(1)}, f32[4,48,256]{2,1,0:T(8,128)S(1)}, bf16[144,256]{1,0:T(8,128)(2,1)S(1)}) custom-call(bf16[304,256]{1,0:T(8,128)(2,1)S(1)} %collective-permute-done.near, bf16[304,256]{1,0:T(8,128)(2,1)S(1)} %collective-permute-done.1.far, bf16[48,256]{1,0:T(8,128)(2,1)S(1)} %collective-permute-done.2.above, ...), custom_call_target="tpu_custom_call" | custom-call | flops 200000000 | bytes 5922816 | tf_op jit(solution)/shard_map/forward_chain/pallas_call | solution.py:447
  17.6 0.0 copy-start.5
  17.6 6.3 %all-gather = bf16[576,256]{1,0:T(8,128)(2,1)S(1)} all-gather(bf16[144,256]{1,0:T(8,128)(2,1)S(1)} %get-tuple-element.44), channel_id=2, replica_groups=mesh['sweep'=4,'cross'=8] {'sweep'}, dimensions={0}, use_global_device_ids=true | all-gather | bytes 368640 | tf_op jit(solution)/shard_map/all_gather | solution.py:529
  24.0 0.0 copy-done
  24.0 1.4 %forward_finish.1 = (bf16[4,144,256]{2,1,0:T(8,128)(2,1)S(1)}, f32[4,144,256]{2,1,0:T(8,128)S(1)}, bf16[304,256]{1,0:T(8,128)(2,1)S(1)}, bf16[304,256]{1,0:T(8,128)(2,1)S(1)}) custom-call(bf16[4,144,256]{2,1,0:T(8,128)(2,1)S(1)} %bitcast.7, f32[4,144,256]{2,1,0:T(8,128)S(1)} %get-tuple-element.45.part, f32[4,48,256]{2,1,0:T(8,128)S(1)} %get-tuple-element.46.traces, ...), custom_call_target="tpu_custom_call" | custom-call | flops 200000000 | bytes 3321856 | tf_op jit(solution)/shard_map/forward_finish/pallas_call | solution.py:447
  25.3 0.1 collective-permute-start.3
  25.4 2.3 %collective-permute-start.4 = (bf16[304,256]{1,0:T(8,128)(2,1)S(1)}, bf16[304,256]{1,0:T(8,128)(2,1)S(1)}, u32[]{:S(2)}, u32[]{:S(2)}) collective-permute-start(bf16[304,256]{1,0:T(8,128)(2,1)S(1)} %get-tuple-element.48), channel_id=1, source_target_pairs={{1,2},{2,1},{3,4},{4,3},{5,6},{6,5},{7,0},{0,7},{9,10},{10,9},{11,... | collective-permute-start | bytes 466952 | tf_op jit(solution)/shard_map/ppermute | solution.py:487
  27.7 0.0 copy-done.5
  27.7 0.8 %middle.1 = (bf16[4,96,256]{2,1,0:T(8,128)(2,1)S(1)}, f32[4,144,256]{2,1,0:T(8,128)S(1)}, bf16[4,2,192,256]{3,2,1,0:T(8,128)(2,1)S(1)}) custom-call(bf16[4,144,256]{2,1,0:T(8,128)(2,1)S(1)} %get-tuple-element.49.middle, f32[4,144,256]{2,1,0:T(8,128)S(1)} %get-tuple-element.50.change, f32[4,144,256]{2,1,0:T(8,128)S(1)} %get-tuple-element.43.base, ...), custom_call_target="tpu_custom_call" | custom-call | flops 2000000000 | bytes 5958656 | tf_op jit(solution)/shard_map/middle/pallas_call | solution.py:447
  28.5 0.7 %collective-permute-start.6 = (bf16[2,48,256]{2,1,0:T(8,128)(2,1)S(1)}, bf16[2,48,256]{2,1,0:T(8,128)(2,1)S(1)}, u32[]{:S(2)}, u32[]{:S(2)}) collective-permute-start(bf16[2,48,256]{2,1,0:T(8,128)(2,1)S(1)} %slice_bitcast_fusion), channel_id=1, source_target_pairs={{16,0},{17,1},{18,2},{19,3},{20,4},{21,5},{22,6},{23,7}} | collective-permute-start | bytes 147464 | tf_op jit(solution)/shard_map/ppermute | solution.py:463
  29.2 3.3 %collective-permute-start.5 = (bf16[2,48,256]{2,1,0:T(8,128)(2,1)S(1)}, bf16[2,48,256]{2,1,0:T(8,128)(2,1)S(1)}, u32[]{:S(2)}, u32[]{:S(2)}) collective-permute-start(bf16[2,48,256]{2,1,0:T(8,128)(2,1)S(1)} %slice_bitcast_fusion), channel_id=1, source_target_pairs={{8,0},{16,8},{9,1},{17,9},{10,2},{18,10},{11,3},{19,11},{12,4},{20... | collective-permute-start | bytes 147464 | tf_op jit(solution)/shard_map/ppermute | solution.py:463
  32.4 0.0 collective-permute-done.3.near
  32.4 1.2 %collective-permute-done.4.far = bf16[304,256]{1,0:T(8,128)(2,1)S(1)} collective-permute-done((bf16[304,256]{1,0:T(8,128)(2,1)S(1)}, bf16[304,256]{1,0:T(8,128)(2,1)S(1)}, u32[]{:S(2)}, u32[]{:S(2)}) %collective-permute-start.4) | collective-permute-done | bytes 155680 | tf_op jit(solution)/shard_map/ppermute | solution.py:487
  33.6 0.0 copy-start.3
  33.6 1.3 %backward_chain.1 = (f32[4,144,256]{2,1,0:T(8,128)S(1)}, f32[4,48,256]{2,1,0:T(8,128)S(1)}, bf16[48,256]{1,0:T(8,128)(2,1)S(1)}) custom-call(bf16[304,256]{1,0:T(8,128)(2,1)S(1)} %collective-permute-done.3.near, bf16[304,256]{1,0:T(8,128)(2,1)S(1)} %collective-permute-done.4.far, bf16[4,96,256]{2,1,0:T(8,128)(2,1)S(1)} %get-tuple-element.53.own, ...), custom_call_target="tpu_custom_call" | custom-call | flops 200000000 | bytes 5750784 | tf_op jit(solution)/shard_map/backward_chain/pallas_call | solution.py:447
  34.9 6.7 %all-gather.1 = bf16[192,256]{1,0:T(8,128)(2,1)S(1)} all-gather(bf16[48,256]{1,0:T(8,128)(2,1)S(1)} %get-tuple-element.55), channel_id=3, replica_groups=mesh['sweep'=4,'cross'=8] {'sweep'}, dimensions={0}, use_global_device_ids=true | all-gather | bytes 122880 | tf_op jit(solution)/shard_map/all_gather | solution.py:552
  41.6 0.0 collective-permute-done.6.next_near
  41.6 0.0 collective-permute-done.5.near
  41.6 0.0 copy-done.3
  41.6 2.3 %backward_finish.1 = bf16[4,8,32,135]{3,2,1,0:T(8,128)(2,1)} custom-call(bf16[4,48,256]{2,1,0:T(8,128)(2,1)S(1)} %bitcast.8, bf16[2,48,256]{2,1,0:T(8,128)(2,1)S(1)} %collective-permute-done.5.near, bf16[2,48,256]{2,1,0:T(8,128)(2,1)S(1)} %collective-permute-done.6.next_near, f32[4,144,256]{2,1,0:T(8,128)S(1)} %get-tuple-element.57.part, ...), custom_call_target="tpu_custom_call" | custom-call | flops 200000000 | bytes 2084832 | tf_op jit(solution)/shard_map/backward_finish/pallas_call | solution.py:447
  (1 shorter events, 0.0 us)
Async XLA Ops:
  0.0 1.0 %copy-start.4 = (bf16[4,8,32,135]{3,2,1,0:T(8,128)(2,1)S(1)}, bf16[4,8,32,135]{3,2,1,0:T(8,128)(2,1)}, u32[]{:S(2)}) copy-start(bf16[4,8,32,135]{3,2,1,0:T(8,128)(2,1)} %initial.2) | copy-start | bytes 829444
  1.4 14.9 %collective-permute-start.2 = (bf16[48,256]{1,0:T(8,128)(2,1)S(1)}, bf16[48,256]{1,0:T(8,128)(2,1)S(1)}, u32[]{:S(2)}, u32[]{:S(2)}) collective-permute-start(bf16[48,256]{1,0:T(8,128)(2,1)S(1)} %get-tuple-element.37), channel_id=1, source_target_pairs={{8,0},{16,8},{24,16},{9,1},{17,9},{25,17},{10,2},{18,10},{26,18},{... | collective-permute-start | bytes 73736 | tf_op jit(solution)/shard_map/ppermute | solution.py:492
  3.4 12.9 %collective-permute-start = (bf16[304,256]{1,0:T(8,128)(2,1)S(1)}, bf16[304,256]{1,0:T(8,128)(2,1)S(1)}, u32[]{:S(2)}, u32[]{:S(2)}) collective-permute-start(bf16[304,256]{1,0:T(8,128)(2,1)S(1)} %get-tuple-element.35), channel_id=1, source_target_pairs={{0,1},{1,0},{2,3},{3,2},{4,5},{5,4},{6,7},{7,6},{8,9},{9,8},{10,11... | collective-permute-start | bytes 466952 | tf_op jit(solution)/shard_map/ppermute | solution.py:487
  6.1 10.2 %collective-permute-start.1 = (bf16[304,256]{1,0:T(8,128)(2,1)S(1)}, bf16[304,256]{1,0:T(8,128)(2,1)S(1)}, u32[]{:S(2)}, u32[]{:S(2)}) collective-permute-start(bf16[304,256]{1,0:T(8,128)(2,1)S(1)} %get-tuple-element.36), channel_id=1, source_target_pairs={{1,2},{2,1},{3,4},{4,3},{5,6},{6,5},{7,0},{0,7},{9,10},{10,9},{11,... | collective-permute-start | bytes 466952 | tf_op jit(solution)/shard_map/ppermute | solution.py:487
  9.4 6.9 %copy-start.1 = (bf16[4,96,112]{2,1,0:T(8,128)(2,1)S(1)}, bf16[4,96,112]{2,1,0:T(8,128)(2,1)}, u32[]{:S(2)}) copy-start(bf16[4,96,112]{2,1,0:T(8,128)(2,1)} %constant.14.clone.down_sel) | copy-start | bytes 258052
  9.4 6.9 %copy-start.2 = (bf16[4,96,112]{2,1,0:T(8,128)(2,1)S(1)}, bf16[4,96,112]{2,1,0:T(8,128)(2,1)}, u32[]{:S(2)}) copy-start(bf16[4,96,112]{2,1,0:T(8,128)(2,1)} %constant.13.clone.up_sel) | copy-start | bytes 258052
  16.4 7.6 %copy-start = (bf16[4,224,144]{2,1,0:T(8,128)(2,1)S(1)}, bf16[4,224,144]{2,1,0:T(8,128)(2,1)}, u32[]{:S(2)}) copy-start(bf16[4,224,144]{2,1,0:T(8,128)(2,1)} %constant.10.clone.send) | copy-start | bytes 774148
  17.6 10.0 %copy-start.5 = (bf16[96,144]{1,0:T(8,128)(2,1)S(1)}, bf16[96,144]{1,0:T(8,128)(2,1)}, u32[]{:S(2)}) copy-start(bf16[96,144]{1,0:T(8,128)(2,1)} %constant.11.clone.own_sel) | copy-start | bytes 82948
  25.3 7.1 %collective-permute-start.3 = (bf16[304,256]{1,0:T(8,128)(2,1)S(1)}, bf16[304,256]{1,0:T(8,128)(2,1)S(1)}, u32[]{:S(2)}, u32[]{:S(2)}) collective-permute-start(bf16[304,256]{1,0:T(8,128)(2,1)S(1)} %get-tuple-element.47), channel_id=1, source_target_pairs={{0,1},{1,0},{2,3},{3,2},{4,5},{5,4},{6,7},{7,6},{8,9},{9,8},{10,11... | collective-permute-start | bytes 466952 | tf_op jit(solution)/shard_map/ppermute | solution.py:487
  25.4 8.2 %collective-permute-start.4 = (bf16[304,256]{1,0:T(8,128)(2,1)S(1)}, bf16[304,256]{1,0:T(8,128)(2,1)S(1)}, u32[]{:S(2)}, u32[]{:S(2)}) collective-permute-start(bf16[304,256]{1,0:T(8,128)(2,1)S(1)} %get-tuple-element.48), channel_id=1, source_target_pairs={{1,2},{2,1},{3,4},{4,3},{5,6},{6,5},{7,0},{0,7},{9,10},{10,9},{11,... | collective-permute-start | bytes 466952 | tf_op jit(solution)/shard_map/ppermute | solution.py:487
  28.5 13.1 %collective-permute-start.6 = (bf16[2,48,256]{2,1,0:T(8,128)(2,1)S(1)}, bf16[2,48,256]{2,1,0:T(8,128)(2,1)S(1)}, u32[]{:S(2)}, u32[]{:S(2)}) collective-permute-start(bf16[2,48,256]{2,1,0:T(8,128)(2,1)S(1)} %slice_bitcast_fusion), channel_id=1, source_target_pairs={{16,0},{17,1},{18,2},{19,3},{20,4},{21,5},{22,6},{23,7}} | collective-permute-start | bytes 147464 | tf_op jit(solution)/shard_map/ppermute | solution.py:463
  29.2 12.5 %collective-permute-start.5 = (bf16[2,48,256]{2,1,0:T(8,128)(2,1)S(1)}, bf16[2,48,256]{2,1,0:T(8,128)(2,1)S(1)}, u32[]{:S(2)}, u32[]{:S(2)}) collective-permute-start(bf16[2,48,256]{2,1,0:T(8,128)(2,1)S(1)} %slice_bitcast_fusion), channel_id=1, source_target_pairs={{8,0},{16,8},{9,1},{17,9},{10,2},{18,10},{11,3},{19,11},{12,4},{20... | collective-permute-start | bytes 147464 | tf_op jit(solution)/shard_map/ppermute | solution.py:463
  33.6 8.0 %copy-start.3 = (bf16[144,135]{1,0:T(8,128)(2,1)S(1)}, bf16[144,135]{1,0:T(8,128)(2,1)}, u32[]{:S(2)}) copy-start(bf16[144,135]{1,0:T(8,128)(2,1)} %constant.12.clone.back) | copy-start | bytes 116644

commit v20 on v18

--- a/solution.py
+++ b/solution.py
@@ -203,19 +203,15 @@
     put_shared(out, near, far)
 
 
-def turned(rows, raw, put):
-    count, columns, width = rows.shape
-    raw[0, : count * columns] = rows[:, :, :128].astype(F32).reshape(count * columns, 128)
-    rest = rows[:, :, 128:].astype(F32).reshape(count * columns, width - 128)
-    raw[1, : count * columns] = jnp.concatenate([rest, jnp.zeros((count * columns, 256 - width), F32)], 1)
-    for c in range(columns):
-        put(c, jnp.concatenate([raw[i, pl.ds(c, FACE, stride=columns), :] for i in range(2)], 1))
+def turned(rows):
+    pad = jnp.zeros((FACE - NT,) + rows.shape[1:], rows.dtype)
+    return jnp.swapaxes(jnp.concatenate([rows, pad], 0), 0, 1)
 
 
 def weight_kernel(
     inverse, couplings, right, initial, neighbours_there,
     known, lower, base, own, gathers,
-    inverse_in, couplings_in, right_in, neighbours, solves, faces, raw, done,
+    inverse_in, couplings_in, right_in, neighbours, solves, faces, done,
 ):
     planes, columns, rhs, width = initial.shape
     size = columns * rhs
@@ -230,7 +226,8 @@
             copy.start()
     for start, stop in ((5 * FACE, 256), (256 + FACE, 256 + 2 * SLOT)):
         faces[:, :, start:stop] = jnp.zeros((2, columns, stop - start, 256), BF)
-    raw[:, :, :, NT * columns :] = jnp.zeros((2, 9, 2, (FACE - NT) * columns, 128), F32)
+    faces[:, :, :, 128:] = jnp.zeros(faces.shape[:3] + (128,), BF)
+    solves[:, :, :, 128:] = jnp.zeros(solves.shape[:3] + (128,), BF)
     own_table = [picks(c_target(rows_of(FACE), which), width) for which in (2, 0)]
     first_table = picks(first_target(rows_of(FACE)), width)
     fields = [initial[p].reshape(size, width) for p in range(planes)]
@@ -255,17 +252,9 @@
         faces[slot, :, 256 + SLOT : 256 + SLOT + rhs, :width] = right_in[p]
         for a in range(3):
             rows = [inverse_in[p, v * 27 + a * 9 : v * 27 + a * 9 + 9] for v in range(5)]
-
-            def put(c, value):
-                solves[slot, c, a * FACE : (a + 1) * FACE] = (-value).astype(BF)
-
-            turned(jnp.concatenate(rows, 0), raw.at[slot, a], put)
+            solves[slot, :, a * FACE : (a + 1) * FACE, :width] = -turned(jnp.concatenate(rows, 0))
         for f, place in enumerate((256, 4 * FACE, 0, FACE, 2 * FACE, 3 * FACE)):
-
-            def put(c, value):
-                faces[slot, c, place : place + FACE] = value.astype(BF)
-
-            turned(couplings_in[p, f], raw.at[slot, 3 + f], put)
+            faces[slot, :, place : place + FACE, :width] = turned(couplings_in[p, f])
 
     for p in range(planes):
         slot = p % 2
@@ -473,7 +462,6 @@
         pltpu.SMEM(neighbours.shape, jnp.int32),
         pltpu.VMEM((2, columns, ROWS, 256), BF),
         pltpu.VMEM((2, columns, 256 + 2 * SLOT, 256), BF),
-        pltpu.VMEM((2, 9, 2, FACE * columns, 128), F32),
         pltpu.SemaphoreType.DMA((4, planes)),
     ]
     return call(weight_kernel, outs, operands, "weights", 1e10, (0, 1, 2, 4), scratch)

time: 44.3 us -> 43.3 us (0.977)
  waiting for transfers between devices: 1.2 us -> 0.02 us
  Pallas kernels: 14.2 us -> 13.2 us
  starting transfers between devices: 14.2 us -> 15.2 us
    ppermute x4, waiting for transfers between devices: 1.19 us -> 0.01 us  [swapped(): lax.ppermute(x, axis, [pair for i, j in pairs for pair in ((i, j), (j, i))])]
    pallas_call x7, Pallas kernels: 14.2 us -> 13.2 us  [call(): pl.pallas_call(kernel, out_shape=shapes, in_specs=[pl.BlockSpec(memory_sp...]
    ppermute x4, starting transfers between devices: 8.34 us -> 9.33 us  [swapped(): lax.ppermute(x, axis, [pair for i, j in pairs for pair in ((i, j), (j, i))])]
  transfers between devices with their start and end apart: 7 -> 7, of which waited for: 1 -> 0; matrix products, arithmetic and copies ran while one was open for 0% -> 0% of each run, Pallas kernels for 20% -> 19%
where the time goes in v20:
time: 43.3 us; the launch traced here: 42.9 us
  starting transfers between devices  15.2 us (35%)
  Pallas kernels  13.2 us (30%)
  blocking collectives  13.2 us (30%)
  local copies, waits for them, and re-layouts  1.07 us (2%)
    all_gather x2, blocking collectives, local(): messages = lax.all_gather(message, 'sweep')  13.2 us
    pallas_call x7, Pallas kernels, call(): pl.pallas_call(kernel, out_shape=shapes, in_specs=[pl.BlockSpec(memory_sp...  13.2 us
    ppermute x4, starting transfers between devices, swapped(): lax.ppermute(x, axis, [pair for i, j in pairs for pair in ((i, j), (j, i))])  9.33 us
    ppermute x2, starting transfers between devices, products(): lax.ppermute(x, 'sweep', [(i, i + step) for i in inner if 0 <= i + step <...  3.93 us
    ppermute x1, starting transfers between devices, shift(): lax.ppermute(x, axis, [(i, i + by) for i in range(n) if 0 <= i + by < n])  1.97 us
    unnamed x12, local copies, waits for them, and re-layouts  1.07 us
  transfers between devices with their start and end apart: 7, of which 0 were waited for; matrix products, arithmetic and copies ran while one was open for 0% of the time, Pallas kernels for 19%

profile of v20, /device:TPU:1, one launch (start us, length us, event | category | flops | bytes accessed | tf_op | source)
XLA Modules:
  0.0 42.9 jit_solution(2561197434388906303)
XLA Ops:
  0.0 0.0 copy-start.4
  0.0 1.0 %copy-done.4 = bf16[4,8,32,135]{3,2,1,0:T(8,128)(2,1)S(1)} copy-done((bf16[4,8,32,135]{3,2,1,0:T(8,128)(2,1)S(1)}, bf16[4,8,32,135]{3,2,1,0:T(8,128)(2,1)}, u32[]{:S(2)}) %copy-start.4) | copy-done | bytes 276504
  1.0 0.4 initial_traces.1
  1.4 2.0 %collective-permute-start.2 = (bf16[48,256]{1,0:T(8,128)(2,1)S(1)}, bf16[48,256]{1,0:T(8,128)(2,1)S(1)}, u32[]{:S(2)}, u32[]{:S(2)}) collective-permute-start(bf16[48,256]{1,0:T(8,128)(2,1)S(1)} %get-tuple-element.37), channel_id=1, source_target_pairs={{8,0},{16,8},{24,16},{9,1},{17,9},{25,17},{10,2},{18,10},{26,18},{... | collective-permute-start | bytes 73736 | tf_op jit(solution)/shard_map/ppermute | solution.py:478
  3.4 2.8 %collective-permute-start = (bf16[304,256]{1,0:T(8,128)(2,1)S(1)}, bf16[304,256]{1,0:T(8,128)(2,1)S(1)}, u32[]{:S(2)}, u32[]{:S(2)}) collective-permute-start(bf16[304,256]{1,0:T(8,128)(2,1)S(1)} %get-tuple-element.35), channel_id=1, source_target_pairs={{0,1},{1,0},{2,3},{3,2},{4,5},{5,4},{6,7},{7,6},{8,9},{9,8},{10,11... | collective-permute-start | bytes 466952 | tf_op jit(solution)/shard_map/ppermute | solution.py:473
  6.1 3.3 %collective-permute-start.1 = (bf16[304,256]{1,0:T(8,128)(2,1)S(1)}, bf16[304,256]{1,0:T(8,128)(2,1)S(1)}, u32[]{:S(2)}, u32[]{:S(2)}) collective-permute-start(bf16[304,256]{1,0:T(8,128)(2,1)S(1)} %get-tuple-element.36), channel_id=1, source_target_pairs={{1,2},{2,1},{3,4},{4,3},{5,6},{6,5},{7,0},{0,7},{9,10},{10,9},{11,... | collective-permute-start | bytes 466952 | tf_op jit(solution)/shard_map/ppermute | solution.py:473
  9.4 0.0 copy-start.1
  9.4 0.0 copy-start.2
  9.4 5.9 %weights.1 = (bf16[4,8,144,256]{3,2,1,0:T(8,128)(2,1)S(1)}, bf16[4,2,192,256]{3,2,1,0:T(8,128)(2,1)S(1)}, f32[4,144,256]{2,1,0:T(8,128)S(1)}, bf16[4,144,256]{2,...) custom-call(bf16[4,135,8,135]{3,2,1,0:T(8,128)(2,1)} %bitcast.10, bf16[4,6,45,8,135]{4,3,2,1,0:T(8,128)(2,1)} %bitcast.9, ...), custom_call_target="tpu_custom_call" | custom-call | flops 10000000000 | bytes 8607040 | tf_op jit(solution)/shard_map/weights/pallas_call | solution.py:434
  15.3 0.0 collective-permute-done.2.above
  15.3 0.0 collective-permute-done.near
  15.3 0.0 collective-permute-done.1.far
  15.3 0.0 copy-done.1
  15.3 0.0 copy-done.2
  15.3 0.0 copy-start
  15.3 1.2 %forward_chain.1 = (f32[4,144,256]{2,1,0:T(8,128)S(1)}, f32[4,48,256]{2,1,0:T(8,128)S(1)}, bf16[144,256]{1,0:T(8,128)(2,1)S(1)}) custom-call(bf16[304,256]{1,0:T(8,128)(2,1)S(1)} %collective-permute-done.near, bf16[304,256]{1,0:T(8,128)(2,1)S(1)} %collective-permute-done.1.far, bf16[48,256]{1,0:T(8,128)(2,1)S(1)} %collective-permute-done.2.above, ...), custom_call_target="tpu_custom_call" | custom-call | flops 200000000 | bytes 5922816 | tf_op jit(solution)/shard_map/forward_chain/pallas_call | solution.py:434
  16.6 0.0 copy-start.5
  16.6 6.4 %all-gather = bf16[576,256]{1,0:T(8,128)(2,1)S(1)} all-gather(bf16[144,256]{1,0:T(8,128)(2,1)S(1)} %get-tuple-element.44), channel_id=2, replica_groups=mesh['sweep'=4,'cross'=8] {'sweep'}, dimensions={0}, use_global_device_ids=true | all-gather | bytes 368640 | tf_op jit(solution)/shard_map/all_gather | solution.py:515
  23.0 0.0 copy-done
  23.0 1.4 %forward_finish.1 = (bf16[4,144,256]{2,1,0:T(8,128)(2,1)S(1)}, f32[4,144,256]{2,1,0:T(8,128)S(1)}, bf16[304,256]{1,0:T(8,128)(2,1)S(1)}, bf16[304,256]{1,0:T(8,128)(2,1)S(1)}) custom-call(bf16[4,144,256]{2,1,0:T(8,128)(2,1)S(1)} %bitcast.7, f32[4,144,256]{2,1,0:T(8,128)S(1)} %get-tuple-element.45.part, f32[4,48,256]{2,1,0:T(8,128)S(1)} %get-tuple-element.46.traces, ...), custom_call_target="tpu_custom_call" | custom-call | flops 200000000 | bytes 3321856 | tf_op jit(solution)/shard_map/forward_finish/pallas_call | solution.py:434
  24.3 0.1 collective-permute-start.3
  24.4 3.2 %collective-permute-start.4 = (bf16[304,256]{1,0:T(8,128)(2,1)S(1)}, bf16[304,256]{1,0:T(8,128)(2,1)S(1)}, u32[]{:S(2)}, u32[]{:S(2)}) collective-permute-start(bf16[304,256]{1,0:T(8,128)(2,1)S(1)} %get-tuple-element.48), channel_id=1, source_target_pairs={{1,2},{2,1},{3,4},{4,3},{5,6},{6,5},{7,0},{0,7},{9,10},{10,9},{11,... | collective-permute-start | bytes 466952 | tf_op jit(solution)/shard_map/ppermute | solution.py:473
  27.7 0.0 copy-done.5
  27.7 0.8 %middle.1 = (bf16[4,96,256]{2,1,0:T(8,128)(2,1)S(1)}, f32[4,144,256]{2,1,0:T(8,128)S(1)}, bf16[4,2,192,256]{3,2,1,0:T(8,128)(2,1)S(1)}) custom-call(bf16[4,144,256]{2,1,0:T(8,128)(2,1)S(1)} %get-tuple-element.49.middle, f32[4,144,256]{2,1,0:T(8,128)S(1)} %get-tuple-element.50.change, f32[4,144,256]{2,1,0:T(8,128)S(1)} %get-tuple-element.43.base, ...), custom_call_target="tpu_custom_call" | custom-call | flops 2000000000 | bytes 5958656 | tf_op jit(solution)/shard_map/middle/pallas_call | solution.py:434
  28.5 0.7 %collective-permute-start.6 = (bf16[2,48,256]{2,1,0:T(8,128)(2,1)S(1)}, bf16[2,48,256]{2,1,0:T(8,128)(2,1)S(1)}, u32[]{:S(2)}, u32[]{:S(2)}) collective-permute-start(bf16[2,48,256]{2,1,0:T(8,128)(2,1)S(1)} %slice_bitcast_fusion), channel_id=1, source_target_pairs={{16,0},{17,1},{18,2},{19,3},{20,4},{21,5},{22,6},{23,7}} | collective-permute-start | bytes 147464 | tf_op jit(solution)/shard_map/ppermute | solution.py:450
  29.2 3.3 %collective-permute-start.5 = (bf16[2,48,256]{2,1,0:T(8,128)(2,1)S(1)}, bf16[2,48,256]{2,1,0:T(8,128)(2,1)S(1)}, u32[]{:S(2)}, u32[]{:S(2)}) collective-permute-start(bf16[2,48,256]{2,1,0:T(8,128)(2,1)S(1)} %slice_bitcast_fusion), channel_id=1, source_target_pairs={{8,0},{16,8},{9,1},{17,9},{10,2},{18,10},{11,3},{19,11},{12,4},{20... | collective-permute-start | bytes 147464 | tf_op jit(solution)/shard_map/ppermute | solution.py:450
  32.4 0.0 collective-permute-done.3.near
  32.4 0.0 collective-permute-done.4.far
  32.5 0.0 copy-start.3
  32.5 1.3 %backward_chain.1 = (f32[4,144,256]{2,1,0:T(8,128)S(1)}, f32[4,48,256]{2,1,0:T(8,128)S(1)}, bf16[48,256]{1,0:T(8,128)(2,1)S(1)}) custom-call(bf16[304,256]{1,0:T(8,128)(2,1)S(1)} %collective-permute-done.3.near, bf16[304,256]{1,0:T(8,128)(2,1)S(1)} %collective-permute-done.4.far, bf16[4,96,256]{2,1,0:T(8,128)(2,1)S(1)} %get-tuple-element.53.own, ...), custom_call_target="tpu_custom_call" | custom-call | flops 200000000 | bytes 5750784 | tf_op jit(solution)/shard_map/backward_chain/pallas_call | solution.py:434
  33.8 6.9 %all-gather.1 = bf16[192,256]{1,0:T(8,128)(2,1)S(1)} all-gather(bf16[48,256]{1,0:T(8,128)(2,1)S(1)} %get-tuple-element.55), channel_id=3, replica_groups=mesh['sweep'=4,'cross'=8] {'sweep'}, dimensions={0}, use_global_device_ids=true | all-gather | bytes 122880 | tf_op jit(solution)/shard_map/all_gather | solution.py:538
  40.6 0.0 collective-permute-done.6.next_near
  40.6 0.0 collective-permute-done.5.near
  40.6 0.0 copy-done.3
  40.6 2.2 %backward_finish.1 = bf16[4,8,32,135]{3,2,1,0:T(8,128)(2,1)} custom-call(bf16[4,48,256]{2,1,0:T(8,128)(2,1)S(1)} %bitcast.8, bf16[2,48,256]{2,1,0:T(8,128)(2,1)S(1)} %collective-permute-done.5.near, bf16[2,48,256]{2,1,0:T(8,128)(2,1)S(1)} %collective-permute-done.6.next_near, f32[4,144,256]{2,1,0:T(8,128)S(1)} %get-tuple-element.57.part, ...), custom_call_target="tpu_custom_call" | custom-call | flops 200000000 | bytes 2084832 | tf_op jit(solution)/shard_map/backward_finish/pallas_call | solution.py:434
  (1 shorter events, 0.0 us)
Async XLA Ops:
  0.0 1.0 %copy-start.4 = (bf16[4,8,32,135]{3,2,1,0:T(8,128)(2,1)S(1)}, bf16[4,8,32,135]{3,2,1,0:T(8,128)(2,1)}, u32[]{:S(2)}) copy-start(bf16[4,8,32,135]{3,2,1,0:T(8,128)(2,1)} %initial.2) | copy-start | bytes 829444
  1.4 13.9 %collective-permute-start.2 = (bf16[48,256]{1,0:T(8,128)(2,1)S(1)}, bf16[48,256]{1,0:T(8,128)(2,1)S(1)}, u32[]{:S(2)}, u32[]{:S(2)}) collective-permute-start(bf16[48,256]{1,0:T(8,128)(2,1)S(1)} %get-tuple-element.37), channel_id=1, source_target_pairs={{8,0},{16,8},{24,16},{9,1},{17,9},{25,17},{10,2},{18,10},{26,18},{... | collective-permute-start | bytes 73736 | tf_op jit(solution)/shard_map/ppermute | solution.py:478
  3.4 11.9 %collective-permute-start = (bf16[304,256]{1,0:T(8,128)(2,1)S(1)}, bf16[304,256]{1,0:T(8,128)(2,1)S(1)}, u32[]{:S(2)}, u32[]{:S(2)}) collective-permute-start(bf16[304,256]{1,0:T(8,128)(2,1)S(1)} %get-tuple-element.35), channel_id=1, source_target_pairs={{0,1},{1,0},{2,3},{3,2},{4,5},{5,4},{6,7},{7,6},{8,9},{9,8},{10,11... | collective-permute-start | bytes 466952 | tf_op jit(solution)/shard_map/ppermute | solution.py:473
  6.1 9.2 %collective-permute-start.1 = (bf16[304,256]{1,0:T(8,128)(2,1)S(1)}, bf16[304,256]{1,0:T(8,128)(2,1)S(1)}, u32[]{:S(2)}, u32[]{:S(2)}) collective-permute-start(bf16[304,256]{1,0:T(8,128)(2,1)S(1)} %get-tuple-element.36), channel_id=1, source_target_pairs={{1,2},{2,1},{3,4},{4,3},{5,6},{6,5},{7,0},{0,7},{9,10},{10,9},{11,... | collective-permute-start | bytes 466952 | tf_op jit(solution)/shard_map/ppermute | solution.py:473
  9.4 5.9 %copy-start.1 = (bf16[4,96,112]{2,1,0:T(8,128)(2,1)S(1)}, bf16[4,96,112]{2,1,0:T(8,128)(2,1)}, u32[]{:S(2)}) copy-start(bf16[4,96,112]{2,1,0:T(8,128)(2,1)} %constant.14.clone.down_sel) | copy-start | bytes 258052
  9.4 5.9 %copy-start.2 = (bf16[4,96,112]{2,1,0:T(8,128)(2,1)S(1)}, bf16[4,96,112]{2,1,0:T(8,128)(2,1)}, u32[]{:S(2)}) copy-start(bf16[4,96,112]{2,1,0:T(8,128)(2,1)} %constant.13.clone.up_sel) | copy-start | bytes 258052
  15.3 7.6 %copy-start = (bf16[4,224,144]{2,1,0:T(8,128)(2,1)S(1)}, bf16[4,224,144]{2,1,0:T(8,128)(2,1)}, u32[]{:S(2)}) copy-start(bf16[4,224,144]{2,1,0:T(8,128)(2,1)} %constant.10.clone.send) | copy-start | bytes 774148
  16.6 11.1 %copy-start.5 = (bf16[96,144]{1,0:T(8,128)(2,1)S(1)}, bf16[96,144]{1,0:T(8,128)(2,1)}, u32[]{:S(2)}) copy-start(bf16[96,144]{1,0:T(8,128)(2,1)} %constant.11.clone.own_sel) | copy-start | bytes 82948
  24.3 8.1 %collective-permute-start.3 = (bf16[304,256]{1,0:T(8,128)(2,1)S(1)}, bf16[304,256]{1,0:T(8,128)(2,1)S(1)}, u32[]{:S(2)}, u32[]{:S(2)}) collective-permute-start(bf16[304,256]{1,0:T(8,128)(2,1)S(1)} %get-tuple-element.47), channel_id=1, source_target_pairs={{0,1},{1,0},{2,3},{3,2},{4,5},{5,4},{6,7},{7,6},{8,9},{9,8},{10,11... | collective-permute-start | bytes 466952 | tf_op jit(solution)/shard_map/ppermute | solution.py:473
  24.4 8.0 %collective-permute-start.4 = (bf16[304,256]{1,0:T(8,128)(2,1)S(1)}, bf16[304,256]{1,0:T(8,128)(2,1)S(1)}, u32[]{:S(2)}, u32[]{:S(2)}) collective-permute-start(bf16[304,256]{1,0:T(8,128)(2,1)S(1)} %get-tuple-element.48), channel_id=1, source_target_pairs={{1,2},{2,1},{3,4},{4,3},{5,6},{6,5},{7,0},{0,7},{9,10},{10,9},{11,... | collective-permute-start | bytes 466952 | tf_op jit(solution)/shard_map/ppermute | solution.py:473
  28.5 12.2 %collective-permute-start.6 = (bf16[2,48,256]{2,1,0:T(8,128)(2,1)S(1)}, bf16[2,48,256]{2,1,0:T(8,128)(2,1)S(1)}, u32[]{:S(2)}, u32[]{:S(2)}) collective-permute-start(bf16[2,48,256]{2,1,0:T(8,128)(2,1)S(1)} %slice_bitcast_fusion), channel_id=1, source_target_pairs={{16,0},{17,1},{18,2},{19,3},{20,4},{21,5},{22,6},{23,7}} | collective-permute-start | bytes 147464 | tf_op jit(solution)/shard_map/ppermute | solution.py:450
  29.2 11.5 %collective-permute-start.5 = (bf16[2,48,256]{2,1,0:T(8,128)(2,1)S(1)}, bf16[2,48,256]{2,1,0:T(8,128)(2,1)S(1)}, u32[]{:S(2)}, u32[]{:S(2)}) collective-permute-start(bf16[2,48,256]{2,1,0:T(8,128)(2,1)S(1)} %slice_bitcast_fusion), channel_id=1, source_target_pairs={{8,0},{16,8},{9,1},{17,9},{10,2},{18,10},{11,3},{19,11},{12,4},{20... | collective-permute-start | bytes 147464 | tf_op jit(solution)/shard_map/ppermute | solution.py:450
  32.5 8.2 %copy-start.3 = (bf16[144,135]{1,0:T(8,128)(2,1)S(1)}, bf16[144,135]{1,0:T(8,128)(2,1)}, u32[]{:S(2)}) copy-start(bf16[144,135]{1,0:T(8,128)(2,1)} %constant.12.clone.back) | copy-start | bytes 116644

commit v21 on v20

--- a/solution.py
+++ b/solution.py
@@ -256,9 +256,19 @@
         for f, place in enumerate((256, 4 * FACE, 0, FACE, 2 * FACE, 3 * FACE)):
             faces[slot, :, place : place + FACE, :width] = turned(couplings_in[p, f])
 
+    totals = [None, None]
+
+    def carry(q):
+        for h in range(2):
+            step = lower[q, h, LAST]
+            totals[h] = mm(step, split_lanes(totals[h], SLOT)) if q else step.astype(F32)
+            lower[q, h, PRODUCT] = totals[h].astype(BF)
+
     for p in range(planes):
         slot = p % 2
         prepare(p)
+        if p:
+            carry(p - 1)
         bases, lowers = [], []
         before = None
         for c in range(columns):
@@ -275,7 +285,7 @@
             lanes = slice(h * half * rhs, (h + 1) * half * rhs)
             lower[p, h, :ROWS] = jnp.concatenate(lowers[2 * h : 2 * h + 2], 1)
             base[p, :, lanes] = -own_lanes(bases[h * half : (h + 1) * half], rhs)
-    chain_products(lower, LAST, range(planes))
+    carry(planes - 1)
 
 
 def chain_products(matrix, rows, order):

time: 43.3 us -> 43 us (level)
  transfers between devices with their start and end apart: 7 -> 7, of which waited for: 0 -> 0; matrix products, arithmetic and copies ran while one was open for 0% -> 0% of each run, Pallas kernels for 19% -> 18%
where the time goes in v21:
time: 43 us; the launch traced here: 42.6 us
  starting transfers between devices  15.5 us (36%)
  blocking collectives  13 us (30%)
  Pallas kernels  12.9 us (30%)
  local copies, waits for them, and re-layouts  1.07 us (2%)
    all_gather x2, blocking collectives, local(): messages = lax.all_gather(message, 'sweep')  13 us
    pallas_call x7, Pallas kernels, call(): pl.pallas_call(kernel, out_shape=shapes, in_specs=[pl.BlockSpec(memory_sp...  12.9 us
    ppermute x4, starting transfers between devices, swapped(): lax.ppermute(x, axis, [pair for i, j in pairs for pair in ((i, j), (j, i))])  9.57 us
    ppermute x2, starting transfers between devices, products(): lax.ppermute(x, 'sweep', [(i, i + step) for i in inner if 0 <= i + step <...  3.93 us
    ppermute x1, starting transfers between devices, shift(): lax.ppermute(x, axis, [(i, i + by) for i in range(n) if 0 <= i + by < n])  1.97 us
    unnamed x12, local copies, waits for them, and re-layouts  1.07 us
  transfers between devices with their start and end apart: 7, of which 0 were waited for; matrix products, arithmetic and copies ran while one was open for 0% of the time, Pallas kernels for 18%

profile of v21, /device:TPU:1, one launch (start us, length us, event | category | flops | bytes accessed | tf_op | source)
XLA Modules:
  0.0 42.6 jit_solution(818488589436425438)
XLA Ops:
  0.0 0.0 copy-start.4
  0.0 1.0 %copy-done.4 = bf16[4,8,32,135]{3,2,1,0:T(8,128)(2,1)S(1)} copy-done((bf16[4,8,32,135]{3,2,1,0:T(8,128)(2,1)S(1)}, bf16[4,8,32,135]{3,2,1,0:T(8,128)(2,1)}, u32[]{:S(2)}) %copy-start.4) | copy-done | bytes 276504
  1.0 0.4 initial_traces.1
  1.4 2.0 %collective-permute-start.2 = (bf16[48,256]{1,0:T(8,128)(2,1)S(1)}, bf16[48,256]{1,0:T(8,128)(2,1)S(1)}, u32[]{:S(2)}, u32[]{:S(2)}) collective-permute-start(bf16[48,256]{1,0:T(8,128)(2,1)S(1)} %get-tuple-element.37), channel_id=1, source_target_pairs={{8,0},{16,8},{24,16},{9,1},{17,9},{25,17},{10,2},{18,10},{26,18},{... | collective-permute-start | bytes 73736 | tf_op jit(solution)/shard_map/ppermute | solution.py:488
  3.4 2.8 %collective-permute-start = (bf16[304,256]{1,0:T(8,128)(2,1)S(1)}, bf16[304,256]{1,0:T(8,128)(2,1)S(1)}, u32[]{:S(2)}, u32[]{:S(2)}) collective-permute-start(bf16[304,256]{1,0:T(8,128)(2,1)S(1)} %get-tuple-element.35), channel_id=1, source_target_pairs={{0,1},{1,0},{2,3},{3,2},{4,5},{5,4},{6,7},{7,6},{8,9},{9,8},{10,11... | collective-permute-start | bytes 466952 | tf_op jit(solution)/shard_map/ppermute | solution.py:483
  6.1 3.3 %collective-permute-start.1 = (bf16[304,256]{1,0:T(8,128)(2,1)S(1)}, bf16[304,256]{1,0:T(8,128)(2,1)S(1)}, u32[]{:S(2)}, u32[]{:S(2)}) collective-permute-start(bf16[304,256]{1,0:T(8,128)(2,1)S(1)} %get-tuple-element.36), channel_id=1, source_target_pairs={{1,2},{2,1},{3,4},{4,3},{5,6},{6,5},{7,0},{0,7},{9,10},{10,9},{11,... | collective-permute-start | bytes 466952 | tf_op jit(solution)/shard_map/ppermute | solution.py:483
  9.4 0.0 copy-start.1
  9.4 0.0 copy-start.2
  9.4 5.6 %weights.1 = (bf16[4,8,144,256]{3,2,1,0:T(8,128)(2,1)S(1)}, bf16[4,2,192,256]{3,2,1,0:T(8,128)(2,1)S(1)}, f32[4,144,256]{2,1,0:T(8,128)S(1)}, bf16[4,144,256]{2,...) custom-call(bf16[4,135,8,135]{3,2,1,0:T(8,128)(2,1)} %bitcast.10, bf16[4,6,45,8,135]{4,3,2,1,0:T(8,128)(2,1)} %bitcast.9, ...), custom_call_target="tpu_custom_call" | custom-call | flops 10000000000 | bytes 8607040 | tf_op jit(solution)/shard_map/weights/pallas_call | solution.py:444
  15.0 0.0 collective-permute-done.2.above
  15.0 0.0 collective-permute-done.near
  15.1 0.0 collective-permute-done.1.far
  15.1 0.0 copy-done.1
  15.1 0.0 copy-done.2
  15.1 0.0 copy-start
  15.1 1.3 %forward_chain.1 = (f32[4,144,256]{2,1,0:T(8,128)S(1)}, f32[4,48,256]{2,1,0:T(8,128)S(1)}, bf16[144,256]{1,0:T(8,128)(2,1)S(1)}) custom-call(bf16[304,256]{1,0:T(8,128)(2,1)S(1)} %collective-permute-done.near, bf16[304,256]{1,0:T(8,128)(2,1)S(1)} %collective-permute-done.1.far, bf16[48,256]{1,0:T(8,128)(2,1)S(1)} %collective-permute-done.2.above, ...), custom_call_target="tpu_custom_call" | custom-call | flops 200000000 | bytes 5922816 | tf_op jit(solution)/shard_map/forward_chain/pallas_call | solution.py:444
  16.4 0.0 copy-start.5
  16.4 6.4 %all-gather = bf16[576,256]{1,0:T(8,128)(2,1)S(1)} all-gather(bf16[144,256]{1,0:T(8,128)(2,1)S(1)} %get-tuple-element.44), channel_id=2, replica_groups=mesh['sweep'=4,'cross'=8] {'sweep'}, dimensions={0}, use_global_device_ids=true | all-gather | bytes 368640 | tf_op jit(solution)/shard_map/all_gather | solution.py:525
  22.7 0.0 copy-done
  22.7 1.4 %forward_finish.1 = (bf16[4,144,256]{2,1,0:T(8,128)(2,1)S(1)}, f32[4,144,256]{2,1,0:T(8,128)S(1)}, bf16[304,256]{1,0:T(8,128)(2,1)S(1)}, bf16[304,256]{1,0:T(8,128)(2,1)S(1)}) custom-call(bf16[4,144,256]{2,1,0:T(8,128)(2,1)S(1)} %bitcast.7, f32[4,144,256]{2,1,0:T(8,128)S(1)} %get-tuple-element.45.part, f32[4,48,256]{2,1,0:T(8,128)S(1)} %get-tuple-element.46.traces, ...), custom_call_target="tpu_custom_call" | custom-call | flops 200000000 | bytes 3321856 | tf_op jit(solution)/shard_map/forward_finish/pallas_call | solution.py:444
  24.1 0.3 collective-permute-start.3
  24.4 3.2 %collective-permute-start.4 = (bf16[304,256]{1,0:T(8,128)(2,1)S(1)}, bf16[304,256]{1,0:T(8,128)(2,1)S(1)}, u32[]{:S(2)}, u32[]{:S(2)}) collective-permute-start(bf16[304,256]{1,0:T(8,128)(2,1)S(1)} %get-tuple-element.48), channel_id=1, source_target_pairs={{1,2},{2,1},{3,4},{4,3},{5,6},{6,5},{7,0},{0,7},{9,10},{10,9},{11,... | collective-permute-start | bytes 466952 | tf_op jit(solution)/shard_map/ppermute | solution.py:483
  27.7 0.0 copy-done.5
  27.7 0.8 %middle.1 = (bf16[4,96,256]{2,1,0:T(8,128)(2,1)S(1)}, f32[4,144,256]{2,1,0:T(8,128)S(1)}, bf16[4,2,192,256]{3,2,1,0:T(8,128)(2,1)S(1)}) custom-call(bf16[4,144,256]{2,1,0:T(8,128)(2,1)S(1)} %get-tuple-element.49.middle, f32[4,144,256]{2,1,0:T(8,128)S(1)} %get-tuple-element.50.change, f32[4,144,256]{2,1,0:T(8,128)S(1)} %get-tuple-element.43.base, ...), custom_call_target="tpu_custom_call" | custom-call | flops 2000000000 | bytes 5958656 | tf_op jit(solution)/shard_map/middle/pallas_call | solution.py:444
  28.5 0.7 %collective-permute-start.6 = (bf16[2,48,256]{2,1,0:T(8,128)(2,1)S(1)}, bf16[2,48,256]{2,1,0:T(8,128)(2,1)S(1)}, u32[]{:S(2)}, u32[]{:S(2)}) collective-permute-start(bf16[2,48,256]{2,1,0:T(8,128)(2,1)S(1)} %slice_bitcast_fusion), channel_id=1, source_target_pairs={{16,0},{17,1},{18,2},{19,3},{20,4},{21,5},{22,6},{23,7}} | collective-permute-start | bytes 147464 | tf_op jit(solution)/shard_map/ppermute | solution.py:460
  29.2 3.3 %collective-permute-start.5 = (bf16[2,48,256]{2,1,0:T(8,128)(2,1)S(1)}, bf16[2,48,256]{2,1,0:T(8,128)(2,1)S(1)}, u32[]{:S(2)}, u32[]{:S(2)}) collective-permute-start(bf16[2,48,256]{2,1,0:T(8,128)(2,1)S(1)} %slice_bitcast_fusion), channel_id=1, source_target_pairs={{8,0},{16,8},{9,1},{17,9},{10,2},{18,10},{11,3},{19,11},{12,4},{20... | collective-permute-start | bytes 147464 | tf_op jit(solution)/shard_map/ppermute | solution.py:460
  32.4 0.0 collective-permute-done.3.near
  32.4 0.0 collective-permute-done.4.far
  32.5 0.0 copy-start.3
  32.5 1.3 %backward_chain.1 = (f32[4,144,256]{2,1,0:T(8,128)S(1)}, f32[4,48,256]{2,1,0:T(8,128)S(1)}, bf16[48,256]{1,0:T(8,128)(2,1)S(1)}) custom-call(bf16[304,256]{1,0:T(8,128)(2,1)S(1)} %collective-permute-done.3.near, bf16[304,256]{1,0:T(8,128)(2,1)S(1)} %collective-permute-done.4.far, bf16[4,96,256]{2,1,0:T(8,128)(2,1)S(1)} %get-tuple-element.53.own, ...), custom_call_target="tpu_custom_call" | custom-call | flops 200000000 | bytes 5750784 | tf_op jit(solution)/shard_map/backward_chain/pallas_call | solution.py:444
  33.8 6.6 %all-gather.1 = bf16[192,256]{1,0:T(8,128)(2,1)S(1)} all-gather(bf16[48,256]{1,0:T(8,128)(2,1)S(1)} %get-tuple-element.55), channel_id=3, replica_groups=mesh['sweep'=4,'cross'=8] {'sweep'}, dimensions={0}, use_global_device_ids=true | all-gather | bytes 122880 | tf_op jit(solution)/shard_map/all_gather | solution.py:548
  40.4 0.0 collective-permute-done.6.next_near
  40.4 0.0 collective-permute-done.5.near
  40.4 0.0 copy-done.3
  40.4 2.2 %backward_finish.1 = bf16[4,8,32,135]{3,2,1,0:T(8,128)(2,1)} custom-call(bf16[4,48,256]{2,1,0:T(8,128)(2,1)S(1)} %bitcast.8, bf16[2,48,256]{2,1,0:T(8,128)(2,1)S(1)} %collective-permute-done.5.near, bf16[2,48,256]{2,1,0:T(8,128)(2,1)S(1)} %collective-permute-done.6.next_near, f32[4,144,256]{2,1,0:T(8,128)S(1)} %get-tuple-element.57.part, ...), custom_call_target="tpu_custom_call" | custom-call | flops 200000000 | bytes 2084832 | tf_op jit(solution)/shard_map/backward_finish/pallas_call | solution.py:444
  (1 shorter events, 0.0 us)
Async XLA Ops:
  0.0 1.0 %copy-start.4 = (bf16[4,8,32,135]{3,2,1,0:T(8,128)(2,1)S(1)}, bf16[4,8,32,135]{3,2,1,0:T(8,128)(2,1)}, u32[]{:S(2)}) copy-start(bf16[4,8,32,135]{3,2,1,0:T(8,128)(2,1)} %initial.2) | copy-start | bytes 829444
  1.4 13.6 %collective-permute-start.2 = (bf16[48,256]{1,0:T(8,128)(2,1)S(1)}, bf16[48,256]{1,0:T(8,128)(2,1)S(1)}, u32[]{:S(2)}, u32[]{:S(2)}) collective-permute-start(bf16[48,256]{1,0:T(8,128)(2,1)S(1)} %get-tuple-element.37), channel_id=1, source_target_pairs={{8,0},{16,8},{24,16},{9,1},{17,9},{25,17},{10,2},{18,10},{26,18},{... | collective-permute-start | bytes 73736 | tf_op jit(solution)/shard_map/ppermute | solution.py:488
  3.4 11.7 %collective-permute-start = (bf16[304,256]{1,0:T(8,128)(2,1)S(1)}, bf16[304,256]{1,0:T(8,128)(2,1)S(1)}, u32[]{:S(2)}, u32[]{:S(2)}) collective-permute-start(bf16[304,256]{1,0:T(8,128)(2,1)S(1)} %get-tuple-element.35), channel_id=1, source_target_pairs={{0,1},{1,0},{2,3},{3,2},{4,5},{5,4},{6,7},{7,6},{8,9},{9,8},{10,11... | collective-permute-start | bytes 466952 | tf_op jit(solution)/shard_map/ppermute | solution.py:483
  6.1 8.9 %collective-permute-start.1 = (bf16[304,256]{1,0:T(8,128)(2,1)S(1)}, bf16[304,256]{1,0:T(8,128)(2,1)S(1)}, u32[]{:S(2)}, u32[]{:S(2)}) collective-permute-start(bf16[304,256]{1,0:T(8,128)(2,1)S(1)} %get-tuple-element.36), channel_id=1, source_target_pairs={{1,2},{2,1},{3,4},{4,3},{5,6},{6,5},{7,0},{0,7},{9,10},{10,9},{11,... | collective-permute-start | bytes 466952 | tf_op jit(solution)/shard_map/ppermute | solution.py:483
  9.4 5.7 %copy-start.1 = (bf16[4,96,112]{2,1,0:T(8,128)(2,1)S(1)}, bf16[4,96,112]{2,1,0:T(8,128)(2,1)}, u32[]{:S(2)}) copy-start(bf16[4,96,112]{2,1,0:T(8,128)(2,1)} %constant.14.clone.down_sel) | copy-start | bytes 258052
  9.4 5.7 %copy-start.2 = (bf16[4,96,112]{2,1,0:T(8,128)(2,1)S(1)}, bf16[4,96,112]{2,1,0:T(8,128)(2,1)}, u32[]{:S(2)}) copy-start(bf16[4,96,112]{2,1,0:T(8,128)(2,1)} %constant.13.clone.up_sel) | copy-start | bytes 258052
  15.1 7.6 %copy-start = (bf16[4,224,144]{2,1,0:T(8,128)(2,1)S(1)}, bf16[4,224,144]{2,1,0:T(8,128)(2,1)}, u32[]{:S(2)}) copy-start(bf16[4,224,144]{2,1,0:T(8,128)(2,1)} %constant.10.clone.send) | copy-start | bytes 774148
  16.4 11.3 %copy-start.5 = (bf16[96,144]{1,0:T(8,128)(2,1)S(1)}, bf16[96,144]{1,0:T(8,128)(2,1)}, u32[]{:S(2)}) copy-start(bf16[96,144]{1,0:T(8,128)(2,1)} %constant.11.clone.own_sel) | copy-start | bytes 82948
  24.1 8.3 %collective-permute-start.3 = (bf16[304,256]{1,0:T(8,128)(2,1)S(1)}, bf16[304,256]{1,0:T(8,128)(2,1)S(1)}, u32[]{:S(2)}, u32[]{:S(2)}) collective-permute-start(bf16[304,256]{1,0:T(8,128)(2,1)S(1)} %get-tuple-element.47), channel_id=1, source_target_pairs={{0,1},{1,0},{2,3},{3,2},{4,5},{5,4},{6,7},{7,6},{8,9},{9,8},{10,11... | collective-permute-start | bytes 466952 | tf_op jit(solution)/shard_map/ppermute | solution.py:483
  24.4 8.0 %collective-permute-start.4 = (bf16[304,256]{1,0:T(8,128)(2,1)S(1)}, bf16[304,256]{1,0:T(8,128)(2,1)S(1)}, u32[]{:S(2)}, u32[]{:S(2)}) collective-permute-start(bf16[304,256]{1,0:T(8,128)(2,1)S(1)} %get-tuple-element.48), channel_id=1, source_target_pairs={{1,2},{2,1},{3,4},{4,3},{5,6},{6,5},{7,0},{0,7},{9,10},{10,9},{11,... | collective-permute-start | bytes 466952 | tf_op jit(solution)/shard_map/ppermute | solution.py:483
  28.5 11.9 %collective-permute-start.6 = (bf16[2,48,256]{2,1,0:T(8,128)(2,1)S(1)}, bf16[2,48,256]{2,1,0:T(8,128)(2,1)S(1)}, u32[]{:S(2)}, u32[]{:S(2)}) collective-permute-start(bf16[2,48,256]{2,1,0:T(8,128)(2,1)S(1)} %slice_bitcast_fusion), channel_id=1, source_target_pairs={{16,0},{17,1},{18,2},{19,3},{20,4},{21,5},{22,6},{23,7}} | collective-permute-start | bytes 147464 | tf_op jit(solution)/shard_map/ppermute | solution.py:460
  29.2 11.2 %collective-permute-start.5 = (bf16[2,48,256]{2,1,0:T(8,128)(2,1)S(1)}, bf16[2,48,256]{2,1,0:T(8,128)(2,1)S(1)}, u32[]{:S(2)}, u32[]{:S(2)}) collective-permute-start(bf16[2,48,256]{2,1,0:T(8,128)(2,1)S(1)} %slice_bitcast_fusion), channel_id=1, source_target_pairs={{8,0},{16,8},{9,1},{17,9},{10,2},{18,10},{11,3},{19,11},{12,4},{20... | collective-permute-start | bytes 147464 | tf_op jit(solution)/shard_map/ppermute | solution.py:460
  32.5 7.9 %copy-start.3 = (bf16[144,135]{1,0:T(8,128)(2,1)S(1)}, bf16[144,135]{1,0:T(8,128)(2,1)}, u32[]{:S(2)}) copy-start(bf16[144,135]{1,0:T(8,128)(2,1)} %constant.12.clone.back) | copy-start | bytes 116644
